TPU v7x, 128 devices: a whole 4x4x4 slice. The times are simulated.
128 devices in a mesh: row: 16 (over x, y), vec: 8 (over z, core).
Axes of the slice: x: 4, y: 4, z: 4, core: 2. Of those that a mesh axis runs over, the one named last changes fastest.
Arguments:
- ham_tiles: bfloat16 [1024, 4, 128, 128], P('row'), may hold values from -0.125 to 0.125
- tile_columns: int32 [1024, 4], P('row'), may hold values from 0 to 1023, as said below
- stack_lengths: int32 [16], P('row'), may hold values from 32 to 64, as said below
- start_vectors: bfloat16 [131072, 1024], P('row', 'vec'), may hold values from -6 to 6
- spectral_scale: float32 [1], replicated, may hold values from 4 to 16
Outputs:
- filtered_basis: bfloat16 [131072, 1024], P('row', 'vec')
Inputs may be any that keep to these rules, and one draw needn't show every extreme that they name: `tile_columns`: row b lists 4 distinct block columns; the first is b itself, the others are (b + o) mod 1024 with nonzero offsets o from -2 to 2. Some stack holds 64 occupied block rows and some other stack exactly half of 64; a stack's occupied rows are its first stack_lengths - 2 and its last 2 block rows.
All inputs are finite; a program needn't handle non-finite values.
Results may differ from a plain program's by a relative error of at most 0.006.
The roundings to bfloat16 on the way count: a program that leaves them out, or rounds other values in their place, can miss the bound.
Values may be sent and summed in bfloat16 or wider, within the bound.
No kernel may reach another device: no remote copies, remote signals or barrier semaphores. Data moves between devices by JAX's collectives and lax.ppermute only.
A program may use at most 128 MiB of HBM per device.

v0:
```python
import jax
import jax.numpy as jnp
from jax import lax
from jax.sharding import PartitionSpec as P

REACH = 2
CHEB = 6
NS_ITERS = 2


def with_halo(block, sides, width):
    for axis, dim in sides:
        count = lax.axis_size(axis)
        forward = [(i, i + 1) for i in range(count - 1)]
        forward.append((count - 1, 0))
        backward = [(target, source) for source, target in forward]
        low = lax.ppermute(
            lax.slice_in_dim(block, block.shape[dim] - width, None, axis=dim), axis, forward
        )
        high = lax.ppermute(lax.slice_in_dim(block, 0, width, axis=dim), axis, backward)
        block = jnp.concatenate([low, block, high], axis=dim)
    return block


def local(ham_tiles, tile_columns, stack_lengths, start_vectors, spectral_scale):
    row_count, panel_width = start_vectors.shape
    block_count = ham_tiles.shape[0]
    tile_size = ham_tiles.shape[2]
    total_blocks = block_count * lax.axis_size("row")
    total_rows = row_count * lax.axis_size("row")
    full_width = panel_width * lax.axis_size("vec")
    first_block = lax.axis_index("row") * block_count
    block_ids = first_block + jnp.arange(block_count, dtype=jnp.int32)
    offsets = (tile_columns - block_ids[:, None] + REACH) % total_blocks - REACH
    local_ids = jnp.arange(block_count, dtype=jnp.int32)[:, None] + offsets + REACH
    local_rows = jnp.arange(block_count, dtype=jnp.int32)
    live = (local_rows < stack_lengths[0] - REACH) | (local_rows >= block_count - REACH)
    live_mask = live.astype(jnp.float32)[:, None, None]

    def apply_hamiltonian(current):
        blocked = current.reshape(block_count, tile_size, panel_width)
        padded = with_halo(blocked, (("row", 0),), REACH)
        picked = padded[local_ids]
        product = jnp.einsum(
            "btij,btjc->bic", ham_tiles, picked, preferred_element_type=jnp.float32
        )
        return (product * live_mask).reshape(row_count, panel_width)

    earlier = start_vectors
    current = apply_hamiltonian(start_vectors).astype(jnp.bfloat16)
    for repeat in range(CHEB - 1):
        following = (2.0 * apply_hamiltonian(current) - earlier.astype(jnp.float32)).astype(
            jnp.bfloat16
        )
        earlier, current = (current, following)
    panel_rows = lax.all_to_all(current, "vec", split_axis=0, concat_axis=1, tiled=True)
    partial_gram = lax.dot_general(
        panel_rows, panel_rows, (((0,), (0,)), ((), ())), preferred_element_type=jnp.float32
    ) / float(total_rows)
    gram = lax.psum(partial_gram, ("row", "vec"))
    scale = spectral_scale[0] * jnp.trace(gram) / full_width
    system = gram / scale
    root = jnp.eye(full_width, dtype=jnp.float32)
    for repeat in range(NS_ITERS):
        product_w = jnp.dot(system, root, precision=lax.Precision.HIGHEST)
        product_p = jnp.dot(product_w, root, precision=lax.Precision.HIGHEST)
        root = 1.5 * root - 0.5 * jnp.dot(product_p, root, precision=lax.Precision.HIGHEST)
    weights = (root / jnp.sqrt(scale)).astype(jnp.bfloat16)
    basis_rows = jnp.dot(panel_rows, weights, preferred_element_type=jnp.float32).astype(
        jnp.bfloat16
    )
    return lax.all_to_all(basis_rows, "vec", split_axis=1, concat_axis=0, tiled=True)


def solution(mesh):
    placed = (P("row", None, None, None), P("row", None), P("row"), P("row", "vec"), P())
    return jax.shard_map(
        local, mesh=mesh, in_specs=placed, out_specs=P("row", "vec"), check_vma=False
    )
```

profile of v0, /device:TPU:1, one launch (start us, length us, event | category | flops | bytes accessed | tf_op | source)
XLA Modules:
  0.0 501.2 jit_solution(6701823993396391410)
XLA Ops:
  6.5 0.9 fusion.46
  7.4 2.2 collective-permute-start
  9.6 3.7 collective-permute-start.1
  13.3 0.7 compare_select_fusion
  14.0 0.1 copy.16
  14.1 0.1 reshape.84
  14.9 1.9 pad_maximum_fusion
  16.8 8.7 %gather_fusion = bf16[256,128,128]{2,1,0:T(8,128)(2,1)} fusion(bf16[68,128,128]{2,1,0:T(8,128)(2,1)S(1)} %pad_maximum_fusion, s32[1024]{0:T(1024)S(1)} %pad_clamp_fusion), kind=kCustom, calls=%fused_computation | custom fusion | bytes 16778240 | tf_op jit(solution)/shard_map/gather | solution.py:43
  25.5 7.3 %fusion.28 = bf16[64,128,128]{1,2,0:T(8,128)(2,1)S(1)} fusion(f32[64]{0:T(128)S(1)} %or_convert_fusion, bf16[64,4,128,128]{3,2,1,0:T(8,128)(2,1)} %bitcast.117, bf16[64,4,128,128]{3,2,1,0:T(8,128)(2,1)} %param.5), kind=kOutput, calls=%fused_computation.58 | convolution fusion | flops 1075838976 | bytes 18874624 | tf_op jit(solution)/shard_map/btij,btjc->bic/dot_general | solution.py:44
  32.8 0.0 copy-start
  32.8 0.1 collective-permute-start.2
  32.9 4.9 collective-permute-start.3
  37.8 1.6 collective-permute-done.2
  39.4 0.3 pad_maximum_fusion.1
  39.7 8.7 %gather_fusion.1 = bf16[256,128,128]{1,2,0:T(8,128)(2,1)} fusion(bf16[68,128,128]{1,2,0:T(8,128)(2,1)S(1)} %pad_maximum_fusion.1, s32[1024]{0:T(1024)S(1)} %pad_clamp_fusion), kind=kCustom, calls=%fused_computation.1 | custom fusion | bytes 16778240 | tf_op jit(solution)/shard_map/gather | solution.py:43
  48.3 10.1 %fusion.12 = f32[64,128,128]{1,2,0:T(8,128)} fusion(bf16[64,4,128,128]{2,3,1,0:T(8,128)(2,1)} %bitcast.119, bf16[64,4,128,128]{3,2,1,0:T(8,128)(2,1)} %param.5, f32[64]{0:T(128)S(1)} %or_convert_fusion), kind=kOutput, calls=%fused_computation.28 | convolution fusion | flops 1075838976 | bytes 20971776 | tf_op jit(solution)/shard_map/btij,btjc->bic/dot_general | solution.py:44
  58.4 5.7 %copy.20 = f32[64,128,128]{2,1,0:T(8,128)} copy(f32[64,128,128]{1,2,0:T(8,128)} %fusion.12) | data formatting | bytes 8388608 | tf_op jit(solution)/shard_map/mul | solution.py:52
  64.2 2.6 fusion.10
  66.8 0.3 collective-permute-start.4
  67.0 4.9 collective-permute-start.5
  72.0 1.6 collective-permute-done.4
  73.6 0.3 pad_maximum_fusion.2
  73.8 8.7 %gather_fusion.2 = bf16[256,128,128]{2,1,0:T(8,128)(2,1)} fusion(bf16[68,128,128]{2,1,0:T(8,128)(2,1)S(1)} %pad_maximum_fusion.2, s32[1024]{0:T(1024)S(1)} %pad_clamp_fusion), kind=kCustom, calls=%fused_computation.2 | custom fusion | bytes 16778240 | tf_op jit(solution)/shard_map/gather | solution.py:43
  82.5 7.9 %fusion.8 = bf16[64,128,128]{1,2,0:T(8,128)(2,1)S(1)} fusion(bf16[64,128,128]{1,2,0:T(8,128)(2,1)} %copy-done, bf16[64,4,128,128]{3,2,1,0:T(8,128)(2,1)} %bitcast.115, bf16[64,4,128,128]{3,2,1,0:T(8,128)(2,1)} %param.5, f32[64]{0:T(128)S(1)} %or_convert_fusion), kind=kOutput, calls=%fused_computation.21 | convolution fusion | flops 1078984704 | bytes 20971776 | tf_op jit(solution)/shard_map/btij,btjc->bic/dot_general | solution.py:44
  90.4 0.1 collective-permute-start.6
  90.5 4.9 collective-permute-start.7
  95.5 1.6 collective-permute-done.6
  97.0 1.7 pad_maximum_fusion.3
  98.7 10.3 %gather_fusion.3 = bf16[256,128,128]{1,2,0:T(8,128)(2,1)} fusion(bf16[68,128,128]{1,2,0:T(8,128)(2,1)} %pad_maximum_fusion.3, s32[1024]{0:T(1024)S(1)} %pad_clamp_fusion), kind=kCustom, calls=%fused_computation.3 | custom fusion | bytes 16778240 | tf_op jit(solution)/shard_map/gather | solution.py:43
  109.0 10.1 %fusion.7 = f32[64,128,128]{1,2,0:T(8,128)} fusion(bf16[64,4,128,128]{2,3,1,0:T(8,128)(2,1)} %bitcast.120, bf16[64,4,128,128]{3,2,1,0:T(8,128)(2,1)} %param.5, f32[64]{0:T(128)S(1)} %or_convert_fusion), kind=kOutput, calls=%fused_computation.19 | convolution fusion | flops 1075838976 | bytes 20971776 | tf_op jit(solution)/shard_map/btij,btjc->bic/dot_general | solution.py:44
  119.1 5.6 %copy.24 = f32[64,128,128]{2,1,0:T(8,128)} copy(f32[64,128,128]{1,2,0:T(8,128)} %fusion.7) | data formatting | bytes 8388608 | tf_op jit(solution)/shard_map/mul | solution.py:52
  124.7 3.3 fusion.5
  128.0 0.0 copy-start.1
  128.0 0.1 collective-permute-start.8
  128.1 5.3 %collective-permute-start.9 = (bf16[2,128,128]{2,1,0:T(8,128)(2,1)S(1)}, bf16[2,128,128]{2,1,0:T(8,128)(2,1)S(1)}, u32[]{:S(2)}, u32[]{:S(2)}) collective-permute-start(bf16[2,128,128]{2,1,0:T(8,128)(2,1)S(1)} %bitcast.132), channel_id=1, source_target_pairs={{8,0},{16,8},{24,16},{32,24},{40,32},{48,40},{56,48},{64,56},{72,6... | collective-permute-start | bytes 196616 | tf_op jit(solution)/shard_map/ppermute | solution.py:20
  133.4 1.2 collective-permute-done.8
  134.6 0.2 collective-permute-done.9
  134.8 1.7 pad_maximum_fusion.4
  136.5 10.3 %gather_fusion.4 = bf16[256,128,128]{2,1,0:T(8,128)(2,1)} fusion(bf16[68,128,128]{2,1,0:T(8,128)(2,1)} %pad_maximum_fusion.4, s32[1024]{0:T(1024)S(1)} %pad_clamp_fusion), kind=kCustom, calls=%fused_computation.4 | custom fusion | bytes 16778240 | tf_op jit(solution)/shard_map/gather | solution.py:43
  146.8 7.4 %fusion.3 = bf16[64,128,128]{1,2,0:T(8,128)(2,1)S(1)} fusion(bf16[64,128,128]{1,2,0:T(8,128)(2,1)S(1)} %fusion.8, bf16[64,4,128,128]{3,2,1,0:T(8,128)(2,1)} %bitcast.116, bf16[64,4,128,128]{3,2,1,0:T(8,128)(2,1)} %param.5, f32[64]{0:T(128)S(1)} %or_convert_fusion), kind=kOutput, calls=%fused_computation.12 | convolution fusion | flops 1078984704 | bytes 20971776 | tf_op jit(solution)/shard_map/btij,btjc->bic/dot_general | solution.py:44
  154.2 0.1 collective-permute-start.10
  154.3 5.2 %collective-permute-start.11 = (bf16[2,128,128]{1,2,0:T(8,128)(2,1)S(1)}, bf16[2,128,128]{1,2,0:T(8,128)(2,1)S(1)}, u32[]{:S(2)}, u32[]{:S(2)}) collective-permute-start(bf16[2,128,128]{1,2,0:T(8,128)(2,1)S(1)} %get-tuple-element.6), channel_id=1, source_target_pairs={{8,0},{16,8},{24,16},{32,24},{40,32},{48,40},{56,48},{64,56},{72,6... | collective-permute-start | bytes 196616 | tf_op jit(solution)/shard_map/ppermute | solution.py:20
  159.4 1.6 collective-permute-done.10
  161.0 0.3 pad_maximum_fusion.5
  161.3 8.7 %gather_fusion.5 = bf16[256,128,128]{1,2,0:T(8,128)(2,1)} fusion(bf16[68,128,128]{1,2,0:T(8,128)(2,1)S(1)} %pad_maximum_fusion.5, s32[1024]{0:T(1024)S(1)} %pad_clamp_fusion), kind=kCustom, calls=%fused_computation.5 | custom fusion | bytes 16778240 | tf_op jit(solution)/shard_map/gather | solution.py:43
  170.0 10.1 %fusion.2 = f32[64,128,128]{1,2,0:T(8,128)} fusion(bf16[64,4,128,128]{2,3,1,0:T(8,128)(2,1)} %bitcast.118, bf16[64,4,128,128]{3,2,1,0:T(8,128)(2,1)} %param.5, f32[64]{0:T(128)S(1)} %or_convert_fusion), kind=kOutput, calls=%fused_computation.10 | convolution fusion | flops 1075838976 | bytes 20971776 | tf_op jit(solution)/shard_map/btij,btjc->bic/dot_general | solution.py:44
  180.1 5.7 %copy.28 = f32[64,128,128]{2,1,0:T(8,128)} copy(f32[64,128,128]{1,2,0:T(8,128)} %fusion.2) | data formatting | bytes 8388608 | tf_op jit(solution)/shard_map/mul | solution.py:52
  185.8 3.9 fusion
  189.7 2.9 copy.29
  192.6 39.1 %all_to_all.38 = bf16[8,1024,128]{1,2,0:T(8,128)(2,1)S(1)} all-to-all(bf16[8,1024,128]{1,2,0:T(8,128)(2,1)S(1)} %copy.29), channel_id=1, replica_groups=mesh['row'=16,'vec'=8] {'vec'}, dimensions={0} | all-to-all | bytes 4194304 | tf_op jit(solution)/shard_map/all_to_all | solution.py:56
  231.7 1.3 copy-done.6
  233.0 4.4 convolution_multiply_fusion
  237.4 0.0 all-reduce.2.cloned.1.call-update
  238.1 153.3 %all-reduce.2.cloned.1.call-done = f32[1024,1024]{1,0:T(8,128)} async-done(((f32[1024,1024]{1,0:T(8,128)}), f32[1024,1024]{1,0:T(8,128)}) %all-reduce.2.cloned.1.call-update) | async-done | bytes 4194320 | tf_op jit(solution)/shard_map/psum | solution.py:60
  391.4 2.9 select_reduce_fusion
  394.9 8.5 %fusion.16 = f32[1024,1024]{1,0:T(8,128)S(1)} fusion(f32[1024,1024]{1,0:T(8,128)} %all-reduce.2.cloned.1.call-done, f32[]{:T(128)S(6)} %div.23), kind=kOutput, calls=%fused_computation.37 | convolution fusion | flops 12886999040 | bytes 8388612 | tf_op jit(solution)/shard_map/dot_general | solution.py:65
  403.4 6.7 %fusion.15 = f32[1024,1024]{1,0:T(8,128)S(1)} fusion(f32[1024,1024]{1,0:T(8,128)S(1)} %fusion.16), kind=kOutput, calls=%fused_computation.36 | convolution fusion | flops 12885950464 | bytes 8388608 | tf_op jit(solution)/shard_map/dot_general | solution.py:66
  410.0 6.7 %fusion.14 = f32[1024,1024]{1,0:T(8,128)S(1)} fusion(f32[1024,1024]{1,0:T(8,128)S(1)} %fusion.15), kind=kOutput, calls=%fused_computation.35 | convolution fusion | flops 12885950464 | bytes 8388608 | tf_op jit(solution)/shard_map/dot_general | solution.py:67
  416.7 13.9 %fusion.18 = f32[1024,1024]{1,0:T(8,128)S(1)} fusion(f32[1024,1024]{1,0:T(8,128)S(1)} %fusion.14, f32[1024,1024]{1,0:T(8,128)S(1)} %copy-done.5, f32[]{:T(128)S(6)} %div.23), kind=kOutput, calls=%fused_computation.46 | convolution fusion | flops 12890144768 | bytes 12582916 | tf_op jit(solution)/shard_map/dot_general | solution.py:65
  430.7 13.7 %fusion.17 = f32[1024,1024]{1,0:T(8,128)S(1)} fusion(f32[1024,1024]{1,0:T(8,128)S(1)} %fusion.18, f32[1024,1024]{1,0:T(8,128)S(1)} %fusion.14), kind=kOutput, calls=%fused_computation.45 | convolution fusion | flops 12889096192 | bytes 12582912 | tf_op jit(solution)/shard_map/dot_general | solution.py:66
  444.4 14.5 %divide_convert_fusion = bf16[1024,1024]{1,0:T(8,128)(2,1)S(1)} fusion(f32[1024,1024]{1,0:T(8,128)S(1)} %fusion.17, f32[1024,1024]{1,0:T(8,128)S(1)} %fusion.14, f32[]{:T(128)S(6)} %sqrt.3), kind=kOutput, calls=%fused_computation.31 | convolution fusion | flops 12898533376 | bytes 10485764 | tf_op jit(solution)/shard_map/dot_general | solution.py:67
  458.9 2.4 convolution_convert_fusion
  461.3 30.5 %all_to_all.39 = bf16[1024,8,128]{0,2,1:T(8,128)(2,1)S(1)} all-to-all(bf16[1024,8,128]{0,2,1:T(8,128)(2,1)S(1)} %bitcast.128), channel_id=1, replica_groups=mesh['row'=16,'vec'=8] {'vec'}, dimensions={1} | all-to-all | bytes 4194304 | tf_op jit(solution)/shard_map/all_to_all | solution.py:72
  491.8 2.4 copy.30
  (28 shorter events, 0.1 us)
Async XLA Ops:
  6.5 384.8 %all-reduce.2.cloned.1.call-start = ((), (), s32[]{:S(2)}) async-start(), calls=%async_computation.2 | async-start | bytes 8388608 | tf_op jit(solution)/shard_map/psum | solution.py:60
  7.4 7.5 %collective-permute-start = (bf16[2,128,128]{2,1,0:T(8,128)(2,1)S(1)}, bf16[2,128,128]{2,1,0:T(8,128)(2,1)S(1)}, u32[]{:S(2)}, u32[]{:S(2)}) collective-permute-start(bf16[2,128,128]{2,1,0:T(8,128)(2,1)S(1)} %bitcast.130), channel_id=1, source_target_pairs={{0,8},{8,16},{16,24},{24,32},{32,40},{40,48},{48,56},{56,64},{64,7... | collective-permute-start | bytes 196616 | tf_op jit(solution)/shard_map/ppermute | solution.py:17
  9.6 5.3 %collective-permute-start.1 = (bf16[2,128,128]{2,1,0:T(8,128)(2,1)S(1)}, bf16[2,128,128]{2,1,0:T(8,128)(2,1)S(1)}, u32[]{:S(2)}, u32[]{:S(2)}) collective-permute-start(bf16[2,128,128]{2,1,0:T(8,128)(2,1)S(1)} %bitcast.129), channel_id=1, source_target_pairs={{8,0},{16,8},{24,16},{32,24},{40,32},{48,40},{56,48},{64,56},{72,6... | collective-permute-start | bytes 196616 | tf_op jit(solution)/shard_map/ppermute | solution.py:20
  32.8 6.6 %copy-start = (bf16[64,128,128]{1,2,0:T(8,128)(2,1)}, bf16[64,128,128]{1,2,0:T(8,128)(2,1)S(1)}, u32[]{:S(2)}) copy-start(bf16[64,128,128]{1,2,0:T(8,128)(2,1)S(1)} %fusion.28) | copy-start | bytes 6291460
  32.8 6.6 %collective-permute-start.2 = (bf16[2,128,128]{1,2,0:T(8,128)(2,1)S(1)}, bf16[2,128,128]{1,2,0:T(8,128)(2,1)S(1)}, u32[]{:S(2)}, u32[]{:S(2)}) collective-permute-start(bf16[2,128,128]{1,2,0:T(8,128)(2,1)S(1)} %get-tuple-element.13), channel_id=1, source_target_pairs={{0,8},{8,16},{16,24},{24,32},{32,40},{40,48},{48,56},{56,64},{64,7... | collective-permute-start | bytes 196616 | tf_op jit(solution)/shard_map/ppermute | solution.py:17
  32.9 6.5 %collective-permute-start.3 = (bf16[2,128,128]{1,2,0:T(8,128)(2,1)S(1)}, bf16[2,128,128]{1,2,0:T(8,128)(2,1)S(1)}, u32[]{:S(2)}, u32[]{:S(2)}) collective-permute-start(bf16[2,128,128]{1,2,0:T(8,128)(2,1)S(1)} %get-tuple-element.14), channel_id=1, source_target_pairs={{8,0},{16,8},{24,16},{32,24},{40,32},{48,40},{56,48},{64,56},{72,6... | collective-permute-start | bytes 196616 | tf_op jit(solution)/shard_map/ppermute | solution.py:20
  58.4 5.7 %copy-start.4 = (bf16[8192,128]{1,0:T(8,128)(2,1)S(1)}, bf16[8192,128]{1,0:T(8,128)(2,1)}, u32[]{:S(2)}) copy-start(bf16[8192,128]{1,0:T(8,128)(2,1)} %param.8) | copy-start | bytes 6291460
  66.8 6.8 %copy-start.3 = (bf16[8192,128]{1,0:T(8,128)(2,1)}, bf16[8192,128]{1,0:T(8,128)(2,1)S(1)}, u32[]{:S(2)}) copy-start(bf16[8192,128]{1,0:T(8,128)(2,1)S(1)} %fusion.10) | copy-start | bytes 6291460
  66.8 6.8 %collective-permute-start.4 = (bf16[2,128,128]{2,1,0:T(8,128)(2,1)S(1)}, bf16[2,128,128]{2,1,0:T(8,128)(2,1)S(1)}, u32[]{:S(2)}, u32[]{:S(2)}) collective-permute-start(bf16[2,128,128]{2,1,0:T(8,128)(2,1)S(1)} %bitcast.133), channel_id=1, source_target_pairs={{0,8},{8,16},{16,24},{24,32},{32,40},{40,48},{48,56},{56,64},{64,7... | collective-permute-start | bytes 196616 | tf_op jit(solution)/shard_map/ppermute | solution.py:17
  67.0 6.5 %collective-permute-start.5 = (bf16[2,128,128]{2,1,0:T(8,128)(2,1)S(1)}, bf16[2,128,128]{2,1,0:T(8,128)(2,1)S(1)}, u32[]{:S(2)}, u32[]{:S(2)}) collective-permute-start(bf16[2,128,128]{2,1,0:T(8,128)(2,1)S(1)} %bitcast.131), channel_id=1, source_target_pairs={{8,0},{16,8},{24,16},{32,24},{40,32},{48,40},{56,48},{64,56},{72,6... | collective-permute-start | bytes 196616 | tf_op jit(solution)/shard_map/ppermute | solution.py:20
  90.4 6.6 %collective-permute-start.6 = (bf16[2,128,128]{1,2,0:T(8,128)(2,1)S(1)}, bf16[2,128,128]{1,2,0:T(8,128)(2,1)S(1)}, u32[]{:S(2)}, u32[]{:S(2)}) collective-permute-start(bf16[2,128,128]{1,2,0:T(8,128)(2,1)S(1)} %get-tuple-element.9), channel_id=1, source_target_pairs={{0,8},{8,16},{16,24},{24,32},{32,40},{40,48},{48,56},{56,64},{64,7... | collective-permute-start | bytes 196616 | tf_op jit(solution)/shard_map/ppermute | solution.py:17
  90.5 6.5 %collective-permute-start.7 = (bf16[2,128,128]{1,2,0:T(8,128)(2,1)S(1)}, bf16[2,128,128]{1,2,0:T(8,128)(2,1)S(1)}, u32[]{:S(2)}, u32[]{:S(2)}) collective-permute-start(bf16[2,128,128]{1,2,0:T(8,128)(2,1)S(1)} %get-tuple-element.10), channel_id=1, source_target_pairs={{8,0},{16,8},{24,16},{32,24},{40,32},{48,40},{56,48},{64,56},{72,6... | collective-permute-start | bytes 196616 | tf_op jit(solution)/shard_map/ppermute | solution.py:20
  128.0 6.8 %copy-start.1 = (bf16[8192,128]{1,0:T(8,128)(2,1)}, bf16[8192,128]{1,0:T(8,128)(2,1)S(1)}, u32[]{:S(2)}) copy-start(bf16[8192,128]{1,0:T(8,128)(2,1)S(1)} %fusion.5) | copy-start | bytes 6291460
  128.0 6.6 %collective-permute-start.8 = (bf16[2,128,128]{2,1,0:T(8,128)(2,1)S(1)}, bf16[2,128,128]{2,1,0:T(8,128)(2,1)S(1)}, u32[]{:S(2)}, u32[]{:S(2)}) collective-permute-start(bf16[2,128,128]{2,1,0:T(8,128)(2,1)S(1)} %bitcast.134), channel_id=1, source_target_pairs={{0,8},{8,16},{16,24},{24,32},{32,40},{40,48},{48,56},{56,64},{64,7... | collective-permute-start | bytes 196616 | tf_op jit(solution)/shard_map/ppermute | solution.py:17
  128.1 6.7 %collective-permute-start.9 = (bf16[2,128,128]{2,1,0:T(8,128)(2,1)S(1)}, bf16[2,128,128]{2,1,0:T(8,128)(2,1)S(1)}, u32[]{:S(2)}, u32[]{:S(2)}) collective-permute-start(bf16[2,128,128]{2,1,0:T(8,128)(2,1)S(1)} %bitcast.132), channel_id=1, source_target_pairs={{8,0},{16,8},{24,16},{32,24},{40,32},{48,40},{56,48},{64,56},{72,6... | collective-permute-start | bytes 196616 | tf_op jit(solution)/shard_map/ppermute | solution.py:20
  154.2 6.8 %collective-permute-start.10 = (bf16[2,128,128]{1,2,0:T(8,128)(2,1)S(1)}, bf16[2,128,128]{1,2,0:T(8,128)(2,1)S(1)}, u32[]{:S(2)}, u32[]{:S(2)}) collective-permute-start(bf16[2,128,128]{1,2,0:T(8,128)(2,1)S(1)} %get-tuple-element.5), channel_id=1, source_target_pairs={{0,8},{8,16},{16,24},{24,32},{32,40},{40,48},{48,56},{56,64},{64,7... | collective-permute-start | bytes 196616 | tf_op jit(solution)/shard_map/ppermute | solution.py:17
  154.3 6.7 %collective-permute-start.11 = (bf16[2,128,128]{1,2,0:T(8,128)(2,1)S(1)}, bf16[2,128,128]{1,2,0:T(8,128)(2,1)S(1)}, u32[]{:S(2)}, u32[]{:S(2)}) collective-permute-start(bf16[2,128,128]{1,2,0:T(8,128)(2,1)S(1)} %get-tuple-element.6), channel_id=1, source_target_pairs={{8,0},{16,8},{24,16},{32,24},{40,32},{48,40},{56,48},{64,56},{72,6... | collective-permute-start | bytes 196616 | tf_op jit(solution)/shard_map/ppermute | solution.py:20
  180.1 5.7 %copy-start.2 = (bf16[8192,128]{1,0:T(8,128)(2,1)S(1)}, bf16[8192,128]{1,0:T(8,128)(2,1)}, u32[]{:S(2)}) copy-start(bf16[8192,128]{1,0:T(8,128)(2,1)} %copy-done.1) | copy-start | bytes 6291460
  231.7 1.3 copy-start.6
  410.0 6.7 %copy-start.5 = (f32[1024,1024]{1,0:T(8,128)S(1)}, f32[1024,1024]{1,0:T(8,128)}, u32[]{:S(2)}) copy-start(f32[1024,1024]{1,0:T(8,128)} %all-reduce.2.cloned.1.call-done) | copy-start | bytes 12582916
  444.4 14.5 %copy-start.7 = (bf16[8,1024,128]{1,2,0:T(8,128)(2,1)S(1)}, bf16[8,1024,128]{1,2,0:T(8,128)(2,1)}, u32[]{:S(2)}) copy-start(bf16[8,1024,128]{1,2,0:T(8,128)(2,1)} %copy-done.6) | copy-start | bytes 6291460
Sparse Core Ops, SparseCore 0:
  237.5 153.7 all-reduce.1
where the time goes:
time: 510 us; the launch traced here: 501 us
  waiting for transfers between devices  161 us (32%)
  matrix products  124 us (24%)
  local copies, waits for them, and re-layouts  80 us (16%)
  blocking collectives  69.7 us (14%)
  starting transfers between devices  31.7 us (6%)
  other arithmetic  19.6 us (4%)
  between operations  15.8 us (3%)
    psum x1, waiting for transfers between devices, local(): gram = lax.psum(partial_gram, ('row', 'vec'))  153 us
    gather x6, local copies, waits for them, and re-layouts, apply_hamiltonian(): picked = padded[local_ids]  55.2 us
    dot_general x6, matrix products, apply_hamiltonian(): jnp.einsum('btij,btjc->bic', ham_tiles, picked, preferred_element_type=jn...  52.9 us
    all_to_all x1, blocking collectives, local(): lax.all_to_all(current, 'vec', split_axis=0, concat_axis=1, tiled=True)  39.1 us
    all_to_all x1, blocking collectives, local(): lax.all_to_all(basis_rows, 'vec', split_axis=1, concat_axis=0, tiled=True)  30.5 us
    ppermute x6, starting transfers between devices, with_halo(): lax.ppermute(lax.slice_in_dim(block, 0, width, axis=dim), axis, backward)  29 us
    dot_general x2, matrix products, local(): product_w = jnp.dot(system, root, precision=lax.Precision.HIGHEST)  22.4 us
    dot_general x2, matrix products, local(): jnp.dot(product_p, root, precision=lax.Precision.HIGHEST)  21.1 us
  transfers between devices with their start and end apart: 13, of which 7 were waited for; matrix products, arithmetic and copies ran while one was open for 0% of the time, Pallas kernels for 0%

commit v1 on v0

v1 whole, which is shorter than its diff:
```python
import functools

import jax
import jax.numpy as jnp
from jax import lax
from jax.experimental import pallas as pl
from jax.experimental.pallas import tpu as pltpu
from jax.sharding import PartitionSpec as P

REACH = 2
CHEB = 6
DEEP = REACH * CHEB
UNROLL = 4
BF = jnp.bfloat16
F32 = jnp.float32
ANY = pl.BlockSpec(memory_space=pl.ANY)
SMEM = pl.BlockSpec(memory_space=pltpu.SMEM)
VMEM = pl.BlockSpec(memory_space=pltpu.VMEM)


def filter_steps(count, row_shift, ids, live, tiles, first, even, odd, out, out_at):
    for step in range(1, CHEB + 1):
        source = first if step == 1 else (odd if step % 2 == 0 else even)
        target = odd if step % 2 else even
        before = first if step == 2 else target
        low = REACH * step

        def body(turn, carry, step=step, source=source, target=target, before=before, low=low):
            for part in range(UNROLL):
                block = low + turn * UNROLL + part
                row = block - row_shift
                left = jnp.concatenate([tiles[row, t] for t in range(4)], axis=1)
                right = jnp.concatenate([source[ids[row * 4 + t]] for t in range(4)], axis=0)
                value = jnp.dot(left, right, preferred_element_type=F32) * live[row]
                if step > 1:
                    value = 2.0 * value - before[block].astype(F32)
                if step == CHEB:
                    out[out_at + block - DEEP] = value.astype(BF)
                else:
                    target[block] = value.astype(BF)
            return carry

        lax.fori_loop(0, (count - 2 * low) // UNROLL, body, 0)


def inner_kernel(count, ids, live, tiles, vectors, out, even, odd):
    filter_steps(count, 0, ids, live, tiles, vectors, even, odd, out, 0)


def edge_kernel(count, edge, pieces, ids0, live0, ids1, live1, core, tiles, vectors, *refs):
    (vlow, vhigh, tlow_a, tlow_b, thigh_a, thigh_b, out, seg_v, seg_t, even, odd, sems) = refs
    deep_rows = DEEP - REACH
    half = deep_rows // 2
    span = 3 * DEEP
    mine = core[0] * half
    other = half - mine
    copies = []

    def copy(source, target):
        copies.append(pltpu.make_async_copy(source, target, sems.at[len(copies)]))
        copies[-1].start()

    copy(vlow, seg_v.at[0, pl.ds(0, DEEP)])
    copy(vectors.at[pl.ds(0, 2 * DEEP)], seg_v.at[0, pl.ds(DEEP, 2 * DEEP)])
    copy(vectors.at[pl.ds(count - 2 * DEEP, 2 * DEEP)], seg_v.at[1, pl.ds(0, 2 * DEEP)])
    copy(vhigh, seg_v.at[1, pl.ds(2 * DEEP, DEEP)])
    own_rows = 2 * DEEP - REACH
    copy(tlow_a, seg_t.at[0, pl.ds(mine, half)])
    copy(tlow_b, seg_t.at[0, pl.ds(other, half)])
    copy(tiles.at[pl.ds(0, own_rows)], seg_t.at[0, pl.ds(deep_rows, own_rows)])
    copy(tiles.at[pl.ds(count - own_rows, own_rows)], seg_t.at[1, pl.ds(0, own_rows)])
    copy(thigh_a, seg_t.at[1, pl.ds(own_rows + mine, half)])
    copy(thigh_b, seg_t.at[1, pl.ds(own_rows + other, half)])
    for c in copies:
        c.wait()
    filter_steps(span, REACH, ids0, live0, seg_t.at[0], seg_v.at[0], even, odd, out, 0)
    filter_steps(span, REACH, ids1, live1, seg_t.at[1], seg_v.at[1], even, odd, out, DEEP)


def gram_kernel(rows, with_base, quarter, *refs):
    if with_base:
        base, refs = refs[0], refs[1:]
    own, twin, ra, ra2, lb, lb2, oa, oa2, ob, ob2, out, flipped = refs
    q = rows // 4
    for part in range(4):
        flipped[part] = own[pl.ds(part * q, q), :].T

    def add(column, value):
        at = pl.ds(column * 128, 128)
        out[:, at] = value

    def dot(part, piece, at):
        return jnp.dot(flipped[part], piece[pl.ds(at * q, q), :], preferred_element_type=F32)

    i = quarter[0]

    def total(*terms):
        value = terms[0]
        for term in terms[1:]:
            value = value + term
        return value

    values = [
        total(*[dot(p, own, p) for p in range(4)]) * 0.5,
        total(*[dot(p, twin, p) for p in range(4)]) * 0.5,
        dot(0, ra, 0) + dot(1, ra, 1),
        dot(0, ra2, 0) + dot(1, ra2, 1),
        dot(i, oa, 0) + dot(2 + i, ob, 0),
        dot(i, oa2, 0) + dot(2 + i, ob2, 0),
        dot(2, lb, 0) + dot(3, lb, 1),
        dot(2, lb2, 0) + dot(3, lb2, 1),
    ]
    for column, value in enumerate(values):
        if with_base:
            value = value + base[:, column * 128 : (column + 1) * 128]
        add(column, value)


def split(value):
    high = value.astype(BF)
    return high, (value - high.astype(F32)).astype(BF)


def final_kernel(place, scale_in, gathered, *refs):
    pieces, (out, rows_buf, table, matrix, sems) = refs[:36], refs[36:]
    x, y, i = place[0], place[1], place[2]
    low = DEEP * 128
    inner = (rows_buf.shape[0] - 2 * low) // 2
    starts = (
        (low, low + inner, inner // 2),
        (0, low + 2 * inner, low // 2),
    )
    copies = []

    def copy(source, row, count, panel):
        target = rows_buf.at[pl.ds(row, count), pl.ds(panel * 128, 128)]
        copies.append(pltpu.make_async_copy(source, target, sems.at[len(copies)]))
        copies[-1].start()

    def sources():
        for group in range(2):
            yield group, pieces[18 * group : 18 * group + 18]

    for group, refs_of in sources():
        first, second, quarter = starts[group]
        half = 2 * quarter
        for e in range(2):
            if group == 0:
                copy(refs_of[e], first, 2 * half, e)
            else:
                copy(refs_of[e].at[pl.ds(0, half)], first, half, e)
                copy(refs_of[e].at[pl.ds(half, half)], second, half, e)
            ra, rb, la, lb, oa1, oa2, ob1, ob2 = refs_of[2 + 8 * e : 10 + 8 * e]
            copy(ra, first, half, 2 + e)
            copy(rb, second, half, 2 + e)
            copy(la, first, half, 6 + e)
            copy(lb, second, half, 6 + e)
            mine, other = i * quarter, (1 - i) * quarter
            copy(oa1, first + mine, quarter, 4 + e)
            copy(oa2, first + other, quarter, 4 + e)
            copy(ob1, second + mine, quarter, 4 + e)
            copy(ob2, second + other, quarter, 4 + e)

    for dx in range(4):
        for dy in range(4):
            chunk = lax.rem(x + dx, 4) * 4 + lax.rem(y + dy, 4)
            for dz in range(4):
                for e in range(2):
                    piece = gathered[(((e * 4 + dx) * 4 + dy) * 4 + dz)].astype(F32)
                    for qz in range(4):
                        for qe in range(2):
                            column = 2 * ((dz + qz) % 4) + (e ^ qe)
                            table[2 * dz + e, chunk, :, pl.ds(column * 128, 128)] = piece[
                                :, (2 * qz + qe) * 128 : (2 * qz + qe + 1) * 128
                            ]
    width = 1024
    diagonal = lax.broadcasted_iota(jnp.int32, (128, 128), 0) == lax.broadcasted_iota(
        jnp.int32, (128, 128), 1
    )
    eye = diagonal.astype(F32)
    trace = jnp.zeros((128, 128), F32)
    for p in range(8):
        panel = table[p].reshape(128, width)
        matrix[pl.ds(p * 128, 128), :] = panel.astype(BF)
        trace = trace + panel[:, p * 128 : (p + 1) * 128] * eye
    mean = 2.0 * jnp.sum(trace) / float(rows_buf.shape[0] * 16)
    scale = scale_in[0] * mean / width
    kappa = 1.0 / (scale * float(rows_buf.shape[0] * 16))
    own_row = table[0].reshape(128, width)
    own_column = jnp.concatenate(
        [table[p].reshape(128, width)[:, 0:128].T for p in range(8)], axis=1
    )
    unit = jnp.concatenate([eye, jnp.zeros((128, width - 128), F32)], axis=1)
    root = 1.5 * unit - (0.5 * kappa) * (own_row + own_column)

    def times(value):
        both = jnp.concatenate(split(value), axis=0)
        whole = matrix[...]
        product = jnp.dot(both, whole, preferred_element_type=F32) + lax.dot_general(
            both, whole, (((1,), (1,)), ((), ())), preferred_element_type=F32
        )
        return kappa * (product[:128] + product[128:])

    second = 1.5 * root - 0.5 * times(root)
    third = 1.5 * second - 0.5 * times(second)
    result = 1.5 * root - 0.5 * times(third)
    weights = (result / jnp.sqrt(jnp.full((128, width), scale, F32))).astype(BF).T
    for c in copies:
        c.wait()
    step = 512

    def body(turn, carry):
        at = pl.ds(pl.multiple_of(turn * step, step), step)
        out[at, :] = jnp.dot(rows_buf[at, :], weights, preferred_element_type=F32).astype(BF)
        return carry

    lax.fori_loop(0, rows_buf.shape[0] // step, body, 0)


def params(limit):
    return pltpu.CompilerParams(vmem_limit_bytes=limit * 2**20)


def cost(flops, data):
    return pl.CostEstimate(flops=flops, bytes_accessed=data, transcendentals=0)


def local(ham_tiles, tile_columns, stack_lengths, start_vectors, spectral_scale):
    row_count, panel = start_vectors.shape
    blocks = ham_tiles.shape[0]
    total_blocks = blocks * lax.axis_size("row")
    row_at, vec_at = lax.axis_index("row"), lax.axis_index("vec")
    z_at, core_at = vec_at // 2, vec_at % 2
    rows16, zs = lax.axis_size("row"), lax.axis_size("vec") // 2

    def z_perm(move, flip=0):
        return [
            (2 * z + c, 2 * ((z + move) % zs) + (c ^ flip)) for z in range(zs) for c in range(2)
        ]

    def by_z(value, move):
        return lax.ppermute(value, "vec", z_perm(move))

    def swap(value):
        return lax.ppermute(value, "vec", z_perm(0, 1))

    forward = [(r, (r + 1) % rows16) for r in range(rows16)]
    backward = [(r, (r - 1) % rows16) for r in range(rows16)]

    block_ids = row_at * blocks + jnp.arange(blocks, dtype=jnp.int32)
    offsets = (tile_columns - block_ids[:, None] + REACH) % total_blocks - REACH
    local_rows = jnp.arange(blocks, dtype=jnp.int32)
    live = ((local_rows < stack_lengths[0] - REACH) | (local_rows >= blocks - REACH)).astype(
        jnp.int32
    )
    meta = jnp.concatenate([offsets, jnp.broadcast_to(live[:, None], (blocks, 4))], axis=1)
    vectors = start_vectors.reshape(blocks, 128, panel)
    deep_rows = DEEP - REACH
    half = deep_rows // 2
    meta_low = lax.ppermute(meta[blocks - deep_rows :], "row", forward)
    meta_high = lax.ppermute(meta[:deep_rows], "row", backward)
    tiles_low_a = lax.ppermute(
        lax.dynamic_slice_in_dim(ham_tiles, blocks - deep_rows + core_at * half, half, 0),
        "row",
        forward,
    )
    tiles_high_a = lax.ppermute(
        lax.dynamic_slice_in_dim(ham_tiles, core_at * half, half, 0), "row", backward
    )
    vlow = lax.ppermute(vectors[blocks - DEEP :], "row", forward)
    vhigh = lax.ppermute(vectors[:DEEP], "row", backward)
    tiles_low_b = swap(tiles_low_a)
    tiles_high_b = swap(tiles_high_a)

    inner_blocks = blocks - 2 * DEEP
    inner_ids = (local_rows[:, None] + offsets).reshape(-1)
    inner = pl.pallas_call(
        functools.partial(inner_kernel, blocks),
        out_shape=jax.ShapeDtypeStruct((inner_blocks, 128, panel), BF),
        in_specs=[SMEM, SMEM, VMEM, VMEM],
        out_specs=VMEM,
        scratch_shapes=[pltpu.VMEM((blocks, 128, panel), BF)] * 2,
        compiler_params=params(32),
        cost_estimate=cost(10 * 10**9, 11 * 2**20),
        name="inner_filter",
    )(inner_ids, live.astype(F32), ham_tiles, vectors)

    def segment(parts):
        part = jnp.concatenate(parts, axis=0)
        places = REACH + jnp.arange(part.shape[0], dtype=jnp.int32)[:, None] + part[:, :4]
        return places.reshape(-1), part[:, 4].astype(F32)

    own_rows = 2 * DEEP - REACH
    ids0, live0 = segment([meta_low, meta[:own_rows]])
    ids1, live1 = segment([meta[blocks - own_rows :], meta_high])
    inner_flat = inner.reshape(inner_blocks * 128, panel)

    quarter_of = jnp.where(z_at < 2, 0, 1).astype(jnp.int32)
    send_left = jnp.where((z_at + zs - 1) % zs < 2, 0, 1).astype(jnp.int32)
    send_right = jnp.where((z_at + 1) % zs < 2, 0, 1).astype(jnp.int32)

    def needed(own):
        rows = own.shape[0]
        h, q = rows // 2, rows // 4
        twin = swap(own)
        ra = by_z(own[:h], -1)
        lb = by_z(own[h:], 1)
        oa1 = by_z(lax.dynamic_slice_in_dim(ra, send_left * q, q, 0), -1)
        ob1 = by_z(lax.dynamic_slice_in_dim(lb, send_right * q, q, 0), 1)
        return twin, ra, lb, oa1, ob1, swap(ra), swap(lb), swap(oa1), swap(ob1)

    def rest(own, got):
        rows = own.shape[0]
        h, q = rows // 2, rows // 4
        twin, ra, lb, oa1, ob1, ra2, lb2, oa12, ob12 = got
        rb = by_z(own[h:], -1)
        la = by_z(own[:h], 1)
        oa2 = by_z(lax.dynamic_slice_in_dim(ra, (1 - send_left) * q, q, 0), -1)
        ob2 = by_z(lax.dynamic_slice_in_dim(lb, (1 - send_right) * q, q, 0), 1)
        return (
            [own, twin]
            + [ra, rb, la, lb, oa1, oa2, ob1, ob2]
            + [ra2, swap(rb), swap(la), lb2, oa12, swap(oa2), ob12, swap(ob2)]
        )

    def gram(own, got, base):
        twin, ra, lb, oa1, ob1, ra2, lb2, oa12, ob12 = got
        args = [own, twin, ra, ra2, lb, lb2, oa1, oa12, ob1, ob12]
        rows = own.shape[0]
        if base is not None:
            args = [base] + args
        return pl.pallas_call(
            functools.partial(gram_kernel, rows, base is not None),
            out_shape=jax.ShapeDtypeStruct((128, 1024), F32),
            in_specs=[SMEM] + [VMEM] * len(args),
            out_specs=VMEM,
            scratch_shapes=[pltpu.VMEM((4, 128, rows // 4), BF)],
            compiler_params=params(24),
            cost_estimate=cost(rows * 128 * 1024, rows * 128 * 12),
            name="gram",
        )(quarter_of[None], *args)

    inner_got = needed(inner_flat)
    inner_gram = gram(inner_flat, inner_got, None)

    core_arg = core_at.astype(jnp.int32)[None]
    edge = pl.pallas_call(
        functools.partial(edge_kernel, blocks, DEEP, None),
        out_shape=jax.ShapeDtypeStruct((2 * DEEP, 128, panel), BF),
        in_specs=[SMEM] * 5 + [ANY] * 8,
        out_specs=VMEM,
        scratch_shapes=[
            pltpu.VMEM((2, 3 * DEEP, 128, panel), BF),
            pltpu.VMEM((2, 3 * DEEP - 2 * REACH, 4, 128, 128), BF),
            pltpu.VMEM((3 * DEEP, 128, panel), BF),
            pltpu.VMEM((3 * DEEP, 128, panel), BF),
            pltpu.SemaphoreType.DMA((10,)),
        ],
        compiler_params=params(32),
        cost_estimate=cost(8 * 10**9, 11 * 2**20),
        name="edge_filter",
    )(ids0, live0, ids1, live1, core_arg, ham_tiles, vectors, vlow, vhigh,
      tiles_low_a, tiles_low_b, tiles_high_a, tiles_high_b)
    edge_flat = edge.reshape(2 * DEEP * 128, panel)
    edge_got = needed(edge_flat)
    whole_gram = gram(edge_flat, edge_got, inner_gram)

    pieces = lax.all_to_all(
        whole_gram.reshape(rows16, 128 // rows16, 1024), "row", split_axis=0, concat_axis=0
    )
    mine = jnp.sum(pieces, axis=0).astype(BF)[None]

    def around(value, axis, perm_of):
        parts = [value] + [lax.ppermute(value, axis, perm_of(d)) for d in (1, 2, 3)]
        return jnp.concatenate(parts, axis=0)

    def row_perm(dx, dy):
        return [
            (4 * a + b, 4 * ((a - dx) % 4) + (b - dy) % 4) for a in range(4) for b in range(4)
        ]

    got = around(mine, "vec", lambda d: z_perm(-d))
    got = around(got, "row", lambda d: row_perm(0, d))
    got = around(got, "row", lambda d: row_perm(d, 0))
    gathered = jnp.concatenate([got, swap(got)], axis=0)

    inner_all = rest(inner_flat, inner_got)
    edge_all = rest(edge_flat, edge_got)
    place = jnp.stack([row_at // 4, row_at % 4, quarter_of]).astype(jnp.int32)
    return pl.pallas_call(
        final_kernel,
        out_shape=jax.ShapeDtypeStruct((row_count, panel), BF),
        in_specs=[SMEM, SMEM, VMEM] + [ANY] * 36,
        out_specs=VMEM,
        scratch_shapes=[
            pltpu.VMEM((row_count, 1024), BF),
            pltpu.VMEM((8, rows16, 128 // rows16, 1024), F32),
            pltpu.VMEM((1024, 1024), BF),
            pltpu.SemaphoreType.DMA((38,)),
        ],
        compiler_params=params(48),
        cost_estimate=cost(6 * 10**9, 20 * 2**20),
        name="final",
    )(place, spectral_scale, gathered, *inner_all, *edge_all)


def solution(mesh):
    placed = (P("row", None, None, None), P("row", None), P("row"), P("row", "vec"), P())
    return jax.shard_map(
        local, mesh=mesh, in_specs=placed, out_specs=P("row", "vec"), check_vma=False
    )
```

time: 510 us -> 238 us (0.47); the launches traced: 501 us -> 238 us
  matrix products: 124 us -> 0 us
  waiting for transfers between devices: 161 us -> 45.5 us
  Pallas kernels: 0 us -> 67.2 us
  blocking collectives: 69.7 us -> 16.2 us
  local copies, waits for them, and re-layouts: 80 us -> 33.2 us
  starting transfers between devices: 31.7 us -> 73.6 us
  other arithmetic: 19.6 us -> 0.32 us
  between operations: 15.8 us -> 1.84 us
    psum x1 -> x0, waiting for transfers between devices: 153 us -> none  [local(): gram = lax.psum(partial_gram, ('row', 'vec'))]
    dot_general x14 -> x0, matrix products: 124 us -> none  [the longest x6 52.9 us: apply_hamiltonian(): jnp.einsum('btij,btjc->bic', ham_tiles, picked, preferred_element_type=jn...]
    pallas_call x0 -> x5, Pallas kernels: none -> 67.2 us  [the longest x1 22.7 us: local(): pl.pallas_call(functools.partial(inner_kernel, blocks), out_shape=jax.Sha...]
    gather x6 -> x0, local copies, waits for them, and re-layouts: 55.2 us -> none  [apply_hamiltonian(): picked = padded[local_ids]]
    all_to_all x2 -> x1, blocking collectives: 69.7 us -> 16.2 us  [local(): lax.all_to_all(whole_gram.reshape(rows16, 128 // rows16, 1024), 'row', sp...]
    ppermute x12 -> x52, starting transfers between devices: 31.7 us -> 73.6 us  [the longest x21 33.5 us: swap(): return lax.ppermute(value, 'vec', z_perm(0, 1))]
    ppermute x12 -> x52, waiting for transfers between devices: 7.64 us -> 45.5 us  [the longest x16 35.7 us: by_z(): return lax.ppermute(value, 'vec', z_perm(move))]
    unnamed x16 -> x59, local copies, waits for them, and re-layouts: 1.35 us -> 18.6 us
  transfers between devices with their start and end apart: 13 -> 52, of which waited for: 7 -> 16; matrix products, arithmetic and copies ran while one was open for 0% -> 7% of each run, Pallas kernels for 0% -> 21%
where the time goes in v1:
time: 238 us
  starting transfers between devices  73.6 us (31%)
  Pallas kernels  67.2 us (28%)
  waiting for transfers between devices  45.5 us (19%)
  local copies, waits for them, and re-layouts  33.2 us (14%)
  blocking collectives  16.2 us (7%)
    ppermute x16, waiting for transfers between devices, by_z(): return lax.ppermute(value, 'vec', z_perm(move))  35.7 us
    ppermute x21, starting transfers between devices, swap(): return lax.ppermute(value, 'vec', z_perm(0, 1))  33.5 us
    pallas_call x1, Pallas kernels, local(): pl.pallas_call(functools.partial(inner_kernel, blocks), out_shape=jax.Sha...  22.7 us
    pallas_call x1, Pallas kernels, local(): pl.pallas_call(functools.partial(edge_kernel, blocks, DEEP, None), out_sh...  22.3 us
    unnamed x59, local copies, waits for them, and re-layouts  18.6 us
    ppermute x16, starting transfers between devices, by_z(): return lax.ppermute(value, 'vec', z_perm(move))  18.3 us
    all_to_all x1, blocking collectives, local(): lax.all_to_all(whole_gram.reshape(rows16, 128 // rows16, 1024), 'row', sp...  16.2 us
    pallas_call x1, Pallas kernels, local(): pl.pallas_call(final_kernel, out_shape=jax.ShapeDtypeStruct((row_count, p...  15.4 us
  transfers between devices with their start and end apart: 52, of which 16 were waited for; matrix products, arithmetic and copies ran while one was open for 7% of the time, Pallas kernels for 21%

profile of v1, /device:TPU:1, one launch (start us, length us, event | category | flops | bytes accessed | tf_op | source)
XLA Modules:
  0.0 237.9 jit_solution(10061514731075370728)
XLA Ops:
  0.0 2.6 %constant_dynamic-slice_fusion.6 = (bf16[5,4,128,128]{3,2,1,0:T(8,128)(2,1)}, bf16[5,4,128,128]{3,2,1,0:T(8,128)(2,1)}) fusion(bf16[64,4,128,128]{3,2,1,0:T(8,128)(2,1)} %tiles.3, s32[]{:T(128)S(6)} %select_n.85, s32[]{:T(128)S(6)} %select_n.84), kind=kLoop, calls=%fused_computation.42 | loop fusion | bytes 2621448 | tf_op jit(solution)/shard_map/dynamic_slice | solution.py:268
  2.6 2.1 collective-permute-start.13
  4.8 3.6 %collective-permute-start.15 = (bf16[5,4,128,128]{3,2,1,0:T(8,128)(2,1)}, bf16[5,4,128,128]{3,2,1,0:T(8,128)(2,1)}, u32[]{:S(2)}, u32[]{:S(2)}) collective-permute-start(bf16[5,4,128,128]{3,2,1,0:T(8,128)(2,1)} %get-tuple-element.7), channel_id=1, source_target_pairs={{0,120},{8,0},{16,8},{24,16},{32,24},{40,32},{48,40},{56,48},{64,5... | collective-permute-start | bytes 1966088 | tf_op jit(solution)/shard_map/ppermute | solution.py:267
  9.2 4.8 %collective-permute-start.10 = (s32[10,8]{0,1:T(8,128)S(1)}, s32[10,8]{0,1:T(8,128)S(1)}, u32[]{:S(2)}, u32[]{:S(2)}) collective-permute-start(s32[10,8]{0,1:T(8,128)S(1)} %get-tuple-element.52), channel_id=1, source_target_pairs={{0,120},{8,0},{16,8},{24,16},{32,24},{40,32},{48,40},{56,48},{64,5... | collective-permute-start | bytes 968 | tf_op jit(solution)/shard_map/ppermute | solution.py:261
  14.0 0.9 fusion.4
  15.2 3.4 %copy-done.12 = bf16[64,4,128,128]{3,2,1,0:T(8,128)(2,1)S(1)} copy-done((bf16[64,4,128,128]{3,2,1,0:T(8,128)(2,1)S(1)}, bf16[64,4,128,128]{3,2,1,0:T(8,128)(2,1)}, u32[]{:S(2)}) %copy-start.12) | copy-done | bytes 8388632
  18.6 22.7 %inner_filter.1 = bf16[40,128,128]{2,1,0:T(8,128)(2,1)S(1)} custom-call(s32[256]{0:T(256)S(1)} %reshape.56.ids, f32[64]{0:T(128)S(1)} %get-tuple-element.57.live, bf16[64,4,128,128]{3,2,1,0:T(8,128)(2,1)S(1)} %copy-done.12, bf16[64,128,128]{2,1,0:T(8,128)(2,1)S(1)} %bitcast.30), custom_call_target="tpu_custom_call" | custom-call | flops 10000000000 | bytes 11534336 | tf_op jit(solution)/shard_map/inner_filter/pallas_call | solution.py:277
  41.4 1.2 fusion.5
  42.6 3.8 %collective-permute-start.1 = (bf16[2560,128]{1,0:T(8,128)(2,1)}, bf16[2560,128]{1,0:T(8,128)(2,1)S(1)}, u32[]{:S(2)}, u32[]{:S(2)}) collective-permute-start(bf16[2560,128]{1,0:T(8,128)(2,1)} %bitcast.6), channel_id=1, source_target_pairs={{0,6},{1,7},{2,0},{3,1},{4,2},{5,3},{6,4},{7,5},{8,14},{9,15},{10,... | collective-permute-start | bytes 1966088 | tf_op jit(solution)/shard_map/ppermute | solution.py:242
  46.6 4.8 %collective-permute-start.12 = (bf16[12,128,128]{2,1,0:T(8,128)(2,1)}, bf16[12,128,128]{2,1,0:T(8,128)(2,1)}, u32[]{:S(2)}, u32[]{:S(2)}) collective-permute-start(bf16[12,128,128]{2,1,0:T(8,128)(2,1)} %bitcast.12), channel_id=1, source_target_pairs={{0,120},{8,0},{16,8},{24,16},{32,24},{40,32},{48,40},{56,48},{64,5... | collective-permute-start | bytes 1179656 | tf_op jit(solution)/shard_map/ppermute | solution.py:271
  51.4 2.5 %collective-permute-start.14 = (bf16[5,4,128,128]{3,2,1,0:T(8,128)(2,1)}, bf16[5,4,128,128]{3,2,1,0:T(8,128)(2,1)S(1)}, u32[]{:S(2)}, u32[]{:S(2)}) collective-permute-start(bf16[5,4,128,128]{3,2,1,0:T(8,128)(2,1)} %collective-permute-done.13.refs_2_), channel_id=1, source_target_pairs={{0,1},{1,0},{2,3},{3,2},{4,5},{5,4},{6,7},{7,6},{8,9},{9,8},{10,11... | collective-permute-start | bytes 1966088 | tf_op jit(solution)/shard_map/ppermute | solution.py:245
  53.9 5.2 %collective-permute-done.1.refs_2_ = bf16[2560,128]{1,0:T(8,128)(2,1)S(1)} collective-permute-done((bf16[2560,128]{1,0:T(8,128)(2,1)}, bf16[2560,128]{1,0:T(8,128)(2,1)S(1)}, u32[]{:S(2)}, u32[]{:S(2)}) %collective-permute-start.1) | collective-permute-done | bytes 655392 | tf_op jit(solution)/shard_map/ppermute | solution.py:242
  59.1 2.6 %collective-permute-start.16 = (bf16[5,4,128,128]{3,2,1,0:T(8,128)(2,1)}, bf16[5,4,128,128]{3,2,1,0:T(8,128)(2,1)}, u32[]{:S(2)}, u32[]{:S(2)}) collective-permute-start(bf16[5,4,128,128]{3,2,1,0:T(8,128)(2,1)} %collective-permute-done.15.refs_4_), channel_id=1, source_target_pairs={{0,1},{1,0},{2,3},{3,2},{4,5},{5,4},{6,7},{7,6},{8,9},{9,8},{10,11... | collective-permute-start | bytes 1966088 | tf_op jit(solution)/shard_map/ppermute | solution.py:245
  61.6 0.9 constant_dynamic-slice_fusion.3
  62.5 3.3 %collective-permute-start.5 = (bf16[1280,128]{1,0:T(8,128)(2,1)}, bf16[1280,128]{1,0:T(8,128)(2,1)}, u32[]{:S(2)}, u32[]{:S(2)}) collective-permute-start(bf16[1280,128]{1,0:T(8,128)(2,1)} %get-tuple-element.18), channel_id=1, source_target_pairs={{0,6},{1,7},{2,0},{3,1},{4,2},{5,3},{6,4},{7,5},{8,14},{9,15},{10,... | collective-permute-start | bytes 983048 | tf_op jit(solution)/shard_map/ppermute | solution.py:242
  66.2 0.8 constant_dynamic-slice_fusion.2
  68.0 5.1 %collective-permute-done.5.refs_6_ = bf16[1280,128]{1,0:T(8,128)(2,1)} collective-permute-done((bf16[1280,128]{1,0:T(8,128)(2,1)}, bf16[1280,128]{1,0:T(8,128)(2,1)}, u32[]{:S(2)}, u32[]{:S(2)}) %collective-permute-start.5) | collective-permute-done | bytes 327712 | tf_op jit(solution)/shard_map/ppermute | solution.py:242
  73.1 0.9 collective-permute-start.6
  74.1 0.8 copy-done.14
  74.9 1.6 copy-done.11
  76.5 3.4 %copy-done.13 = bf16[64,4,128,128]{3,2,1,0:T(8,128)(2,1)S(1)} copy-done((bf16[64,4,128,128]{3,2,1,0:T(8,128)(2,1)S(1)}, bf16[64,4,128,128]{3,2,1,0:T(8,128)(2,1)}, u32[]{:S(2)}) %copy-start.13) | copy-done | bytes 8388632
  79.9 1.1 copy-done.15
  81.0 22.3 %edge_filter.1 = bf16[24,128,128]{2,1,0:T(8,128)(2,1)S(1)} custom-call(s32[128]{0:T(128)S(1)} %reshape.59.ids0, f32[32]{0:T(128)S(1)} %convert_bitcast_fusion.2.live0, s32[128]{0:T(128)S(1)} %reshape.60.ids1, f32[32]{0:T(128)S(1)} %convert_bitcast_fusion.1.live1, s32[1]{0:T(128)} %bitcast.10.core, bf16[64,4,128,128]{3,2,1,0:T(8,128)(2,1)S(1)} %copy-done.13, ...), custom_call_target="tpu_custom_call" | custom-call | flops 8000000000 | bytes 11534336 | tf_op jit(solution)/shard_map/edge_filter/pallas_call | solution.py:347
  103.2 0.9 fusion.6
  104.1 3.4 %collective-permute-start.18 = (bf16[1536,128]{1,0:T(8,128)(2,1)}, bf16[1536,128]{1,0:T(8,128)(2,1)S(1)}, u32[]{:S(2)}, u32[]{:S(2)}) collective-permute-start(bf16[1536,128]{1,0:T(8,128)(2,1)} %bitcast.14), channel_id=1, source_target_pairs={{0,6},{1,7},{2,0},{3,1},{4,2},{5,3},{6,4},{7,5},{8,14},{9,15},{10,... | collective-permute-start | bytes 1179656 | tf_op jit(solution)/shard_map/ppermute | solution.py:242
  108.8 7.6 %collective-permute-done.18.refs_3_.refs_20_ = bf16[1536,128]{1,0:T(8,128)(2,1)S(1)} collective-permute-done((bf16[1536,128]{1,0:T(8,128)(2,1)}, bf16[1536,128]{1,0:T(8,128)(2,1)S(1)}, u32[]{:S(2)}, u32[]{:S(2)}) %collective-permute-start.18) | collective-permute-done | bytes 393248 | tf_op jit(solution)/shard_map/ppermute | solution.py:242
  117.9 1.3 collective-permute-done.20.refs_5_.refs_23_
  119.3 1.1 collective-permute-start.8
  120.4 1.7 constant_dynamic-slice_fusion.1
  122.1 1.7 constant_dynamic-slice_fusion
  123.8 0.9 collective-permute-start.22
  125.8 4.6 %collective-permute-done.22.refs_7_.refs_24_ = bf16[768,128]{1,0:T(8,128)(2,1)} collective-permute-done((bf16[768,128]{1,0:T(8,128)(2,1)S(1)}, bf16[768,128]{1,0:T(8,128)(2,1)}, u32[]{:S(2)}, u32[]{:S(2)}) %collective-permute-start.22) | collective-permute-done | bytes 196640 | tf_op jit(solution)/shard_map/ppermute | solution.py:242
  131.3 1.7 collective-permute-done.24.refs_9_.refs_26_
  133.0 1.3 collective-permute-start.25
  134.2 1.0 copy-done.8
  135.2 3.9 %gram.2.refs_0_ = f32[128,1024]{1,0:T(8,128)S(1)} custom-call(s32[1]{0:T(128)} %bitcast.2.quarter, bf16[5120,128]{1,0:T(8,128)(2,1)S(1)} %bitcast.24, bf16[5120,128]{1,0:T(8,128)(2,1)} %collective-permute-done.refs_1_, bf16[2560,128]{1,0:T(8,128)(2,1)S(1)} %collective-permute-done.1.refs_2_, bf16[2560,128]{1,0:T(8,128)(2,1)} %collective-permute-done.2.refs_3_.refs_10_, ...), custom_call_target="tpu_custom_call" | custom-call | flops 671088640 | bytes 7864320 | tf_op jit(solution)/shard_map/gram/pallas_call | solution.py:332
  139.2 2.9 %gram.3 = f32[128,1024]{1,0:T(8,128)S(1)} custom-call(s32[1]{0:T(128)} %bitcast.2.quarter, f32[128,1024]{1,0:T(8,128)S(1)} %gram.2.refs_0_, bf16[3072,128]{1,0:T(8,128)(2,1)S(1)} %bitcast.27, bf16[3072,128]{1,0:T(8,128)(2,1)} %collective-permute-done.17.refs_2_.refs_19_, bf16[1536,128]{1,0:T(8,128)(2,1)S(1)} %copy-done.5, ...), custom_call_target="tpu_custom_call" | custom-call | flops 402653184 | bytes 4718592 | tf_op jit(solution)/shard_map/gram/pallas_call | solution.py:332
  142.2 16.2 %all_to_all.5 = f32[16,8,1024]{2,1,0:T(8,128)S(1)} all-to-all(f32[16,8,1024]{2,1,0:T(8,128)S(1)} %bitcast.29), channel_id=1, replica_groups=mesh['row'=16,'vec'=8] {'row'}, dimensions={0} | all-to-all | bytes 1048576 | tf_op jit(solution)/shard_map/all_to_all | solution.py:368
  158.5 0.8 collective-permute-start.27
  161.1 1.6 collective-permute-done.27
  162.7 0.8 collective-permute-done.28
  163.5 1.6 collective-permute-start.29
  168.6 1.1 collective-permute-done.30
  171.0 1.2 collective-permute-start.32
  172.2 1.8 collective-permute-start.36
  175.0 1.3 collective-permute-done.32
  176.3 1.8 collective-permute-start.38
  178.8 2.1 collective-permute-done.33
  181.6 2.3 collective-permute-done.34
  184.7 6.0 %collective-permute-start.35 = (bf16[64,8,1024]{2,1,0:T(8,128)(2,1)}, bf16[64,8,1024]{2,1,0:T(8,128)(2,1)}, u32[]{:S(2)}, u32[]{:S(2)}) collective-permute-start(bf16[64,8,1024]{2,1,0:T(8,128)(2,1)} %get-tuple-element.23), channel_id=1, source_target_pairs={{0,1},{1,0},{2,3},{3,2},{4,5},{5,4},{6,7},{7,6},{8,9},{9,8},{10,11... | collective-permute-start | bytes 3145736 | tf_op jit(solution)/shard_map/ppermute | solution.py:245
  190.7 2.4 %collective-permute-start.40 = (bf16[2560,128]{1,0:T(8,128)(2,1)S(1)}, bf16[2560,128]{1,0:T(8,128)(2,1)S(1)}, u32[]{:S(2)}, u32[]{:S(2)}) collective-permute-start(bf16[2560,128]{1,0:T(8,128)(2,1)S(1)} %collective-permute-done.36.refs_3_), channel_id=1, source_target_pairs={{0,1},{1,0},{2,3},{3,2},{4,5},{5,4},{6,7},{7,6},{8,9},{9,8},{10,11... | collective-permute-start | bytes 1966088 | tf_op jit(solution)/shard_map/ppermute | solution.py:245
  193.1 3.5 %collective-permute-start.42 = (bf16[1280,128]{1,0:T(8,128)(2,1)S(1)}, bf16[1280,128]{1,0:T(8,128)(2,1)S(1)}, u32[]{:S(2)}, u32[]{:S(2)}) collective-permute-start(bf16[1280,128]{1,0:T(8,128)(2,1)S(1)} %collective-permute-done.38.refs_7_), channel_id=1, source_target_pairs={{0,1},{1,0},{2,3},{3,2},{4,5},{5,4},{6,7},{7,6},{8,9},{9,8},{10,11... | collective-permute-start | bytes 983048 | tf_op jit(solution)/shard_map/ppermute | solution.py:245
  196.6 3.9 %collective-permute-start.43 = (bf16[1280,128]{1,0:T(8,128)(2,1)S(1)}, bf16[1280,128]{1,0:T(8,128)(2,1)S(1)}, u32[]{:S(2)}, u32[]{:S(2)}) collective-permute-start(bf16[1280,128]{1,0:T(8,128)(2,1)S(1)} %collective-permute-done.39.refs_9_), channel_id=1, source_target_pairs={{0,1},{1,0},{2,3},{3,2},{4,5},{5,4},{6,7},{7,6},{8,9},{9,8},{10,11... | collective-permute-start | bytes 983048 | tf_op jit(solution)/shard_map/ppermute | solution.py:245
  200.6 1.5 collective-permute-start.45
  202.0 0.9 collective-permute-start.41
  202.9 1.1 collective-permute-start.46
  204.0 7.0 %collective-permute-done.44.refs_21_ = bf16[1536,128]{1,0:T(8,128)(2,1)S(1)} collective-permute-done((bf16[1536,128]{1,0:T(8,128)(2,1)S(1)}, bf16[1536,128]{1,0:T(8,128)(2,1)S(1)}, u32[]{:S(2)}, u32[]{:S(2)}) %collective-permute-start.44) | collective-permute-done | bytes 393248 | tf_op jit(solution)/shard_map/ppermute | solution.py:242
  211.0 1.5 collective-permute-done.45.refs_22_
  212.5 1.1 collective-permute-start.48
  213.6 1.6 collective-permute-done.46.refs_25_
  215.2 1.2 collective-permute-start.49
  217.1 2.8 %collective-permute-start.50 = (bf16[768,128]{1,0:T(8,128)(2,1)S(1)}, bf16[768,128]{1,0:T(8,128)(2,1)S(1)}, u32[]{:S(2)}, u32[]{:S(2)}) collective-permute-start(bf16[768,128]{1,0:T(8,128)(2,1)S(1)} %collective-permute-done.46.refs_25_), channel_id=1, source_target_pairs={{0,1},{1,0},{2,3},{3,2},{4,5},{5,4},{6,7},{7,6},{8,9},{9,8},{10,11... | collective-permute-start | bytes 589832 | tf_op jit(solution)/shard_map/ppermute | solution.py:245
  220.0 2.3 constant_dynamic-update-slice_fusion.17.gathered
  222.3 15.4 %final.1 = bf16[8192,128]{1,0:T(8,128)(2,1)} custom-call(s32[3]{0:T(128)S(1)} %pad_add_fusion.3.place, f32[1]{0:T(128)S(6)} %copy.37.scale_in, bf16[128,8,1024]{2,1,0:T(8,128)(2,1)} %constant_dynamic-update-slice_fusion.17.gathered, bf16[5120,128]{1,0:T(8,128)(2,1)} %bitcast.25, bf16[5120,128]{1,0:T(8,128)(2,1)} %collective-permute-done.refs_1_, ...), custom_call_target="tpu_custom_call" | custom-call | flops 6000000000 | bytes 20971520 | tf_op jit(solution)/shard_map/final/pallas_call | solution.py:390
  (137 shorter events, 16.7 us)
Async XLA Ops:
  2.6 43.9 %collective-permute-start.13 = (bf16[5,4,128,128]{3,2,1,0:T(8,128)(2,1)}, bf16[5,4,128,128]{3,2,1,0:T(8,128)(2,1)}, u32[]{:S(2)}, u32[]{:S(2)}) collective-permute-start(bf16[5,4,128,128]{3,2,1,0:T(8,128)(2,1)} %get-tuple-element.8), channel_id=1, source_target_pairs={{0,8},{8,16},{16,24},{24,32},{32,40},{40,48},{48,56},{56,64},{64,7... | collective-permute-start | bytes 1966088 | tf_op jit(solution)/shard_map/ppermute | solution.py:262
  4.8 46.6 %collective-permute-start.15 = (bf16[5,4,128,128]{3,2,1,0:T(8,128)(2,1)}, bf16[5,4,128,128]{3,2,1,0:T(8,128)(2,1)}, u32[]{:S(2)}, u32[]{:S(2)}) collective-permute-start(bf16[5,4,128,128]{3,2,1,0:T(8,128)(2,1)} %get-tuple-element.7), channel_id=1, source_target_pairs={{0,120},{8,0},{16,8},{24,16},{32,24},{40,32},{48,40},{56,48},{64,5... | collective-permute-start | bytes 1966088 | tf_op jit(solution)/shard_map/ppermute | solution.py:267
  9.2 33.4 %collective-permute-start.9 = (s32[10,8]{0,1:T(8,128)S(1)}, s32[10,8]{0,1:T(8,128)S(1)}, u32[]{:S(2)}, u32[]{:S(2)}) collective-permute-start(s32[10,8]{0,1:T(8,128)S(1)} %get-tuple-element.53), channel_id=1, source_target_pairs={{0,8},{8,16},{16,24},{24,32},{32,40},{40,48},{48,56},{56,64},{64,7... | collective-permute-start | bytes 968 | tf_op jit(solution)/shard_map/ppermute | solution.py:260
  9.2 37.2 %collective-permute-start.10 = (s32[10,8]{0,1:T(8,128)S(1)}, s32[10,8]{0,1:T(8,128)S(1)}, u32[]{:S(2)}, u32[]{:S(2)}) collective-permute-start(s32[10,8]{0,1:T(8,128)S(1)} %get-tuple-element.52), channel_id=1, source_target_pairs={{0,120},{8,0},{16,8},{24,16},{32,24},{40,32},{48,40},{56,48},{64,5... | collective-permute-start | bytes 968 | tf_op jit(solution)/shard_map/ppermute | solution.py:261
  14.9 52.1 %collective-permute-start.11 = (bf16[12,128,128]{2,1,0:T(8,128)(2,1)}, bf16[12,128,128]{2,1,0:T(8,128)(2,1)}, u32[]{:S(2)}, u32[]{:S(2)}) collective-permute-start(bf16[12,128,128]{2,1,0:T(8,128)(2,1)} %bitcast.11), channel_id=1, source_target_pairs={{0,8},{8,16},{16,24},{24,32},{32,40},{40,48},{48,56},{56,64},{64,7... | collective-permute-start | bytes 1179656 | tf_op jit(solution)/shard_map/ppermute | solution.py:270
  41.4 92.9 %copy-start = (bf16[40,128,128]{2,1,0:T(8,128)(2,1)}, bf16[40,128,128]{2,1,0:T(8,128)(2,1)S(1)}, u32[]{:S(2)}) copy-start(bf16[40,128,128]{2,1,0:T(8,128)(2,1)S(1)} %inner_filter.1) | copy-start | bytes 3932164
  42.6 16.5 %collective-permute-start.1 = (bf16[2560,128]{1,0:T(8,128)(2,1)}, bf16[2560,128]{1,0:T(8,128)(2,1)S(1)}, u32[]{:S(2)}, u32[]{:S(2)}) collective-permute-start(bf16[2560,128]{1,0:T(8,128)(2,1)} %bitcast.6), channel_id=1, source_target_pairs={{0,6},{1,7},{2,0},{3,1},{4,2},{5,3},{6,4},{7,5},{8,14},{9,15},{10,... | collective-permute-start | bytes 1966088 | tf_op jit(solution)/shard_map/ppermute | solution.py:242
  46.5 16.1 %collective-permute-start.3 = (bf16[2560,128]{1,0:T(8,128)(2,1)}, bf16[2560,128]{1,0:T(8,128)(2,1)S(1)}, u32[]{:S(2)}, u32[]{:S(2)}) collective-permute-start(bf16[2560,128]{1,0:T(8,128)(2,1)} %bitcast.7), channel_id=1, source_target_pairs={{0,2},{1,3},{2,4},{3,5},{4,6},{5,7},{6,0},{7,1},{8,10},{9,11},{10,... | collective-permute-start | bytes 1966088 | tf_op jit(solution)/shard_map/ppermute | solution.py:242
  46.6 20.9 %collective-permute-start.12 = (bf16[12,128,128]{2,1,0:T(8,128)(2,1)}, bf16[12,128,128]{2,1,0:T(8,128)(2,1)}, u32[]{:S(2)}, u32[]{:S(2)}) collective-permute-start(bf16[12,128,128]{2,1,0:T(8,128)(2,1)} %bitcast.12), channel_id=1, source_target_pairs={{0,120},{8,0},{16,8},{24,16},{32,24},{40,32},{48,40},{56,48},{64,5... | collective-permute-start | bytes 1179656 | tf_op jit(solution)/shard_map/ppermute | solution.py:271
  51.4 22.7 %collective-permute-start.14 = (bf16[5,4,128,128]{3,2,1,0:T(8,128)(2,1)}, bf16[5,4,128,128]{3,2,1,0:T(8,128)(2,1)S(1)}, u32[]{:S(2)}, u32[]{:S(2)}) collective-permute-start(bf16[5,4,128,128]{3,2,1,0:T(8,128)(2,1)} %collective-permute-done.13.refs_2_), channel_id=1, source_target_pairs={{0,1},{1,0},{2,3},{3,2},{4,5},{5,4},{6,7},{7,6},{8,9},{9,8},{10,11... | collective-permute-start | bytes 1966088 | tf_op jit(solution)/shard_map/ppermute | solution.py:245
  59.1 75.2 %copy-start.2 = (bf16[2560,128]{1,0:T(8,128)(2,1)}, bf16[2560,128]{1,0:T(8,128)(2,1)S(1)}, u32[]{:S(2)}) copy-start(bf16[2560,128]{1,0:T(8,128)(2,1)S(1)} %collective-permute-done.1.refs_2_) | copy-start | bytes 1966084
  59.1 15.8 %collective-permute-start.16 = (bf16[5,4,128,128]{3,2,1,0:T(8,128)(2,1)}, bf16[5,4,128,128]{3,2,1,0:T(8,128)(2,1)}, u32[]{:S(2)}, u32[]{:S(2)}) collective-permute-start(bf16[5,4,128,128]{3,2,1,0:T(8,128)(2,1)} %collective-permute-done.15.refs_4_), channel_id=1, source_target_pairs={{0,1},{1,0},{2,3},{3,2},{4,5},{5,4},{6,7},{7,6},{8,9},{9,8},{10,11... | collective-permute-start | bytes 1966088 | tf_op jit(solution)/shard_map/ppermute | solution.py:245
  62.5 71.7 %copy-start.3 = (bf16[2560,128]{1,0:T(8,128)(2,1)}, bf16[2560,128]{1,0:T(8,128)(2,1)S(1)}, u32[]{:S(2)}) copy-start(bf16[2560,128]{1,0:T(8,128)(2,1)S(1)} %collective-permute-done.3.refs_4_.refs_5_) | copy-start | bytes 1966084
  62.5 10.6 %collective-permute-start.5 = (bf16[1280,128]{1,0:T(8,128)(2,1)}, bf16[1280,128]{1,0:T(8,128)(2,1)}, u32[]{:S(2)}, u32[]{:S(2)}) collective-permute-start(bf16[1280,128]{1,0:T(8,128)(2,1)} %get-tuple-element.18), channel_id=1, source_target_pairs={{0,6},{1,7},{2,0},{3,1},{4,2},{5,3},{6,4},{7,5},{8,14},{9,15},{10,... | collective-permute-start | bytes 983048 | tf_op jit(solution)/shard_map/ppermute | solution.py:242
  67.0 58.6 %collective-permute-start = (bf16[5120,128]{1,0:T(8,128)(2,1)S(1)}, bf16[5120,128]{1,0:T(8,128)(2,1)}, u32[]{:S(2)}, u32[]{:S(2)}) collective-permute-start(bf16[5120,128]{1,0:T(8,128)(2,1)S(1)} %bitcast.23), channel_id=1, source_target_pairs={{0,1},{1,0},{2,3},{3,2},{4,5},{5,4},{6,7},{7,6},{8,9},{9,8},{10,11... | collective-permute-start | bytes 3932168 | tf_op jit(solution)/shard_map/ppermute | solution.py:245
  67.5 40.1 %collective-permute-start.7 = (bf16[1280,128]{1,0:T(8,128)(2,1)S(1)}, bf16[1280,128]{1,0:T(8,128)(2,1)}, u32[]{:S(2)}, u32[]{:S(2)}) collective-permute-start(bf16[1280,128]{1,0:T(8,128)(2,1)S(1)} %get-tuple-element.16), channel_id=1, source_target_pairs={{0,2},{1,3},{2,4},{3,5},{4,6},{5,7},{6,0},{7,1},{8,10},{9,11},{10,... | collective-permute-start | bytes 983048 | tf_op jit(solution)/shard_map/ppermute | solution.py:242
  73.1 34.7 %collective-permute-start.6 = (bf16[1280,128]{1,0:T(8,128)(2,1)}, bf16[1280,128]{1,0:T(8,128)(2,1)S(1)}, u32[]{:S(2)}, u32[]{:S(2)}) collective-permute-start(bf16[1280,128]{1,0:T(8,128)(2,1)} %collective-permute-done.5.refs_6_), channel_id=1, source_target_pairs={{0,1},{1,0},{2,3},{3,2},{4,5},{5,4},{6,7},{7,6},{8,9},{9,8},{10,11... | collective-permute-start | bytes 983048 | tf_op jit(solution)/shard_map/ppermute | solution.py:245
  103.2 36.0 %copy-start.1 = (bf16[24,128,128]{2,1,0:T(8,128)(2,1)}, bf16[24,128,128]{2,1,0:T(8,128)(2,1)S(1)}, u32[]{:S(2)}) copy-start(bf16[24,128,128]{2,1,0:T(8,128)(2,1)S(1)} %edge_filter.1) | copy-start | bytes 2359300
  104.1 12.3 %collective-permute-start.18 = (bf16[1536,128]{1,0:T(8,128)(2,1)}, bf16[1536,128]{1,0:T(8,128)(2,1)S(1)}, u32[]{:S(2)}, u32[]{:S(2)}) collective-permute-start(bf16[1536,128]{1,0:T(8,128)(2,1)} %bitcast.14), channel_id=1, source_target_pairs={{0,6},{1,7},{2,0},{3,1},{4,2},{5,3},{6,4},{7,5},{8,14},{9,15},{10,... | collective-permute-start | bytes 1179656 | tf_op jit(solution)/shard_map/ppermute | solution.py:242
  107.5 11.7 %collective-permute-start.20 = (bf16[1536,128]{1,0:T(8,128)(2,1)S(1)}, bf16[1536,128]{1,0:T(8,128)(2,1)}, u32[]{:S(2)}, u32[]{:S(2)}) collective-permute-start(bf16[1536,128]{1,0:T(8,128)(2,1)S(1)} %bitcast.32), channel_id=1, source_target_pairs={{0,2},{1,3},{2,4},{3,5},{4,6},{5,7},{6,0},{7,1},{8,10},{9,11},{10,... | collective-permute-start | bytes 1179656 | tf_op jit(solution)/shard_map/ppermute | solution.py:242
  107.5 17.3 %collective-permute-start.2 = (bf16[2560,128]{1,0:T(8,128)(2,1)S(1)}, bf16[2560,128]{1,0:T(8,128)(2,1)}, u32[]{:S(2)}, u32[]{:S(2)}) collective-permute-start(bf16[2560,128]{1,0:T(8,128)(2,1)S(1)} %collective-permute-done.1.refs_2_), channel_id=1, source_target_pairs={{0,1},{1,0},{2,3},{3,2},{4,5},{5,4},{6,7},{7,6},{8,9},{9,8},{10,11... | collective-permute-start | bytes 1966088 | tf_op jit(solution)/shard_map/ppermute | solution.py:245
  108.6 16.9 %collective-permute-start.4 = (bf16[2560,128]{1,0:T(8,128)(2,1)S(1)}, bf16[2560,128]{1,0:T(8,128)(2,1)}, u32[]{:S(2)}, u32[]{:S(2)}) collective-permute-start(bf16[2560,128]{1,0:T(8,128)(2,1)S(1)} %collective-permute-done.3.refs_4_.refs_5_), channel_id=1, source_target_pairs={{0,1},{1,0},{2,3},{3,2},{4,5},{5,4},{6,7},{7,6},{8,9},{9,8},{10,11... | collective-permute-start | bytes 1966088 | tf_op jit(solution)/shard_map/ppermute | solution.py:245
  117.1 22.0 %collective-permute-start.17 = (bf16[3072,128]{1,0:T(8,128)(2,1)S(1)}, bf16[3072,128]{1,0:T(8,128)(2,1)}, u32[]{:S(2)}, u32[]{:S(2)}) collective-permute-start(bf16[3072,128]{1,0:T(8,128)(2,1)S(1)} %bitcast.26), channel_id=1, source_target_pairs={{0,1},{1,0},{2,3},{3,2},{4,5},{5,4},{6,7},{7,6},{8,9},{9,8},{10,11... | collective-permute-start | bytes 2359304 | tf_op jit(solution)/shard_map/ppermute | solution.py:245
  119.3 4.6 %collective-permute-start.8 = (bf16[1280,128]{1,0:T(8,128)(2,1)}, bf16[1280,128]{1,0:T(8,128)(2,1)}, u32[]{:S(2)}, u32[]{:S(2)}) collective-permute-start(bf16[1280,128]{1,0:T(8,128)(2,1)} %collective-permute-done.7.refs_8_), channel_id=1, source_target_pairs={{0,1},{1,0},{2,3},{3,2},{4,5},{5,4},{6,7},{7,6},{8,9},{9,8},{10,11... | collective-permute-start | bytes 983048 | tf_op jit(solution)/shard_map/ppermute | solution.py:245
  123.8 6.6 %collective-permute-start.22 = (bf16[768,128]{1,0:T(8,128)(2,1)S(1)}, bf16[768,128]{1,0:T(8,128)(2,1)}, u32[]{:S(2)}, u32[]{:S(2)}) collective-permute-start(bf16[768,128]{1,0:T(8,128)(2,1)S(1)} %get-tuple-element.22), channel_id=1, source_target_pairs={{0,6},{1,7},{2,0},{3,1},{4,2},{5,3},{6,4},{7,5},{8,14},{9,15},{10,... | collective-permute-start | bytes 589832 | tf_op jit(solution)/shard_map/ppermute | solution.py:242
  124.8 14.3 %collective-permute-start.19 = (bf16[1536,128]{1,0:T(8,128)(2,1)}, bf16[1536,128]{1,0:T(8,128)(2,1)}, u32[]{:S(2)}, u32[]{:S(2)}) collective-permute-start(bf16[1536,128]{1,0:T(8,128)(2,1)} %copy-done.4), channel_id=1, source_target_pairs={{0,1},{1,0},{2,3},{3,2},{4,5},{5,4},{6,7},{7,6},{8,9},{9,8},{10,11... | collective-permute-start | bytes 1179656 | tf_op jit(solution)/shard_map/ppermute | solution.py:245
  125.5 13.6 %collective-permute-start.21 = (bf16[1536,128]{1,0:T(8,128)(2,1)}, bf16[1536,128]{1,0:T(8,128)(2,1)}, u32[]{:S(2)}, u32[]{:S(2)}) collective-permute-start(bf16[1536,128]{1,0:T(8,128)(2,1)} %collective-permute-done.20.refs_5_.refs_23_), channel_id=1, source_target_pairs={{0,1},{1,0},{2,3},{3,2},{4,5},{5,4},{6,7},{7,6},{8,9},{9,8},{10,11... | collective-permute-start | bytes 1179656 | tf_op jit(solution)/shard_map/ppermute | solution.py:245
  125.6 7.4 %collective-permute-start.24 = (bf16[768,128]{1,0:T(8,128)(2,1)S(1)}, bf16[768,128]{1,0:T(8,128)(2,1)}, u32[]{:S(2)}, u32[]{:S(2)}) collective-permute-start(bf16[768,128]{1,0:T(8,128)(2,1)S(1)} %get-tuple-element.20), channel_id=1, source_target_pairs={{0,2},{1,3},{2,4},{3,5},{4,6},{5,7},{6,0},{7,1},{8,10},{9,11},{10,... | collective-permute-start | bytes 589832 | tf_op jit(solution)/shard_map/ppermute | solution.py:242
  130.5 8.7 %collective-permute-start.23 = (bf16[768,128]{1,0:T(8,128)(2,1)}, bf16[768,128]{1,0:T(8,128)(2,1)}, u32[]{:S(2)}, u32[]{:S(2)}) collective-permute-start(bf16[768,128]{1,0:T(8,128)(2,1)} %collective-permute-done.22.refs_7_.refs_24_), channel_id=1, source_target_pairs={{0,1},{1,0},{2,3},{3,2},{4,5},{5,4},{6,7},{7,6},{8,9},{9,8},{10,11... | collective-permute-start | bytes 589832 | tf_op jit(solution)/shard_map/ppermute | solution.py:245
  133.0 6.2 %collective-permute-start.25 = (bf16[768,128]{1,0:T(8,128)(2,1)}, bf16[768,128]{1,0:T(8,128)(2,1)}, u32[]{:S(2)}, u32[]{:S(2)}) collective-permute-start(bf16[768,128]{1,0:T(8,128)(2,1)} %collective-permute-done.24.refs_9_.refs_26_), channel_id=1, source_target_pairs={{0,1},{1,0},{2,3},{3,2},{4,5},{5,4},{6,7},{7,6},{8,9},{9,8},{10,11... | collective-permute-start | bytes 589832 | tf_op jit(solution)/shard_map/ppermute | solution.py:245
  142.1 34.1 %copy-start.18 = (bf16[1280,128]{1,0:T(8,128)(2,1)S(1)}, bf16[1280,128]{1,0:T(8,128)(2,1)}, u32[]{:S(2)}) copy-start(bf16[1280,128]{1,0:T(8,128)(2,1)} %get-tuple-element.17) | copy-start | bytes 983044
  142.2 38.7 %copy-start.19 = (bf16[1280,128]{1,0:T(8,128)(2,1)S(1)}, bf16[1280,128]{1,0:T(8,128)(2,1)}, u32[]{:S(2)}) copy-start(bf16[1280,128]{1,0:T(8,128)(2,1)} %get-tuple-element.15) | copy-start | bytes 983044
  158.4 42.2 %copy-start.17 = (bf16[12,128,128]{2,1,0:T(8,128)(2,1)S(1)}, bf16[12,128,128]{2,1,0:T(8,128)(2,1)}, u32[]{:S(2)}) copy-start(bf16[12,128,128]{2,1,0:T(8,128)(2,1)} %copy-done.16) | copy-start | bytes 1179652
  158.4 44.5 %copy-start.20 = (bf16[768,128]{1,0:T(8,128)(2,1)S(1)}, bf16[768,128]{1,0:T(8,128)(2,1)}, u32[]{:S(2)}) copy-start(bf16[768,128]{1,0:T(8,128)(2,1)} %get-tuple-element.21) | copy-start | bytes 589828
  158.4 2.7 %collective-permute-start.26 = (bf16[1,8,1024]{2,1,0:T(8,128)(2,1)S(1)}, bf16[1,8,1024]{2,1,0:T(8,128)(2,1)S(1)}, u32[]{:S(2)}, u32[]{:S(2)}) collective-permute-start(bf16[1,8,1024]{2,1,0:T(8,128)(2,1)S(1)} %bitcast.34), channel_id=1, source_target_pairs={{0,6},{1,7},{2,0},{3,1},{4,2},{5,3},{6,4},{7,5},{8,14},{9,15},{10,... | collective-permute-start | bytes 49160 | tf_op jit(solution)/shard_map/ppermute | solution.py:374
  158.5 4.2 %collective-permute-start.27 = (bf16[1,8,1024]{2,1,0:T(8,128)(2,1)S(1)}, bf16[1,8,1024]{2,1,0:T(8,128)(2,1)S(1)}, u32[]{:S(2)}, u32[]{:S(2)}) collective-permute-start(bf16[1,8,1024]{2,1,0:T(8,128)(2,1)S(1)} %bitcast.35), channel_id=1, source_target_pairs={{0,4},{1,5},{2,6},{3,7},{4,0},{5,1},{6,2},{7,3},{8,12},{9,13},{10,... | collective-permute-start | bytes 49160 | tf_op jit(solution)/shard_map/ppermute | solution.py:374
  159.3 4.2 %collective-permute-start.28 = (bf16[1,8,1024]{2,1,0:T(8,128)(2,1)S(1)}, bf16[1,8,1024]{2,1,0:T(8,128)(2,1)S(1)}, u32[]{:S(2)}, u32[]{:S(2)}) collective-permute-start(bf16[1,8,1024]{2,1,0:T(8,128)(2,1)S(1)} %bitcast.36), channel_id=1, source_target_pairs={{0,2},{1,3},{2,4},{3,5},{4,6},{5,7},{6,0},{7,1},{8,10},{9,11},{10,... | collective-permute-start | bytes 49160 | tf_op jit(solution)/shard_map/ppermute | solution.py:374
  163.5 4.5 %collective-permute-start.29 = (bf16[4,8,1024]{2,1,0:T(8,128)(2,1)S(1)}, bf16[4,8,1024]{2,1,0:T(8,128)(2,1)S(1)}, u32[]{:S(2)}, u32[]{:S(2)}) collective-permute-start(bf16[4,8,1024]{2,1,0:T(8,128)(2,1)S(1)} %pad_maximum_fusion), channel_id=1, source_target_pairs={{0,24},{8,0},{16,8},{24,16},{32,56},{40,32},{48,40},{56,48},{64,88... | collective-permute-start | bytes 196616 | tf_op jit(solution)/shard_map/ppermute | solution.py:374
  165.1 4.6 %collective-permute-start.30 = (bf16[4,8,1024]{2,1,0:T(8,128)(2,1)S(1)}, bf16[4,8,1024]{2,1,0:T(8,128)(2,1)S(1)}, u32[]{:S(2)}, u32[]{:S(2)}) collective-permute-start(bf16[4,8,1024]{2,1,0:T(8,128)(2,1)S(1)} %pad_maximum_fusion), channel_id=1, source_target_pairs={{0,16},{8,24},{16,0},{24,8},{32,48},{40,56},{48,32},{56,40},{64,80... | collective-permute-start | bytes 196616 | tf_op jit(solution)/shard_map/ppermute | solution.py:374
  165.9 4.5 %collective-permute-start.31 = (bf16[4,8,1024]{2,1,0:T(8,128)(2,1)S(1)}, bf16[4,8,1024]{2,1,0:T(8,128)(2,1)S(1)}, u32[]{:S(2)}, u32[]{:S(2)}) collective-permute-start(bf16[4,8,1024]{2,1,0:T(8,128)(2,1)S(1)} %pad_maximum_fusion), channel_id=1, source_target_pairs={{0,8},{8,16},{16,24},{24,0},{32,40},{40,48},{48,56},{56,32},{64,72... | collective-permute-start | bytes 196616 | tf_op jit(solution)/shard_map/ppermute | solution.py:374
  171.0 5.2 %collective-permute-start.32 = (bf16[16,8,1024]{2,1,0:T(8,128)(2,1)S(1)}, bf16[16,8,1024]{2,1,0:T(8,128)(2,1)S(1)}, u32[]{:S(2)}, u32[]{:S(2)}) collective-permute-start(bf16[16,8,1024]{2,1,0:T(8,128)(2,1)S(1)} %get-tuple-element.31), channel_id=1, source_target_pairs={{0,96},{8,104},{16,112},{24,120},{32,0},{40,8},{48,16},{56,24},{64... | collective-permute-start | bytes 786440 | tf_op jit(solution)/shard_map/ppermute | solution.py:374
  172.2 18.5 %collective-permute-start.36 = (bf16[2560,128]{1,0:T(8,128)(2,1)}, bf16[2560,128]{1,0:T(8,128)(2,1)S(1)}, u32[]{:S(2)}, u32[]{:S(2)}) collective-permute-start(bf16[2560,128]{1,0:T(8,128)(2,1)} %bitcast.7), channel_id=1, source_target_pairs={{0,6},{1,7},{2,0},{3,1},{4,2},{5,3},{6,4},{7,5},{8,14},{9,15},{10,... | collective-permute-start | bytes 1966088 | tf_op jit(solution)/shard_map/ppermute | solution.py:242
  174.0 6.8 %collective-permute-start.33 = (bf16[16,8,1024]{2,1,0:T(8,128)(2,1)S(1)}, bf16[16,8,1024]{2,1,0:T(8,128)(2,1)S(1)}, u32[]{:S(2)}, u32[]{:S(2)}) collective-permute-start(bf16[16,8,1024]{2,1,0:T(8,128)(2,1)S(1)} %get-tuple-element.31), channel_id=1, source_target_pairs={{0,64},{8,72},{16,80},{24,88},{32,96},{40,104},{48,112},{56,120},{... | collective-permute-start | bytes 786440 | tf_op jit(solution)/shard_map/ppermute | solution.py:374
  174.4 9.5 %collective-permute-start.34 = (bf16[16,8,1024]{2,1,0:T(8,128)(2,1)S(1)}, bf16[16,8,1024]{2,1,0:T(8,128)(2,1)S(1)}, u32[]{:S(2)}, u32[]{:S(2)}) collective-permute-start(bf16[16,8,1024]{2,1,0:T(8,128)(2,1)S(1)} %get-tuple-element.31), channel_id=1, source_target_pairs={{0,32},{8,40},{16,48},{24,56},{32,64},{40,72},{48,80},{56,88},{64,... | collective-permute-start | bytes 786440 | tf_op jit(solution)/shard_map/ppermute | solution.py:374
  175.0 25.6 %collective-permute-start.37 = (bf16[2560,128]{1,0:T(8,128)(2,1)}, bf16[2560,128]{1,0:T(8,128)(2,1)}, u32[]{:S(2)}, u32[]{:S(2)}) collective-permute-start(bf16[2560,128]{1,0:T(8,128)(2,1)} %bitcast.6), channel_id=1, source_target_pairs={{0,2},{1,3},{2,4},{3,5},{4,6},{5,7},{6,0},{7,1},{8,10},{9,11},{10,... | collective-permute-start | bytes 1966088 | tf_op jit(solution)/shard_map/ppermute | solution.py:242
  176.3 16.8 %collective-permute-start.38 = (bf16[1280,128]{1,0:T(8,128)(2,1)S(1)}, bf16[1280,128]{1,0:T(8,128)(2,1)S(1)}, u32[]{:S(2)}, u32[]{:S(2)}) collective-permute-start(bf16[1280,128]{1,0:T(8,128)(2,1)S(1)} %copy-done.18), channel_id=1, source_target_pairs={{0,6},{1,7},{2,0},{3,1},{4,2},{5,3},{6,4},{7,5},{8,14},{9,15},{10,... | collective-permute-start | bytes 983048 | tf_op jit(solution)/shard_map/ppermute | solution.py:242
  178.0 44.3 %copy-start.6 = (bf16[1536,128]{1,0:T(8,128)(2,1)S(1)}, bf16[1536,128]{1,0:T(8,128)(2,1)}, u32[]{:S(2)}) copy-start(bf16[1536,128]{1,0:T(8,128)(2,1)} %copy-done.4) | copy-start | bytes 1179652
  178.0 44.3 %copy-start.9 = (bf16[1280,128]{1,0:T(8,128)(2,1)S(1)}, bf16[1280,128]{1,0:T(8,128)(2,1)}, u32[]{:S(2)}) copy-start(bf16[1280,128]{1,0:T(8,128)(2,1)} %copy-done.7) | copy-start | bytes 983044
  180.9 15.7 %collective-permute-start.39 = (bf16[1280,128]{1,0:T(8,128)(2,1)S(1)}, bf16[1280,128]{1,0:T(8,128)(2,1)S(1)}, u32[]{:S(2)}, u32[]{:S(2)}) collective-permute-start(bf16[1280,128]{1,0:T(8,128)(2,1)S(1)} %copy-done.19), channel_id=1, source_target_pairs={{0,2},{1,3},{2,4},{3,5},{4,6},{5,7},{6,0},{7,1},{8,10},{9,11},{10,... | collective-permute-start | bytes 983048 | tf_op jit(solution)/shard_map/ppermute | solution.py:242
  184.7 30.5 %copy-start.22 = (bf16[128,8,1024]{2,1,0:T(8,128)(2,1)}, bf16[128,8,1024]{2,1,0:T(8,128)(2,1)S(1)}, u32[]{:S(2)}) copy-start(bf16[128,8,1024]{2,1,0:T(8,128)(2,1)S(1)} %get-tuple-element.24) | copy-start | bytes 6291460
  184.7 35.2 %collective-permute-start.35 = (bf16[64,8,1024]{2,1,0:T(8,128)(2,1)}, bf16[64,8,1024]{2,1,0:T(8,128)(2,1)}, u32[]{:S(2)}, u32[]{:S(2)}) collective-permute-start(bf16[64,8,1024]{2,1,0:T(8,128)(2,1)} %get-tuple-element.23), channel_id=1, source_target_pairs={{0,1},{1,0},{2,3},{3,2},{4,5},{5,4},{6,7},{7,6},{8,9},{9,8},{10,11... | collective-permute-start | bytes 3145736 | tf_op jit(solution)/shard_map/ppermute | solution.py:245
  190.7 24.5 %copy-start.23 = (bf16[2560,128]{1,0:T(8,128)(2,1)}, bf16[2560,128]{1,0:T(8,128)(2,1)S(1)}, u32[]{:S(2)}) copy-start(bf16[2560,128]{1,0:T(8,128)(2,1)S(1)} %collective-permute-done.36.refs_3_) | copy-start | bytes 1966084
  190.7 12.2 %collective-permute-start.40 = (bf16[2560,128]{1,0:T(8,128)(2,1)S(1)}, bf16[2560,128]{1,0:T(8,128)(2,1)S(1)}, u32[]{:S(2)}, u32[]{:S(2)}) collective-permute-start(bf16[2560,128]{1,0:T(8,128)(2,1)S(1)} %collective-permute-done.36.refs_3_), channel_id=1, source_target_pairs={{0,1},{1,0},{2,3},{3,2},{4,5},{5,4},{6,7},{7,6},{8,9},{9,8},{10,11... | collective-permute-start | bytes 1966088 | tf_op jit(solution)/shard_map/ppermute | solution.py:245
  193.1 7.5 %collective-permute-start.42 = (bf16[1280,128]{1,0:T(8,128)(2,1)S(1)}, bf16[1280,128]{1,0:T(8,128)(2,1)S(1)}, u32[]{:S(2)}, u32[]{:S(2)}) collective-permute-start(bf16[1280,128]{1,0:T(8,128)(2,1)S(1)} %collective-permute-done.38.refs_7_), channel_id=1, source_target_pairs={{0,1},{1,0},{2,3},{3,2},{4,5},{5,4},{6,7},{7,6},{8,9},{9,8},{10,11... | collective-permute-start | bytes 983048 | tf_op jit(solution)/shard_map/ppermute | solution.py:245
  196.6 5.4 %collective-permute-start.43 = (bf16[1280,128]{1,0:T(8,128)(2,1)S(1)}, bf16[1280,128]{1,0:T(8,128)(2,1)S(1)}, u32[]{:S(2)}, u32[]{:S(2)}) collective-permute-start(bf16[1280,128]{1,0:T(8,128)(2,1)S(1)} %collective-permute-done.39.refs_9_), channel_id=1, source_target_pairs={{0,1},{1,0},{2,3},{3,2},{4,5},{5,4},{6,7},{7,6},{8,9},{9,8},{10,11... | collective-permute-start | bytes 983048 | tf_op jit(solution)/shard_map/ppermute | solution.py:245
  200.6 10.4 %collective-permute-start.44 = (bf16[1536,128]{1,0:T(8,128)(2,1)S(1)}, bf16[1536,128]{1,0:T(8,128)(2,1)S(1)}, u32[]{:S(2)}, u32[]{:S(2)}) collective-permute-start(bf16[1536,128]{1,0:T(8,128)(2,1)S(1)} %bitcast.33), channel_id=1, source_target_pairs={{0,6},{1,7},{2,0},{3,1},{4,2},{5,3},{6,4},{7,5},{8,14},{9,15},{10,... | collective-permute-start | bytes 1179656 | tf_op jit(solution)/shard_map/ppermute | solution.py:242
  200.6 11.9 %collective-permute-start.45 = (bf16[1536,128]{1,0:T(8,128)(2,1)}, bf16[1536,128]{1,0:T(8,128)(2,1)S(1)}, u32[]{:S(2)}, u32[]{:S(2)}) collective-permute-start(bf16[1536,128]{1,0:T(8,128)(2,1)} %bitcast.14), channel_id=1, source_target_pairs={{0,2},{1,3},{2,4},{3,5},{4,6},{5,7},{6,0},{7,1},{8,10},{9,11},{10,... | collective-permute-start | bytes 1179656 | tf_op jit(solution)/shard_map/ppermute | solution.py:242
  202.0 20.2 %collective-permute-start.41 = (bf16[2560,128]{1,0:T(8,128)(2,1)}, bf16[2560,128]{1,0:T(8,128)(2,1)}, u32[]{:S(2)}, u32[]{:S(2)}) collective-permute-start(bf16[2560,128]{1,0:T(8,128)(2,1)} %collective-permute-done.37.refs_4_), channel_id=1, source_target_pairs={{0,1},{1,0},{2,3},{3,2},{4,5},{5,4},{6,7},{7,6},{8,9},{9,8},{10,11... | collective-permute-start | bytes 1966088 | tf_op jit(solution)/shard_map/ppermute | solution.py:245
  202.9 12.3 %collective-permute-start.46 = (bf16[768,128]{1,0:T(8,128)(2,1)S(1)}, bf16[768,128]{1,0:T(8,128)(2,1)S(1)}, u32[]{:S(2)}, u32[]{:S(2)}) collective-permute-start(bf16[768,128]{1,0:T(8,128)(2,1)S(1)} %copy-done.20), channel_id=1, source_target_pairs={{0,6},{1,7},{2,0},{3,1},{4,2},{5,3},{6,4},{7,5},{8,14},{9,15},{10,... | collective-permute-start | bytes 589832 | tf_op jit(solution)/shard_map/ppermute | solution.py:242
  211.0 6.1 %collective-permute-start.47 = (bf16[768,128]{1,0:T(8,128)(2,1)}, bf16[768,128]{1,0:T(8,128)(2,1)S(1)}, u32[]{:S(2)}, u32[]{:S(2)}) collective-permute-start(bf16[768,128]{1,0:T(8,128)(2,1)} %get-tuple-element.19), channel_id=1, source_target_pairs={{0,2},{1,3},{2,4},{3,5},{4,6},{5,7},{6,0},{7,1},{8,10},{9,11},{10,... | collective-permute-start | bytes 589832 | tf_op jit(solution)/shard_map/ppermute | solution.py:242
  212.5 9.8 %collective-permute-start.48 = (bf16[1536,128]{1,0:T(8,128)(2,1)S(1)}, bf16[1536,128]{1,0:T(8,128)(2,1)}, u32[]{:S(2)}, u32[]{:S(2)}) collective-permute-start(bf16[1536,128]{1,0:T(8,128)(2,1)S(1)} %collective-permute-done.44.refs_21_), channel_id=1, source_target_pairs={{0,1},{1,0},{2,3},{3,2},{4,5},{5,4},{6,7},{7,6},{8,9},{9,8},{10,11... | collective-permute-start | bytes 1179656 | tf_op jit(solution)/shard_map/ppermute | solution.py:245
  215.2 7.1 %collective-permute-start.49 = (bf16[1536,128]{1,0:T(8,128)(2,1)S(1)}, bf16[1536,128]{1,0:T(8,128)(2,1)}, u32[]{:S(2)}, u32[]{:S(2)}) collective-permute-start(bf16[1536,128]{1,0:T(8,128)(2,1)S(1)} %collective-permute-done.45.refs_22_), channel_id=1, source_target_pairs={{0,1},{1,0},{2,3},{3,2},{4,5},{5,4},{6,7},{7,6},{8,9},{9,8},{10,11... | collective-permute-start | bytes 1179656 | tf_op jit(solution)/shard_map/ppermute | solution.py:245
  217.1 5.2 %collective-permute-start.50 = (bf16[768,128]{1,0:T(8,128)(2,1)S(1)}, bf16[768,128]{1,0:T(8,128)(2,1)S(1)}, u32[]{:S(2)}, u32[]{:S(2)}) collective-permute-start(bf16[768,128]{1,0:T(8,128)(2,1)S(1)} %collective-permute-done.46.refs_25_), channel_id=1, source_target_pairs={{0,1},{1,0},{2,3},{3,2},{4,5},{5,4},{6,7},{7,6},{8,9},{9,8},{10,11... | collective-permute-start | bytes 589832 | tf_op jit(solution)/shard_map/ppermute | solution.py:245
  219.9 2.4 %collective-permute-start.51 = (bf16[768,128]{1,0:T(8,128)(2,1)S(1)}, bf16[768,128]{1,0:T(8,128)(2,1)S(1)}, u32[]{:S(2)}, u32[]{:S(2)}) collective-permute-start(bf16[768,128]{1,0:T(8,128)(2,1)S(1)} %collective-permute-done.47.refs_27_), channel_id=1, source_target_pairs={{0,1},{1,0},{2,3},{3,2},{4,5},{5,4},{6,7},{7,6},{8,9},{9,8},{10,11... | collective-permute-start | bytes 589832 | tf_op jit(solution)/shard_map/ppermute | solution.py:245
  (13 other events, 65.1 us)

commit v2 on v1

v2 whole, which is shorter than its diff:
```python
import functools

import jax
import jax.numpy as jnp
from jax import lax
from jax.experimental import pallas as pl
from jax.experimental.pallas import tpu as pltpu
from jax.sharding import PartitionSpec as P

REACH = 2
CHEB = 6
DEEP = REACH * CHEB
BF = jnp.bfloat16
F32 = jnp.float32
ANY = pl.BlockSpec(memory_space=pl.ANY)
SMEM = pl.BlockSpec(memory_space=pltpu.SMEM)
VMEM = pl.BlockSpec(memory_space=pltpu.VMEM)


def filter_steps(count, row_shift, segments, even_odd, out, ready):
    for step in range(1, CHEB + 1):
        low = REACH * step
        turns = 2
        unroll = (count - 2 * low) // turns

        def body(turn, step=step, low=low, unroll=unroll):
            for part in range(unroll):
                for which, (ids, live, tiles, first) in enumerate(segments):
                    even, odd = even_odd[which]
                    source = first if step == 1 else (odd if step % 2 == 0 else even)
                    target = odd if step % 2 else even
                    before = first if step == 2 else target
                    block = low + turn * unroll + part
                    row = block - row_shift
                    left = jnp.concatenate([tiles[row, t] for t in range(4)], axis=1)
                    right = jnp.concatenate([source[ids[row * 4 + t]] for t in range(4)], axis=0)
                    value = jnp.dot(left, right, preferred_element_type=F32) * live[row]
                    if step > 1:
                        value = 2.0 * value - before[block].astype(F32)
                    if step == CHEB:
                        out[which * (count - 2 * low) + turn * unroll + part] = value.astype(BF)
                    else:
                        target[block] = value.astype(BF)

        if step == 1 and ready is not None:
            for turn in range(turns):
                ready(turn)
                body(turn)
        else:

            def looped(turn, carry, body=body):
                body(turn)
                return carry

            lax.fori_loop(0, turns, looped, 0)


def inner_kernel(count, ids, live, tiles, vectors, out, seg_t, seg_v, even, odd, sems):
    half = count // 2
    copies = [
        pltpu.make_async_copy(vectors, seg_v, sems.at[0]),
        pltpu.make_async_copy(tiles.at[pl.ds(0, half)], seg_t.at[pl.ds(0, half)], sems.at[1]),
        pltpu.make_async_copy(
            tiles.at[pl.ds(half, half)], seg_t.at[pl.ds(half, half)], sems.at[2]
        ),
    ]
    for c in copies:
        c.start()

    def ready(turn):
        if turn == 0:
            copies[0].wait()
        copies[1 + turn].wait()

    filter_steps(count, 0, [(ids, live, seg_t, seg_v)], [(even, odd)], out, ready)


def edge_kernel(count, ids0, live0, ids1, live1, core, tiles, vectors, near, far, vlow, vhigh,
                out, seg_v, seg_t, even, odd, even1, odd1, sems):
    deep_rows = DEEP - REACH
    span = 3 * DEEP
    c = core[0]
    own_rows = 2 * DEEP - REACH
    copies = []

    def copy(source, target):
        copies.append(pltpu.make_async_copy(source, target, sems.at[len(copies)]))
        copies[-1].start()

    moved = deep_rows * 4
    for segment, halo, near_v, far_v, far_t in (
        (0, vlow, 0, DEEP, deep_rows),
        (1, vhigh, 2 * DEEP, 0, 0),
    ):
        own_v = 0 if segment == 0 else count - 2 * DEEP
        own_t = 0 if segment == 0 else count - own_rows
        copy(halo.at[pl.ds(0, DEEP)], seg_v.at[segment, pl.ds(near_v, DEEP)])
        copy(vectors.at[pl.ds(own_v, 2 * DEEP)], seg_v.at[segment, pl.ds(far_v, 2 * DEEP)])
        copy(
            tiles.at[pl.ds(own_t * 4, own_rows * 4)],
            seg_t.at[segment, pl.ds(far_t * 4, own_rows * 4)],
        )
    copy(near, seg_t.at[c, pl.ds(c * (own_rows * 4), moved)])
    copy(far, seg_t.at[1 - c, pl.ds((1 - c) * (own_rows * 4), moved)])
    for c in copies:
        c.wait()

    class Rows:
        def __init__(self, which):
            self.which = which

        def __getitem__(self, at):
            return seg_t[self.which, at[0] * 4 + at[1]]

    filter_steps(
        span,
        REACH,
        [
            (ids0, live0, Rows(0), seg_v.at[0]),
            (ids1, live1, Rows(1), seg_v.at[1]),
        ],
        [(even, odd), (even1, odd1)],
        out,
        None,
    )


def gram_kernel(half, with_base, place, *refs):
    if with_base:
        base, refs = refs[0], refs[1:]
    own_in, twin_in, n1, s1, o1, os1, out, flipped, own, twin, beside, across, sems = refs
    i, c = place[2], place[3]
    copies = []

    def copy(source, target):
        copies.append(pltpu.make_async_copy(source, target, sems.at[len(copies)]))
        copies[-1].start()

    copy(own_in, own)
    copy(twin_in, twin)
    for e in range(2):
        copy(n1.at[e], beside.at[c, e])
        copy(s1.at[1 - e], beside.at[1 - c, e])
        copy(o1.at[e], across.at[c, e])
        copy(os1.at[1 - e], across.at[1 - c, e])
    for copied in copies:
        copied.wait()
    q = half // 2
    for part in range(4):
        flipped[part] = own[part * q : (part + 1) * q, :].T

    def dot(part, piece):
        return jnp.dot(flipped[part], piece, preferred_element_type=F32)

    def all_rows(piece):
        return sum(dot(p, piece[p * q : (p + 1) * q]) for p in range(4)) * 0.5

    values = [all_rows(own), all_rows(twin)]
    for e in range(2):
        values.append(dot(0, beside[0, e, :q]) + dot(1, beside[0, e, q:]))
    for e in range(2):
        values.append(dot(i, across[0, e]) + dot(2 + i, across[1, e]))
    for e in range(2):
        values.append(dot(2, beside[1, e, :q]) + dot(3, beside[1, e, q:]))
    for column, value in enumerate(values):
        if with_base:
            value = value + base[:, column * 128 : (column + 1) * 128]
        out[:, column * 128 : (column + 1) * 128] = value


def split(value):
    high = value.astype(BF)
    return high, (value - high.astype(F32)).astype(BF)


def final_kernel(place, scale_in, gathered, gathered_twin, *refs):
    pieces, (out, rows_buf, table, matrix, sems) = refs[:18], refs[18:]
    x, y, i, c = place[0], place[1], place[2], place[3]
    low = DEEP * 128
    total = rows_buf.shape[1]
    inner = (total - 2 * low) // 2
    copies = [[], []]

    def copy(group, source, row, count, panel):
        copied = pltpu.make_async_copy(
            source, rows_buf.at[panel, pl.ds(row, count)], sems.at[len(copies[0]) + len(copies[1])]
        )
        copied.start()
        copies[group].append(copied)

    o2, os2 = pieces[16:18]
    groups = ((low, low + inner, inner, 0), (0, low + 2 * inner, low, inner))
    for group, (first, second, half, at) in enumerate(groups):
        own, twin, n1, s1, o1, os1, n2, s2 = pieces[8 * group : 8 * group + 8]
        q = half // 2
        step = c * (second - first)
        up, down = first + step, second - step
        for e, piece in enumerate((own, twin)):
            copy(group, piece.at[pl.ds(0, half)], first, half, e)
            copy(group, piece.at[pl.ds(half, half)], second, half, e)
        for e in range(2):
            mine, other = i * q, (1 - i) * q
            copy(group, n1.at[e], up, half, 2 + e + 4 * c)
            copy(group, s1.at[1 - e], down, half, 6 + e - 4 * c)
            copy(group, o1.at[e], up + mine, q, 4 + e)
            copy(group, os1.at[1 - e], down + mine, q, 4 + e)
            copy(group, n2.at[e], down, half, 2 + e + 4 * c)
            copy(group, s2.at[1 - e], up, half, 6 + e - 4 * c)
            copy(group, o2.at[pl.ds(at + e * q, q)], up + other, q, 4 + e)
            copy(group, os2.at[pl.ds(at + (1 - e) * q, q)], down + other, q, 4 + e)

    for dx in range(4):
        for dy in range(4):
            chunk = lax.rem(x + dx, 4) * 4 + lax.rem(y + dy, 4)
            for dz in range(4):
                for e in range(2):
                    piece = (gathered_twin if e else gathered)[(dx * 4 + dy) * 4 + dz].astype(F32)
                    for qz in range(4):
                        for qe in range(2):
                            column = 2 * ((dz + qz) % 4) + (e ^ qe)
                            table[2 * dz + e, chunk, :, pl.ds(column * 128, 128)] = piece[
                                :, (2 * qz + qe) * 128 : (2 * qz + qe + 1) * 128
                            ]
    width = 1024
    diagonal = lax.broadcasted_iota(jnp.int32, (128, 128), 0) == lax.broadcasted_iota(
        jnp.int32, (128, 128), 1
    )
    eye = diagonal.astype(F32)
    trace = jnp.zeros((128, 128), F32)
    for p in range(8):
        panel = table[p].reshape(128, width)
        matrix[pl.ds(p * 128, 128), :] = panel.astype(BF)
        trace = trace + panel[:, p * 128 : (p + 1) * 128] * eye
    mean = 2.0 * jnp.sum(trace) / float(total * 16)
    scale = scale_in[0] * mean / width
    kappa = 1.0 / (scale * float(total * 16))
    own_row = table[0].reshape(128, width)
    own_column = jnp.concatenate(
        [table[p].reshape(128, width)[:, 0:128].T for p in range(8)], axis=1
    )
    unit = jnp.concatenate([eye, jnp.zeros((128, width - 128), F32)], axis=1)
    root = 1.5 * unit - (0.5 * kappa) * (own_row + own_column)

    def times(value):
        both = jnp.concatenate(split(value), axis=0)
        whole = matrix[...]
        product = jnp.dot(both, whole, preferred_element_type=F32) + lax.dot_general(
            both, whole, (((1,), (1,)), ((), ())), preferred_element_type=F32
        )
        return kappa * (product[:128] + product[128:])

    second = 1.5 * root - 0.5 * times(root)
    third = 1.5 * second - 0.5 * times(second)
    result = 1.5 * root - 0.5 * times(third)
    weights = (result / jnp.sqrt(jnp.full((128, width), scale, F32))).astype(BF).T
    step = 512
    ranges = ([(low, low + 2 * inner)], [(0, low), (low + 2 * inner, total)])
    for group in range(2):
        for copied in copies[group]:
            copied.wait()
        for begin, end in ranges[group]:
            for row in range(begin, end, step):
                left = jnp.concatenate([rows_buf[p, row : row + step] for p in range(8)], axis=1)
                product = jnp.dot(left, weights, preferred_element_type=F32)
                out[row : row + step] = product.astype(BF)


def params(limit):
    return pltpu.CompilerParams(vmem_limit_bytes=limit * 2**20)


def cost(flops, data):
    return pl.CostEstimate(flops=flops, bytes_accessed=data, transcendentals=0)


def local(ham_tiles, tile_columns, stack_lengths, start_vectors, spectral_scale):
    row_count, panel = start_vectors.shape
    blocks = ham_tiles.shape[0]
    total_blocks = blocks * lax.axis_size("row")
    row_at, vec_at = lax.axis_index("row"), lax.axis_index("vec")
    z_at, core_at = vec_at // 2, vec_at % 2
    rows16, zs = lax.axis_size("row"), lax.axis_size("vec") // 2

    def z_perm(move, flip=0):
        return [
            (2 * z + c, 2 * ((z + move) % zs) + (c ^ flip)) for z in range(zs) for c in range(2)
        ]

    def by_z(value, move):
        return lax.ppermute(value, "vec", z_perm(move))

    def swap(value):
        return lax.ppermute(value, "vec", z_perm(0, 1))

    forward = [(r, (r + 1) % rows16) for r in range(rows16)]
    backward = [(r, (r - 1) % rows16) for r in range(rows16)]

    block_ids = row_at * blocks + jnp.arange(blocks, dtype=jnp.int32)
    offsets = (tile_columns - block_ids[:, None] + REACH) % total_blocks - REACH
    local_rows = jnp.arange(blocks, dtype=jnp.int32)
    live = ((local_rows < stack_lengths[0] - REACH) | (local_rows >= blocks - REACH)).astype(
        jnp.int32
    )
    meta = jnp.concatenate([offsets, jnp.broadcast_to(live[:, None], (blocks, 4))], axis=1)
    vectors = start_vectors.reshape(blocks, 128, panel)
    flat_tiles = ham_tiles.reshape(blocks * 4, 128, 128)
    deep_rows = DEEP - REACH

    devices = [(r, z, c) for r in range(rows16) for z in range(zs) for c in range(2)]
    row_sides = [
        ((r * zs + z) * 2 + c, ((r + 1 - 2 * c) % rows16 * zs + z) * 2 + c) for r, z, c in devices
    ]
    sides = [(2 * z + c, 2 * ((z - 1 + 2 * c) % zs) + c) for z in range(zs) for c in range(2)]

    def with_facts(part, facts):
        block = jnp.pad(facts.astype(BF), ((0, 128 - deep_rows), (0, 120)))[None]
        return jnp.concatenate([part, block], axis=0)

    near = lax.ppermute(
        lax.dynamic_slice_in_dim(
            flat_tiles, (1 - core_at) * (4 * (blocks - deep_rows)), 4 * deep_rows, 0
        ),
        ("row", "vec"),
        row_sides,
    )
    vlow = lax.ppermute(
        with_facts(vectors[blocks - DEEP :], meta[blocks - deep_rows :]), "row", forward
    )
    vhigh = lax.ppermute(with_facts(vectors[:DEEP], meta[:deep_rows]), "row", backward)
    near, vlow, vhigh = lax.optimization_barrier((near, vlow, vhigh))
    far = swap(near)
    meta_low = vlow[-1, :deep_rows, :8].astype(jnp.int32)
    meta_high = vhigh[-1, :deep_rows, :8].astype(jnp.int32)

    inner_blocks = blocks - 2 * DEEP
    inner_ids = (local_rows[:, None] + offsets).reshape(-1)
    inner = pl.pallas_call(
        functools.partial(inner_kernel, blocks),
        out_shape=jax.ShapeDtypeStruct((inner_blocks, 128, panel), BF),
        in_specs=[SMEM, SMEM, ANY, ANY],
        out_specs=VMEM,
        scratch_shapes=[
            pltpu.VMEM((blocks, 4, 128, 128), BF),
            pltpu.VMEM((blocks, 128, panel), BF),
            pltpu.VMEM((blocks, 128, panel), BF),
            pltpu.VMEM((blocks, 128, panel), BF),
            pltpu.SemaphoreType.DMA((3,)),
        ],
        compiler_params=params(58),
        cost_estimate=cost(10**6, 2**20),
        name="inner_filter",
    )(inner_ids, live.astype(F32), ham_tiles, vectors)

    def segment(parts):
        part = jnp.concatenate(parts, axis=0)
        places = REACH + jnp.arange(part.shape[0], dtype=jnp.int32)[:, None] + part[:, :4]
        return places.reshape(-1), part[:, 4].astype(F32)

    own_rows = 2 * DEEP - REACH
    ids0, live0 = segment([meta_low, meta[:own_rows]])
    ids1, live1 = segment([meta[blocks - own_rows :], meta_high])
    inner_own = inner.reshape(inner_blocks * 128, panel)

    quarter_of = jnp.where(z_at < 2, 0, 1).astype(jnp.int32)
    send_left = jnp.where((z_at + zs - 1) % zs < 2, 0, 1).astype(jnp.int32)
    send_right = jnp.where((z_at + 1) % zs < 2, 0, 1).astype(jnp.int32)

    place = jnp.stack([row_at // 4, row_at % 4, quarter_of, core_at]).astype(jnp.int32)
    forward_part = jnp.where(core_at == 0, send_left, send_right)

    def half_of(value, which):
        h = value.shape[0] // 2
        return lax.dynamic_slice_in_dim(value, which * h, h, 0)

    def pieces_of(pair_value, which):
        h = pair_value.shape[0] // 2
        q = h // 2
        return [lax.dynamic_slice_in_dim(pair_value, e * h + which * q, q, 0) for e in range(2)]

    def join(parts):
        return jnp.concatenate(parts, axis=0)

    def by_side(value):
        return lax.ppermute(value, "vec", sides)

    def needed(own, before_send, before_forward):
        twin = swap(own)
        sent, *_ = lax.optimization_barrier(
            (join([half_of(own, core_at), half_of(twin, core_at)]), *before_send)
        )
        n1 = by_side(sent)
        n1_late, *_ = lax.optimization_barrier((n1, *before_forward))
        o1 = by_side(join(pieces_of(n1_late, forward_part)))
        return own, twin, n1, swap(n1), o1, swap(o1)

    def rest_of(own, twin):
        return join([half_of(own, 1 - core_at), half_of(twin, 1 - core_at)])

    def two(value):
        return value.reshape(2, value.shape[0] // 2, panel)

    def gram(got, base):
        args = list(got[:2]) + [two(v) for v in got[2:]]
        half = got[0].shape[0] // 2
        return pl.pallas_call(
            functools.partial(gram_kernel, half, base is not None),
            out_shape=jax.ShapeDtypeStruct((128, 1024), F32),
            in_specs=[SMEM] + [VMEM] * (base is not None) + [ANY] * len(args),
            out_specs=VMEM,
            scratch_shapes=[
                pltpu.VMEM((4, 128, half // 2), BF),
                pltpu.VMEM((2 * half, panel), BF),
                pltpu.VMEM((2 * half, panel), BF),
                pltpu.VMEM((2, 2, half, panel), BF),
                pltpu.VMEM((2, 2, half // 2, panel), BF),
                pltpu.SemaphoreType.DMA((10,)),
            ],
            compiler_params=params(56),
            cost_estimate=cost(half * 256 * 1024, half * 128 * 24),
            name="gram",
        )(place, *([base] if base is not None else []), *args)

    inner_got = needed(inner_own, (far, vlow, vhigh), ())
    inner_gram = gram(inner_got, None)
    inner_rest, _ = lax.optimization_barrier((rest_of(*inner_got[:2]), inner_got[4]))
    inner_n2 = by_side(inner_rest)
    core_arg = core_at.astype(jnp.int32)[None]
    edge = pl.pallas_call(
        functools.partial(edge_kernel, blocks),
        out_shape=jax.ShapeDtypeStruct((2 * DEEP, 128, panel), BF),
        in_specs=[SMEM] * 5 + [ANY] * 6,
        out_specs=VMEM,
        scratch_shapes=[
            pltpu.VMEM((2, 3 * DEEP, 128, panel), BF),
            pltpu.VMEM((2, (3 * DEEP - 2 * REACH) * 4, 128, 128), BF),
        ]
        + [pltpu.VMEM((3 * DEEP, 128, panel), BF)] * 4
        + [pltpu.SemaphoreType.DMA((10,))],
        compiler_params=params(58),
        cost_estimate=cost(8 * 10**9, 11 * 2**20),
        name="edge_filter",
    )(ids0, live0, ids1, live1, core_arg, flat_tiles, vectors, near, far, vlow, vhigh)
    edge_own = edge.reshape(2 * DEEP * 128, panel)
    edge_got = needed(edge_own, (), (inner_gram, inner_n2))
    whole_gram = gram(edge_got, inner_gram)

    pieces = lax.all_to_all(
        whole_gram.reshape(rows16, 128 // rows16, 1024), "row", split_axis=0, concat_axis=0
    )
    mine = jnp.sum(pieces, axis=0).astype(BF)[None]

    def around(value, axis, perm_of):
        parts = [value] + [lax.ppermute(value, axis, perm_of(d)) for d in (1, 2, 3)]
        return jnp.concatenate(parts, axis=0)

    def row_perm(dx, dy):
        return [
            (4 * a + b, 4 * ((a - dx) % 4) + (b - dy) % 4) for a in range(4) for b in range(4)
        ]

    got = around(mine, "vec", lambda d: z_perm(-d))
    later = lax.optimization_barrier(
        (
            rest_of(*edge_got[:2]),
            join(pieces_of(inner_got[2], 1 - forward_part) + pieces_of(edge_got[2], 1 - forward_part)),
            got,
        )
    )
    edge_n2, o2 = by_side(later[0]), by_side(later[1])
    got = around(got, "row", lambda d: row_perm(0, d))
    got = around(got, "row", lambda d: row_perm(d, 0))
    parts = []
    for values, n2 in ((inner_got, inner_n2), (edge_got, edge_n2)):
        parts += list(values[:2]) + [two(v) for v in (*values[2:], n2, swap(n2))]
    parts += [o2, swap(o2)]
    return pl.pallas_call(
        final_kernel,
        out_shape=jax.ShapeDtypeStruct((row_count, panel), BF),
        in_specs=[SMEM, SMEM, VMEM, VMEM] + [ANY] * len(parts),
        out_specs=VMEM,
        scratch_shapes=[
            pltpu.VMEM((8, row_count, 128), BF),
            pltpu.VMEM((8, rows16, 128 // rows16, 1024), F32),
            pltpu.VMEM((1024, 1024), BF),
            pltpu.SemaphoreType.DMA((40,)),
        ],
        compiler_params=params(58),
        cost_estimate=cost(6 * 10**9, 20 * 2**20),
        name="final",
    )(place, spectral_scale, got, swap(got), *parts)


def solution(mesh):
    placed = (P("row", None, None, None), P("row", None), P("row"), P("row", "vec"), P())
    return jax.shard_map(
        local, mesh=mesh, in_specs=placed, out_specs=P("row", "vec"), check_vma=False
    )
```

time: 238 us -> 188 us (0.79)
  starting transfers between devices: 73.6 us -> 52.5 us
  local copies, waits for them, and re-layouts: 33.2 us -> 13.7 us
  blocking collectives: 16.2 us -> 0 us
  other arithmetic: 0.32 us -> 9.09 us
  Pallas kernels: 67.2 us -> 59.7 us
  waiting for transfers between devices: 45.5 us -> 50.3 us
    ppermute x22 -> x10, starting transfers between devices: 33.7 us -> 12.4 us  [the longest x1 5.76 us: local(): lax.ppermute(lax.dynamic_slice_in_dim(flat_tiles, (1 - core_at) * (4 * (b...]
    all_to_all x1 -> x0, blocking collectives: 16.2 us -> none  [local(): lax.all_to_all(whole_gram.reshape(rows16, 128 // rows16, 1024), 'row', sp...]
    unnamed x59 -> x48, local copies, waits for them, and re-layouts: 18.6 us -> 4.61 us
    all_to_all x0 -> x1, waiting for transfers between devices: none -> 10.2 us  [local(): lax.all_to_all(whole_gram.reshape(rows16, 128 // rows16, 1024), 'row', sp...]
    ppermute x21 -> x11, starting transfers between devices: 33.5 us -> 25.8 us  [swap(): return lax.ppermute(value, 'vec', z_perm(0, 1))]
    ppermute x22 -> x10, waiting for transfers between devices: 35.7 us -> 29.3 us  [the longest x7 29.3 us: by_side(): return lax.ppermute(value, 'vec', sides)]
    pallas_call x1, Pallas kernels: 22.7 us -> 16.8 us  [local(): pl.pallas_call(functools.partial(inner_kernel, blocks), out_shape=jax.Sha...]
    concatenate x0 -> x9, other arithmetic: none -> 5.16 us  [the longest x7 5.08 us: join(): return jnp.concatenate(parts, axis=0)]
  transfers between devices with their start and end apart: 52 -> 31, of which waited for: 16 -> 12; matrix products, arithmetic and copies ran while one was open for 7% -> 8% of each run, Pallas kernels for 21% -> 21%
where the time goes in v2:
time: 188 us; the launch traced here: 187 us
  Pallas kernels  59.7 us (32%)
  starting transfers between devices  52.5 us (28%)
  waiting for transfers between devices  50.3 us (27%)
  local copies, waits for them, and re-layouts  13.7 us (7%)
  other arithmetic  9.09 us (5%)
  between operations  2.04 us (1%)
    ppermute x7, waiting for transfers between devices, by_side(): return lax.ppermute(value, 'vec', sides)  29.3 us
    ppermute x11, starting transfers between devices, swap(): return lax.ppermute(value, 'vec', z_perm(0, 1))  25.8 us
    pallas_call x1, Pallas kernels, local(): pl.pallas_call(functools.partial(inner_kernel, blocks), out_shape=jax.Sha...  16.8 us
    pallas_call x1, Pallas kernels, local(): pl.pallas_call(functools.partial(edge_kernel, blocks), out_shape=jax.Shap...  16.7 us
    pallas_call x1, Pallas kernels, local(): pl.pallas_call(final_kernel, out_shape=jax.ShapeDtypeStruct((row_count, p...  14.7 us
    pallas_call x2, Pallas kernels, gram(): pl.pallas_call(functools.partial(gram_kernel, half, base is not None), ou...  11.5 us
    ppermute x9, starting transfers between devices, around(): parts = [value] + [lax.ppermute(value, axis, perm_of(d)) for d in (1, 2, 3)]  10.4 us
    all_to_all x1, waiting for transfers between devices, local(): lax.all_to_all(whole_gram.reshape(rows16, 128 // rows16, 1024), 'row', sp...  10.2 us
  transfers between devices with their start and end apart: 31, of which 12 were waited for; matrix products, arithmetic and copies ran while one was open for 8% of the time, Pallas kernels for 21%

profile of v2, /device:TPU:1, one launch (start us, length us, event | category | flops | bytes accessed | tf_op | source)
XLA Modules:
  0.0 187.4 jit_solution(12417769478363035086)
XLA Ops:
  0.0 2.5 %constant_dynamic-slice_fusion.14 = bf16[40,128,128]{2,1,0:T(8,128)(2,1)} fusion(bf16[256,128,128]{2,1,0:T(8,128)(2,1)} %bitcast.42, s32[]{:T(128)S(6)} %select_n.95), kind=kLoop, calls=%fused_computation.44 | loop fusion | bytes 2621444 | tf_op jit(solution)/shard_map/dynamic_slice | solution.py:320
  2.5 5.8 %collective-permute-start.1 = (bf16[40,128,128]{2,1,0:T(8,128)(2,1)}, bf16[40,128,128]{2,1,0:T(8,128)(2,1)}, u32[]{:S(2)}, u32[]{:S(2)}) collective-permute-start(bf16[40,128,128]{2,1,0:T(8,128)(2,1)} %constant_dynamic-slice_fusion.14), channel_id=1, source_target_pairs={{0,8},{1,121},{2,10},{3,123},{4,12},{5,125},{6,14},{7,127},{8,16},... | collective-permute-start | bytes 3932168 | tf_op jit(solution)/shard_map/ppermute | solution.py:319
  9.0 0.6 or_convert_fusion
  9.7 1.2 fusion.4
  11.1 4.8 %collective-permute-start.3 = (bf16[13,128,128]{2,1,0:T(8,128)(2,1)S(1)}, bf16[13,128,128]{2,1,0:T(8,128)(2,1)}, u32[]{:S(2)}, u32[]{:S(2)}) collective-permute-start(bf16[13,128,128]{2,1,0:T(8,128)(2,1)S(1)} %pad_maximum_fusion.7), channel_id=1, source_target_pairs={{0,120},{8,0},{16,8},{24,16},{32,24},{40,32},{48,40},{56,48},{64,5... | collective-permute-start | bytes 1277960 | tf_op jit(solution)/shard_map/ppermute | solution.py:329
  16.0 0.7 reshape.103.ids
  16.7 16.8 %inner_filter.1 = bf16[40,128,128]{2,1,0:T(8,128)(2,1)} custom-call(s32[256]{0:T(256)} %reshape.103.ids, f32[64]{0:T(128)} %get-tuple-element.62.live, bf16[64,4,128,128]{3,2,1,0:T(8,128)(2,1)} %tiles.1, bf16[64,128,128]{2,1,0:T(8,128)(2,1)} %bitcast.46), custom_call_target="tpu_custom_call" | custom-call | flops 1000000 | bytes 1048576 | tf_op jit(solution)/shard_map/inner_filter/pallas_call | solution.py:337
  33.7 1.4 constant_dynamic-slice_fusion.9
  35.1 0.7 slice_convert_fusion.1
  35.8 0.5 collective-permute-start.4
  36.3 0.7 slice_convert_fusion
  37.2 1.0 constant_dynamic-slice_fusion.8
  38.2 0.2 copy-done
  38.5 1.1 pad_maximum_fusion
  39.6 1.6 collective-permute-start.5
  41.3 0.7 reshape.112.ids1
  42.1 0.6 reshape.111.ids0
  42.8 0.6 convert_bitcast_fusion.2.live0
  43.4 0.5 convert_bitcast_fusion.1.live1
  43.9 16.7 %edge_filter.1 = bf16[24,128,128]{2,1,0:T(8,128)(2,1)} custom-call(s32[128]{0:T(128)} %reshape.111.ids0, f32[32]{0:T(128)} %convert_bitcast_fusion.2.live0, s32[128]{0:T(128)} %reshape.112.ids1, f32[32]{0:T(128)} %convert_bitcast_fusion.1.live1, s32[1]{0:T(128)} %bitcast.3.core, bf16[256,128,128]{2,1,0:T(8,128)(2,1)} %bitcast.43, ...), custom_call_target="tpu_custom_call" | custom-call | flops 8000000000 | bytes 11534336 | tf_op jit(solution)/shard_map/edge_filter/pallas_call | solution.py:428
  60.6 2.5 %collective-permute-start.9 = (bf16[3072,128]{1,0:T(8,128)(2,1)}, bf16[3072,128]{1,0:T(8,128)(2,1)S(1)}, u32[]{:S(2)}, u32[]{:S(2)}) collective-permute-start(bf16[3072,128]{1,0:T(8,128)(2,1)} %bitcast.50), channel_id=1, source_target_pairs={{0,1},{1,0},{2,3},{3,2},{4,5},{5,4},{6,7},{7,6},{8,9},{9,8},{10,11... | collective-permute-start | bytes 2359304 | tf_op jit(solution)/shard_map/ppermute | solution.py:293
  63.4 1.1 pad_maximum_fusion.1
  64.5 0.6 copy-done.5
  65.1 0.8 collective-permute-start.6
  65.9 8.2 %collective-permute-done.7 = bf16[2560,128]{1,0:T(8,128)(2,1)} collective-permute-done((bf16[2560,128]{1,0:T(8,128)(2,1)S(1)}, bf16[2560,128]{1,0:T(8,128)(2,1)}, u32[]{:S(2)}, u32[]{:S(2)}) %collective-permute-start.7) | collective-permute-done | bytes 655392 | tf_op jit(solution)/shard_map/ppermute | solution.py:384
  74.2 0.8 copy-done.6
  75.0 1.0 pad_maximum_fusion.3
  75.9 2.1 %collective-permute-start.8 = (bf16[2560,128]{1,0:T(8,128)(2,1)}, bf16[2560,128]{1,0:T(8,128)(2,1)S(1)}, u32[]{:S(2)}, u32[]{:S(2)}) collective-permute-start(bf16[2560,128]{1,0:T(8,128)(2,1)} %collective-permute-done.7), channel_id=1, source_target_pairs={{0,1},{1,0},{2,3},{3,2},{4,5},{5,4},{6,7},{7,6},{8,9},{9,8},{10,11... | collective-permute-start | bytes 1966088 | tf_op jit(solution)/shard_map/ppermute | solution.py:293
  78.1 0.7 pad_add_fusion.3.place
  78.7 1.3 collective-permute-done.8
  80.0 0.8 copy-done.9
  80.8 6.3 %gram.2.refs_0_ = f32[128,1024]{1,0:T(8,128)} custom-call(s32[4]{0:T(128)} %pad_add_fusion.3.place, bf16[5120,128]{1,0:T(8,128)(2,1)} %bitcast.40, bf16[5120,128]{1,0:T(8,128)(2,1)} %copy-done, bf16[2,2560,128]{2,1,0:T(8,128)(2,1)} %bitcast.44, bf16[2,2560,128]{2,1,0:T(8,128)(2,1)} %bitcast.13.refs_3_, bf16[2,1280,128]{2,1,0:T(8,128)(2,1)} %bitcast.14.refs_4_, ...), custom_call_target="tpu_custom_call" | custom-call | flops 671088640 | bytes 7864320 | tf_op jit(solution)/shard_map/gram/pallas_call | solution.py:405
  87.2 13.2 %collective-permute-done.10 = bf16[3072,128]{1,0:T(8,128)(2,1)S(1)} collective-permute-done((bf16[3072,128]{1,0:T(8,128)(2,1)}, bf16[3072,128]{1,0:T(8,128)(2,1)S(1)}, u32[]{:S(2)}, u32[]{:S(2)}) %collective-permute-start.10) | collective-permute-done | bytes 786464 | tf_op jit(solution)/shard_map/ppermute | solution.py:384
  100.4 0.8 pad_maximum_fusion.8
  101.2 2.7 %collective-permute-start.11 = (bf16[3072,128]{1,0:T(8,128)(2,1)S(1)}, bf16[3072,128]{1,0:T(8,128)(2,1)}, u32[]{:S(2)}, u32[]{:S(2)}) collective-permute-start(bf16[3072,128]{1,0:T(8,128)(2,1)S(1)} %collective-permute-done.10), channel_id=1, source_target_pairs={{0,1},{1,0},{2,3},{3,2},{4,5},{5,4},{6,7},{7,6},{8,9},{9,8},{10,11... | collective-permute-start | bytes 2359304 | tf_op jit(solution)/shard_map/ppermute | solution.py:293
  104.0 5.3 %collective-permute-done.13 = bf16[1536,128]{1,0:T(8,128)(2,1)S(1)} collective-permute-done((bf16[1536,128]{1,0:T(8,128)(2,1)}, bf16[1536,128]{1,0:T(8,128)(2,1)S(1)}, u32[]{:S(2)}, u32[]{:S(2)}) %collective-permute-start.13) | collective-permute-done | bytes 393248 | tf_op jit(solution)/shard_map/ppermute | solution.py:384
  109.2 0.3 collective-permute-start.14
  109.6 0.9 pad_maximum_fusion.4
  110.6 0.4 collective-permute-done.14
  111.0 0.8 copy-done.11
  111.7 5.2 %gram.3 = f32[128,1024]{1,0:T(8,128)} custom-call(s32[4]{0:T(128)} %pad_add_fusion.3.place, f32[128,1024]{1,0:T(8,128)} %gram.2.refs_0_, bf16[3072,128]{1,0:T(8,128)(2,1)} %bitcast.51, bf16[3072,128]{1,0:T(8,128)(2,1)} %copy-done.6, bf16[2,1536,128]{2,1,0:T(8,128)(2,1)} %bitcast.48, bf16[2,1536,128]{2,1,0:T(8,128)(2,1)} %bitcast.22.refs_4_.refs_11_, ...), custom_call_target="tpu_custom_call" | custom-call | flops 402653184 | bytes 4718592 | tf_op jit(solution)/shard_map/gram/pallas_call | solution.py:405
  117.0 4.0 %all-to-all-start = ((f32[16,8,1024]{2,1,0:T(8,128)}), f32[16,8,1024]{2,1,0:T(8,128)S(1)}, u32[]{:S(2)}, u32[]{:S(2)}) async-start(f32[16,8,1024]{2,1,0:T(8,128)} %bitcast.54), calls=%async_computation | async-start | bytes 1048576 | tf_op jit(solution)/shard_map/all_to_all | solution.py:447
  121.1 10.2 %all-to-all-done = f32[16,8,1024]{2,1,0:T(8,128)S(1)} async-done(((f32[16,8,1024]{2,1,0:T(8,128)}), f32[16,8,1024]{2,1,0:T(8,128)S(1)}, u32[]{:S(2)}, u32[]{:S(2)}) %all-to-all-start) | async-done | bytes 524320 | tf_op jit(solution)/shard_map/all_to_all | solution.py:447
  131.4 4.4 %collective-permute-start.16 = (bf16[1,8,1024]{2,1,0:T(8,128)(2,1)S(1)}, bf16[1,8,1024]{2,1,0:T(8,128)(2,1)S(1)}, u32[]{:S(2)}, u32[]{:S(2)}) collective-permute-start(bf16[1,8,1024]{2,1,0:T(8,128)(2,1)S(1)} %bitcast.64), channel_id=1, source_target_pairs={{0,4},{1,5},{2,6},{3,7},{4,0},{5,1},{6,2},{7,3},{8,12},{9,13},{10,... | collective-permute-start | bytes 49160 | tf_op jit(solution)/shard_map/ppermute | solution.py:453
  135.8 1.3 collective-permute-done.16
  137.1 1.3 collective-permute-done.15
  138.4 0.5 collective-permute-start.20
  138.9 2.1 %collective-permute-start.19 = (bf16[4,8,1024]{2,1,0:T(8,128)(2,1)S(1)}, bf16[4,8,1024]{2,1,0:T(8,128)(2,1)S(1)}, u32[]{:S(2)}, u32[]{:S(2)}) collective-permute-start(bf16[4,8,1024]{2,1,0:T(8,128)(2,1)S(1)} %pad_maximum_fusion.9), channel_id=1, source_target_pairs={{0,16},{8,24},{16,0},{24,8},{32,48},{40,56},{48,32},{56,40},{64,80... | collective-permute-start | bytes 196616 | tf_op jit(solution)/shard_map/ppermute | solution.py:453
  141.0 1.1 collective-permute-start.18
  142.1 2.0 %collective-permute-done.18 = bf16[4,8,1024]{2,1,0:T(8,128)(2,1)S(1)} collective-permute-done((bf16[4,8,1024]{2,1,0:T(8,128)(2,1)S(1)}, bf16[4,8,1024]{2,1,0:T(8,128)(2,1)S(1)}, u32[]{:S(2)}, u32[]{:S(2)}) %collective-permute-start.18) | collective-permute-done | bytes 65568 | tf_op jit(solution)/shard_map/ppermute | solution.py:453
  144.2 1.5 collective-permute-start.21
  145.7 0.4 collective-permute-start.22
  146.1 0.4 collective-permute-start.23
  146.5 3.3 %collective-permute-done.21 = bf16[16,8,1024]{2,1,0:T(8,128)(2,1)S(1)} collective-permute-done((bf16[16,8,1024]{2,1,0:T(8,128)(2,1)S(1)}, bf16[16,8,1024]{2,1,0:T(8,128)(2,1)S(1)}, u32[]{:S(2)}, u32[]{:S(2)}) %collective-permute-start.21) | collective-permute-done | bytes 262176 | tf_op jit(solution)/shard_map/ppermute | solution.py:453
  149.8 6.1 %collective-permute-start.25 = (bf16[5120,128]{1,0:T(8,128)(2,1)}, bf16[5120,128]{1,0:T(8,128)(2,1)S(1)}, u32[]{:S(2)}, u32[]{:S(2)}) collective-permute-start(bf16[5120,128]{1,0:T(8,128)(2,1)} %collective-permute-done.12), channel_id=1, source_target_pairs={{0,1},{1,0},{2,3},{3,2},{4,5},{5,4},{6,7},{7,6},{8,9},{9,8},{10,11... | collective-permute-start | bytes 3932168 | tf_op jit(solution)/shard_map/ppermute | solution.py:293
  156.0 6.6 %collective-permute-start.24 = (bf16[64,8,1024]{2,1,0:T(8,128)(2,1)S(1)}, bf16[64,8,1024]{2,1,0:T(8,128)(2,1)S(1)}, u32[]{:S(2)}, u32[]{:S(2)}) collective-permute-start(bf16[64,8,1024]{2,1,0:T(8,128)(2,1)S(1)} %constant_dynamic-update-slice_fusion.7.gathered), channel_id=1, source_target_pairs={{0,1},{1,0},{2,3},{3,2},{4,5},{5,4},{6,7},{7,6},{8,9},{9,8},{10,11... | collective-permute-start | bytes 3145736 | tf_op jit(solution)/shard_map/ppermute | solution.py:293
  162.6 0.1 collective-permute-start.29
  162.7 2.7 %collective-permute-done.26 = bf16[3072,128]{1,0:T(8,128)(2,1)S(1)} collective-permute-done((bf16[3072,128]{1,0:T(8,128)(2,1)S(1)}, bf16[3072,128]{1,0:T(8,128)(2,1)S(1)}, u32[]{:S(2)}, u32[]{:S(2)}) %collective-permute-start.26) | collective-permute-done | bytes 786464 | tf_op jit(solution)/shard_map/ppermute | solution.py:384
  165.4 3.9 %collective-permute-start.27 = (bf16[3072,128]{1,0:T(8,128)(2,1)S(1)}, bf16[3072,128]{1,0:T(8,128)(2,1)S(1)}, u32[]{:S(2)}, u32[]{:S(2)}) collective-permute-start(bf16[3072,128]{1,0:T(8,128)(2,1)S(1)} %collective-permute-done.26), channel_id=1, source_target_pairs={{0,1},{1,0},{2,3},{3,2},{4,5},{5,4},{6,7},{7,6},{8,9},{9,8},{10,11... | collective-permute-start | bytes 2359304 | tf_op jit(solution)/shard_map/ppermute | solution.py:293
  170.0 1.2 collective-permute-done.27
  171.2 0.2 copy-done.16
  171.4 0.7 copy-done.19
  172.1 0.4 copy-done.17
  172.5 14.7 %final.1 = bf16[8192,128]{1,0:T(8,128)(2,1)} custom-call(s32[4]{0:T(128)} %pad_add_fusion.3.place, f32[1]{0:T(128)S(6)} %copy.46.scale_in, bf16[64,8,1024]{2,1,0:T(8,128)(2,1)} %copy-done.13, bf16[64,8,1024]{2,1,0:T(8,128)(2,1)} %copy-done.16, bf16[5120,128]{1,0:T(8,128)(2,1)} %bitcast.41, bf16[5120,128]{1,0:T(8,128)(2,1)} %copy-done, ...), custom_call_target="tpu_custom_call" | custom-call | flops 6000000000 | bytes 20971520 | tf_op jit(solution)/shard_map/final/pallas_call | solution.py:476
  (102 shorter events, 1.9 us)
Async XLA Ops:
  0.0 9.5 %copy-start.12 = (s32[64,4]{0,1:T(4,128)S(1)}, s32[64,4]{0,1:T(4,128)}, u32[]{:S(2)}) copy-start(s32[64,4]{0,1:T(4,128)} %param.6) | copy-start | bytes 3076
  2.5 32.5 %collective-permute-start.1 = (bf16[40,128,128]{2,1,0:T(8,128)(2,1)}, bf16[40,128,128]{2,1,0:T(8,128)(2,1)}, u32[]{:S(2)}, u32[]{:S(2)}) collective-permute-start(bf16[40,128,128]{2,1,0:T(8,128)(2,1)} %constant_dynamic-slice_fusion.14), channel_id=1, source_target_pairs={{0,8},{1,121},{2,10},{3,123},{4,12},{5,125},{6,14},{7,127},{8,16},... | collective-permute-start | bytes 3932168 | tf_op jit(solution)/shard_map/ppermute | solution.py:319
  10.9 24.1 %collective-permute-start.2 = (bf16[13,128,128]{2,1,0:T(8,128)(2,1)S(1)}, bf16[13,128,128]{2,1,0:T(8,128)(2,1)}, u32[]{:S(2)}, u32[]{:S(2)}) collective-permute-start(bf16[13,128,128]{2,1,0:T(8,128)(2,1)S(1)} %pad_maximum_fusion.6), channel_id=1, source_target_pairs={{0,8},{8,16},{16,24},{24,32},{32,40},{40,48},{48,56},{56,64},{64,7... | collective-permute-start | bytes 1277960 | tf_op jit(solution)/shard_map/ppermute | solution.py:326
  11.1 24.0 %collective-permute-start.3 = (bf16[13,128,128]{2,1,0:T(8,128)(2,1)S(1)}, bf16[13,128,128]{2,1,0:T(8,128)(2,1)}, u32[]{:S(2)}, u32[]{:S(2)}) collective-permute-start(bf16[13,128,128]{2,1,0:T(8,128)(2,1)S(1)} %pad_maximum_fusion.7), channel_id=1, source_target_pairs={{0,120},{8,0},{16,8},{24,16},{32,24},{40,32},{48,40},{56,48},{64,5... | collective-permute-start | bytes 1277960 | tf_op jit(solution)/shard_map/ppermute | solution.py:329
  33.5 3.8 %collective-permute-start = (bf16[5120,128]{1,0:T(8,128)(2,1)}, bf16[5120,128]{1,0:T(8,128)(2,1)S(1)}, u32[]{:S(2)}, u32[]{:S(2)}) collective-permute-start(bf16[5120,128]{1,0:T(8,128)(2,1)} %bitcast.38), channel_id=1, source_target_pairs={{0,1},{1,0},{2,3},{3,2},{4,5},{5,4},{6,7},{7,6},{8,9},{9,8},{10,11... | collective-permute-start | bytes 3932168 | tf_op jit(solution)/shard_map/ppermute | solution.py:293
  35.8 3.8 %collective-permute-start.4 = (bf16[40,128,128]{2,1,0:T(8,128)(2,1)}, bf16[40,128,128]{2,1,0:T(8,128)(2,1)}, u32[]{:S(2)}, u32[]{:S(2)}) collective-permute-start(bf16[40,128,128]{2,1,0:T(8,128)(2,1)} %collective-permute-done.1.near), channel_id=1, source_target_pairs={{0,1},{1,0},{2,3},{3,2},{4,5},{5,4},{6,7},{7,6},{8,9},{9,8},{10,11... | collective-permute-start | bytes 3932168 | tf_op jit(solution)/shard_map/ppermute | solution.py:293
  37.2 1.3 copy-start
  39.6 23.5 %collective-permute-start.5 = (bf16[5120,128]{1,0:T(8,128)(2,1)}, bf16[5120,128]{1,0:T(8,128)(2,1)S(1)}, u32[]{:S(2)}, u32[]{:S(2)}) collective-permute-start(bf16[5120,128]{1,0:T(8,128)(2,1)} %pad_maximum_fusion), channel_id=1, source_target_pairs={{0,6},{1,3},{2,0},{3,5},{4,2},{5,7},{6,4},{7,1},{8,14},{9,11},{10,... | collective-permute-start | bytes 3932168 | tf_op jit(solution)/shard_map/ppermute | solution.py:384
  60.6 2.7 %copy-start.7 = (bf16[2560,128]{1,0:T(8,128)(2,1)S(1)}, bf16[2560,128]{1,0:T(8,128)(2,1)}, u32[]{:S(2)}) copy-start(bf16[2560,128]{1,0:T(8,128)(2,1)} %get-tuple-element.29) | copy-start | bytes 1966084
  60.6 13.5 %collective-permute-start.9 = (bf16[3072,128]{1,0:T(8,128)(2,1)}, bf16[3072,128]{1,0:T(8,128)(2,1)S(1)}, u32[]{:S(2)}, u32[]{:S(2)}) collective-permute-start(bf16[3072,128]{1,0:T(8,128)(2,1)} %bitcast.50), channel_id=1, source_target_pairs={{0,1},{1,0},{2,3},{3,2},{4,5},{5,4},{6,7},{7,6},{8,9},{9,8},{10,11... | collective-permute-start | bytes 2359304 | tf_op jit(solution)/shard_map/ppermute | solution.py:293
  63.1 2.0 %copy-start.1 = (bf16[5120,128]{1,0:T(8,128)(2,1)}, bf16[5120,128]{1,0:T(8,128)(2,1)S(1)}, u32[]{:S(2)}) copy-start(bf16[5120,128]{1,0:T(8,128)(2,1)S(1)} %collective-permute-done.5) | copy-start | bytes 3932164
  63.3 10.8 %collective-permute-start.7 = (bf16[2560,128]{1,0:T(8,128)(2,1)S(1)}, bf16[2560,128]{1,0:T(8,128)(2,1)}, u32[]{:S(2)}, u32[]{:S(2)}) collective-permute-start(bf16[2560,128]{1,0:T(8,128)(2,1)S(1)} %pad_maximum_fusion.5), channel_id=1, source_target_pairs={{0,6},{1,3},{2,0},{3,5},{4,2},{5,7},{6,4},{7,1},{8,14},{9,11},{10,... | collective-permute-start | bytes 1966088 | tf_op jit(solution)/shard_map/ppermute | solution.py:384
  63.3 1.7 copy-start.5
  65.1 14.9 %collective-permute-start.6 = (bf16[5120,128]{1,0:T(8,128)(2,1)S(1)}, bf16[5120,128]{1,0:T(8,128)(2,1)}, u32[]{:S(2)}, u32[]{:S(2)}) collective-permute-start(bf16[5120,128]{1,0:T(8,128)(2,1)S(1)} %collective-permute-done.5), channel_id=1, source_target_pairs={{0,1},{1,0},{2,3},{3,2},{4,5},{5,4},{6,7},{7,6},{8,9},{9,8},{10,11... | collective-permute-start | bytes 3932168 | tf_op jit(solution)/shard_map/ppermute | solution.py:293
  74.1 26.3 %collective-permute-start.12 = (bf16[5120,128]{1,0:T(8,128)(2,1)}, bf16[5120,128]{1,0:T(8,128)(2,1)}, u32[]{:S(2)}, u32[]{:S(2)}) collective-permute-start(bf16[5120,128]{1,0:T(8,128)(2,1)} %pad_maximum_fusion.1), channel_id=1, source_target_pairs={{0,6},{1,3},{2,0},{3,5},{4,2},{5,7},{6,4},{7,1},{8,14},{9,11},{10,... | collective-permute-start | bytes 3932168 | tf_op jit(solution)/shard_map/ppermute | solution.py:384
  74.1 0.9 copy-start.6
  75.9 24.4 %collective-permute-start.10 = (bf16[3072,128]{1,0:T(8,128)(2,1)}, bf16[3072,128]{1,0:T(8,128)(2,1)S(1)}, u32[]{:S(2)}, u32[]{:S(2)}) collective-permute-start(bf16[3072,128]{1,0:T(8,128)(2,1)} %pad_maximum_fusion.3), channel_id=1, source_target_pairs={{0,6},{1,3},{2,0},{3,5},{4,2},{5,7},{6,4},{7,1},{8,14},{9,11},{10,... | collective-permute-start | bytes 2359304 | tf_op jit(solution)/shard_map/ppermute | solution.py:384
  75.9 4.1 %collective-permute-start.8 = (bf16[2560,128]{1,0:T(8,128)(2,1)}, bf16[2560,128]{1,0:T(8,128)(2,1)S(1)}, u32[]{:S(2)}, u32[]{:S(2)}) collective-permute-start(bf16[2560,128]{1,0:T(8,128)(2,1)} %collective-permute-done.7), channel_id=1, source_target_pairs={{0,1},{1,0},{2,3},{3,2},{4,5},{5,4},{6,7},{7,6},{8,9},{9,8},{10,11... | collective-permute-start | bytes 1966088 | tf_op jit(solution)/shard_map/ppermute | solution.py:293
  80.0 0.8 copy-start.9
  100.4 10.1 %copy-start.3 = (bf16[3072,128]{1,0:T(8,128)(2,1)}, bf16[3072,128]{1,0:T(8,128)(2,1)S(1)}, u32[]{:S(2)}) copy-start(bf16[3072,128]{1,0:T(8,128)(2,1)S(1)} %collective-permute-done.10) | copy-start | bytes 2359300
  100.4 10.1 %copy-start.2 = (bf16[5120,128]{1,0:T(8,128)(2,1)S(1)}, bf16[5120,128]{1,0:T(8,128)(2,1)}, u32[]{:S(2)}) copy-start(bf16[5120,128]{1,0:T(8,128)(2,1)} %copy-done.1) | copy-start | bytes 3932164
  101.2 8.0 %collective-permute-start.13 = (bf16[1536,128]{1,0:T(8,128)(2,1)}, bf16[1536,128]{1,0:T(8,128)(2,1)S(1)}, u32[]{:S(2)}, u32[]{:S(2)}) collective-permute-start(bf16[1536,128]{1,0:T(8,128)(2,1)} %pad_maximum_fusion.8), channel_id=1, source_target_pairs={{0,6},{1,3},{2,0},{3,5},{4,2},{5,7},{6,4},{7,1},{8,14},{9,11},{10,... | collective-permute-start | bytes 1179656 | tf_op jit(solution)/shard_map/ppermute | solution.py:384
  101.2 9.4 %collective-permute-start.11 = (bf16[3072,128]{1,0:T(8,128)(2,1)S(1)}, bf16[3072,128]{1,0:T(8,128)(2,1)}, u32[]{:S(2)}, u32[]{:S(2)}) collective-permute-start(bf16[3072,128]{1,0:T(8,128)(2,1)S(1)} %collective-permute-done.10), channel_id=1, source_target_pairs={{0,1},{1,0},{2,3},{3,2},{4,5},{5,4},{6,7},{7,6},{8,9},{9,8},{10,11... | collective-permute-start | bytes 2359304 | tf_op jit(solution)/shard_map/ppermute | solution.py:293
  109.2 1.3 copy-start.10
  109.2 1.7 collective-permute-start.14
  111.0 0.8 copy-start.11
  117.0 4.0 %copy-start.4 = (bf16[3072,128]{1,0:T(8,128)(2,1)S(1)}, bf16[3072,128]{1,0:T(8,128)(2,1)}, u32[]{:S(2)}) copy-start(bf16[3072,128]{1,0:T(8,128)(2,1)} %copy-done.3) | copy-start | bytes 2359300
  117.0 14.4 %all-to-all-start = ((f32[16,8,1024]{2,1,0:T(8,128)}), f32[16,8,1024]{2,1,0:T(8,128)S(1)}, u32[]{:S(2)}, u32[]{:S(2)}) async-start(f32[16,8,1024]{2,1,0:T(8,128)} %bitcast.54), calls=%async_computation | async-start | bytes 1048576 | tf_op jit(solution)/shard_map/all_to_all | solution.py:447
  121.0 24.7 %copy-start.8 = (bf16[3072,128]{1,0:T(8,128)(2,1)S(1)}, bf16[3072,128]{1,0:T(8,128)(2,1)}, u32[]{:S(2)}) copy-start(bf16[3072,128]{1,0:T(8,128)(2,1)} %pad_maximum_fusion.4) | copy-start | bytes 2359300
  131.4 4.5 %collective-permute-start.17 = (bf16[1,8,1024]{2,1,0:T(8,128)(2,1)S(1)}, bf16[1,8,1024]{2,1,0:T(8,128)(2,1)S(1)}, u32[]{:S(2)}, u32[]{:S(2)}) collective-permute-start(bf16[1,8,1024]{2,1,0:T(8,128)(2,1)S(1)} %bitcast.63), channel_id=1, source_target_pairs={{0,2},{1,3},{2,4},{3,5},{4,6},{5,7},{6,0},{7,1},{8,10},{9,11},{10,... | collective-permute-start | bytes 49160 | tf_op jit(solution)/shard_map/ppermute | solution.py:453
  131.4 5.7 %collective-permute-start.16 = (bf16[1,8,1024]{2,1,0:T(8,128)(2,1)S(1)}, bf16[1,8,1024]{2,1,0:T(8,128)(2,1)S(1)}, u32[]{:S(2)}, u32[]{:S(2)}) collective-permute-start(bf16[1,8,1024]{2,1,0:T(8,128)(2,1)S(1)} %bitcast.64), channel_id=1, source_target_pairs={{0,4},{1,5},{2,6},{3,7},{4,0},{5,1},{6,2},{7,3},{8,12},{9,13},{10,... | collective-permute-start | bytes 49160 | tf_op jit(solution)/shard_map/ppermute | solution.py:453
  135.8 2.6 %collective-permute-start.15 = (bf16[1,8,1024]{2,1,0:T(8,128)(2,1)S(1)}, bf16[1,8,1024]{2,1,0:T(8,128)(2,1)S(1)}, u32[]{:S(2)}, u32[]{:S(2)}) collective-permute-start(bf16[1,8,1024]{2,1,0:T(8,128)(2,1)S(1)} %bitcast.65), channel_id=1, source_target_pairs={{0,6},{1,7},{2,0},{3,1},{4,2},{5,3},{6,4},{7,5},{8,14},{9,15},{10,... | collective-permute-start | bytes 49160 | tf_op jit(solution)/shard_map/ppermute | solution.py:453
  138.4 5.7 %collective-permute-start.20 = (bf16[4,8,1024]{2,1,0:T(8,128)(2,1)S(1)}, bf16[4,8,1024]{2,1,0:T(8,128)(2,1)S(1)}, u32[]{:S(2)}, u32[]{:S(2)}) collective-permute-start(bf16[4,8,1024]{2,1,0:T(8,128)(2,1)S(1)} %pad_maximum_fusion.9), channel_id=1, source_target_pairs={{0,8},{8,16},{16,24},{24,0},{32,40},{40,48},{48,56},{56,32},{64,72... | collective-permute-start | bytes 196616 | tf_op jit(solution)/shard_map/ppermute | solution.py:453
  138.9 5.2 %collective-permute-start.19 = (bf16[4,8,1024]{2,1,0:T(8,128)(2,1)S(1)}, bf16[4,8,1024]{2,1,0:T(8,128)(2,1)S(1)}, u32[]{:S(2)}, u32[]{:S(2)}) collective-permute-start(bf16[4,8,1024]{2,1,0:T(8,128)(2,1)S(1)} %pad_maximum_fusion.9), channel_id=1, source_target_pairs={{0,16},{8,24},{16,0},{24,8},{32,48},{40,56},{48,32},{56,40},{64,80... | collective-permute-start | bytes 196616 | tf_op jit(solution)/shard_map/ppermute | solution.py:453
  141.0 3.1 %collective-permute-start.18 = (bf16[4,8,1024]{2,1,0:T(8,128)(2,1)S(1)}, bf16[4,8,1024]{2,1,0:T(8,128)(2,1)S(1)}, u32[]{:S(2)}, u32[]{:S(2)}) collective-permute-start(bf16[4,8,1024]{2,1,0:T(8,128)(2,1)S(1)} %pad_maximum_fusion.9), channel_id=1, source_target_pairs={{0,24},{8,0},{16,8},{24,16},{32,56},{40,32},{48,40},{56,48},{64,88... | collective-permute-start | bytes 196616 | tf_op jit(solution)/shard_map/ppermute | solution.py:453
  142.1 20.5 %collective-permute-start.28 = (bf16[4096,128]{1,0:T(8,128)(2,1)S(1)}, bf16[4096,128]{1,0:T(8,128)(2,1)S(1)}, u32[]{:S(2)}, u32[]{:S(2)}) collective-permute-start(bf16[4096,128]{1,0:T(8,128)(2,1)S(1)} %pad_maximum_fusion.2), channel_id=1, source_target_pairs={{0,6},{1,3},{2,0},{3,5},{4,2},{5,7},{6,4},{7,1},{8,14},{9,11},{10,... | collective-permute-start | bytes 3145736 | tf_op jit(solution)/shard_map/ppermute | solution.py:384
  144.2 5.6 %collective-permute-start.21 = (bf16[16,8,1024]{2,1,0:T(8,128)(2,1)S(1)}, bf16[16,8,1024]{2,1,0:T(8,128)(2,1)S(1)}, u32[]{:S(2)}, u32[]{:S(2)}) collective-permute-start(bf16[16,8,1024]{2,1,0:T(8,128)(2,1)S(1)} %get-tuple-element.41), channel_id=1, source_target_pairs={{0,96},{8,104},{16,112},{24,120},{32,0},{40,8},{48,16},{56,24},{64... | collective-permute-start | bytes 786440 | tf_op jit(solution)/shard_map/ppermute | solution.py:453
  145.7 19.7 %collective-permute-start.26 = (bf16[3072,128]{1,0:T(8,128)(2,1)S(1)}, bf16[3072,128]{1,0:T(8,128)(2,1)S(1)}, u32[]{:S(2)}, u32[]{:S(2)}) collective-permute-start(bf16[3072,128]{1,0:T(8,128)(2,1)S(1)} %copy-done.8), channel_id=1, source_target_pairs={{0,6},{1,3},{2,0},{3,5},{4,2},{5,7},{6,4},{7,1},{8,14},{9,11},{10,... | collective-permute-start | bytes 2359304 | tf_op jit(solution)/shard_map/ppermute | solution.py:384
  145.7 10.2 %collective-permute-start.22 = (bf16[16,8,1024]{2,1,0:T(8,128)(2,1)S(1)}, bf16[16,8,1024]{2,1,0:T(8,128)(2,1)S(1)}, u32[]{:S(2)}, u32[]{:S(2)}) collective-permute-start(bf16[16,8,1024]{2,1,0:T(8,128)(2,1)S(1)} %get-tuple-element.41), channel_id=1, source_target_pairs={{0,64},{8,72},{16,80},{24,88},{32,96},{40,104},{48,112},{56,120},{... | collective-permute-start | bytes 786440 | tf_op jit(solution)/shard_map/ppermute | solution.py:453
  146.1 9.8 %collective-permute-start.23 = (bf16[16,8,1024]{2,1,0:T(8,128)(2,1)S(1)}, bf16[16,8,1024]{2,1,0:T(8,128)(2,1)S(1)}, u32[]{:S(2)}, u32[]{:S(2)}) collective-permute-start(bf16[16,8,1024]{2,1,0:T(8,128)(2,1)S(1)} %get-tuple-element.41), channel_id=1, source_target_pairs={{0,32},{8,40},{16,48},{24,56},{32,64},{40,72},{48,80},{56,88},{64,... | collective-permute-start | bytes 786440 | tf_op jit(solution)/shard_map/ppermute | solution.py:453
  149.8 20.1 %collective-permute-start.25 = (bf16[5120,128]{1,0:T(8,128)(2,1)}, bf16[5120,128]{1,0:T(8,128)(2,1)S(1)}, u32[]{:S(2)}, u32[]{:S(2)}) collective-permute-start(bf16[5120,128]{1,0:T(8,128)(2,1)} %collective-permute-done.12), channel_id=1, source_target_pairs={{0,1},{1,0},{2,3},{3,2},{4,5},{5,4},{6,7},{7,6},{8,9},{9,8},{10,11... | collective-permute-start | bytes 3932168 | tf_op jit(solution)/shard_map/ppermute | solution.py:293
  155.9 15.3 %copy-start.13 = (bf16[64,8,1024]{2,1,0:T(8,128)(2,1)}, bf16[64,8,1024]{2,1,0:T(8,128)(2,1)S(1)}, u32[]{:S(2)}) copy-start(bf16[64,8,1024]{2,1,0:T(8,128)(2,1)S(1)} %constant_dynamic-update-slice_fusion.7.gathered) | copy-start | bytes 3145732
  156.0 14.0 %collective-permute-start.24 = (bf16[64,8,1024]{2,1,0:T(8,128)(2,1)S(1)}, bf16[64,8,1024]{2,1,0:T(8,128)(2,1)S(1)}, u32[]{:S(2)}, u32[]{:S(2)}) collective-permute-start(bf16[64,8,1024]{2,1,0:T(8,128)(2,1)S(1)} %constant_dynamic-update-slice_fusion.7.gathered), channel_id=1, source_target_pairs={{0,1},{1,0},{2,3},{3,2},{4,5},{5,4},{6,7},{7,6},{8,9},{9,8},{10,11... | collective-permute-start | bytes 3145736 | tf_op jit(solution)/shard_map/ppermute | solution.py:293
  162.6 7.4 %copy-start.15 = (bf16[4096,128]{1,0:T(8,128)(2,1)}, bf16[4096,128]{1,0:T(8,128)(2,1)S(1)}, u32[]{:S(2)}) copy-start(bf16[4096,128]{1,0:T(8,128)(2,1)S(1)} %collective-permute-done.28.refs_16_) | copy-start | bytes 3145732
  162.6 8.6 %collective-permute-start.29 = (bf16[4096,128]{1,0:T(8,128)(2,1)S(1)}, bf16[4096,128]{1,0:T(8,128)(2,1)S(1)}, u32[]{:S(2)}, u32[]{:S(2)}) collective-permute-start(bf16[4096,128]{1,0:T(8,128)(2,1)S(1)} %collective-permute-done.28.refs_16_), channel_id=1, source_target_pairs={{0,1},{1,0},{2,3},{3,2},{4,5},{5,4},{6,7},{7,6},{8,9},{9,8},{10,11... | collective-permute-start | bytes 3145736 | tf_op jit(solution)/shard_map/ppermute | solution.py:293
  165.4 5.8 %copy-start.18 = (bf16[3072,128]{1,0:T(8,128)(2,1)}, bf16[3072,128]{1,0:T(8,128)(2,1)S(1)}, u32[]{:S(2)}) copy-start(bf16[3072,128]{1,0:T(8,128)(2,1)S(1)} %collective-permute-done.26) | copy-start | bytes 2359300
  165.4 5.8 %collective-permute-start.27 = (bf16[3072,128]{1,0:T(8,128)(2,1)S(1)}, bf16[3072,128]{1,0:T(8,128)(2,1)S(1)}, u32[]{:S(2)}, u32[]{:S(2)}) collective-permute-start(bf16[3072,128]{1,0:T(8,128)(2,1)S(1)} %collective-permute-done.26), channel_id=1, source_target_pairs={{0,1},{1,0},{2,3},{3,2},{4,5},{5,4},{6,7},{7,6},{8,9},{9,8},{10,11... | collective-permute-start | bytes 2359304 | tf_op jit(solution)/shard_map/ppermute | solution.py:293
  169.9 1.3 copy-start.14
  170.0 1.4 copy-start.16
  171.2 0.9 copy-start.19
  171.2 1.3 copy-start.17

commit v3 on v2

--- a/solution.py
+++ b/solution.py
@@ -174,7 +174,7 @@
 
 
 def final_kernel(place, scale_in, gathered, gathered_twin, *refs):
-    pieces, (out, rows_buf, table, matrix, sems) = refs[:18], refs[18:]
+    pieces, (out, rows_buf, table, matrix, sems) = refs[:16], refs[16:]
     x, y, i, c = place[0], place[1], place[2], place[3]
     low = DEEP * 128
     total = rows_buf.shape[1]
@@ -188,10 +188,10 @@
         copied.start()
         copies[group].append(copied)
 
-    o2, os2 = pieces[16:18]
+    n2, s2, o2, os2 = pieces[12:16]
     groups = ((low, low + inner, inner, 0), (0, low + 2 * inner, low, inner))
     for group, (first, second, half, at) in enumerate(groups):
-        own, twin, n1, s1, o1, os1, n2, s2 = pieces[8 * group : 8 * group + 8]
+        own, twin, n1, s1, o1, os1 = pieces[6 * group : 6 * group + 6]
         q = half // 2
         step = c * (second - first)
         up, down = first + step, second - step
@@ -204,8 +204,8 @@
             copy(group, s1.at[1 - e], down, half, 6 + e - 4 * c)
             copy(group, o1.at[e], up + mine, q, 4 + e)
             copy(group, os1.at[1 - e], down + mine, q, 4 + e)
-            copy(group, n2.at[e], down, half, 2 + e + 4 * c)
-            copy(group, s2.at[1 - e], up, half, 6 + e - 4 * c)
+            copy(group, n2.at[pl.ds(2 * at + e * half, half)], down, half, 2 + e + 4 * c)
+            copy(group, s2.at[pl.ds(2 * at + (1 - e) * half, half)], up, half, 6 + e - 4 * c)
             copy(group, o2.at[pl.ds(at + e * q, q)], up + other, q, 4 + e)
             copy(group, os2.at[pl.ds(at + (1 - e) * q, q)], down + other, q, 4 + e)
 
@@ -383,15 +383,12 @@
     def by_side(value):
         return lax.ppermute(value, "vec", sides)
 
-    def needed(own, before_send, before_forward):
+    def send_near(own, before):
         twin = swap(own)
         sent, *_ = lax.optimization_barrier(
-            (join([half_of(own, core_at), half_of(twin, core_at)]), *before_send)
+            (join([half_of(own, core_at), half_of(twin, core_at)]), *before)
         )
-        n1 = by_side(sent)
-        n1_late, *_ = lax.optimization_barrier((n1, *before_forward))
-        o1 = by_side(join(pieces_of(n1_late, forward_part)))
-        return own, twin, n1, swap(n1), o1, swap(o1)
+        return own, twin, sent, by_side(sent)
 
     def rest_of(own, twin):
         return join([half_of(own, 1 - core_at), half_of(twin, 1 - core_at)])
@@ -420,10 +417,8 @@
             name="gram",
         )(place, *([base] if base is not None else []), *args)
 
-    inner_got = needed(inner_own, (far, vlow, vhigh), ())
-    inner_gram = gram(inner_got, None)
-    inner_rest, _ = lax.optimization_barrier((rest_of(*inner_got[:2]), inner_got[4]))
-    inner_n2 = by_side(inner_rest)
+    own, twin, _, n1 = send_near(inner_own, (far, vlow, vhigh))
+    inner_near = [own, twin, n1, swap(n1), by_side(join(pieces_of(n1, forward_part)))]
     core_arg = core_at.astype(jnp.int32)[None]
     edge = pl.pallas_call(
         functools.partial(edge_kernel, blocks),
@@ -441,13 +436,25 @@
         name="edge_filter",
     )(ids0, live0, ids1, live1, core_arg, flat_tiles, vectors, near, far, vlow, vhigh)
     edge_own = edge.reshape(2 * DEEP * 128, panel)
-    edge_got = needed(edge_own, (), (inner_gram, inner_n2))
+    own, twin, sent, n1 = send_near(edge_own, ())
+    o1, _ = lax.optimization_barrier((inner_near[4], sent))
+    inner_got = inner_near[:4] + [o1, swap(o1)]
+    inner_gram = gram(inner_got, None)
+    n1_late, _ = lax.optimization_barrier((n1, inner_gram))
+    o1 = by_side(join(pieces_of(n1_late, forward_part)))
+    edge_got = [own, twin, n1, swap(n1), o1, swap(o1)]
     whole_gram = gram(edge_got, inner_gram)
+
+    late, _ = lax.optimization_barrier(
+        (join([rest_of(*inner_got[:2]), rest_of(*edge_got[:2])]), o1)
+    )
+    n2 = by_side(late)
 
     pieces = lax.all_to_all(
         whole_gram.reshape(rows16, 128 // rows16, 1024), "row", split_axis=0, concat_axis=0
     )
     mine = jnp.sum(pieces, axis=0).astype(BF)[None]
+    mine, n2 = lax.optimization_barrier((mine, n2))
 
     def around(value, axis, perm_of):
         parts = [value] + [lax.ppermute(value, axis, perm_of(d)) for d in (1, 2, 3)]
@@ -459,20 +466,19 @@
         ]
 
     got = around(mine, "vec", lambda d: z_perm(-d))
-    later = lax.optimization_barrier(
+    later, _ = lax.optimization_barrier(
         (
-            rest_of(*edge_got[:2]),
             join(pieces_of(inner_got[2], 1 - forward_part) + pieces_of(edge_got[2], 1 - forward_part)),
             got,
         )
     )
-    edge_n2, o2 = by_side(later[0]), by_side(later[1])
+    o2 = by_side(later)
     got = around(got, "row", lambda d: row_perm(0, d))
     got = around(got, "row", lambda d: row_perm(d, 0))
     parts = []
-    for values, n2 in ((inner_got, inner_n2), (edge_got, edge_n2)):
-        parts += list(values[:2]) + [two(v) for v in (*values[2:], n2, swap(n2))]
-    parts += [o2, swap(o2)]
+    for values in (inner_got, edge_got):
+        parts += list(values[:2]) + [two(v) for v in values[2:]]
+    parts += [n2, swap(n2), o2, swap(o2)]
     return pl.pallas_call(
         final_kernel,
         out_shape=jax.ShapeDtypeStruct((row_count, panel), BF),

time: 188 us -> 171 us (0.910)
  starting transfers between devices: 52.5 us -> 40.7 us
  waiting for transfers between devices: 50.3 us -> 45.5 us
    ppermute x7 -> x6, waiting for transfers between devices: 29.3 us -> 14.8 us  [by_side(): return lax.ppermute(value, 'vec', sides)]
    ppermute x11 -> x10, starting transfers between devices: 25.8 us -> 15.3 us  [swap(): return lax.ppermute(value, 'vec', z_perm(0, 1))]
    ppermute x9, waiting for transfers between devices: 7.86 us -> 13.5 us  [around(): parts = [value] + [lax.ppermute(value, axis, perm_of(d)) for d in (1, 2, 3)]]
    ppermute x9, starting transfers between devices: 10.4 us -> 6.26 us  [around(): parts = [value] + [lax.ppermute(value, axis, perm_of(d)) for d in (1, 2, 3)]]
    ppermute x11 -> x10, waiting for transfers between devices: 2.91 us -> 6.99 us  [swap(): return lax.ppermute(value, 'vec', z_perm(0, 1))]
    ppermute x7 -> x6, starting transfers between devices: 1.72 us -> 4.87 us  [by_side(): return lax.ppermute(value, 'vec', sides)]
    dynamic_slice x4, local copies, waits for them, and re-layouts: 2.52 us -> 5.21 us  [half_of(): return lax.dynamic_slice_in_dim(value, which * h, h, 0)]
    unnamed x48 -> x46, local copies, waits for them, and re-layouts: 4.61 us -> 2.04 us
  transfers between devices with their start and end apart: 31 -> 29, of which waited for: 12 -> 14; matrix products, arithmetic and copies ran while one was open for 8% -> 10% of each run, Pallas kernels for 21% -> 27%
where the time goes in v3:
time: 171 us
  Pallas kernels  60 us (35%)
  waiting for transfers between devices  45.5 us (27%)
  starting transfers between devices  40.7 us (24%)
  local copies, waits for them, and re-layouts  14.7 us (9%)
  other arithmetic  7.68 us (4%)
  between operations  1.96 us (1%)
    pallas_call x1, Pallas kernels, local(): pl.pallas_call(functools.partial(inner_kernel, blocks), out_shape=jax.Sha...  16.8 us
    pallas_call x1, Pallas kernels, local(): pl.pallas_call(functools.partial(edge_kernel, blocks), out_shape=jax.Shap...  16.7 us
    ppermute x10, starting transfers between devices, swap(): return lax.ppermute(value, 'vec', z_perm(0, 1))  15.3 us
    ppermute x6, waiting for transfers between devices, by_side(): return lax.ppermute(value, 'vec', sides)  14.8 us
    pallas_call x1, Pallas kernels, local(): pl.pallas_call(final_kernel, out_shape=jax.ShapeDtypeStruct((row_count, p...  14.7 us
    ppermute x9, waiting for transfers between devices, around(): parts = [value] + [lax.ppermute(value, axis, perm_of(d)) for d in (1, 2, 3)]  13.5 us
    pallas_call x2, Pallas kernels, gram(): pl.pallas_call(functools.partial(gram_kernel, half, base is not None), ou...  11.7 us
    all_to_all x1, waiting for transfers between devices, local(): lax.all_to_all(whole_gram.reshape(rows16, 128 // rows16, 1024), 'row', sp...  10.2 us
  transfers between devices with their start and end apart: 29, of which 14 were waited for; matrix products, arithmetic and copies ran while one was open for 10% of the time, Pallas kernels for 27%

profile of v3, /device:TPU:1, one launch (start us, length us, event | category | flops | bytes accessed | tf_op | source)
XLA Modules:
  0.0 170.6 jit_solution(2660041292309062429)
XLA Ops:
  0.0 2.5 %constant_dynamic-slice_fusion.14 = bf16[40,128,128]{2,1,0:T(8,128)(2,1)} fusion(bf16[256,128,128]{2,1,0:T(8,128)(2,1)} %bitcast.37, s32[]{:T(128)S(6)} %select_n.95), kind=kLoop, calls=%fused_computation.46 | loop fusion | bytes 2621444 | tf_op jit(solution)/shard_map/dynamic_slice | solution.py:320
  2.5 5.8 %collective-permute-start.1 = (bf16[40,128,128]{2,1,0:T(8,128)(2,1)}, bf16[40,128,128]{2,1,0:T(8,128)(2,1)}, u32[]{:S(2)}, u32[]{:S(2)}) collective-permute-start(bf16[40,128,128]{2,1,0:T(8,128)(2,1)} %constant_dynamic-slice_fusion.14), channel_id=1, source_target_pairs={{0,8},{1,121},{2,10},{3,123},{4,12},{5,125},{6,14},{7,127},{8,16},... | collective-permute-start | bytes 3932168 | tf_op jit(solution)/shard_map/ppermute | solution.py:319
  9.0 0.5 or_convert_fusion
  9.6 0.1 copy.25
  9.6 1.2 fusion.4
  11.0 4.8 %collective-permute-start.3 = (bf16[13,128,128]{2,1,0:T(8,128)(2,1)S(1)}, bf16[13,128,128]{2,1,0:T(8,128)(2,1)}, u32[]{:S(2)}, u32[]{:S(2)}) collective-permute-start(bf16[13,128,128]{2,1,0:T(8,128)(2,1)S(1)} %pad_maximum_fusion.6), channel_id=1, source_target_pairs={{0,120},{8,0},{16,8},{24,16},{32,24},{40,32},{48,40},{56,48},{64,5... | collective-permute-start | bytes 1277960 | tf_op jit(solution)/shard_map/ppermute | solution.py:329
  15.9 0.1 copy.24
  16.0 0.7 reshape.91.ids
  16.7 16.8 %inner_filter.1 = bf16[40,128,128]{2,1,0:T(8,128)(2,1)} custom-call(s32[256]{0:T(256)} %reshape.91.ids, f32[64]{0:T(128)} %get-tuple-element.70.live, bf16[64,4,128,128]{3,2,1,0:T(8,128)(2,1)} %tiles.1, bf16[64,128,128]{2,1,0:T(8,128)(2,1)} %bitcast.41), custom_call_target="tpu_custom_call" | custom-call | flops 1000000 | bytes 1048576 | tf_op jit(solution)/shard_map/inner_filter/pallas_call | solution.py:337
  33.5 0.1 collective-permute-start
  33.7 1.4 constant_dynamic-slice_fusion.7
  35.1 0.7 slice_convert_fusion.1
  35.9 0.5 collective-permute-start.4
  36.4 0.7 slice_convert_fusion
  37.3 1.0 constant_dynamic-slice_fusion.6
  38.3 1.1 pad_maximum_fusion.1
  39.5 1.6 collective-permute-start.5
  41.1 0.6 convert_bitcast_fusion.2.live0
  41.7 0.1 copy.29
  41.8 0.7 reshape.98.ids1
  42.4 0.1 copy.27
  42.5 0.6 reshape.97.ids0
  43.2 0.5 convert_bitcast_fusion.1.live1
  43.7 16.7 %edge_filter.1 = bf16[24,128,128]{2,1,0:T(8,128)(2,1)} custom-call(s32[128]{0:T(128)} %reshape.97.ids0, f32[32]{0:T(128)} %convert_bitcast_fusion.2.live0, s32[128]{0:T(128)} %reshape.98.ids1, f32[32]{0:T(128)} %convert_bitcast_fusion.1.live1, s32[1]{0:T(128)} %bitcast.3.core, bf16[256,128,128]{2,1,0:T(8,128)(2,1)} %bitcast.38, ...), custom_call_target="tpu_custom_call" | custom-call | flops 8000000000 | bytes 11534336 | tf_op jit(solution)/shard_map/edge_filter/pallas_call | solution.py:423
  60.4 2.8 %collective-permute-start.8 = (bf16[3072,128]{1,0:T(8,128)(2,1)}, bf16[3072,128]{1,0:T(8,128)(2,1)S(1)}, u32[]{:S(2)}, u32[]{:S(2)}) collective-permute-start(bf16[3072,128]{1,0:T(8,128)(2,1)} %bitcast.45), channel_id=1, source_target_pairs={{0,1},{1,0},{2,3},{3,2},{4,5},{5,4},{6,7},{7,6},{8,9},{9,8},{10,11... | collective-permute-start | bytes 2359304 | tf_op jit(solution)/shard_map/ppermute | solution.py:293
  63.1 1.9 %constant_dynamic-slice_fusion.5 = (bf16[1536,128]{1,0:T(8,128)(2,1)}, bf16[1536,128]{1,0:T(8,128)(2,1)S(1)}) fusion(bf16[3072,128]{1,0:T(8,128)(2,1)} %bitcast.46, s32[]{:T(128)S(6)} %select_n.107, s32[]{:T(128)S(6)} %select_n.103), kind=kLoop, calls=%fused_computation.37 | loop fusion | bytes 1572872 | tf_op jit(solution)/shard_map/dynamic_slice | solution.py:373
  65.1 1.0 constant_dynamic-slice_fusion.3
  66.2 0.4 collective-permute-start.6
  66.7 0.9 constant_dynamic-slice_fusion.4
  67.5 0.9 pad_maximum_fusion.3
  68.5 1.3 collective-permute-start.10
  69.8 7.2 %collective-permute-done.7 = bf16[2560,128]{1,0:T(8,128)(2,1)} collective-permute-done((bf16[2560,128]{1,0:T(8,128)(2,1)S(1)}, bf16[2560,128]{1,0:T(8,128)(2,1)}, u32[]{:S(2)}, u32[]{:S(2)}) %collective-permute-start.7) | collective-permute-done | bytes 655392 | tf_op jit(solution)/shard_map/ppermute | solution.py:384
  77.0 0.7 pad_add_fusion.3.place
  77.7 1.8 %collective-permute-done.9 = bf16[2560,128]{1,0:T(8,128)(2,1)} collective-permute-done((bf16[2560,128]{1,0:T(8,128)(2,1)}, bf16[2560,128]{1,0:T(8,128)(2,1)}, u32[]{:S(2)}, u32[]{:S(2)}) %collective-permute-start.9) | collective-permute-done | bytes 655392 | tf_op jit(solution)/shard_map/ppermute | solution.py:293
  79.4 6.4 %gram.2.refs_0_ = f32[128,1024]{1,0:T(8,128)} custom-call(s32[4]{0:T(128)} %pad_add_fusion.3.place, bf16[5120,128]{1,0:T(8,128)(2,1)} %bitcast.35, bf16[5120,128]{1,0:T(8,128)(2,1)} %copy-done, bf16[2,2560,128]{2,1,0:T(8,128)(2,1)} %bitcast.39, bf16[2,2560,128]{2,1,0:T(8,128)(2,1)} %bitcast.13.refs_3_, bf16[2,1280,128]{2,1,0:T(8,128)(2,1)} %bitcast.19.refs_4_, ...), custom_call_target="tpu_custom_call" | custom-call | flops 671088640 | bytes 7864320 | tf_op jit(solution)/shard_map/gram/pallas_call | solution.py:402
  86.1 1.5 pad_maximum_fusion
  87.5 6.3 %collective-permute-done.12 = bf16[1536,128]{1,0:T(8,128)(2,1)S(1)} collective-permute-done((bf16[1536,128]{1,0:T(8,128)(2,1)S(1)}, bf16[1536,128]{1,0:T(8,128)(2,1)S(1)}, u32[]{:S(2)}, u32[]{:S(2)}) %collective-permute-start.12) | collective-permute-done | bytes 393248 | tf_op jit(solution)/shard_map/ppermute | solution.py:384
  93.9 2.7 %collective-permute-start.11 = (bf16[3072,128]{1,0:T(8,128)(2,1)S(1)}, bf16[3072,128]{1,0:T(8,128)(2,1)S(1)}, u32[]{:S(2)}, u32[]{:S(2)}) collective-permute-start(bf16[3072,128]{1,0:T(8,128)(2,1)S(1)} %collective-permute-done.10), channel_id=1, source_target_pairs={{0,1},{1,0},{2,3},{3,2},{4,5},{5,4},{6,7},{7,6},{8,9},{9,8},{10,11... | collective-permute-start | bytes 2359304 | tf_op jit(solution)/shard_map/ppermute | solution.py:293
  96.6 1.9 %collective-permute-done.11 = bf16[3072,128]{1,0:T(8,128)(2,1)S(1)} collective-permute-done((bf16[3072,128]{1,0:T(8,128)(2,1)S(1)}, bf16[3072,128]{1,0:T(8,128)(2,1)S(1)}, u32[]{:S(2)}, u32[]{:S(2)}) %collective-permute-start.11) | collective-permute-done | bytes 786464 | tf_op jit(solution)/shard_map/ppermute | solution.py:293
  98.5 0.6 collective-permute-done.13
  99.1 0.8 copy-done.12
  99.9 5.3 %gram.3 = f32[128,1024]{1,0:T(8,128)} custom-call(s32[4]{0:T(128)} %pad_add_fusion.3.place, f32[128,1024]{1,0:T(8,128)} %gram.2.refs_0_, bf16[3072,128]{1,0:T(8,128)(2,1)} %bitcast.47, bf16[3072,128]{1,0:T(8,128)(2,1)} %copy-done.4, bf16[2,1536,128]{2,1,0:T(8,128)(2,1)} %bitcast.43, bf16[2,1536,128]{2,1,0:T(8,128)(2,1)} %bitcast.52, ...), custom_call_target="tpu_custom_call" | custom-call | flops 402653184 | bytes 4718592 | tf_op jit(solution)/shard_map/gram/pallas_call | solution.py:402
  105.2 3.6 %all-to-all-start = ((f32[16,8,1024]{2,1,0:T(8,128)}), f32[16,8,1024]{2,1,0:T(8,128)S(1)}, u32[]{:S(2)}, u32[]{:S(2)}) async-start(f32[16,8,1024]{2,1,0:T(8,128)} %bitcast.49), calls=%async_computation | async-start | bytes 1048576 | tf_op jit(solution)/shard_map/all_to_all | solution.py:453
  108.9 10.2 %all-to-all-done = f32[16,8,1024]{2,1,0:T(8,128)S(1)} async-done(((f32[16,8,1024]{2,1,0:T(8,128)}), f32[16,8,1024]{2,1,0:T(8,128)S(1)}, u32[]{:S(2)}, u32[]{:S(2)}) %all-to-all-start) | async-done | bytes 524320 | tf_op jit(solution)/shard_map/all_to_all | solution.py:453
  119.2 1.3 collective-permute-done.14.refs_12_
  120.5 0.6 collective-permute-start.16
  121.0 2.1 %collective-permute-start.15 = (bf16[1,8,1024]{2,1,0:T(8,128)(2,1)S(1)}, bf16[1,8,1024]{2,1,0:T(8,128)(2,1)S(1)}, u32[]{:S(2)}, u32[]{:S(2)}) collective-permute-start(bf16[1,8,1024]{2,1,0:T(8,128)(2,1)S(1)} %bitcast.60), channel_id=1, source_target_pairs={{0,6},{1,7},{2,0},{3,1},{4,2},{5,3},{6,4},{7,5},{8,14},{9,15},{10,... | collective-permute-start | bytes 49160 | tf_op jit(solution)/shard_map/ppermute | solution.py:460
  123.2 2.5 %collective-permute-start.25 = (bf16[8192,128]{1,0:T(8,128)(2,1)}, bf16[8192,128]{1,0:T(8,128)(2,1)S(1)}, u32[]{:S(2)}, u32[]{:S(2)}) collective-permute-start(bf16[8192,128]{1,0:T(8,128)(2,1)} %collective-permute-done.14.refs_12_), channel_id=1, source_target_pairs={{0,1},{1,0},{2,3},{3,2},{4,5},{5,4},{6,7},{7,6},{8,9},{9,8},{10,11... | collective-permute-start | bytes 6291464 | tf_op jit(solution)/shard_map/ppermute | solution.py:293
  125.8 1.7 %collective-permute-start.26 = (bf16[4096,128]{1,0:T(8,128)(2,1)S(1)}, bf16[4096,128]{1,0:T(8,128)(2,1)S(1)}, u32[]{:S(2)}, u32[]{:S(2)}) collective-permute-start(bf16[4096,128]{1,0:T(8,128)(2,1)S(1)} %pad_maximum_fusion.2), channel_id=1, source_target_pairs={{0,6},{1,3},{2,0},{3,5},{4,2},{5,7},{6,4},{7,1},{8,14},{9,11},{10,... | collective-permute-start | bytes 3145736 | tf_op jit(solution)/shard_map/ppermute | solution.py:384
  127.5 1.5 collective-permute-start.20
  129.0 1.6 collective-permute-done.18
  130.6 3.0 %collective-permute-done.19 = bf16[4,8,1024]{2,1,0:T(8,128)(2,1)S(1)} collective-permute-done((bf16[4,8,1024]{2,1,0:T(8,128)(2,1)S(1)}, bf16[4,8,1024]{2,1,0:T(8,128)(2,1)S(1)}, u32[]{:S(2)}, u32[]{:S(2)}) %collective-permute-start.19) | collective-permute-done | bytes 65568 | tf_op jit(solution)/shard_map/ppermute | solution.py:460
  133.6 1.4 collective-permute-start.21
  135.1 0.7 collective-permute-start.23
  135.7 3.5 %collective-permute-done.21 = bf16[16,8,1024]{2,1,0:T(8,128)(2,1)S(1)} collective-permute-done((bf16[16,8,1024]{2,1,0:T(8,128)(2,1)S(1)}, bf16[16,8,1024]{2,1,0:T(8,128)(2,1)S(1)}, u32[]{:S(2)}, u32[]{:S(2)}) %collective-permute-start.21) | collective-permute-done | bytes 262176 | tf_op jit(solution)/shard_map/ppermute | solution.py:460
  139.2 2.7 %collective-permute-done.22 = bf16[16,8,1024]{2,1,0:T(8,128)(2,1)S(1)} collective-permute-done((bf16[16,8,1024]{2,1,0:T(8,128)(2,1)S(1)}, bf16[16,8,1024]{2,1,0:T(8,128)(2,1)S(1)}, u32[]{:S(2)}, u32[]{:S(2)}) %collective-permute-start.22) | collective-permute-done | bytes 262176 | tf_op jit(solution)/shard_map/ppermute | solution.py:460
  141.9 2.8 %collective-permute-done.23 = bf16[16,8,1024]{2,1,0:T(8,128)(2,1)S(1)} collective-permute-done((bf16[16,8,1024]{2,1,0:T(8,128)(2,1)S(1)}, bf16[16,8,1024]{2,1,0:T(8,128)(2,1)S(1)}, u32[]{:S(2)}, u32[]{:S(2)}) %collective-permute-start.23) | collective-permute-done | bytes 262176 | tf_op jit(solution)/shard_map/ppermute | solution.py:460
  144.7 6.0 %collective-permute-start.24 = (bf16[64,8,1024]{2,1,0:T(8,128)(2,1)S(1)}, bf16[64,8,1024]{2,1,0:T(8,128)(2,1)S(1)}, u32[]{:S(2)}, u32[]{:S(2)}) collective-permute-start(bf16[64,8,1024]{2,1,0:T(8,128)(2,1)S(1)} %constant_dynamic-update-slice_fusion.11.gathered), channel_id=1, source_target_pairs={{0,1},{1,0},{2,3},{3,2},{4,5},{5,4},{6,7},{7,6},{8,9},{9,8},{10,11... | collective-permute-start | bytes 3145736 | tf_op jit(solution)/shard_map/ppermute | solution.py:293
  150.7 0.4 collective-permute-start.27
  151.8 1.3 collective-permute-done.24.gathered_twin
  153.0 1.5 collective-permute-done.27.refs_15_
  154.5 0.2 copy-done.15
  154.7 1.0 copy-done.18
  155.7 14.7 %final.1 = bf16[8192,128]{1,0:T(8,128)(2,1)} custom-call(s32[4]{0:T(128)} %pad_add_fusion.3.place, f32[1]{0:T(128)S(6)} %copy.49.scale_in, bf16[64,8,1024]{2,1,0:T(8,128)(2,1)} %copy-done.14, bf16[64,8,1024]{2,1,0:T(8,128)(2,1)} %copy-done.17, bf16[5120,128]{1,0:T(8,128)(2,1)} %bitcast.36, bf16[5120,128]{1,0:T(8,128)(2,1)} %copy-done, ...), custom_call_target="tpu_custom_call" | custom-call | flops 6000000000 | bytes 20971520 | tf_op jit(solution)/shard_map/final/pallas_call | solution.py:482
  (93 shorter events, 1.2 us)
Async XLA Ops:
  0.0 9.5 %copy-start.13 = (s32[64,4]{0,1:T(4,128)S(1)}, s32[64,4]{0,1:T(4,128)}, u32[]{:S(2)}) copy-start(s32[64,4]{0,1:T(4,128)} %param.6) | copy-start | bytes 3076
  2.5 32.6 %collective-permute-start.1 = (bf16[40,128,128]{2,1,0:T(8,128)(2,1)}, bf16[40,128,128]{2,1,0:T(8,128)(2,1)}, u32[]{:S(2)}, u32[]{:S(2)}) collective-permute-start(bf16[40,128,128]{2,1,0:T(8,128)(2,1)} %constant_dynamic-slice_fusion.14), channel_id=1, source_target_pairs={{0,8},{1,121},{2,10},{3,123},{4,12},{5,125},{6,14},{7,127},{8,16},... | collective-permute-start | bytes 3932168 | tf_op jit(solution)/shard_map/ppermute | solution.py:319
  10.9 24.2 %collective-permute-start.2 = (bf16[13,128,128]{2,1,0:T(8,128)(2,1)S(1)}, bf16[13,128,128]{2,1,0:T(8,128)(2,1)}, u32[]{:S(2)}, u32[]{:S(2)}) collective-permute-start(bf16[13,128,128]{2,1,0:T(8,128)(2,1)S(1)} %pad_maximum_fusion.5), channel_id=1, source_target_pairs={{0,8},{8,16},{16,24},{24,32},{32,40},{40,48},{48,56},{56,64},{64,7... | collective-permute-start | bytes 1277960 | tf_op jit(solution)/shard_map/ppermute | solution.py:326
  11.0 24.1 %collective-permute-start.3 = (bf16[13,128,128]{2,1,0:T(8,128)(2,1)S(1)}, bf16[13,128,128]{2,1,0:T(8,128)(2,1)}, u32[]{:S(2)}, u32[]{:S(2)}) collective-permute-start(bf16[13,128,128]{2,1,0:T(8,128)(2,1)S(1)} %pad_maximum_fusion.6), channel_id=1, source_target_pairs={{0,120},{8,0},{16,8},{24,16},{32,24},{40,32},{48,40},{56,48},{64,5... | collective-permute-start | bytes 1277960 | tf_op jit(solution)/shard_map/ppermute | solution.py:329
  33.5 3.8 %collective-permute-start = (bf16[5120,128]{1,0:T(8,128)(2,1)}, bf16[5120,128]{1,0:T(8,128)(2,1)S(1)}, u32[]{:S(2)}, u32[]{:S(2)}) collective-permute-start(bf16[5120,128]{1,0:T(8,128)(2,1)} %bitcast.33), channel_id=1, source_target_pairs={{0,1},{1,0},{2,3},{3,2},{4,5},{5,4},{6,7},{7,6},{8,9},{9,8},{10,11... | collective-permute-start | bytes 3932168 | tf_op jit(solution)/shard_map/ppermute | solution.py:293
  35.9 3.6 %collective-permute-start.4 = (bf16[40,128,128]{2,1,0:T(8,128)(2,1)}, bf16[40,128,128]{2,1,0:T(8,128)(2,1)}, u32[]{:S(2)}, u32[]{:S(2)}) collective-permute-start(bf16[40,128,128]{2,1,0:T(8,128)(2,1)} %collective-permute-done.1.near), channel_id=1, source_target_pairs={{0,1},{1,0},{2,3},{3,2},{4,5},{5,4},{6,7},{7,6},{8,9},{9,8},{10,11... | collective-permute-start | bytes 3932168 | tf_op jit(solution)/shard_map/ppermute | solution.py:293
  37.3 2.2 %copy-start = (bf16[5120,128]{1,0:T(8,128)(2,1)}, bf16[5120,128]{1,0:T(8,128)(2,1)S(1)}, u32[]{:S(2)}) copy-start(bf16[5120,128]{1,0:T(8,128)(2,1)S(1)} %collective-permute-done.refs_1_) | copy-start | bytes 3932164
  39.5 25.6 %collective-permute-start.5 = (bf16[5120,128]{1,0:T(8,128)(2,1)}, bf16[5120,128]{1,0:T(8,128)(2,1)S(1)}, u32[]{:S(2)}, u32[]{:S(2)}) collective-permute-start(bf16[5120,128]{1,0:T(8,128)(2,1)} %pad_maximum_fusion.1), channel_id=1, source_target_pairs={{0,6},{1,3},{2,0},{3,5},{4,2},{5,7},{6,4},{7,1},{8,14},{9,11},{10,... | collective-permute-start | bytes 3932168 | tf_op jit(solution)/shard_map/ppermute | solution.py:384
  60.4 6.3 %collective-permute-start.8 = (bf16[3072,128]{1,0:T(8,128)(2,1)}, bf16[3072,128]{1,0:T(8,128)(2,1)S(1)}, u32[]{:S(2)}, u32[]{:S(2)}) collective-permute-start(bf16[3072,128]{1,0:T(8,128)(2,1)} %bitcast.45), channel_id=1, source_target_pairs={{0,1},{1,0},{2,3},{3,2},{4,5},{5,4},{6,7},{7,6},{8,9},{9,8},{10,11... | collective-permute-start | bytes 2359304 | tf_op jit(solution)/shard_map/ppermute | solution.py:293
  65.1 2.5 %copy-start.1 = (bf16[5120,128]{1,0:T(8,128)(2,1)}, bf16[5120,128]{1,0:T(8,128)(2,1)S(1)}, u32[]{:S(2)}) copy-start(bf16[5120,128]{1,0:T(8,128)(2,1)S(1)} %collective-permute-done.5) | copy-start | bytes 3932164
  66.2 10.8 %collective-permute-start.7 = (bf16[2560,128]{1,0:T(8,128)(2,1)S(1)}, bf16[2560,128]{1,0:T(8,128)(2,1)}, u32[]{:S(2)}, u32[]{:S(2)}) collective-permute-start(bf16[2560,128]{1,0:T(8,128)(2,1)S(1)} %pad_maximum_fusion.4), channel_id=1, source_target_pairs={{0,6},{1,3},{2,0},{3,5},{4,2},{5,7},{6,4},{7,1},{8,14},{9,11},{10,... | collective-permute-start | bytes 1966088 | tf_op jit(solution)/shard_map/ppermute | solution.py:384
  66.2 13.2 %collective-permute-start.6 = (bf16[5120,128]{1,0:T(8,128)(2,1)S(1)}, bf16[5120,128]{1,0:T(8,128)(2,1)}, u32[]{:S(2)}, u32[]{:S(2)}) collective-permute-start(bf16[5120,128]{1,0:T(8,128)(2,1)S(1)} %collective-permute-done.5), channel_id=1, source_target_pairs={{0,1},{1,0},{2,3},{3,2},{4,5},{5,4},{6,7},{7,6},{8,9},{9,8},{10,11... | collective-permute-start | bytes 3932168 | tf_op jit(solution)/shard_map/ppermute | solution.py:293
  66.7 19.2 %copy-start.4 = (bf16[3072,128]{1,0:T(8,128)(2,1)}, bf16[3072,128]{1,0:T(8,128)(2,1)S(1)}, u32[]{:S(2)}) copy-start(bf16[3072,128]{1,0:T(8,128)(2,1)S(1)} %collective-permute-done.8.refs_2_.refs_7_) | copy-start | bytes 2359300
  68.5 17.4 %collective-permute-start.10 = (bf16[3072,128]{1,0:T(8,128)(2,1)}, bf16[3072,128]{1,0:T(8,128)(2,1)S(1)}, u32[]{:S(2)}, u32[]{:S(2)}) collective-permute-start(bf16[3072,128]{1,0:T(8,128)(2,1)} %pad_maximum_fusion.3), channel_id=1, source_target_pairs={{0,6},{1,3},{2,0},{3,5},{4,2},{5,7},{6,4},{7,1},{8,14},{9,11},{10,... | collective-permute-start | bytes 2359304 | tf_op jit(solution)/shard_map/ppermute | solution.py:384
  77.0 2.4 %collective-permute-start.9 = (bf16[2560,128]{1,0:T(8,128)(2,1)}, bf16[2560,128]{1,0:T(8,128)(2,1)}, u32[]{:S(2)}, u32[]{:S(2)}) collective-permute-start(bf16[2560,128]{1,0:T(8,128)(2,1)} %collective-permute-done.7), channel_id=1, source_target_pairs={{0,1},{1,0},{2,3},{3,2},{4,5},{5,4},{6,7},{7,6},{8,9},{9,8},{10,11... | collective-permute-start | bytes 1966088 | tf_op jit(solution)/shard_map/ppermute | solution.py:293
  79.4 6.6 %copy-start.5 = (bf16[2560,128]{1,0:T(8,128)(2,1)S(1)}, bf16[2560,128]{1,0:T(8,128)(2,1)}, u32[]{:S(2)}) copy-start(bf16[2560,128]{1,0:T(8,128)(2,1)} %get-tuple-element.35) | copy-start | bytes 1966084
  79.4 6.6 %copy-start.6 = (bf16[1536,128]{1,0:T(8,128)(2,1)S(1)}, bf16[1536,128]{1,0:T(8,128)(2,1)}, u32[]{:S(2)}) copy-start(bf16[1536,128]{1,0:T(8,128)(2,1)} %get-tuple-element.39) | copy-start | bytes 1179652
  79.4 6.7 %copy-start.7 = (bf16[1536,128]{1,0:T(8,128)(2,1)S(1)}, bf16[1536,128]{1,0:T(8,128)(2,1)}, u32[]{:S(2)}) copy-start(bf16[1536,128]{1,0:T(8,128)(2,1)} %get-tuple-element.41) | copy-start | bytes 1179652
  85.9 8.0 %copy-start.2 = (bf16[3072,128]{1,0:T(8,128)(2,1)}, bf16[3072,128]{1,0:T(8,128)(2,1)S(1)}, u32[]{:S(2)}) copy-start(bf16[3072,128]{1,0:T(8,128)(2,1)S(1)} %collective-permute-done.10) | copy-start | bytes 2359300
  86.0 7.9 %collective-permute-start.12 = (bf16[1536,128]{1,0:T(8,128)(2,1)S(1)}, bf16[1536,128]{1,0:T(8,128)(2,1)S(1)}, u32[]{:S(2)}, u32[]{:S(2)}) collective-permute-start(bf16[1536,128]{1,0:T(8,128)(2,1)S(1)} %pad_maximum_fusion.7), channel_id=1, source_target_pairs={{0,6},{1,3},{2,0},{3,5},{4,2},{5,7},{6,4},{7,1},{8,14},{9,11},{10,... | collective-permute-start | bytes 1179656 | tf_op jit(solution)/shard_map/ppermute | solution.py:384
  93.9 6.0 %copy-start.11 = (bf16[1536,128]{1,0:T(8,128)(2,1)}, bf16[1536,128]{1,0:T(8,128)(2,1)S(1)}, u32[]{:S(2)}) copy-start(bf16[1536,128]{1,0:T(8,128)(2,1)S(1)} %collective-permute-done.12) | copy-start | bytes 1179652
  93.9 26.6 %collective-permute-start.14 = (bf16[8192,128]{1,0:T(8,128)(2,1)}, bf16[8192,128]{1,0:T(8,128)(2,1)}, u32[]{:S(2)}, u32[]{:S(2)}) collective-permute-start(bf16[8192,128]{1,0:T(8,128)(2,1)} %pad_maximum_fusion), channel_id=1, source_target_pairs={{0,6},{1,3},{2,0},{3,5},{4,2},{5,7},{6,4},{7,1},{8,14},{9,11},{10,... | collective-permute-start | bytes 6291464 | tf_op jit(solution)/shard_map/ppermute | solution.py:384
  93.9 4.6 %collective-permute-start.11 = (bf16[3072,128]{1,0:T(8,128)(2,1)S(1)}, bf16[3072,128]{1,0:T(8,128)(2,1)S(1)}, u32[]{:S(2)}, u32[]{:S(2)}) collective-permute-start(bf16[3072,128]{1,0:T(8,128)(2,1)S(1)} %collective-permute-done.10), channel_id=1, source_target_pairs={{0,1},{1,0},{2,3},{3,2},{4,5},{5,4},{6,7},{7,6},{8,9},{9,8},{10,11... | collective-permute-start | bytes 2359304 | tf_op jit(solution)/shard_map/ppermute | solution.py:293
  96.6 2.5 %collective-permute-start.13 = (bf16[1536,128]{1,0:T(8,128)(2,1)S(1)}, bf16[1536,128]{1,0:T(8,128)(2,1)S(1)}, u32[]{:S(2)}, u32[]{:S(2)}) collective-permute-start(bf16[1536,128]{1,0:T(8,128)(2,1)S(1)} %collective-permute-done.12), channel_id=1, source_target_pairs={{0,1},{1,0},{2,3},{3,2},{4,5},{5,4},{6,7},{7,6},{8,9},{9,8},{10,11... | collective-permute-start | bytes 1179656 | tf_op jit(solution)/shard_map/ppermute | solution.py:293
  98.5 1.3 copy-start.10
  99.1 0.8 copy-start.12
  99.8 8.9 %copy-start.3 = (bf16[3072,128]{1,0:T(8,128)(2,1)S(1)}, bf16[3072,128]{1,0:T(8,128)(2,1)}, u32[]{:S(2)}) copy-start(bf16[3072,128]{1,0:T(8,128)(2,1)} %copy-done.2) | copy-start | bytes 2359300
  99.8 9.0 %copy-start.8 = (bf16[1280,128]{1,0:T(8,128)(2,1)S(1)}, bf16[1280,128]{1,0:T(8,128)(2,1)}, u32[]{:S(2)}) copy-start(bf16[1280,128]{1,0:T(8,128)(2,1)} %get-tuple-element.29) | copy-start | bytes 983044
  99.9 9.0 %copy-start.9 = (bf16[1280,128]{1,0:T(8,128)(2,1)S(1)}, bf16[1280,128]{1,0:T(8,128)(2,1)}, u32[]{:S(2)}) copy-start(bf16[1280,128]{1,0:T(8,128)(2,1)} %get-tuple-element.30) | copy-start | bytes 983044
  105.2 13.9 %all-to-all-start = ((f32[16,8,1024]{2,1,0:T(8,128)}), f32[16,8,1024]{2,1,0:T(8,128)S(1)}, u32[]{:S(2)}, u32[]{:S(2)}) async-start(f32[16,8,1024]{2,1,0:T(8,128)} %bitcast.49), calls=%async_computation | async-start | bytes 1048576 | tf_op jit(solution)/shard_map/all_to_all | solution.py:453
  120.5 5.3 %collective-permute-start.17 = (bf16[1,8,1024]{2,1,0:T(8,128)(2,1)S(1)}, bf16[1,8,1024]{2,1,0:T(8,128)(2,1)S(1)}, u32[]{:S(2)}, u32[]{:S(2)}) collective-permute-start(bf16[1,8,1024]{2,1,0:T(8,128)(2,1)S(1)} %bitcast.58), channel_id=1, source_target_pairs={{0,2},{1,3},{2,4},{3,5},{4,6},{5,7},{6,0},{7,1},{8,10},{9,11},{10,... | collective-permute-start | bytes 49160 | tf_op jit(solution)/shard_map/ppermute | solution.py:460
  120.5 5.2 %collective-permute-start.16 = (bf16[1,8,1024]{2,1,0:T(8,128)(2,1)S(1)}, bf16[1,8,1024]{2,1,0:T(8,128)(2,1)S(1)}, u32[]{:S(2)}, u32[]{:S(2)}) collective-permute-start(bf16[1,8,1024]{2,1,0:T(8,128)(2,1)S(1)} %bitcast.59), channel_id=1, source_target_pairs={{0,4},{1,5},{2,6},{3,7},{4,0},{5,1},{6,2},{7,3},{8,12},{9,13},{10,... | collective-permute-start | bytes 49160 | tf_op jit(solution)/shard_map/ppermute | solution.py:460
  121.0 4.7 %collective-permute-start.15 = (bf16[1,8,1024]{2,1,0:T(8,128)(2,1)S(1)}, bf16[1,8,1024]{2,1,0:T(8,128)(2,1)S(1)}, u32[]{:S(2)}, u32[]{:S(2)}) collective-permute-start(bf16[1,8,1024]{2,1,0:T(8,128)(2,1)S(1)} %bitcast.60), channel_id=1, source_target_pairs={{0,6},{1,7},{2,0},{3,1},{4,2},{5,3},{6,4},{7,5},{8,14},{9,15},{10,... | collective-permute-start | bytes 49160 | tf_op jit(solution)/shard_map/ppermute | solution.py:460
  123.2 29.9 %collective-permute-start.25 = (bf16[8192,128]{1,0:T(8,128)(2,1)}, bf16[8192,128]{1,0:T(8,128)(2,1)S(1)}, u32[]{:S(2)}, u32[]{:S(2)}) collective-permute-start(bf16[8192,128]{1,0:T(8,128)(2,1)} %collective-permute-done.14.refs_12_), channel_id=1, source_target_pairs={{0,1},{1,0},{2,3},{3,2},{4,5},{5,4},{6,7},{7,6},{8,9},{9,8},{10,11... | collective-permute-start | bytes 6291464 | tf_op jit(solution)/shard_map/ppermute | solution.py:293
  125.8 25.0 %collective-permute-start.26 = (bf16[4096,128]{1,0:T(8,128)(2,1)S(1)}, bf16[4096,128]{1,0:T(8,128)(2,1)S(1)}, u32[]{:S(2)}, u32[]{:S(2)}) collective-permute-start(bf16[4096,128]{1,0:T(8,128)(2,1)S(1)} %pad_maximum_fusion.2), channel_id=1, source_target_pairs={{0,6},{1,3},{2,0},{3,5},{4,2},{5,7},{6,4},{7,1},{8,14},{9,11},{10,... | collective-permute-start | bytes 3145736 | tf_op jit(solution)/shard_map/ppermute | solution.py:384
  127.5 3.1 %collective-permute-start.18 = (bf16[4,8,1024]{2,1,0:T(8,128)(2,1)S(1)}, bf16[4,8,1024]{2,1,0:T(8,128)(2,1)S(1)}, u32[]{:S(2)}, u32[]{:S(2)}) collective-permute-start(bf16[4,8,1024]{2,1,0:T(8,128)(2,1)S(1)} %get-tuple-element.53), channel_id=1, source_target_pairs={{0,24},{8,0},{16,8},{24,16},{32,56},{40,32},{48,40},{56,48},{64,88... | collective-permute-start | bytes 196616 | tf_op jit(solution)/shard_map/ppermute | solution.py:460
  127.5 6.1 %collective-permute-start.20 = (bf16[4,8,1024]{2,1,0:T(8,128)(2,1)S(1)}, bf16[4,8,1024]{2,1,0:T(8,128)(2,1)S(1)}, u32[]{:S(2)}, u32[]{:S(2)}) collective-permute-start(bf16[4,8,1024]{2,1,0:T(8,128)(2,1)S(1)} %get-tuple-element.53), channel_id=1, source_target_pairs={{0,8},{8,16},{16,24},{24,0},{32,40},{40,48},{48,56},{56,32},{64,72... | collective-permute-start | bytes 196616 | tf_op jit(solution)/shard_map/ppermute | solution.py:460
  129.0 4.6 %collective-permute-start.19 = (bf16[4,8,1024]{2,1,0:T(8,128)(2,1)S(1)}, bf16[4,8,1024]{2,1,0:T(8,128)(2,1)S(1)}, u32[]{:S(2)}, u32[]{:S(2)}) collective-permute-start(bf16[4,8,1024]{2,1,0:T(8,128)(2,1)S(1)} %get-tuple-element.53), channel_id=1, source_target_pairs={{0,16},{8,24},{16,0},{24,8},{32,48},{40,56},{48,32},{56,40},{64,80... | collective-permute-start | bytes 196616 | tf_op jit(solution)/shard_map/ppermute | solution.py:460
  133.6 5.6 %collective-permute-start.21 = (bf16[16,8,1024]{2,1,0:T(8,128)(2,1)S(1)}, bf16[16,8,1024]{2,1,0:T(8,128)(2,1)S(1)}, u32[]{:S(2)}, u32[]{:S(2)}) collective-permute-start(bf16[16,8,1024]{2,1,0:T(8,128)(2,1)S(1)} %get-tuple-element.45), channel_id=1, source_target_pairs={{0,96},{8,104},{16,112},{24,120},{32,0},{40,8},{48,16},{56,24},{64... | collective-permute-start | bytes 786440 | tf_op jit(solution)/shard_map/ppermute | solution.py:460
  135.1 6.8 %collective-permute-start.22 = (bf16[16,8,1024]{2,1,0:T(8,128)(2,1)S(1)}, bf16[16,8,1024]{2,1,0:T(8,128)(2,1)S(1)}, u32[]{:S(2)}, u32[]{:S(2)}) collective-permute-start(bf16[16,8,1024]{2,1,0:T(8,128)(2,1)S(1)} %get-tuple-element.45), channel_id=1, source_target_pairs={{0,64},{8,72},{16,80},{24,88},{32,96},{40,104},{48,112},{56,120},{... | collective-permute-start | bytes 786440 | tf_op jit(solution)/shard_map/ppermute | solution.py:460
  135.1 9.6 %collective-permute-start.23 = (bf16[16,8,1024]{2,1,0:T(8,128)(2,1)S(1)}, bf16[16,8,1024]{2,1,0:T(8,128)(2,1)S(1)}, u32[]{:S(2)}, u32[]{:S(2)}) collective-permute-start(bf16[16,8,1024]{2,1,0:T(8,128)(2,1)S(1)} %get-tuple-element.45), channel_id=1, source_target_pairs={{0,32},{8,40},{16,48},{24,56},{32,64},{40,72},{48,80},{56,88},{64,... | collective-permute-start | bytes 786440 | tf_op jit(solution)/shard_map/ppermute | solution.py:460
  144.7 9.8 %copy-start.14 = (bf16[64,8,1024]{2,1,0:T(8,128)(2,1)}, bf16[64,8,1024]{2,1,0:T(8,128)(2,1)S(1)}, u32[]{:S(2)}) copy-start(bf16[64,8,1024]{2,1,0:T(8,128)(2,1)S(1)} %constant_dynamic-update-slice_fusion.11.gathered) | copy-start | bytes 3145732
  144.7 8.3 %collective-permute-start.24 = (bf16[64,8,1024]{2,1,0:T(8,128)(2,1)S(1)}, bf16[64,8,1024]{2,1,0:T(8,128)(2,1)S(1)}, u32[]{:S(2)}, u32[]{:S(2)}) collective-permute-start(bf16[64,8,1024]{2,1,0:T(8,128)(2,1)S(1)} %constant_dynamic-update-slice_fusion.11.gathered), channel_id=1, source_target_pairs={{0,1},{1,0},{2,3},{3,2},{4,5},{5,4},{6,7},{7,6},{8,9},{9,8},{10,11... | collective-permute-start | bytes 3145736 | tf_op jit(solution)/shard_map/ppermute | solution.py:293
  150.7 2.3 %copy-start.16 = (bf16[4096,128]{1,0:T(8,128)(2,1)}, bf16[4096,128]{1,0:T(8,128)(2,1)S(1)}, u32[]{:S(2)}) copy-start(bf16[4096,128]{1,0:T(8,128)(2,1)S(1)} %collective-permute-done.26.refs_14_) | copy-start | bytes 3145732
  150.7 3.8 %collective-permute-start.27 = (bf16[4096,128]{1,0:T(8,128)(2,1)S(1)}, bf16[4096,128]{1,0:T(8,128)(2,1)S(1)}, u32[]{:S(2)}, u32[]{:S(2)}) collective-permute-start(bf16[4096,128]{1,0:T(8,128)(2,1)S(1)} %collective-permute-done.26.refs_14_), channel_id=1, source_target_pairs={{0,1},{1,0},{2,3},{3,2},{4,5},{5,4},{6,7},{7,6},{8,9},{9,8},{10,11... | collective-permute-start | bytes 3145736 | tf_op jit(solution)/shard_map/ppermute | solution.py:293
  153.0 1.5 copy-start.17
  153.0 1.7 copy-start.15
  154.7 1.0 copy-start.18

commit v4 on v3

--- a/solution.py
+++ b/solution.py
@@ -17,15 +17,15 @@
 VMEM = pl.BlockSpec(memory_space=pltpu.VMEM)
 
 
-def filter_steps(count, row_shift, segments, even_odd, out, ready):
+def filter_steps(count, row_shift, segments, even_odd, out, ready, first_turns=2):
     for step in range(1, CHEB + 1):
         low = REACH * step
-        turns = 2
+        turns = first_turns if step == 1 else 2
         unroll = (count - 2 * low) // turns
 
         def body(turn, step=step, low=low, unroll=unroll):
             for part in range(unroll):
-                for which, (ids, live, tiles, first) in enumerate(segments):
+                for which, (facts, base, tiles, first) in enumerate(segments):
                     even, odd = even_odd[which]
                     source = first if step == 1 else (odd if step % 2 == 0 else even)
                     target = odd if step % 2 else even
@@ -33,8 +33,9 @@
                     block = low + turn * unroll + part
                     row = block - row_shift
                     left = jnp.concatenate([tiles[row, t] for t in range(4)], axis=1)
-                    right = jnp.concatenate([source[ids[row * 4 + t]] for t in range(4)], axis=0)
-                    value = jnp.dot(left, right, preferred_element_type=F32) * live[row]
+                    right = jnp.concatenate([source[facts[base + row, t]] for t in range(4)], axis=0)
+                    value = jnp.dot(left, right, preferred_element_type=F32)
+                    value = value * facts[base + row, 4].astype(F32)
                     if step > 1:
                         value = 2.0 * value - before[block].astype(F32)
                     if step == CHEB:
@@ -55,27 +56,32 @@
             lax.fori_loop(0, turns, looped, 0)
 
 
-def inner_kernel(count, ids, live, tiles, vectors, out, seg_t, seg_v, even, odd, sems):
-    half = count // 2
-    copies = [
-        pltpu.make_async_copy(vectors, seg_v, sems.at[0]),
-        pltpu.make_async_copy(tiles.at[pl.ds(0, half)], seg_t.at[pl.ds(0, half)], sems.at[1]),
-        pltpu.make_async_copy(
-            tiles.at[pl.ds(half, half)], seg_t.at[pl.ds(half, half)], sems.at[2]
-        ),
-    ]
-    for c in copies:
-        c.start()
+def inner_kernel(count, facts, tiles, vectors, out, seg_t, seg_v, even, odd, sems):
+    copies = []
+
+    def copy(source, target, begin, end):
+        at = pl.ds(begin, end - begin)
+        copies.append(pltpu.make_async_copy(source.at[at], target.at[at], sems.at[len(copies)]))
+        copies[-1].start()
+
+    turns = 4
+    per_turn = (count - 2 * REACH) // turns
+    ends = [REACH + per_turn * (turn + 1) for turn in range(turns - 1)] + [count]
+    middle = ends[1] + REACH
+    copy(vectors, seg_v, 0, middle)
+    for turn in range(turns):
+        if turn == 2:
+            copy(vectors, seg_v, middle, count)
+        copy(tiles, seg_t, ends[turn - 1] if turn else 0, ends[turn])
 
     def ready(turn):
-        if turn == 0:
-            copies[0].wait()
-        copies[1 + turn].wait()
-
-    filter_steps(count, 0, [(ids, live, seg_t, seg_v)], [(even, odd)], out, ready)
-
-
-def edge_kernel(count, ids0, live0, ids1, live1, core, tiles, vectors, near, far, vlow, vhigh,
+        for copied in {0: copies[0:2], 1: copies[2:3], 2: copies[3:5], 3: copies[5:6]}[turn]:
+            copied.wait()
+
+    filter_steps(count, 0, [(facts, 0, seg_t, seg_v)], [(even, odd)], out, ready, turns)
+
+
+def edge_kernel(count, facts, core, tiles, vectors, near, far, vlow, vhigh,
                 out, seg_v, seg_t, even, odd, even1, odd1, sems):
     deep_rows = DEEP - REACH
     span = 3 * DEEP
@@ -116,8 +122,8 @@
         span,
         REACH,
         [
-            (ids0, live0, Rows(0), seg_v.at[0]),
-            (ids1, live1, Rows(1), seg_v.at[1]),
+            (facts, 0, Rows(0), seg_v.at[0]),
+            (facts, span - 2 * REACH, Rows(1), seg_v.at[1]),
         ],
         [(even, odd), (even1, odd1)],
         out,
@@ -165,7 +171,7 @@
     for column, value in enumerate(values):
         if with_base:
             value = value + base[:, column * 128 : (column + 1) * 128]
-        out[:, column * 128 : (column + 1) * 128] = value
+        out[:, column * 128 : (column + 1) * 128] = value.astype(out.dtype)
 
 
 def split(value):
@@ -191,6 +197,7 @@
     n2, s2, o2, os2 = pieces[12:16]
     groups = ((low, low + inner, inner, 0), (0, low + 2 * inner, low, inner))
     for group, (first, second, half, at) in enumerate(groups):
+        m2, t2, skip = ((n2, s2, 0), (o2, os2, inner + low))[group]
         own, twin, n1, s1, o1, os1 = pieces[6 * group : 6 * group + 6]
         q = half // 2
         step = c * (second - first)
@@ -204,8 +211,8 @@
             copy(group, s1.at[1 - e], down, half, 6 + e - 4 * c)
             copy(group, o1.at[e], up + mine, q, 4 + e)
             copy(group, os1.at[1 - e], down + mine, q, 4 + e)
-            copy(group, n2.at[pl.ds(2 * at + e * half, half)], down, half, 2 + e + 4 * c)
-            copy(group, s2.at[pl.ds(2 * at + (1 - e) * half, half)], up, half, 6 + e - 4 * c)
+            copy(group, m2.at[pl.ds(skip + e * half, half)], down, half, 2 + e + 4 * c)
+            copy(group, t2.at[pl.ds(skip + (1 - e) * half, half)], up, half, 6 + e - 4 * c)
             copy(group, o2.at[pl.ds(at + e * q, q)], up + other, q, 4 + e)
             copy(group, os2.at[pl.ds(at + (1 - e) * q, q)], down + other, q, 4 + e)
 
@@ -333,32 +340,32 @@
     meta_high = vhigh[-1, :deep_rows, :8].astype(jnp.int32)
 
     inner_blocks = blocks - 2 * DEEP
-    inner_ids = (local_rows[:, None] + offsets).reshape(-1)
+    places = (jnp.arange(8) < 4).astype(jnp.int32)[None, :]
+    inner_facts = meta + places * local_rows[:, None]
     inner = pl.pallas_call(
         functools.partial(inner_kernel, blocks),
         out_shape=jax.ShapeDtypeStruct((inner_blocks, 128, panel), BF),
-        in_specs=[SMEM, SMEM, ANY, ANY],
+        in_specs=[SMEM, ANY, ANY],
         out_specs=VMEM,
         scratch_shapes=[
             pltpu.VMEM((blocks, 4, 128, 128), BF),
             pltpu.VMEM((blocks, 128, panel), BF),
             pltpu.VMEM((blocks, 128, panel), BF),
             pltpu.VMEM((blocks, 128, panel), BF),
-            pltpu.SemaphoreType.DMA((3,)),
+            pltpu.SemaphoreType.DMA((6,)),
         ],
         compiler_params=params(58),
         cost_estimate=cost(10**6, 2**20),
         name="inner_filter",
-    )(inner_ids, live.astype(F32), ham_tiles, vectors)
-
-    def segment(parts):
-        part = jnp.concatenate(parts, axis=0)
-        places = REACH + jnp.arange(part.shape[0], dtype=jnp.int32)[:, None] + part[:, :4]
-        return places.reshape(-1), part[:, 4].astype(F32)
+    )(inner_facts, ham_tiles, vectors)
 
     own_rows = 2 * DEEP - REACH
-    ids0, live0 = segment([meta_low, meta[:own_rows]])
-    ids1, live1 = segment([meta[blocks - own_rows :], meta_high])
+    edge_facts = jnp.concatenate(
+        [meta_low, meta[:own_rows], meta[blocks - own_rows :], meta_high], axis=0
+    )
+    edge_facts = edge_facts + places * (
+        REACH + jnp.arange(2 * (own_rows + deep_rows), dtype=jnp.int32) % (own_rows + deep_rows)
+    )[:, None]
     inner_own = inner.reshape(inner_blocks * 128, panel)
 
     quarter_of = jnp.where(z_at < 2, 0, 1).astype(jnp.int32)
@@ -383,8 +390,9 @@
     def by_side(value):
         return lax.ppermute(value, "vec", sides)
 
-    def send_near(own, before):
-        twin = swap(own)
+    def send_near(own, before_twin, before):
+        early, *_ = lax.optimization_barrier((own, *before_twin))
+        twin = swap(early)
         sent, *_ = lax.optimization_barrier(
             (join([half_of(own, core_at), half_of(twin, core_at)]), *before)
         )
@@ -401,7 +409,7 @@
         half = got[0].shape[0] // 2
         return pl.pallas_call(
             functools.partial(gram_kernel, half, base is not None),
-            out_shape=jax.ShapeDtypeStruct((128, 1024), F32),
+            out_shape=jax.ShapeDtypeStruct((128, 1024), F32 if base is None else BF),
             in_specs=[SMEM] + [VMEM] * (base is not None) + [ANY] * len(args),
             out_specs=VMEM,
             scratch_shapes=[
@@ -417,13 +425,13 @@
             name="gram",
         )(place, *([base] if base is not None else []), *args)
 
-    own, twin, _, n1 = send_near(inner_own, (far, vlow, vhigh))
+    own, twin, _, n1 = send_near(inner_own, (near, vlow, vhigh), (far,))
     inner_near = [own, twin, n1, swap(n1), by_side(join(pieces_of(n1, forward_part)))]
     core_arg = core_at.astype(jnp.int32)[None]
     edge = pl.pallas_call(
         functools.partial(edge_kernel, blocks),
         out_shape=jax.ShapeDtypeStruct((2 * DEEP, 128, panel), BF),
-        in_specs=[SMEM] * 5 + [ANY] * 6,
+        in_specs=[SMEM] * 2 + [ANY] * 6,
         out_specs=VMEM,
         scratch_shapes=[
             pltpu.VMEM((2, 3 * DEEP, 128, panel), BF),
@@ -434,26 +442,30 @@
         compiler_params=params(58),
         cost_estimate=cost(8 * 10**9, 11 * 2**20),
         name="edge_filter",
-    )(ids0, live0, ids1, live1, core_arg, flat_tiles, vectors, near, far, vlow, vhigh)
+    )(edge_facts, core_arg, flat_tiles, vectors, near, far, vlow, vhigh)
     edge_own = edge.reshape(2 * DEEP * 128, panel)
-    own, twin, sent, n1 = send_near(edge_own, ())
+    own, twin, sent, n1 = send_near(edge_own, (), ())
+    s1 = swap(n1)
     o1, _ = lax.optimization_barrier((inner_near[4], sent))
-    inner_got = inner_near[:4] + [o1, swap(o1)]
+    os1 = swap(o1)
+    n1_late, os1_early = lax.optimization_barrier((n1, os1))
+    os1, _ = lax.optimization_barrier((os1_early, s1))
+    inner_got = inner_near[:4] + [o1, os1]
     inner_gram = gram(inner_got, None)
-    n1_late, _ = lax.optimization_barrier((n1, inner_gram))
     o1 = by_side(join(pieces_of(n1_late, forward_part)))
-    edge_got = [own, twin, n1, swap(n1), o1, swap(o1)]
+    o1_late, _ = lax.optimization_barrier((o1, inner_gram))
+    edge_got = [own, twin, n1, s1, o1, swap(o1_late)]
     whole_gram = gram(edge_got, inner_gram)
 
     late, _ = lax.optimization_barrier(
-        (join([rest_of(*inner_got[:2]), rest_of(*edge_got[:2])]), o1)
+        (rest_of(*inner_got[:2]), o1_late)
     )
     n2 = by_side(late)
 
     pieces = lax.all_to_all(
         whole_gram.reshape(rows16, 128 // rows16, 1024), "row", split_axis=0, concat_axis=0
     )
-    mine = jnp.sum(pieces, axis=0).astype(BF)[None]
+    mine = jnp.sum(pieces.astype(F32), axis=0).astype(BF)[None]
     mine, n2 = lax.optimization_barrier((mine, n2))
 
     def around(value, axis, perm_of):
@@ -468,7 +480,11 @@
     got = around(mine, "vec", lambda d: z_perm(-d))
     later, _ = lax.optimization_barrier(
         (
-            join(pieces_of(inner_got[2], 1 - forward_part) + pieces_of(edge_got[2], 1 - forward_part)),
+            join(
+                pieces_of(inner_got[2], 1 - forward_part)
+                + pieces_of(edge_got[2], 1 - forward_part)
+                + [rest_of(*edge_got[:2])]
+            ),
             got,
         )
     )
@@ -478,7 +494,8 @@
     parts = []
     for values in (inner_got, edge_got):
         parts += list(values[:2]) + [two(v) for v in values[2:]]
-    parts += [n2, swap(n2), o2, swap(o2)]
+    o2_late, _ = lax.optimization_barrier((o2, got))
+    parts += [n2, swap(n2), o2, swap(o2_late)]
     return pl.pallas_call(
         final_kernel,
         out_shape=jax.ShapeDtypeStruct((row_count, panel), BF),

time: 171 us -> 171 us (level)
  waiting for transfers between devices: 45.5 us -> 50.4 us
  starting transfers between devices: 40.7 us -> 36.9 us
  other arithmetic: 7.68 us -> 5.63 us
    ppermute x6, waiting for transfers between devices: 14.8 us -> 23.1 us  [by_side(): return lax.ppermute(value, 'vec', sides)]
    unnamed x46 -> x49, local copies, waits for them, and re-layouts: 2.04 us -> 8 us
    ppermute x10, starting transfers between devices: 15.3 us -> 10.3 us  [swap(): return lax.ppermute(value, 'vec', z_perm(0, 1))]
    all_to_all x1, waiting for transfers between devices: 10.2 us -> 5.98 us  [local(): lax.all_to_all(whole_gram.reshape(rows16, 128 // rows16, 1024), 'row', sp...]
    ppermute x9, starting transfers between devices: 6.26 us -> 8.58 us  [around(): parts = [value] + [lax.ppermute(value, axis, perm_of(d)) for d in (1, 2, 3)]]
    ppermute x6, starting transfers between devices: 4.87 us -> 2.78 us  [by_side(): return lax.ppermute(value, 'vec', sides)]
    reshape x3 -> x0, local copies, waits for them, and re-layouts: 2.02 us -> none  [the longest x2 1.32 us: segment(): return (places.reshape(-1), part[:, 4].astype(F32))]
    convert_element_type x3 -> x1, other arithmetic: 1.81 us -> 0.01 us  [local(): places = (jnp.arange(8) < 4).astype(jnp.int32)[None, :]]
  transfers between devices with their start and end apart: 29 -> 29, of which waited for: 14 -> 14; matrix products, arithmetic and copies ran while one was open for 10% -> 8% of each run, Pallas kernels for 27% -> 27%
where the time goes in v4:
time: 171 us
  Pallas kernels  60.4 us (35%)
  waiting for transfers between devices  50.4 us (29%)
  starting transfers between devices  36.9 us (22%)
  local copies, waits for them, and re-layouts  15.3 us (9%)
  other arithmetic  5.63 us (3%)
  between operations  1.94 us (1%)
    ppermute x6, waiting for transfers between devices, by_side(): return lax.ppermute(value, 'vec', sides)  23.1 us
    pallas_call x1, Pallas kernels, local(): pl.pallas_call(functools.partial(edge_kernel, blocks), out_shape=jax.Shap...  17.2 us
    pallas_call x1, Pallas kernels, local(): pl.pallas_call(functools.partial(inner_kernel, blocks), out_shape=jax.Sha...  16.9 us
    pallas_call x1, Pallas kernels, local(): pl.pallas_call(final_kernel, out_shape=jax.ShapeDtypeStruct((row_count, p...  14.7 us
    ppermute x9, waiting for transfers between devices, around(): parts = [value] + [lax.ppermute(value, axis, perm_of(d)) for d in (1, 2, 3)]  13.5 us
    pallas_call x2, Pallas kernels, gram(): pl.pallas_call(functools.partial(gram_kernel, half, base is not None), ou...  11.5 us
    ppermute x10, starting transfers between devices, swap(): return lax.ppermute(value, 'vec', z_perm(0, 1))  10.3 us
    ppermute x9, starting transfers between devices, around(): parts = [value] + [lax.ppermute(value, axis, perm_of(d)) for d in (1, 2, 3)]  8.58 us
  transfers between devices with their start and end apart: 29, of which 14 were waited for; matrix products, arithmetic and copies ran while one was open for 8% of the time, Pallas kernels for 27%

profile of v4, /device:TPU:1, one launch (start us, length us, event | category | flops | bytes accessed | tf_op | source)
XLA Modules:
  0.0 170.6 jit_solution(962224049390856365)
XLA Ops:
  0.0 1.4 constant_dynamic-slice_fusion.10
  1.4 5.8 %collective-permute-start = (bf16[40,128,128]{2,1,0:T(8,128)(2,1)S(1)}, bf16[40,128,128]{2,1,0:T(8,128)(2,1)}, u32[]{:S(2)}, u32[]{:S(2)}) collective-permute-start(bf16[40,128,128]{2,1,0:T(8,128)(2,1)S(1)} %constant_dynamic-slice_fusion.10), channel_id=1, source_target_pairs={{0,8},{1,121},{2,10},{3,123},{4,12},{5,125},{6,14},{7,127},{8,16},... | collective-permute-start | bytes 3932168 | tf_op jit(solution)/shard_map/ppermute | solution.py:326
  8.1 0.6 fusion.4
  8.7 1.2 fusion.3
  10.1 4.8 %collective-permute-start.2 = (bf16[13,128,128]{2,1,0:T(8,128)(2,1)S(1)}, bf16[13,128,128]{2,1,0:T(8,128)(2,1)S(1)}, u32[]{:S(2)}, u32[]{:S(2)}) collective-permute-start(bf16[13,128,128]{2,1,0:T(8,128)(2,1)S(1)} %pad_maximum_fusion.5), channel_id=1, source_target_pairs={{0,120},{8,0},{16,8},{24,16},{32,24},{40,32},{48,40},{56,48},{64,5... | collective-permute-start | bytes 1277960 | tf_op jit(solution)/shard_map/ppermute | solution.py:336
  14.9 16.9 %inner_filter.1 = bf16[40,128,128]{2,1,0:T(8,128)(2,1)} custom-call(s32[64,8]{1,0:T(8,128)} %get-tuple-element.53.facts, bf16[64,4,128,128]{3,2,1,0:T(8,128)(2,1)} %tiles.1, bf16[64,128,128]{2,1,0:T(8,128)(2,1)} %bitcast.35), custom_call_target="tpu_custom_call" | custom-call | flops 1000000 | bytes 1048576 | tf_op jit(solution)/shard_map/inner_filter/pallas_call | solution.py:345
  31.9 1.2 collective-permute-start.3
  33.1 1.4 constant_dynamic-slice_fusion.1
  34.4 0.3 collective-permute-start.4
  35.0 1.0 collective-permute-done.3.refs_1_
  35.9 1.0 constant_dynamic-slice_fusion
  37.0 1.1 pad_maximum_fusion
  38.1 1.7 %collective-permute-start.5 = (bf16[5120,128]{1,0:T(8,128)(2,1)}, bf16[5120,128]{1,0:T(8,128)(2,1)S(1)}, u32[]{:S(2)}, u32[]{:S(2)}) collective-permute-start(bf16[5120,128]{1,0:T(8,128)(2,1)} %pad_maximum_fusion), channel_id=1, source_target_pairs={{0,6},{1,3},{2,0},{3,5},{4,2},{5,7},{6,4},{7,1},{8,14},{9,11},{10,... | collective-permute-start | bytes 3932168 | tf_op jit(solution)/shard_map/ppermute | solution.py:391
  39.9 0.1 copy.23
  40.0 0.7 multiply_add_fusion.facts
  40.7 17.2 %edge_filter.1 = bf16[24,128,128]{2,1,0:T(8,128)(2,1)} custom-call(s32[64,8]{1,0:T(8,128)} %multiply_add_fusion.facts, s32[1]{0:T(128)} %bitcast.3.core, bf16[256,128,128]{2,1,0:T(8,128)(2,1)} %bitcast.32, bf16[64,128,128]{2,1,0:T(8,128)(2,1)} %bitcast.36, bf16[40,128,128]{2,1,0:T(8,128)(2,1)} %collective-permute-done.near, ...), custom_call_target="tpu_custom_call" | custom-call | flops 8000000000 | bytes 11534336 | tf_op jit(solution)/shard_map/edge_filter/pallas_call | solution.py:431
  57.9 2.9 %collective-permute-start.8 = (bf16[3072,128]{1,0:T(8,128)(2,1)}, bf16[3072,128]{1,0:T(8,128)(2,1)S(1)}, u32[]{:S(2)}, u32[]{:S(2)}) collective-permute-start(bf16[3072,128]{1,0:T(8,128)(2,1)} %bitcast.39), channel_id=1, source_target_pairs={{0,1},{1,0},{2,3},{3,2},{4,5},{5,4},{6,7},{7,6},{8,9},{9,8},{10,11... | collective-permute-start | bytes 2359304 | tf_op jit(solution)/shard_map/ppermute | solution.py:300
  60.8 1.0 constant_dynamic-slice_fusion.5
  61.9 0.1 dynamic-slice_dynamic-update-slice_fusion.2
  62.0 1.3 copy-done.9
  63.5 1.0 pad_maximum_fusion.2
  64.6 0.2 collective-permute-start.9
  64.7 9.4 %collective-permute-done.7 = bf16[2560,128]{1,0:T(8,128)(2,1)} collective-permute-done((bf16[2560,128]{1,0:T(8,128)(2,1)S(1)}, bf16[2560,128]{1,0:T(8,128)(2,1)}, u32[]{:S(2)}, u32[]{:S(2)}) %collective-permute-start.7) | collective-permute-done | bytes 655392 | tf_op jit(solution)/shard_map/ppermute | solution.py:391
  74.2 0.5 collective-permute-start.6
  74.7 0.6 pad_add_fusion.2.place
  75.3 7.2 %collective-permute-done.9 = bf16[3072,128]{1,0:T(8,128)(2,1)S(1)} collective-permute-done((bf16[3072,128]{1,0:T(8,128)(2,1)}, bf16[3072,128]{1,0:T(8,128)(2,1)S(1)}, u32[]{:S(2)}, u32[]{:S(2)}) %collective-permute-start.9) | collective-permute-done | bytes 786464 | tf_op jit(solution)/shard_map/ppermute | solution.py:391
  82.7 1.2 pad_maximum_fusion.1
  83.9 0.9 collective-permute-done.11
  84.8 0.9 copy-done.7
  85.7 6.3 %gram.2.refs_0_ = f32[128,1024]{1,0:T(8,128)} custom-call(s32[4]{0:T(128)} %pad_add_fusion.2.place, bf16[5120,128]{1,0:T(8,128)(2,1)} %bitcast.29, bf16[5120,128]{1,0:T(8,128)(2,1)} %copy-done, bf16[2,2560,128]{2,1,0:T(8,128)(2,1)} %bitcast.33, bf16[2,2560,128]{2,1,0:T(8,128)(2,1)} %bitcast.13.refs_3_, bf16[2,1280,128]{2,1,0:T(8,128)(2,1)} %bitcast.17.refs_4_, ...), custom_call_target="tpu_custom_call" | custom-call | flops 671088640 | bytes 7864320 | tf_op jit(solution)/shard_map/gram/pallas_call | solution.py:410
  92.1 1.6 collective-permute-start.13
  93.6 0.7 dynamic-slice_dynamic-update-slice_fusion.5
  94.3 0.7 dynamic-slice_dynamic-update-slice_fusion.4
  95.0 0.2 collective-permute-done.13
  95.2 0.8 copy-done.8
  96.0 5.2 %gram.3 = bf16[128,1024]{1,0:T(8,128)(2,1)} custom-call(s32[4]{0:T(128)} %pad_add_fusion.2.place, f32[128,1024]{1,0:T(8,128)} %gram.2.refs_0_, bf16[3072,128]{1,0:T(8,128)(2,1)} %bitcast.41, bf16[3072,128]{1,0:T(8,128)(2,1)} %copy-done.4, bf16[2,1536,128]{2,1,0:T(8,128)(2,1)} %bitcast.37, bf16[2,1536,128]{2,1,0:T(8,128)(2,1)} %bitcast.47, ...), custom_call_target="tpu_custom_call" | custom-call | flops 402653184 | bytes 4718592 | tf_op jit(solution)/shard_map/gram/pallas_call | solution.py:410
  101.2 4.5 %all-to-all-start = ((bf16[16,8,1024]{2,1,0:T(8,128)(2,1)}), bf16[16,8,1024]{2,1,0:T(8,128)(2,1)S(1)}, u32[]{:S(2)}, u32[]{:S(2)}) async-start(bf16[16,8,1024]{2,1,0:T(8,128)(2,1)} %bitcast.46), calls=%async_computation | async-start | bytes 524288 | tf_op jit(solution)/shard_map/all_to_all | solution.py:465
  105.8 0.8 dynamic-slice_dynamic-update-slice_fusion.1
  106.6 0.8 dynamic-slice_dynamic-update-slice_fusion
  107.3 6.0 %all-to-all-done = bf16[16,8,1024]{2,1,0:T(8,128)(2,1)S(1)} async-done(((bf16[16,8,1024]{2,1,0:T(8,128)(2,1)}), bf16[16,8,1024]{2,1,0:T(8,128)(2,1)S(1)}, u32[]{:S(2)}, u32[]{:S(2)}) %all-to-all-start) | async-done | bytes 262176 | tf_op jit(solution)/shard_map/all_to_all | solution.py:465
  113.4 0.9 collective-permute-start.17
  114.3 2.1 %collective-permute-start.16 = (bf16[1,8,1024]{2,1,0:T(8,128)(2,1)S(1)}, bf16[1,8,1024]{2,1,0:T(8,128)(2,1)S(1)}, u32[]{:S(2)}, u32[]{:S(2)}) collective-permute-start(bf16[1,8,1024]{2,1,0:T(8,128)(2,1)S(1)} %bitcast.52), channel_id=1, source_target_pairs={{0,4},{1,5},{2,6},{3,7},{4,0},{5,1},{6,2},{7,3},{8,12},{9,13},{10,... | collective-permute-start | bytes 49160 | tf_op jit(solution)/shard_map/ppermute | solution.py:472
  116.3 1.0 collective-permute-start.15
  117.3 1.6 collective-permute-done.15
  119.0 0.6 collective-permute-start.26
  119.6 0.8 collective-permute-start.18
  120.4 0.7 collective-permute-start.20
  121.1 1.2 collective-permute-start.19
  122.3 0.4 collective-permute-done.18
  122.8 3.0 %collective-permute-done.19 = bf16[4,8,1024]{2,1,0:T(8,128)(2,1)S(1)} collective-permute-done((bf16[4,8,1024]{2,1,0:T(8,128)(2,1)S(1)}, bf16[4,8,1024]{2,1,0:T(8,128)(2,1)S(1)}, u32[]{:S(2)}, u32[]{:S(2)}) %collective-permute-start.19) | collective-permute-done | bytes 65568 | tf_op jit(solution)/shard_map/ppermute | solution.py:472
  125.8 1.0 collective-permute-start.21
  126.8 0.8 collective-permute-start.22
  127.6 0.2 collective-permute-start.23
  127.7 3.6 %collective-permute-done.21 = bf16[16,8,1024]{2,1,0:T(8,128)(2,1)S(1)} collective-permute-done((bf16[16,8,1024]{2,1,0:T(8,128)(2,1)S(1)}, bf16[16,8,1024]{2,1,0:T(8,128)(2,1)S(1)}, u32[]{:S(2)}, u32[]{:S(2)}) %collective-permute-start.21) | collective-permute-done | bytes 262176 | tf_op jit(solution)/shard_map/ppermute | solution.py:472
  131.4 2.2 %collective-permute-done.22 = bf16[16,8,1024]{2,1,0:T(8,128)(2,1)S(1)} collective-permute-done((bf16[16,8,1024]{2,1,0:T(8,128)(2,1)S(1)}, bf16[16,8,1024]{2,1,0:T(8,128)(2,1)S(1)}, u32[]{:S(2)}, u32[]{:S(2)}) %collective-permute-start.22) | collective-permute-done | bytes 262176 | tf_op jit(solution)/shard_map/ppermute | solution.py:472
  133.6 2.7 %collective-permute-done.23 = bf16[16,8,1024]{2,1,0:T(8,128)(2,1)S(1)} collective-permute-done((bf16[16,8,1024]{2,1,0:T(8,128)(2,1)S(1)}, bf16[16,8,1024]{2,1,0:T(8,128)(2,1)S(1)}, u32[]{:S(2)}, u32[]{:S(2)}) %collective-permute-start.23) | collective-permute-done | bytes 262176 | tf_op jit(solution)/shard_map/ppermute | solution.py:472
  136.3 6.5 %collective-permute-done.26.refs_14_ = bf16[7168,128]{1,0:T(8,128)(2,1)S(1)} collective-permute-done((bf16[7168,128]{1,0:T(8,128)(2,1)}, bf16[7168,128]{1,0:T(8,128)(2,1)S(1)}, u32[]{:S(2)}, u32[]{:S(2)}) %collective-permute-start.26) | collective-permute-done | bytes 1835040 | tf_op jit(solution)/shard_map/ppermute | solution.py:391
  142.8 3.4 %collective-permute-start.27 = (bf16[7168,128]{1,0:T(8,128)(2,1)S(1)}, bf16[7168,128]{1,0:T(8,128)(2,1)S(1)}, u32[]{:S(2)}, u32[]{:S(2)}) collective-permute-start(bf16[7168,128]{1,0:T(8,128)(2,1)S(1)} %collective-permute-done.26.refs_14_), channel_id=1, source_target_pairs={{0,1},{1,0},{2,3},{3,2},{4,5},{5,4},{6,7},{7,6},{8,9},{9,8},{10,11... | collective-permute-start | bytes 5505032 | tf_op jit(solution)/shard_map/ppermute | solution.py:300
  146.2 0.5 collective-permute-start.24
  147.4 5.7 %collective-permute-done.25.refs_13_ = bf16[5120,128]{1,0:T(8,128)(2,1)S(1)} collective-permute-done((bf16[5120,128]{1,0:T(8,128)(2,1)}, bf16[5120,128]{1,0:T(8,128)(2,1)S(1)}, u32[]{:S(2)}, u32[]{:S(2)}) %collective-permute-start.25) | collective-permute-done | bytes 1310752 | tf_op jit(solution)/shard_map/ppermute | solution.py:300
  153.1 1.0 copy-done.17
  154.1 0.4 copy-done.16
  154.5 1.2 copy-done.15
  155.7 14.7 %final.1 = bf16[8192,128]{1,0:T(8,128)(2,1)} custom-call(s32[4]{0:T(128)} %pad_add_fusion.2.place, f32[1]{0:T(128)S(6)} %copy.48.scale_in, bf16[64,8,1024]{2,1,0:T(8,128)(2,1)} %copy-done.11, bf16[64,8,1024]{2,1,0:T(8,128)(2,1)} %copy-done.17, bf16[5120,128]{1,0:T(8,128)(2,1)} %bitcast.30, bf16[5120,128]{1,0:T(8,128)(2,1)} %copy-done, ...), custom_call_target="tpu_custom_call" | custom-call | flops 6000000000 | bytes 20971520 | tf_op jit(solution)/shard_map/final/pallas_call | solution.py:499
  (86 shorter events, 1.3 us)
Async XLA Ops:
  0.0 7.9 %copy-start.10 = (s32[64,4]{0,1:T(4,128)S(1)}, s32[64,4]{0,1:T(4,128)}, u32[]{:S(2)}) copy-start(s32[64,4]{0,1:T(4,128)} %param.6) | copy-start | bytes 3076
  1.4 30.5 %collective-permute-start = (bf16[40,128,128]{2,1,0:T(8,128)(2,1)S(1)}, bf16[40,128,128]{2,1,0:T(8,128)(2,1)}, u32[]{:S(2)}, u32[]{:S(2)}) collective-permute-start(bf16[40,128,128]{2,1,0:T(8,128)(2,1)S(1)} %constant_dynamic-slice_fusion.10), channel_id=1, source_target_pairs={{0,8},{1,121},{2,10},{3,123},{4,12},{5,125},{6,14},{7,127},{8,16},... | collective-permute-start | bytes 3932168 | tf_op jit(solution)/shard_map/ppermute | solution.py:326
  9.9 21.9 %collective-permute-start.1 = (bf16[13,128,128]{2,1,0:T(8,128)(2,1)S(1)}, bf16[13,128,128]{2,1,0:T(8,128)(2,1)S(1)}, u32[]{:S(2)}, u32[]{:S(2)}) collective-permute-start(bf16[13,128,128]{2,1,0:T(8,128)(2,1)S(1)} %pad_maximum_fusion.4), channel_id=1, source_target_pairs={{0,8},{8,16},{16,24},{24,32},{32,40},{40,48},{48,56},{56,64},{64,7... | collective-permute-start | bytes 1277960 | tf_op jit(solution)/shard_map/ppermute | solution.py:333
  10.1 21.8 %collective-permute-start.2 = (bf16[13,128,128]{2,1,0:T(8,128)(2,1)S(1)}, bf16[13,128,128]{2,1,0:T(8,128)(2,1)S(1)}, u32[]{:S(2)}, u32[]{:S(2)}) collective-permute-start(bf16[13,128,128]{2,1,0:T(8,128)(2,1)S(1)} %pad_maximum_fusion.5), channel_id=1, source_target_pairs={{0,120},{8,0},{16,8},{24,16},{32,24},{40,32},{48,40},{56,48},{64,5... | collective-permute-start | bytes 1277960 | tf_op jit(solution)/shard_map/ppermute | solution.py:336
  31.9 5.1 %copy-start.12 = (bf16[13,128,128]{2,1,0:T(8,128)(2,1)}, bf16[13,128,128]{2,1,0:T(8,128)(2,1)S(1)}, u32[]{:S(2)}) copy-start(bf16[13,128,128]{2,1,0:T(8,128)(2,1)S(1)} %collective-permute-done.1.vlow) | copy-start | bytes 1277956
  31.9 5.1 %copy-start.13 = (bf16[13,128,128]{2,1,0:T(8,128)(2,1)}, bf16[13,128,128]{2,1,0:T(8,128)(2,1)S(1)}, u32[]{:S(2)}) copy-start(bf16[13,128,128]{2,1,0:T(8,128)(2,1)S(1)} %collective-permute-done.2.vhigh) | copy-start | bytes 1277956
  31.9 4.0 %collective-permute-start.3 = (bf16[5120,128]{1,0:T(8,128)(2,1)}, bf16[5120,128]{1,0:T(8,128)(2,1)S(1)}, u32[]{:S(2)}, u32[]{:S(2)}) collective-permute-start(bf16[5120,128]{1,0:T(8,128)(2,1)} %bitcast.27), channel_id=1, source_target_pairs={{0,1},{1,0},{2,3},{3,2},{4,5},{5,4},{6,7},{7,6},{8,9},{9,8},{10,11... | collective-permute-start | bytes 3932168 | tf_op jit(solution)/shard_map/ppermute | solution.py:300
  34.4 3.7 %collective-permute-start.4 = (bf16[40,128,128]{2,1,0:T(8,128)(2,1)}, bf16[40,128,128]{2,1,0:T(8,128)(2,1)}, u32[]{:S(2)}, u32[]{:S(2)}) collective-permute-start(bf16[40,128,128]{2,1,0:T(8,128)(2,1)} %collective-permute-done.near), channel_id=1, source_target_pairs={{0,1},{1,0},{2,3},{3,2},{4,5},{5,4},{6,7},{7,6},{8,9},{9,8},{10,11... | collective-permute-start | bytes 3932168 | tf_op jit(solution)/shard_map/ppermute | solution.py:300
  35.9 2.2 %copy-start = (bf16[5120,128]{1,0:T(8,128)(2,1)}, bf16[5120,128]{1,0:T(8,128)(2,1)S(1)}, u32[]{:S(2)}) copy-start(bf16[5120,128]{1,0:T(8,128)(2,1)S(1)} %collective-permute-done.3.refs_1_) | copy-start | bytes 3932164
  38.1 23.7 %collective-permute-start.5 = (bf16[5120,128]{1,0:T(8,128)(2,1)}, bf16[5120,128]{1,0:T(8,128)(2,1)S(1)}, u32[]{:S(2)}, u32[]{:S(2)}) collective-permute-start(bf16[5120,128]{1,0:T(8,128)(2,1)} %pad_maximum_fusion), channel_id=1, source_target_pairs={{0,6},{1,3},{2,0},{3,5},{4,2},{5,7},{6,4},{7,1},{8,14},{9,11},{10,... | collective-permute-start | bytes 3932168 | tf_op jit(solution)/shard_map/ppermute | solution.py:391
  57.9 5.5 %collective-permute-start.8 = (bf16[3072,128]{1,0:T(8,128)(2,1)}, bf16[3072,128]{1,0:T(8,128)(2,1)S(1)}, u32[]{:S(2)}, u32[]{:S(2)}) collective-permute-start(bf16[3072,128]{1,0:T(8,128)(2,1)} %bitcast.39), channel_id=1, source_target_pairs={{0,1},{1,0},{2,3},{3,2},{4,5},{5,4},{6,7},{7,6},{8,9},{9,8},{10,11... | collective-permute-start | bytes 2359304 | tf_op jit(solution)/shard_map/ppermute | solution.py:300
  61.8 12.4 %copy-start.1 = (bf16[5120,128]{1,0:T(8,128)(2,1)}, bf16[5120,128]{1,0:T(8,128)(2,1)S(1)}, u32[]{:S(2)}) copy-start(bf16[5120,128]{1,0:T(8,128)(2,1)S(1)} %collective-permute-done.5) | copy-start | bytes 3932164
  62.0 1.3 copy-start.9
  63.4 10.8 %collective-permute-start.7 = (bf16[2560,128]{1,0:T(8,128)(2,1)S(1)}, bf16[2560,128]{1,0:T(8,128)(2,1)}, u32[]{:S(2)}, u32[]{:S(2)}) collective-permute-start(bf16[2560,128]{1,0:T(8,128)(2,1)S(1)} %pad_maximum_fusion.3), channel_id=1, source_target_pairs={{0,6},{1,3},{2,0},{3,5},{4,2},{5,7},{6,4},{7,1},{8,14},{9,11},{10,... | collective-permute-start | bytes 1966088 | tf_op jit(solution)/shard_map/ppermute | solution.py:391
  63.5 19.1 %copy-start.4 = (bf16[3072,128]{1,0:T(8,128)(2,1)}, bf16[3072,128]{1,0:T(8,128)(2,1)S(1)}, u32[]{:S(2)}) copy-start(bf16[3072,128]{1,0:T(8,128)(2,1)S(1)} %collective-permute-done.8.refs_2_.refs_7_) | copy-start | bytes 2359300
  64.6 17.9 %collective-permute-start.9 = (bf16[3072,128]{1,0:T(8,128)(2,1)}, bf16[3072,128]{1,0:T(8,128)(2,1)S(1)}, u32[]{:S(2)}, u32[]{:S(2)}) collective-permute-start(bf16[3072,128]{1,0:T(8,128)(2,1)} %pad_maximum_fusion.2), channel_id=1, source_target_pairs={{0,6},{1,3},{2,0},{3,5},{4,2},{5,7},{6,4},{7,1},{8,14},{9,11},{10,... | collective-permute-start | bytes 2359304 | tf_op jit(solution)/shard_map/ppermute | solution.py:391
  74.2 8.3 %collective-permute-start.10 = (bf16[2560,128]{1,0:T(8,128)(2,1)}, bf16[2560,128]{1,0:T(8,128)(2,1)}, u32[]{:S(2)}, u32[]{:S(2)}) collective-permute-start(bf16[2560,128]{1,0:T(8,128)(2,1)} %collective-permute-done.7), channel_id=1, source_target_pairs={{0,1},{1,0},{2,3},{3,2},{4,5},{5,4},{6,7},{7,6},{8,9},{9,8},{10,11... | collective-permute-start | bytes 1966088 | tf_op jit(solution)/shard_map/ppermute | solution.py:300
  74.2 10.6 %collective-permute-start.6 = (bf16[5120,128]{1,0:T(8,128)(2,1)S(1)}, bf16[5120,128]{1,0:T(8,128)(2,1)}, u32[]{:S(2)}, u32[]{:S(2)}) collective-permute-start(bf16[5120,128]{1,0:T(8,128)(2,1)S(1)} %collective-permute-done.5), channel_id=1, source_target_pairs={{0,1},{1,0},{2,3},{3,2},{4,5},{5,4},{6,7},{7,6},{8,9},{9,8},{10,11... | collective-permute-start | bytes 3932168 | tf_op jit(solution)/shard_map/ppermute | solution.py:300
  74.7 8.0 %copy-start.6 = (bf16[2560,128]{1,0:T(8,128)(2,1)S(1)}, bf16[2560,128]{1,0:T(8,128)(2,1)}, u32[]{:S(2)}) copy-start(bf16[2560,128]{1,0:T(8,128)(2,1)} %get-tuple-element.42) | copy-start | bytes 1966084
  82.5 11.8 %copy-start.2 = (bf16[3072,128]{1,0:T(8,128)(2,1)}, bf16[3072,128]{1,0:T(8,128)(2,1)S(1)}, u32[]{:S(2)}) copy-start(bf16[3072,128]{1,0:T(8,128)(2,1)S(1)} %collective-permute-done.9) | copy-start | bytes 2359300
  82.5 2.3 %collective-permute-start.11 = (bf16[3072,128]{1,0:T(8,128)(2,1)S(1)}, bf16[3072,128]{1,0:T(8,128)(2,1)S(1)}, u32[]{:S(2)}, u32[]{:S(2)}) collective-permute-start(bf16[3072,128]{1,0:T(8,128)(2,1)S(1)} %collective-permute-done.9), channel_id=1, source_target_pairs={{0,1},{1,0},{2,3},{3,2},{4,5},{5,4},{6,7},{7,6},{8,9},{9,8},{10,11... | collective-permute-start | bytes 2359304 | tf_op jit(solution)/shard_map/ppermute | solution.py:300
  82.6 9.4 %collective-permute-start.12 = (bf16[1536,128]{1,0:T(8,128)(2,1)S(1)}, bf16[1536,128]{1,0:T(8,128)(2,1)}, u32[]{:S(2)}, u32[]{:S(2)}) collective-permute-start(bf16[1536,128]{1,0:T(8,128)(2,1)S(1)} %pad_maximum_fusion.6), channel_id=1, source_target_pairs={{0,6},{1,3},{2,0},{3,5},{4,2},{5,7},{6,4},{7,1},{8,14},{9,11},{10,... | collective-permute-start | bytes 1179656 | tf_op jit(solution)/shard_map/ppermute | solution.py:391
  84.8 0.9 copy-start.7
  92.0 21.4 %collective-permute-start.14 = (bf16[5120,128]{1,0:T(8,128)(2,1)}, bf16[5120,128]{1,0:T(8,128)(2,1)}, u32[]{:S(2)}, u32[]{:S(2)}) collective-permute-start(bf16[5120,128]{1,0:T(8,128)(2,1)} %pad_maximum_fusion.1), channel_id=1, source_target_pairs={{0,6},{1,3},{2,0},{3,5},{4,2},{5,7},{6,4},{7,1},{8,14},{9,11},{10,... | collective-permute-start | bytes 3932168 | tf_op jit(solution)/shard_map/ppermute | solution.py:391
  92.1 3.1 %collective-permute-start.13 = (bf16[1536,128]{1,0:T(8,128)(2,1)}, bf16[1536,128]{1,0:T(8,128)(2,1)S(1)}, u32[]{:S(2)}, u32[]{:S(2)}) collective-permute-start(bf16[1536,128]{1,0:T(8,128)(2,1)} %collective-permute-done.12), channel_id=1, source_target_pairs={{0,1},{1,0},{2,3},{3,2},{4,5},{5,4},{6,7},{7,6},{8,9},{9,8},{10,11... | collective-permute-start | bytes 1179656 | tf_op jit(solution)/shard_map/ppermute | solution.py:300
  95.2 0.8 copy-start.8
  96.0 9.8 %copy-start.3 = (bf16[24,128,128]{2,1,0:T(8,128)(2,1)S(1)}, bf16[24,128,128]{2,1,0:T(8,128)(2,1)}, u32[]{:S(2)}) copy-start(bf16[24,128,128]{2,1,0:T(8,128)(2,1)} %edge_filter.1) | copy-start | bytes 2359300
  96.0 10.6 %copy-start.5 = (bf16[3072,128]{1,0:T(8,128)(2,1)S(1)}, bf16[3072,128]{1,0:T(8,128)(2,1)}, u32[]{:S(2)}) copy-start(bf16[3072,128]{1,0:T(8,128)(2,1)} %copy-done.4) | copy-start | bytes 2359300
  101.2 12.1 %all-to-all-start = ((bf16[16,8,1024]{2,1,0:T(8,128)(2,1)}), bf16[16,8,1024]{2,1,0:T(8,128)(2,1)S(1)}, u32[]{:S(2)}, u32[]{:S(2)}) async-start(bf16[16,8,1024]{2,1,0:T(8,128)(2,1)} %bitcast.46), calls=%async_computation | async-start | bytes 524288 | tf_op jit(solution)/shard_map/all_to_all | solution.py:465
  113.4 5.6 %collective-permute-start.17 = (bf16[1,8,1024]{2,1,0:T(8,128)(2,1)S(1)}, bf16[1,8,1024]{2,1,0:T(8,128)(2,1)S(1)}, u32[]{:S(2)}, u32[]{:S(2)}) collective-permute-start(bf16[1,8,1024]{2,1,0:T(8,128)(2,1)S(1)} %bitcast.51), channel_id=1, source_target_pairs={{0,2},{1,3},{2,4},{3,5},{4,6},{5,7},{6,0},{7,1},{8,10},{9,11},{10,... | collective-permute-start | bytes 49160 | tf_op jit(solution)/shard_map/ppermute | solution.py:472
  114.3 4.7 %collective-permute-start.16 = (bf16[1,8,1024]{2,1,0:T(8,128)(2,1)S(1)}, bf16[1,8,1024]{2,1,0:T(8,128)(2,1)S(1)}, u32[]{:S(2)}, u32[]{:S(2)}) collective-permute-start(bf16[1,8,1024]{2,1,0:T(8,128)(2,1)S(1)} %bitcast.52), channel_id=1, source_target_pairs={{0,4},{1,5},{2,6},{3,7},{4,0},{5,1},{6,2},{7,3},{8,12},{9,13},{10,... | collective-permute-start | bytes 49160 | tf_op jit(solution)/shard_map/ppermute | solution.py:472
  116.3 2.6 %collective-permute-start.15 = (bf16[1,8,1024]{2,1,0:T(8,128)(2,1)S(1)}, bf16[1,8,1024]{2,1,0:T(8,128)(2,1)S(1)}, u32[]{:S(2)}, u32[]{:S(2)}) collective-permute-start(bf16[1,8,1024]{2,1,0:T(8,128)(2,1)S(1)} %bitcast.53), channel_id=1, source_target_pairs={{0,6},{1,7},{2,0},{3,1},{4,2},{5,3},{6,4},{7,5},{8,14},{9,15},{10,... | collective-permute-start | bytes 49160 | tf_op jit(solution)/shard_map/ppermute | solution.py:472
  119.0 23.9 %collective-permute-start.26 = (bf16[7168,128]{1,0:T(8,128)(2,1)}, bf16[7168,128]{1,0:T(8,128)(2,1)S(1)}, u32[]{:S(2)}, u32[]{:S(2)}) collective-permute-start(bf16[7168,128]{1,0:T(8,128)(2,1)} %dynamic-slice_dynamic-update-slice_fusion), channel_id=1, source_target_pairs={{0,6},{1,3},{2,0},{3,5},{4,2},{5,7},{6,4},{7,1},{8,14},{9,11},{10,... | collective-permute-start | bytes 5505032 | tf_op jit(solution)/shard_map/ppermute | solution.py:391
  119.6 3.1 %collective-permute-start.18 = (bf16[4,8,1024]{2,1,0:T(8,128)(2,1)S(1)}, bf16[4,8,1024]{2,1,0:T(8,128)(2,1)S(1)}, u32[]{:S(2)}, u32[]{:S(2)}) collective-permute-start(bf16[4,8,1024]{2,1,0:T(8,128)(2,1)S(1)} %get-tuple-element.56), channel_id=1, source_target_pairs={{0,24},{8,0},{16,8},{24,16},{32,56},{40,32},{48,40},{56,48},{64,88... | collective-permute-start | bytes 196616 | tf_op jit(solution)/shard_map/ppermute | solution.py:472
  120.4 5.3 %collective-permute-start.20 = (bf16[4,8,1024]{2,1,0:T(8,128)(2,1)S(1)}, bf16[4,8,1024]{2,1,0:T(8,128)(2,1)S(1)}, u32[]{:S(2)}, u32[]{:S(2)}) collective-permute-start(bf16[4,8,1024]{2,1,0:T(8,128)(2,1)S(1)} %get-tuple-element.56), channel_id=1, source_target_pairs={{0,8},{8,16},{16,24},{24,0},{32,40},{40,48},{48,56},{56,32},{64,72... | collective-permute-start | bytes 196616 | tf_op jit(solution)/shard_map/ppermute | solution.py:472
  121.1 4.6 %collective-permute-start.19 = (bf16[4,8,1024]{2,1,0:T(8,128)(2,1)S(1)}, bf16[4,8,1024]{2,1,0:T(8,128)(2,1)S(1)}, u32[]{:S(2)}, u32[]{:S(2)}) collective-permute-start(bf16[4,8,1024]{2,1,0:T(8,128)(2,1)S(1)} %get-tuple-element.56), channel_id=1, source_target_pairs={{0,16},{8,24},{16,0},{24,8},{32,48},{40,56},{48,32},{56,40},{64,80... | collective-permute-start | bytes 196616 | tf_op jit(solution)/shard_map/ppermute | solution.py:472
  125.8 5.6 %collective-permute-start.21 = (bf16[16,8,1024]{2,1,0:T(8,128)(2,1)S(1)}, bf16[16,8,1024]{2,1,0:T(8,128)(2,1)S(1)}, u32[]{:S(2)}, u32[]{:S(2)}) collective-permute-start(bf16[16,8,1024]{2,1,0:T(8,128)(2,1)S(1)} %get-tuple-element.46), channel_id=1, source_target_pairs={{0,96},{8,104},{16,112},{24,120},{32,0},{40,8},{48,16},{56,24},{64... | collective-permute-start | bytes 786440 | tf_op jit(solution)/shard_map/ppermute | solution.py:472
  126.8 6.8 %collective-permute-start.22 = (bf16[16,8,1024]{2,1,0:T(8,128)(2,1)S(1)}, bf16[16,8,1024]{2,1,0:T(8,128)(2,1)S(1)}, u32[]{:S(2)}, u32[]{:S(2)}) collective-permute-start(bf16[16,8,1024]{2,1,0:T(8,128)(2,1)S(1)} %get-tuple-element.46), channel_id=1, source_target_pairs={{0,64},{8,72},{16,80},{24,88},{32,96},{40,104},{48,112},{56,120},{... | collective-permute-start | bytes 786440 | tf_op jit(solution)/shard_map/ppermute | solution.py:472
  127.6 8.8 %collective-permute-start.23 = (bf16[16,8,1024]{2,1,0:T(8,128)(2,1)S(1)}, bf16[16,8,1024]{2,1,0:T(8,128)(2,1)S(1)}, u32[]{:S(2)}, u32[]{:S(2)}) collective-permute-start(bf16[16,8,1024]{2,1,0:T(8,128)(2,1)S(1)} %get-tuple-element.46), channel_id=1, source_target_pairs={{0,32},{8,40},{16,48},{24,56},{32,64},{40,72},{48,80},{56,88},{64,... | collective-permute-start | bytes 786440 | tf_op jit(solution)/shard_map/ppermute | solution.py:472
  136.3 17.7 %copy-start.11 = (bf16[64,8,1024]{2,1,0:T(8,128)(2,1)}, bf16[64,8,1024]{2,1,0:T(8,128)(2,1)S(1)}, u32[]{:S(2)}) copy-start(bf16[64,8,1024]{2,1,0:T(8,128)(2,1)S(1)} %constant_dynamic-update-slice_fusion.11.gathered) | copy-start | bytes 3145732
  142.8 11.2 %copy-start.14 = (bf16[7168,128]{1,0:T(8,128)(2,1)}, bf16[7168,128]{1,0:T(8,128)(2,1)S(1)}, u32[]{:S(2)}) copy-start(bf16[7168,128]{1,0:T(8,128)(2,1)S(1)} %collective-permute-done.26.refs_14_) | copy-start | bytes 5505028
  142.8 11.2 %collective-permute-start.27 = (bf16[7168,128]{1,0:T(8,128)(2,1)S(1)}, bf16[7168,128]{1,0:T(8,128)(2,1)S(1)}, u32[]{:S(2)}, u32[]{:S(2)}) collective-permute-start(bf16[7168,128]{1,0:T(8,128)(2,1)S(1)} %collective-permute-done.26.refs_14_), channel_id=1, source_target_pairs={{0,1},{1,0},{2,3},{3,2},{4,5},{5,4},{6,7},{7,6},{8,9},{9,8},{10,11... | collective-permute-start | bytes 5505032 | tf_op jit(solution)/shard_map/ppermute | solution.py:300
  146.2 6.9 %collective-permute-start.25 = (bf16[5120,128]{1,0:T(8,128)(2,1)}, bf16[5120,128]{1,0:T(8,128)(2,1)S(1)}, u32[]{:S(2)}, u32[]{:S(2)}) collective-permute-start(bf16[5120,128]{1,0:T(8,128)(2,1)} %collective-permute-done.14.refs_12_), channel_id=1, source_target_pairs={{0,1},{1,0},{2,3},{3,2},{4,5},{5,4},{6,7},{7,6},{8,9},{9,8},{10,11... | collective-permute-start | bytes 3932168 | tf_op jit(solution)/shard_map/ppermute | solution.py:300
  146.2 6.9 %collective-permute-start.24 = (bf16[64,8,1024]{2,1,0:T(8,128)(2,1)S(1)}, bf16[64,8,1024]{2,1,0:T(8,128)(2,1)S(1)}, u32[]{:S(2)}, u32[]{:S(2)}) collective-permute-start(bf16[64,8,1024]{2,1,0:T(8,128)(2,1)S(1)} %constant_dynamic-update-slice_fusion.11.gathered), channel_id=1, source_target_pairs={{0,1},{1,0},{2,3},{3,2},{4,5},{5,4},{6,7},{7,6},{8,9},{9,8},{10,11... | collective-permute-start | bytes 3145736 | tf_op jit(solution)/shard_map/ppermute | solution.py:300
  153.1 1.4 copy-start.16
  153.1 1.0 copy-start.17
  154.5 1.2 copy-start.15

commit v5 on v4

--- a/solution.py
+++ b/solution.py
@@ -180,7 +180,7 @@
 
 
 def final_kernel(place, scale_in, gathered, gathered_twin, *refs):
-    pieces, (out, rows_buf, table, matrix, sems) = refs[:16], refs[16:]
+    pieces, (out, rows_buf, table, matrix, sems) = refs[:18], refs[18:]
     x, y, i, c = place[0], place[1], place[2], place[3]
     low = DEEP * 128
     total = rows_buf.shape[1]
@@ -194,10 +194,10 @@
         copied.start()
         copies[group].append(copied)
 
-    n2, s2, o2, os2 = pieces[12:16]
+    o2, os2 = pieces[16:18]
     groups = ((low, low + inner, inner, 0), (0, low + 2 * inner, low, inner))
     for group, (first, second, half, at) in enumerate(groups):
-        m2, t2, skip = ((n2, s2, 0), (o2, os2, inner + low))[group]
+        m2, t2 = pieces[12 + 2 * group : 14 + 2 * group]
         own, twin, n1, s1, o1, os1 = pieces[6 * group : 6 * group + 6]
         q = half // 2
         step = c * (second - first)
@@ -211,8 +211,8 @@
             copy(group, s1.at[1 - e], down, half, 6 + e - 4 * c)
             copy(group, o1.at[e], up + mine, q, 4 + e)
             copy(group, os1.at[1 - e], down + mine, q, 4 + e)
-            copy(group, m2.at[pl.ds(skip + e * half, half)], down, half, 2 + e + 4 * c)
-            copy(group, t2.at[pl.ds(skip + (1 - e) * half, half)], up, half, 6 + e - 4 * c)
+            copy(group, m2.at[pl.ds(e * half, half)], down, half, 2 + e + 4 * c)
+            copy(group, t2.at[pl.ds((1 - e) * half, half)], up, half, 6 + e - 4 * c)
             copy(group, o2.at[pl.ds(at + e * q, q)], up + other, q, 4 + e)
             copy(group, os2.at[pl.ds(at + (1 - e) * q, q)], down + other, q, 4 + e)
 
@@ -425,8 +425,12 @@
             name="gram",
         )(place, *([base] if base is not None else []), *args)
 
-    own, twin, _, n1 = send_near(inner_own, (near, vlow, vhigh), (far,))
-    inner_near = [own, twin, n1, swap(n1), by_side(join(pieces_of(n1, forward_part)))]
+    own, twin, sent, n1 = send_near(inner_own, (near, vlow, vhigh), (far,))
+    late, _ = lax.optimization_barrier((rest_of(own, twin), sent))
+    n2 = by_side(late)
+    n1_late, n2 = lax.optimization_barrier((n1, n2))
+    s2 = swap(n2)
+    inner_near = [own, twin, n1, swap(n1), by_side(join(pieces_of(n1_late, forward_part)))]
     core_arg = core_at.astype(jnp.int32)[None]
     edge = pl.pallas_call(
         functools.partial(edge_kernel, blocks),
@@ -449,7 +453,7 @@
     o1, _ = lax.optimization_barrier((inner_near[4], sent))
     os1 = swap(o1)
     n1_late, os1_early = lax.optimization_barrier((n1, os1))
-    os1, _ = lax.optimization_barrier((os1_early, s1))
+    os1, _, s2 = lax.optimization_barrier((os1_early, s1, s2))
     inner_got = inner_near[:4] + [o1, os1]
     inner_gram = gram(inner_got, None)
     o1 = by_side(join(pieces_of(n1_late, forward_part)))
@@ -457,16 +461,15 @@
     edge_got = [own, twin, n1, s1, o1, swap(o1_late)]
     whole_gram = gram(edge_got, inner_gram)
 
-    late, _ = lax.optimization_barrier(
-        (rest_of(*inner_got[:2]), o1_late)
-    )
-    n2 = by_side(late)
+    late, _ = lax.optimization_barrier((rest_of(*edge_got[:2]), o1_late))
+    edge_n2 = by_side(late)
+    edge_s2 = swap(edge_n2)
 
     pieces = lax.all_to_all(
         whole_gram.reshape(rows16, 128 // rows16, 1024), "row", split_axis=0, concat_axis=0
     )
     mine = jnp.sum(pieces.astype(F32), axis=0).astype(BF)[None]
-    mine, n2 = lax.optimization_barrier((mine, n2))
+    mine, edge_n2 = lax.optimization_barrier((mine, edge_n2))
 
     def around(value, axis, perm_of):
         parts = [value] + [lax.ppermute(value, axis, perm_of(d)) for d in (1, 2, 3)]
@@ -483,19 +486,19 @@
             join(
                 pieces_of(inner_got[2], 1 - forward_part)
                 + pieces_of(edge_got[2], 1 - forward_part)
-                + [rest_of(*edge_got[:2])]
             ),
             got,
         )
     )
     o2 = by_side(later)
     got = around(got, "row", lambda d: row_perm(0, d))
+    got, edge_s2 = lax.optimization_barrier((got, edge_s2))
     got = around(got, "row", lambda d: row_perm(d, 0))
     parts = []
     for values in (inner_got, edge_got):
         parts += list(values[:2]) + [two(v) for v in values[2:]]
     o2_late, _ = lax.optimization_barrier((o2, got))
-    parts += [n2, swap(n2), o2, swap(o2_late)]
+    parts += [n2, s2, edge_n2, edge_s2, o2, swap(o2_late)]
     return pl.pallas_call(
         final_kernel,
         out_shape=jax.ShapeDtypeStruct((row_count, panel), BF),

time: 171 us -> 176 us (1.029)
  starting transfers between devices: 36.9 us -> 49.5 us
  local copies, waits for them, and re-layouts: 15.3 us -> 10.5 us
  waiting for transfers between devices: 50.4 us -> 47.3 us
    ppermute x10 -> x11, starting transfers between devices: 10.3 us -> 17.9 us  [swap(): return lax.ppermute(value, 'vec', z_perm(0, 1))]
    unnamed x49 -> x42, local copies, waits for them, and re-layouts: 8 us -> 2.96 us
    ppermute x6 -> x7, starting transfers between devices: 2.78 us -> 6.24 us  [by_side(): return lax.ppermute(value, 'vec', sides)]
    ppermute x10 -> x11, waiting for transfers between devices: 7.76 us -> 4.62 us  [swap(): return lax.ppermute(value, 'vec', z_perm(0, 1))]
    ppermute x6 -> x7, waiting for transfers between devices: 23.1 us -> 23.4 us  [by_side(): return lax.ppermute(value, 'vec', sides)]
  transfers between devices with their start and end apart: 29 -> 31, of which waited for: 14 -> 16; matrix products, arithmetic and copies ran while one was open for 8% -> 7% of each run, Pallas kernels for 27% -> 26%
where the time goes in v5:
time: 176 us; the launch traced here: 175 us
  Pallas kernels  60.5 us (34%)
  starting transfers between devices  49.5 us (28%)
  waiting for transfers between devices  47.3 us (27%)
  local copies, waits for them, and re-layouts  10.5 us (6%)
  other arithmetic  5.53 us (3%)
  between operations  1.94 us (1%)
    ppermute x7, waiting for transfers between devices, by_side(): return lax.ppermute(value, 'vec', sides)  23.4 us
    ppermute x11, starting transfers between devices, swap(): return lax.ppermute(value, 'vec', z_perm(0, 1))  17.9 us
    pallas_call x1, Pallas kernels, local(): pl.pallas_call(functools.partial(edge_kernel, blocks), out_shape=jax.Shap...  17.3 us
    pallas_call x1, Pallas kernels, local(): pl.pallas_call(functools.partial(inner_kernel, blocks), out_shape=jax.Sha...  16.9 us
    pallas_call x1, Pallas kernels, local(): pl.pallas_call(final_kernel, out_shape=jax.ShapeDtypeStruct((row_count, p...  14.7 us
    ppermute x9, waiting for transfers between devices, around(): parts = [value] + [lax.ppermute(value, axis, perm_of(d)) for d in (1, 2, 3)]  12 us
    pallas_call x2, Pallas kernels, gram(): pl.pallas_call(functools.partial(gram_kernel, half, base is not None), ou...  11.6 us
    ppermute x9, starting transfers between devices, around(): parts = [value] + [lax.ppermute(value, axis, perm_of(d)) for d in (1, 2, 3)]  10.1 us
  transfers between devices with their start and end apart: 31, of which 16 were waited for; matrix products, arithmetic and copies ran while one was open for 7% of the time, Pallas kernels for 26%

profile of v5, /device:TPU:1, one launch (start us, length us, event | category | flops | bytes accessed | tf_op | source)
XLA Modules:
  0.0 175.2 jit_solution(11210955305810156778)
XLA Ops:
  0.0 1.4 constant_dynamic-slice_fusion.16
  1.4 5.8 %collective-permute-start = (bf16[40,128,128]{2,1,0:T(8,128)(2,1)S(1)}, bf16[40,128,128]{2,1,0:T(8,128)(2,1)}, u32[]{:S(2)}, u32[]{:S(2)}) collective-permute-start(bf16[40,128,128]{2,1,0:T(8,128)(2,1)S(1)} %constant_dynamic-slice_fusion.16), channel_id=1, source_target_pairs={{0,8},{1,121},{2,10},{3,123},{4,12},{5,125},{6,14},{7,127},{8,16},... | collective-permute-start | bytes 3932168 | tf_op jit(solution)/shard_map/ppermute | solution.py:326
  8.1 0.6 fusion.4
  8.7 1.2 fusion.3
  10.1 4.8 %collective-permute-start.2 = (bf16[13,128,128]{2,1,0:T(8,128)(2,1)S(1)}, bf16[13,128,128]{2,1,0:T(8,128)(2,1)S(1)}, u32[]{:S(2)}, u32[]{:S(2)}) collective-permute-start(bf16[13,128,128]{2,1,0:T(8,128)(2,1)S(1)} %pad_maximum_fusion.7), channel_id=1, source_target_pairs={{0,120},{8,0},{16,8},{24,16},{32,24},{40,32},{48,40},{56,48},{64,5... | collective-permute-start | bytes 1277960 | tf_op jit(solution)/shard_map/ppermute | solution.py:336
  14.9 16.9 %inner_filter.1 = bf16[40,128,128]{2,1,0:T(8,128)(2,1)} custom-call(s32[64,8]{1,0:T(8,128)} %get-tuple-element.66.facts, bf16[64,4,128,128]{3,2,1,0:T(8,128)(2,1)} %tiles.1, bf16[64,128,128]{2,1,0:T(8,128)(2,1)} %bitcast.35), custom_call_target="tpu_custom_call" | custom-call | flops 1000000 | bytes 1048576 | tf_op jit(solution)/shard_map/inner_filter/pallas_call | solution.py:345
  31.9 1.2 collective-permute-start.3
  33.1 1.4 constant_dynamic-slice_fusion.13
  34.4 0.3 collective-permute-start.4
  35.0 0.9 collective-permute-done.3.refs_1_
  36.0 1.0 copy-done
  37.0 1.1 pad_maximum_fusion
  38.2 1.7 collective-permute-start.5
  39.9 1.2 pad_maximum_fusion.1
  41.1 1.6 collective-permute-start.7
  42.8 0.1 copy.23
  42.9 0.7 multiply_add_fusion.facts
  43.6 17.3 %edge_filter.1 = bf16[24,128,128]{2,1,0:T(8,128)(2,1)} custom-call(s32[64,8]{1,0:T(8,128)} %multiply_add_fusion.facts, s32[1]{0:T(128)} %bitcast.3.core, bf16[256,128,128]{2,1,0:T(8,128)(2,1)} %bitcast.32, bf16[64,128,128]{2,1,0:T(8,128)(2,1)} %bitcast.36, bf16[40,128,128]{2,1,0:T(8,128)(2,1)} %collective-permute-done.near, ...), custom_call_target="tpu_custom_call" | custom-call | flops 8000000000 | bytes 11534336 | tf_op jit(solution)/shard_map/edge_filter/pallas_call | solution.py:435
  60.9 1.6 collective-permute-start.9
  62.5 1.2 constant_dynamic-slice_fusion.5
  63.7 7.7 %collective-permute-done.7.refs_12_ = bf16[5120,128]{1,0:T(8,128)(2,1)} collective-permute-done((bf16[5120,128]{1,0:T(8,128)(2,1)}, bf16[5120,128]{1,0:T(8,128)(2,1)}, u32[]{:S(2)}, u32[]{:S(2)}) %collective-permute-start.7) | collective-permute-done | bytes 1310752 | tf_op jit(solution)/shard_map/ppermute | solution.py:391
  71.6 1.0 constant_dynamic-slice_fusion.4
  72.7 0.1 copy-done.4
  72.8 1.1 collective-permute-start.10
  73.8 8.4 %collective-permute-done.8 = bf16[2560,128]{1,0:T(8,128)(2,1)} collective-permute-done((bf16[2560,128]{1,0:T(8,128)(2,1)S(1)}, bf16[2560,128]{1,0:T(8,128)(2,1)}, u32[]{:S(2)}, u32[]{:S(2)}) %collective-permute-start.8) | collective-permute-done | bytes 655392 | tf_op jit(solution)/shard_map/ppermute | solution.py:391
  82.3 1.8 %collective-permute-start.11 = (bf16[2560,128]{1,0:T(8,128)(2,1)}, bf16[2560,128]{1,0:T(8,128)(2,1)}, u32[]{:S(2)}, u32[]{:S(2)}) collective-permute-start(bf16[2560,128]{1,0:T(8,128)(2,1)} %collective-permute-done.8), channel_id=1, source_target_pairs={{0,1},{1,0},{2,3},{3,2},{4,5},{5,4},{6,7},{7,6},{8,9},{9,8},{10,11... | collective-permute-start | bytes 1966088 | tf_op jit(solution)/shard_map/ppermute | solution.py:300
  84.1 0.5 collective-permute-start.6
  84.6 6.0 %collective-permute-done.10 = bf16[3072,128]{1,0:T(8,128)(2,1)S(1)} collective-permute-done((bf16[3072,128]{1,0:T(8,128)(2,1)S(1)}, bf16[3072,128]{1,0:T(8,128)(2,1)S(1)}, u32[]{:S(2)}, u32[]{:S(2)}) %collective-permute-start.10) | collective-permute-done | bytes 786464 | tf_op jit(solution)/shard_map/ppermute | solution.py:391
  90.6 1.9 %collective-permute-start.12 = (bf16[3072,128]{1,0:T(8,128)(2,1)S(1)}, bf16[3072,128]{1,0:T(8,128)(2,1)S(1)}, u32[]{:S(2)}, u32[]{:S(2)}) collective-permute-start(bf16[3072,128]{1,0:T(8,128)(2,1)S(1)} %collective-permute-done.10), channel_id=1, source_target_pairs={{0,1},{1,0},{2,3},{3,2},{4,5},{5,4},{6,7},{7,6},{8,9},{9,8},{10,11... | collective-permute-start | bytes 2359304 | tf_op jit(solution)/shard_map/ppermute | solution.py:300
  92.6 0.8 pad_maximum_fusion.8
  93.4 0.6 pad_add_fusion.2.place
  94.0 0.5 collective-permute-done.12
  94.5 6.4 %gram.2.refs_0_ = f32[128,1024]{1,0:T(8,128)} custom-call(s32[4]{0:T(128)} %pad_add_fusion.2.place, bf16[5120,128]{1,0:T(8,128)(2,1)} %bitcast.29, bf16[5120,128]{1,0:T(8,128)(2,1)} %copy-done, bf16[2,2560,128]{2,1,0:T(8,128)(2,1)} %bitcast.33, bf16[2,2560,128]{2,1,0:T(8,128)(2,1)} %bitcast.13.refs_3_, bf16[2,1280,128]{2,1,0:T(8,128)(2,1)} %bitcast.17.refs_4_, ...), custom_call_target="tpu_custom_call" | custom-call | flops 671088640 | bytes 7864320 | tf_op jit(solution)/shard_map/gram/pallas_call | solution.py:410
  100.9 1.3 collective-permute-done.14
  102.2 2.1 %collective-permute-start.15 = (bf16[1536,128]{1,0:T(8,128)(2,1)}, bf16[1536,128]{1,0:T(8,128)(2,1)S(1)}, u32[]{:S(2)}, u32[]{:S(2)}) collective-permute-start(bf16[1536,128]{1,0:T(8,128)(2,1)} %collective-permute-done.14), channel_id=1, source_target_pairs={{0,1},{1,0},{2,3},{3,2},{4,5},{5,4},{6,7},{7,6},{8,9},{9,8},{10,11... | collective-permute-start | bytes 1179656 | tf_op jit(solution)/shard_map/ppermute | solution.py:300
  104.4 0.3 collective-permute-start.16
  104.8 0.7 constant_dynamic-slice_fusion.1
  105.5 0.4 collective-permute-done.15
  105.9 0.8 copy-done.8
  106.7 5.2 %gram.3 = bf16[128,1024]{1,0:T(8,128)(2,1)} custom-call(s32[4]{0:T(128)} %pad_add_fusion.2.place, f32[128,1024]{1,0:T(8,128)} %gram.2.refs_0_, bf16[3072,128]{1,0:T(8,128)(2,1)} %bitcast.41, bf16[3072,128]{1,0:T(8,128)(2,1)} %copy-done.4, bf16[2,1536,128]{2,1,0:T(8,128)(2,1)} %bitcast.37, bf16[2,1536,128]{2,1,0:T(8,128)(2,1)} %bitcast.46, ...), custom_call_target="tpu_custom_call" | custom-call | flops 402653184 | bytes 4718592 | tf_op jit(solution)/shard_map/gram/pallas_call | solution.py:410
  111.8 4.5 %all-to-all-start = ((bf16[16,8,1024]{2,1,0:T(8,128)(2,1)}), bf16[16,8,1024]{2,1,0:T(8,128)(2,1)S(1)}, u32[]{:S(2)}, u32[]{:S(2)}) async-start(bf16[16,8,1024]{2,1,0:T(8,128)(2,1)} %bitcast.45), calls=%async_computation | async-start | bytes 524288 | tf_op jit(solution)/shard_map/all_to_all | solution.py:468
  116.5 7.3 %all-to-all-done = bf16[16,8,1024]{2,1,0:T(8,128)(2,1)S(1)} async-done(((bf16[16,8,1024]{2,1,0:T(8,128)(2,1)}), bf16[16,8,1024]{2,1,0:T(8,128)(2,1)S(1)}, u32[]{:S(2)}, u32[]{:S(2)}) %all-to-all-start) | async-done | bytes 262176 | tf_op jit(solution)/shard_map/all_to_all | solution.py:468
  123.9 3.9 %collective-permute-start.18 = (bf16[1,8,1024]{2,1,0:T(8,128)(2,1)S(1)}, bf16[1,8,1024]{2,1,0:T(8,128)(2,1)S(1)}, u32[]{:S(2)}, u32[]{:S(2)}) collective-permute-start(bf16[1,8,1024]{2,1,0:T(8,128)(2,1)S(1)} %bitcast.51), channel_id=1, source_target_pairs={{0,4},{1,5},{2,6},{3,7},{4,0},{5,1},{6,2},{7,3},{8,12},{9,13},{10,... | collective-permute-start | bytes 49160 | tf_op jit(solution)/shard_map/ppermute | solution.py:475
  127.8 1.6 collective-permute-start.17
  129.4 0.8 collective-permute-start.23
  130.2 0.1 collective-permute-done.17
  130.4 1.4 collective-permute-start.28
  131.8 0.7 collective-permute-start.20
  132.5 0.8 collective-permute-start.22
  133.3 1.2 collective-permute-start.21
  134.5 0.5 collective-permute-done.20
  134.9 3.0 %collective-permute-done.21 = bf16[4,8,1024]{2,1,0:T(8,128)(2,1)S(1)} collective-permute-done((bf16[4,8,1024]{2,1,0:T(8,128)(2,1)S(1)}, bf16[4,8,1024]{2,1,0:T(8,128)(2,1)S(1)}, u32[]{:S(2)}, u32[]{:S(2)}) %collective-permute-start.21) | collective-permute-done | bytes 65568 | tf_op jit(solution)/shard_map/ppermute | solution.py:475
  138.0 0.8 collective-permute-start.24
  138.8 1.0 collective-permute-start.25
  139.8 0.1 collective-permute-start.26
  139.9 3.7 %collective-permute-done.24 = bf16[16,8,1024]{2,1,0:T(8,128)(2,1)S(1)} collective-permute-done((bf16[16,8,1024]{2,1,0:T(8,128)(2,1)S(1)}, bf16[16,8,1024]{2,1,0:T(8,128)(2,1)S(1)}, u32[]{:S(2)}, u32[]{:S(2)}) %collective-permute-start.24) | collective-permute-done | bytes 262176 | tf_op jit(solution)/shard_map/ppermute | solution.py:475
  143.6 2.0 %collective-permute-done.25 = bf16[16,8,1024]{2,1,0:T(8,128)(2,1)S(1)} collective-permute-done((bf16[16,8,1024]{2,1,0:T(8,128)(2,1)S(1)}, bf16[16,8,1024]{2,1,0:T(8,128)(2,1)S(1)}, u32[]{:S(2)}, u32[]{:S(2)}) %collective-permute-start.25) | collective-permute-done | bytes 262176 | tf_op jit(solution)/shard_map/ppermute | solution.py:475
  145.6 2.7 %collective-permute-done.26 = bf16[16,8,1024]{2,1,0:T(8,128)(2,1)S(1)} collective-permute-done((bf16[16,8,1024]{2,1,0:T(8,128)(2,1)S(1)}, bf16[16,8,1024]{2,1,0:T(8,128)(2,1)S(1)}, u32[]{:S(2)}, u32[]{:S(2)}) %collective-permute-start.26) | collective-permute-done | bytes 262176 | tf_op jit(solution)/shard_map/ppermute | solution.py:475
  148.3 7.2 %collective-permute-start.27 = (bf16[64,8,1024]{2,1,0:T(8,128)(2,1)S(1)}, bf16[64,8,1024]{2,1,0:T(8,128)(2,1)S(1)}, u32[]{:S(2)}, u32[]{:S(2)}) collective-permute-start(bf16[64,8,1024]{2,1,0:T(8,128)(2,1)S(1)} %constant_dynamic-update-slice_fusion.11.gathered), channel_id=1, source_target_pairs={{0,1},{1,0},{2,3},{3,2},{4,5},{5,4},{6,7},{7,6},{8,9},{9,8},{10,11... | collective-permute-start | bytes 3145736 | tf_op jit(solution)/shard_map/ppermute | solution.py:300
  155.5 0.4 collective-permute-start.29
  156.5 1.3 collective-permute-done.27.gathered_twin
  157.8 1.5 collective-permute-done.29.refs_17_
  159.3 1.0 copy-done.15
  160.3 14.7 %final.1 = bf16[8192,128]{1,0:T(8,128)(2,1)} custom-call(s32[4]{0:T(128)} %pad_add_fusion.2.place, f32[1]{0:T(128)S(6)} %copy.37.scale_in, bf16[64,8,1024]{2,1,0:T(8,128)(2,1)} %copy-done.9, bf16[64,8,1024]{2,1,0:T(8,128)(2,1)} %copy-done.14, bf16[5120,128]{1,0:T(8,128)(2,1)} %bitcast.30, bf16[5120,128]{1,0:T(8,128)(2,1)} %copy-done, ...), custom_call_target="tpu_custom_call" | custom-call | flops 6000000000 | bytes 20971520 | tf_op jit(solution)/shard_map/final/pallas_call | solution.py:502
  (88 shorter events, 1.4 us)
Async XLA Ops:
  0.0 7.9 %copy-start.10 = (s32[64,4]{0,1:T(4,128)S(1)}, s32[64,4]{0,1:T(4,128)}, u32[]{:S(2)}) copy-start(s32[64,4]{0,1:T(4,128)} %param.6) | copy-start | bytes 3076
  1.4 30.5 %collective-permute-start = (bf16[40,128,128]{2,1,0:T(8,128)(2,1)S(1)}, bf16[40,128,128]{2,1,0:T(8,128)(2,1)}, u32[]{:S(2)}, u32[]{:S(2)}) collective-permute-start(bf16[40,128,128]{2,1,0:T(8,128)(2,1)S(1)} %constant_dynamic-slice_fusion.16), channel_id=1, source_target_pairs={{0,8},{1,121},{2,10},{3,123},{4,12},{5,125},{6,14},{7,127},{8,16},... | collective-permute-start | bytes 3932168 | tf_op jit(solution)/shard_map/ppermute | solution.py:326
  9.9 21.9 %collective-permute-start.1 = (bf16[13,128,128]{2,1,0:T(8,128)(2,1)S(1)}, bf16[13,128,128]{2,1,0:T(8,128)(2,1)S(1)}, u32[]{:S(2)}, u32[]{:S(2)}) collective-permute-start(bf16[13,128,128]{2,1,0:T(8,128)(2,1)S(1)} %pad_maximum_fusion.6), channel_id=1, source_target_pairs={{0,8},{8,16},{16,24},{24,32},{32,40},{40,48},{48,56},{56,64},{64,7... | collective-permute-start | bytes 1277960 | tf_op jit(solution)/shard_map/ppermute | solution.py:333
  10.1 21.8 %collective-permute-start.2 = (bf16[13,128,128]{2,1,0:T(8,128)(2,1)S(1)}, bf16[13,128,128]{2,1,0:T(8,128)(2,1)S(1)}, u32[]{:S(2)}, u32[]{:S(2)}) collective-permute-start(bf16[13,128,128]{2,1,0:T(8,128)(2,1)S(1)} %pad_maximum_fusion.7), channel_id=1, source_target_pairs={{0,120},{8,0},{16,8},{24,16},{32,24},{40,32},{48,40},{56,48},{64,5... | collective-permute-start | bytes 1277960 | tf_op jit(solution)/shard_map/ppermute | solution.py:336
  31.8 3.0 %copy-start.11 = (bf16[13,128,128]{2,1,0:T(8,128)(2,1)}, bf16[13,128,128]{2,1,0:T(8,128)(2,1)S(1)}, u32[]{:S(2)}) copy-start(bf16[13,128,128]{2,1,0:T(8,128)(2,1)S(1)} %collective-permute-done.1.vlow) | copy-start | bytes 1277956
  31.9 3.0 %copy-start.12 = (bf16[13,128,128]{2,1,0:T(8,128)(2,1)}, bf16[13,128,128]{2,1,0:T(8,128)(2,1)S(1)}, u32[]{:S(2)}) copy-start(bf16[13,128,128]{2,1,0:T(8,128)(2,1)S(1)} %collective-permute-done.2.vhigh) | copy-start | bytes 1277956
  31.9 4.0 %collective-permute-start.3 = (bf16[5120,128]{1,0:T(8,128)(2,1)}, bf16[5120,128]{1,0:T(8,128)(2,1)S(1)}, u32[]{:S(2)}, u32[]{:S(2)}) collective-permute-start(bf16[5120,128]{1,0:T(8,128)(2,1)} %bitcast.27), channel_id=1, source_target_pairs={{0,1},{1,0},{2,3},{3,2},{4,5},{5,4},{6,7},{7,6},{8,9},{9,8},{10,11... | collective-permute-start | bytes 3932168 | tf_op jit(solution)/shard_map/ppermute | solution.py:300
  34.4 3.7 %collective-permute-start.4 = (bf16[40,128,128]{2,1,0:T(8,128)(2,1)}, bf16[40,128,128]{2,1,0:T(8,128)(2,1)}, u32[]{:S(2)}, u32[]{:S(2)}) collective-permute-start(bf16[40,128,128]{2,1,0:T(8,128)(2,1)} %collective-permute-done.near), channel_id=1, source_target_pairs={{0,1},{1,0},{2,3},{3,2},{4,5},{5,4},{6,7},{7,6},{8,9},{9,8},{10,11... | collective-permute-start | bytes 3932168 | tf_op jit(solution)/shard_map/ppermute | solution.py:300
  35.9 1.1 copy-start
  38.2 33.2 %collective-permute-start.5 = (bf16[5120,128]{1,0:T(8,128)(2,1)}, bf16[5120,128]{1,0:T(8,128)(2,1)S(1)}, u32[]{:S(2)}, u32[]{:S(2)}) collective-permute-start(bf16[5120,128]{1,0:T(8,128)(2,1)} %pad_maximum_fusion), channel_id=1, source_target_pairs={{0,6},{1,3},{2,0},{3,5},{4,2},{5,7},{6,4},{7,1},{8,14},{9,11},{10,... | collective-permute-start | bytes 3932168 | tf_op jit(solution)/shard_map/ppermute | solution.py:391
  41.1 30.2 %collective-permute-start.7 = (bf16[5120,128]{1,0:T(8,128)(2,1)}, bf16[5120,128]{1,0:T(8,128)(2,1)}, u32[]{:S(2)}, u32[]{:S(2)}) collective-permute-start(bf16[5120,128]{1,0:T(8,128)(2,1)} %pad_maximum_fusion.1), channel_id=1, source_target_pairs={{0,6},{1,3},{2,0},{3,5},{4,2},{5,7},{6,4},{7,1},{8,14},{9,11},{10,... | collective-permute-start | bytes 3932168 | tf_op jit(solution)/shard_map/ppermute | solution.py:391
  60.9 10.7 %collective-permute-start.9 = (bf16[3072,128]{1,0:T(8,128)(2,1)}, bf16[3072,128]{1,0:T(8,128)(2,1)S(1)}, u32[]{:S(2)}, u32[]{:S(2)}) collective-permute-start(bf16[3072,128]{1,0:T(8,128)(2,1)} %bitcast.39), channel_id=1, source_target_pairs={{0,1},{1,0},{2,3},{3,2},{4,5},{5,4},{6,7},{7,6},{8,9},{9,8},{10,11... | collective-permute-start | bytes 2359304 | tf_op jit(solution)/shard_map/ppermute | solution.py:300
  71.4 12.8 %copy-start.1 = (bf16[5120,128]{1,0:T(8,128)(2,1)}, bf16[5120,128]{1,0:T(8,128)(2,1)S(1)}, u32[]{:S(2)}) copy-start(bf16[5120,128]{1,0:T(8,128)(2,1)S(1)} %collective-permute-done.5) | copy-start | bytes 3932164
  71.5 10.8 %collective-permute-start.8 = (bf16[2560,128]{1,0:T(8,128)(2,1)S(1)}, bf16[2560,128]{1,0:T(8,128)(2,1)}, u32[]{:S(2)}, u32[]{:S(2)}) collective-permute-start(bf16[2560,128]{1,0:T(8,128)(2,1)S(1)} %pad_maximum_fusion.5), channel_id=1, source_target_pairs={{0,6},{1,3},{2,0},{3,5},{4,2},{5,7},{6,4},{7,1},{8,14},{9,11},{10,... | collective-permute-start | bytes 1966088 | tf_op jit(solution)/shard_map/ppermute | solution.py:391
  71.6 1.2 copy-start.4
  72.8 17.8 %collective-permute-start.10 = (bf16[3072,128]{1,0:T(8,128)(2,1)S(1)}, bf16[3072,128]{1,0:T(8,128)(2,1)S(1)}, u32[]{:S(2)}, u32[]{:S(2)}) collective-permute-start(bf16[3072,128]{1,0:T(8,128)(2,1)S(1)} %pad_maximum_fusion.3), channel_id=1, source_target_pairs={{0,6},{1,3},{2,0},{3,5},{4,2},{5,7},{6,4},{7,1},{8,14},{9,11},{10,... | collective-permute-start | bytes 2359304 | tf_op jit(solution)/shard_map/ppermute | solution.py:391
  82.3 10.3 %collective-permute-start.11 = (bf16[2560,128]{1,0:T(8,128)(2,1)}, bf16[2560,128]{1,0:T(8,128)(2,1)}, u32[]{:S(2)}, u32[]{:S(2)}) collective-permute-start(bf16[2560,128]{1,0:T(8,128)(2,1)} %collective-permute-done.8), channel_id=1, source_target_pairs={{0,1},{1,0},{2,3},{3,2},{4,5},{5,4},{6,7},{7,6},{8,9},{9,8},{10,11... | collective-permute-start | bytes 1966088 | tf_op jit(solution)/shard_map/ppermute | solution.py:300
  84.1 10.3 %collective-permute-start.13 = (bf16[5120,128]{1,0:T(8,128)(2,1)}, bf16[5120,128]{1,0:T(8,128)(2,1)}, u32[]{:S(2)}, u32[]{:S(2)}) collective-permute-start(bf16[5120,128]{1,0:T(8,128)(2,1)} %collective-permute-done.7.refs_12_), channel_id=1, source_target_pairs={{0,1},{1,0},{2,3},{3,2},{4,5},{5,4},{6,7},{7,6},{8,9},{9,8},{10,11... | collective-permute-start | bytes 3932168 | tf_op jit(solution)/shard_map/ppermute | solution.py:300
  84.1 10.3 %collective-permute-start.6 = (bf16[5120,128]{1,0:T(8,128)(2,1)S(1)}, bf16[5120,128]{1,0:T(8,128)(2,1)}, u32[]{:S(2)}, u32[]{:S(2)}) collective-permute-start(bf16[5120,128]{1,0:T(8,128)(2,1)S(1)} %collective-permute-done.5), channel_id=1, source_target_pairs={{0,1},{1,0},{2,3},{3,2},{4,5},{5,4},{6,7},{7,6},{8,9},{9,8},{10,11... | collective-permute-start | bytes 3932168 | tf_op jit(solution)/shard_map/ppermute | solution.py:300
  90.6 14.2 %copy-start.3 = (bf16[3072,128]{1,0:T(8,128)(2,1)}, bf16[3072,128]{1,0:T(8,128)(2,1)S(1)}, u32[]{:S(2)}) copy-start(bf16[3072,128]{1,0:T(8,128)(2,1)S(1)} %collective-permute-done.10) | copy-start | bytes 2359300
  90.6 3.8 %collective-permute-start.12 = (bf16[3072,128]{1,0:T(8,128)(2,1)S(1)}, bf16[3072,128]{1,0:T(8,128)(2,1)S(1)}, u32[]{:S(2)}, u32[]{:S(2)}) collective-permute-start(bf16[3072,128]{1,0:T(8,128)(2,1)S(1)} %collective-permute-done.10), channel_id=1, source_target_pairs={{0,1},{1,0},{2,3},{3,2},{4,5},{5,4},{6,7},{7,6},{8,9},{9,8},{10,11... | collective-permute-start | bytes 2359304 | tf_op jit(solution)/shard_map/ppermute | solution.py:300
  93.4 8.9 %collective-permute-start.14 = (bf16[1536,128]{1,0:T(8,128)(2,1)}, bf16[1536,128]{1,0:T(8,128)(2,1)}, u32[]{:S(2)}, u32[]{:S(2)}) collective-permute-start(bf16[1536,128]{1,0:T(8,128)(2,1)} %pad_maximum_fusion.8), channel_id=1, source_target_pairs={{0,6},{1,3},{2,0},{3,5},{4,2},{5,7},{6,4},{7,1},{8,14},{9,11},{10,... | collective-permute-start | bytes 1179656 | tf_op jit(solution)/shard_map/ppermute | solution.py:391
  94.4 6.4 %copy-start.6 = (bf16[3072,128]{1,0:T(8,128)(2,1)}, bf16[3072,128]{1,0:T(8,128)(2,1)S(1)}, u32[]{:S(2)}) copy-start(bf16[3072,128]{1,0:T(8,128)(2,1)S(1)} %collective-permute-done.12) | copy-start | bytes 2359300
  94.5 9.9 %copy-start.5 = (bf16[1536,128]{1,0:T(8,128)(2,1)S(1)}, bf16[1536,128]{1,0:T(8,128)(2,1)}, u32[]{:S(2)}) copy-start(bf16[1536,128]{1,0:T(8,128)(2,1)} %get-tuple-element.61) | copy-start | bytes 1179652
  100.9 3.8 %copy-start.2 = (bf16[5120,128]{1,0:T(8,128)(2,1)S(1)}, bf16[5120,128]{1,0:T(8,128)(2,1)}, u32[]{:S(2)}) copy-start(bf16[5120,128]{1,0:T(8,128)(2,1)} %copy-done.1) | copy-start | bytes 3932164
  102.2 3.7 %collective-permute-start.15 = (bf16[1536,128]{1,0:T(8,128)(2,1)}, bf16[1536,128]{1,0:T(8,128)(2,1)S(1)}, u32[]{:S(2)}, u32[]{:S(2)}) collective-permute-start(bf16[1536,128]{1,0:T(8,128)(2,1)} %collective-permute-done.14), channel_id=1, source_target_pairs={{0,1},{1,0},{2,3},{3,2},{4,5},{5,4},{6,7},{7,6},{8,9},{9,8},{10,11... | collective-permute-start | bytes 1179656 | tf_op jit(solution)/shard_map/ppermute | solution.py:300
  104.4 19.4 %collective-permute-start.16 = (bf16[3072,128]{1,0:T(8,128)(2,1)S(1)}, bf16[3072,128]{1,0:T(8,128)(2,1)}, u32[]{:S(2)}, u32[]{:S(2)}) collective-permute-start(bf16[3072,128]{1,0:T(8,128)(2,1)S(1)} %pad_maximum_fusion.4), channel_id=1, source_target_pairs={{0,6},{1,3},{2,0},{3,5},{4,2},{5,7},{6,4},{7,1},{8,14},{9,11},{10,... | collective-permute-start | bytes 2359304 | tf_op jit(solution)/shard_map/ppermute | solution.py:391
  105.9 0.8 copy-start.8
  106.7 9.7 %copy-start.7 = (bf16[768,128]{1,0:T(8,128)(2,1)S(1)}, bf16[768,128]{1,0:T(8,128)(2,1)}, u32[]{:S(2)}) copy-start(bf16[768,128]{1,0:T(8,128)(2,1)} %get-tuple-element.58) | copy-start | bytes 589828
  111.8 11.9 %all-to-all-start = ((bf16[16,8,1024]{2,1,0:T(8,128)(2,1)}), bf16[16,8,1024]{2,1,0:T(8,128)(2,1)S(1)}, u32[]{:S(2)}, u32[]{:S(2)}) async-start(bf16[16,8,1024]{2,1,0:T(8,128)(2,1)} %bitcast.45), calls=%async_computation | async-start | bytes 524288 | tf_op jit(solution)/shard_map/all_to_all | solution.py:468
  123.8 6.6 %collective-permute-start.19 = (bf16[1,8,1024]{2,1,0:T(8,128)(2,1)S(1)}, bf16[1,8,1024]{2,1,0:T(8,128)(2,1)S(1)}, u32[]{:S(2)}, u32[]{:S(2)}) collective-permute-start(bf16[1,8,1024]{2,1,0:T(8,128)(2,1)S(1)} %bitcast.50), channel_id=1, source_target_pairs={{0,2},{1,3},{2,4},{3,5},{4,6},{5,7},{6,0},{7,1},{8,10},{9,11},{10,... | collective-permute-start | bytes 49160 | tf_op jit(solution)/shard_map/ppermute | solution.py:475
  123.9 6.5 %collective-permute-start.18 = (bf16[1,8,1024]{2,1,0:T(8,128)(2,1)S(1)}, bf16[1,8,1024]{2,1,0:T(8,128)(2,1)S(1)}, u32[]{:S(2)}, u32[]{:S(2)}) collective-permute-start(bf16[1,8,1024]{2,1,0:T(8,128)(2,1)S(1)} %bitcast.51), channel_id=1, source_target_pairs={{0,4},{1,5},{2,6},{3,7},{4,0},{5,1},{6,2},{7,3},{8,12},{9,13},{10,... | collective-permute-start | bytes 49160 | tf_op jit(solution)/shard_map/ppermute | solution.py:475
  127.8 2.6 %collective-permute-start.17 = (bf16[1,8,1024]{2,1,0:T(8,128)(2,1)S(1)}, bf16[1,8,1024]{2,1,0:T(8,128)(2,1)S(1)}, u32[]{:S(2)}, u32[]{:S(2)}) collective-permute-start(bf16[1,8,1024]{2,1,0:T(8,128)(2,1)S(1)} %bitcast.52), channel_id=1, source_target_pairs={{0,6},{1,7},{2,0},{3,1},{4,2},{5,3},{6,4},{7,5},{8,14},{9,15},{10,... | collective-permute-start | bytes 49160 | tf_op jit(solution)/shard_map/ppermute | solution.py:475
  129.4 8.6 %collective-permute-start.23 = (bf16[3072,128]{1,0:T(8,128)(2,1)}, bf16[3072,128]{1,0:T(8,128)(2,1)S(1)}, u32[]{:S(2)}, u32[]{:S(2)}) collective-permute-start(bf16[3072,128]{1,0:T(8,128)(2,1)} %collective-permute-done.16.refs_14_), channel_id=1, source_target_pairs={{0,1},{1,0},{2,3},{3,2},{4,5},{5,4},{6,7},{7,6},{8,9},{9,8},{10,11... | collective-permute-start | bytes 2359304 | tf_op jit(solution)/shard_map/ppermute | solution.py:300
  130.4 25.1 %collective-permute-start.28 = (bf16[4096,128]{1,0:T(8,128)(2,1)S(1)}, bf16[4096,128]{1,0:T(8,128)(2,1)S(1)}, u32[]{:S(2)}, u32[]{:S(2)}) collective-permute-start(bf16[4096,128]{1,0:T(8,128)(2,1)S(1)} %pad_maximum_fusion.2), channel_id=1, source_target_pairs={{0,6},{1,3},{2,0},{3,5},{4,2},{5,7},{6,4},{7,1},{8,14},{9,11},{10,... | collective-permute-start | bytes 3145736 | tf_op jit(solution)/shard_map/ppermute | solution.py:391
  131.8 3.1 %collective-permute-start.20 = (bf16[4,8,1024]{2,1,0:T(8,128)(2,1)S(1)}, bf16[4,8,1024]{2,1,0:T(8,128)(2,1)S(1)}, u32[]{:S(2)}, u32[]{:S(2)}) collective-permute-start(bf16[4,8,1024]{2,1,0:T(8,128)(2,1)S(1)} %get-tuple-element.67), channel_id=1, source_target_pairs={{0,24},{8,0},{16,8},{24,16},{32,56},{40,32},{48,40},{56,48},{64,88... | collective-permute-start | bytes 196616 | tf_op jit(solution)/shard_map/ppermute | solution.py:475
  132.5 5.4 %collective-permute-start.22 = (bf16[4,8,1024]{2,1,0:T(8,128)(2,1)S(1)}, bf16[4,8,1024]{2,1,0:T(8,128)(2,1)S(1)}, u32[]{:S(2)}, u32[]{:S(2)}) collective-permute-start(bf16[4,8,1024]{2,1,0:T(8,128)(2,1)S(1)} %get-tuple-element.67), channel_id=1, source_target_pairs={{0,8},{8,16},{16,24},{24,0},{32,40},{40,48},{48,56},{56,32},{64,72... | collective-permute-start | bytes 196616 | tf_op jit(solution)/shard_map/ppermute | solution.py:475
  133.3 4.6 %collective-permute-start.21 = (bf16[4,8,1024]{2,1,0:T(8,128)(2,1)S(1)}, bf16[4,8,1024]{2,1,0:T(8,128)(2,1)S(1)}, u32[]{:S(2)}, u32[]{:S(2)}) collective-permute-start(bf16[4,8,1024]{2,1,0:T(8,128)(2,1)S(1)} %get-tuple-element.67), channel_id=1, source_target_pairs={{0,16},{8,24},{16,0},{24,8},{32,48},{40,56},{48,32},{56,40},{64,80... | collective-permute-start | bytes 196616 | tf_op jit(solution)/shard_map/ppermute | solution.py:475
  138.0 21.4 %copy-start.16 = (bf16[3072,128]{1,0:T(8,128)(2,1)}, bf16[3072,128]{1,0:T(8,128)(2,1)S(1)}, u32[]{:S(2)}) copy-start(bf16[3072,128]{1,0:T(8,128)(2,1)S(1)} %collective-permute-done.23.refs_15_) | copy-start | bytes 2359300
  138.0 5.6 %collective-permute-start.24 = (bf16[16,8,1024]{2,1,0:T(8,128)(2,1)S(1)}, bf16[16,8,1024]{2,1,0:T(8,128)(2,1)S(1)}, u32[]{:S(2)}, u32[]{:S(2)}) collective-permute-start(bf16[16,8,1024]{2,1,0:T(8,128)(2,1)S(1)} %constant_dynamic-update-slice_fusion.4), channel_id=1, source_target_pairs={{0,96},{8,104},{16,112},{24,120},{32,0},{40,8},{48,16},{56,24},{64... | collective-permute-start | bytes 786440 | tf_op jit(solution)/shard_map/ppermute | solution.py:475
  138.8 6.8 %collective-permute-start.25 = (bf16[16,8,1024]{2,1,0:T(8,128)(2,1)S(1)}, bf16[16,8,1024]{2,1,0:T(8,128)(2,1)S(1)}, u32[]{:S(2)}, u32[]{:S(2)}) collective-permute-start(bf16[16,8,1024]{2,1,0:T(8,128)(2,1)S(1)} %constant_dynamic-update-slice_fusion.4), channel_id=1, source_target_pairs={{0,64},{8,72},{16,80},{24,88},{32,96},{40,104},{48,112},{56,120},{... | collective-permute-start | bytes 786440 | tf_op jit(solution)/shard_map/ppermute | solution.py:475
  139.8 8.6 %collective-permute-start.26 = (bf16[16,8,1024]{2,1,0:T(8,128)(2,1)S(1)}, bf16[16,8,1024]{2,1,0:T(8,128)(2,1)S(1)}, u32[]{:S(2)}, u32[]{:S(2)}) collective-permute-start(bf16[16,8,1024]{2,1,0:T(8,128)(2,1)S(1)} %constant_dynamic-update-slice_fusion.4), channel_id=1, source_target_pairs={{0,32},{8,40},{16,48},{24,56},{32,64},{40,72},{48,80},{56,88},{64,... | collective-permute-start | bytes 786440 | tf_op jit(solution)/shard_map/ppermute | solution.py:475
  148.3 11.0 %copy-start.9 = (bf16[64,8,1024]{2,1,0:T(8,128)(2,1)}, bf16[64,8,1024]{2,1,0:T(8,128)(2,1)S(1)}, u32[]{:S(2)}) copy-start(bf16[64,8,1024]{2,1,0:T(8,128)(2,1)S(1)} %constant_dynamic-update-slice_fusion.11.gathered) | copy-start | bytes 3145732
  148.3 9.5 %collective-permute-start.27 = (bf16[64,8,1024]{2,1,0:T(8,128)(2,1)S(1)}, bf16[64,8,1024]{2,1,0:T(8,128)(2,1)S(1)}, u32[]{:S(2)}, u32[]{:S(2)}) collective-permute-start(bf16[64,8,1024]{2,1,0:T(8,128)(2,1)S(1)} %constant_dynamic-update-slice_fusion.11.gathered), channel_id=1, source_target_pairs={{0,1},{1,0},{2,3},{3,2},{4,5},{5,4},{6,7},{7,6},{8,9},{9,8},{10,11... | collective-permute-start | bytes 3145736 | tf_op jit(solution)/shard_map/ppermute | solution.py:300
  155.5 3.8 %copy-start.13 = (bf16[4096,128]{1,0:T(8,128)(2,1)}, bf16[4096,128]{1,0:T(8,128)(2,1)S(1)}, u32[]{:S(2)}) copy-start(bf16[4096,128]{1,0:T(8,128)(2,1)S(1)} %collective-permute-done.28.refs_16_) | copy-start | bytes 3145732
  155.5 3.8 %collective-permute-start.29 = (bf16[4096,128]{1,0:T(8,128)(2,1)S(1)}, bf16[4096,128]{1,0:T(8,128)(2,1)S(1)}, u32[]{:S(2)}, u32[]{:S(2)}) collective-permute-start(bf16[4096,128]{1,0:T(8,128)(2,1)S(1)} %collective-permute-done.28.refs_16_), channel_id=1, source_target_pairs={{0,1},{1,0},{2,3},{3,2},{4,5},{5,4},{6,7},{7,6},{8,9},{9,8},{10,11... | collective-permute-start | bytes 3145736 | tf_op jit(solution)/shard_map/ppermute | solution.py:300
  157.8 1.5 copy-start.14
  159.3 1.0 copy-start.15

commit v6 on v4

--- a/solution.py
+++ b/solution.py
@@ -490,12 +490,13 @@
     )
     o2 = by_side(later)
     got = around(got, "row", lambda d: row_perm(0, d))
+    got, s2 = lax.optimization_barrier((got, swap(n2)))
     got = around(got, "row", lambda d: row_perm(d, 0))
     parts = []
     for values in (inner_got, edge_got):
         parts += list(values[:2]) + [two(v) for v in values[2:]]
     o2_late, _ = lax.optimization_barrier((o2, got))
-    parts += [n2, swap(n2), o2, swap(o2_late)]
+    parts += [n2, s2, o2, swap(o2_late)]
     return pl.pallas_call(
         final_kernel,
         out_shape=jax.ShapeDtypeStruct((row_count, panel), BF),

time: 171 us -> 169 us (0.988)
  waiting for transfers between devices: 50.4 us -> 47.7 us
    ppermute x9, waiting for transfers between devices: 13.5 us -> 11.7 us  [around(): parts = [value] + [lax.ppermute(value, axis, perm_of(d)) for d in (1, 2, 3)]]
  transfers between devices with their start and end apart: 29 -> 29, of which waited for: 14 -> 13; matrix products, arithmetic and copies ran while one was open for 8% -> 8% of each run, Pallas kernels for 27% -> 27%
where the time goes in v6:
time: 169 us; the launch traced here: 168 us
  Pallas kernels  60.4 us (36%)
  waiting for transfers between devices  47.7 us (28%)
  starting transfers between devices  37.7 us (22%)
  local copies, waits for them, and re-layouts  14.9 us (9%)
  other arithmetic  5.59 us (3%)
  between operations  1.97 us (1%)
    ppermute x6, waiting for transfers between devices, by_side(): return lax.ppermute(value, 'vec', sides)  23.7 us
    pallas_call x1, Pallas kernels, local(): pl.pallas_call(functools.partial(edge_kernel, blocks), out_shape=jax.Shap...  17.2 us
    pallas_call x1, Pallas kernels, local(): pl.pallas_call(functools.partial(inner_kernel, blocks), out_shape=jax.Sha...  16.9 us
    pallas_call x1, Pallas kernels, local(): pl.pallas_call(final_kernel, out_shape=jax.ShapeDtypeStruct((row_count, p...  14.7 us
    ppermute x9, waiting for transfers between devices, around(): parts = [value] + [lax.ppermute(value, axis, perm_of(d)) for d in (1, 2, 3)]  11.7 us
    pallas_call x2, Pallas kernels, gram(): pl.pallas_call(functools.partial(gram_kernel, half, base is not None), ou...  11.5 us
    ppermute x10, starting transfers between devices, swap(): return lax.ppermute(value, 'vec', z_perm(0, 1))  11.3 us
    ppermute x9, starting transfers between devices, around(): parts = [value] + [lax.ppermute(value, axis, perm_of(d)) for d in (1, 2, 3)]  8.6 us
  transfers between devices with their start and end apart: 29, of which 13 were waited for; matrix products, arithmetic and copies ran while one was open for 8% of the time, Pallas kernels for 27%

profile of v6, /device:TPU:1, one launch (start us, length us, event | category | flops | bytes accessed | tf_op | source)
XLA Modules:
  0.0 168.2 jit_solution(15947836750908660903)
XLA Ops:
  0.0 1.4 constant_dynamic-slice_fusion.10
  1.4 5.8 %collective-permute-start = (bf16[40,128,128]{2,1,0:T(8,128)(2,1)S(1)}, bf16[40,128,128]{2,1,0:T(8,128)(2,1)}, u32[]{:S(2)}, u32[]{:S(2)}) collective-permute-start(bf16[40,128,128]{2,1,0:T(8,128)(2,1)S(1)} %constant_dynamic-slice_fusion.10), channel_id=1, source_target_pairs={{0,8},{1,121},{2,10},{3,123},{4,12},{5,125},{6,14},{7,127},{8,16},... | collective-permute-start | bytes 3932168 | tf_op jit(solution)/shard_map/ppermute | solution.py:326
  8.0 0.1 copy.18
  8.1 0.6 fusion.4
  8.7 1.2 fusion.3
  10.1 4.8 %collective-permute-start.2 = (bf16[13,128,128]{2,1,0:T(8,128)(2,1)S(1)}, bf16[13,128,128]{2,1,0:T(8,128)(2,1)S(1)}, u32[]{:S(2)}, u32[]{:S(2)}) collective-permute-start(bf16[13,128,128]{2,1,0:T(8,128)(2,1)S(1)} %pad_maximum_fusion.5), channel_id=1, source_target_pairs={{0,120},{8,0},{16,8},{24,16},{32,24},{40,32},{48,40},{56,48},{64,5... | collective-permute-start | bytes 1277960 | tf_op jit(solution)/shard_map/ppermute | solution.py:336
  14.9 16.9 %inner_filter.1 = bf16[40,128,128]{2,1,0:T(8,128)(2,1)} custom-call(s32[64,8]{1,0:T(8,128)} %get-tuple-element.51.facts, bf16[64,4,128,128]{3,2,1,0:T(8,128)(2,1)} %tiles.1, bf16[64,128,128]{2,1,0:T(8,128)(2,1)} %bitcast.35), custom_call_target="tpu_custom_call" | custom-call | flops 1000000 | bytes 1048576 | tf_op jit(solution)/shard_map/inner_filter/pallas_call | solution.py:345
  31.9 1.2 collective-permute-start.3
  33.1 1.4 constant_dynamic-slice_fusion.1
  34.4 0.3 collective-permute-start.4
  34.8 0.1 copy.21
  35.0 1.0 collective-permute-done.3.refs_1_
  35.9 1.0 constant_dynamic-slice_fusion
  37.0 1.1 pad_maximum_fusion
  38.1 1.7 %collective-permute-start.5 = (bf16[5120,128]{1,0:T(8,128)(2,1)}, bf16[5120,128]{1,0:T(8,128)(2,1)S(1)}, u32[]{:S(2)}, u32[]{:S(2)}) collective-permute-start(bf16[5120,128]{1,0:T(8,128)(2,1)} %pad_maximum_fusion), channel_id=1, source_target_pairs={{0,6},{1,3},{2,0},{3,5},{4,2},{5,7},{6,4},{7,1},{8,14},{9,11},{10,... | collective-permute-start | bytes 3932168 | tf_op jit(solution)/shard_map/ppermute | solution.py:391
  39.9 0.1 copy.23
  40.0 0.7 multiply_add_fusion.facts
  40.7 17.2 %edge_filter.1 = bf16[24,128,128]{2,1,0:T(8,128)(2,1)} custom-call(s32[64,8]{1,0:T(8,128)} %multiply_add_fusion.facts, s32[1]{0:T(128)} %bitcast.3.core, bf16[256,128,128]{2,1,0:T(8,128)(2,1)} %bitcast.32, bf16[64,128,128]{2,1,0:T(8,128)(2,1)} %bitcast.36, bf16[40,128,128]{2,1,0:T(8,128)(2,1)} %collective-permute-done.near, ...), custom_call_target="tpu_custom_call" | custom-call | flops 8000000000 | bytes 11534336 | tf_op jit(solution)/shard_map/edge_filter/pallas_call | solution.py:431
  57.9 2.8 %collective-permute-start.8 = (bf16[3072,128]{1,0:T(8,128)(2,1)}, bf16[3072,128]{1,0:T(8,128)(2,1)S(1)}, u32[]{:S(2)}, u32[]{:S(2)}) collective-permute-start(bf16[3072,128]{1,0:T(8,128)(2,1)} %bitcast.39), channel_id=1, source_target_pairs={{0,1},{1,0},{2,3},{3,2},{4,5},{5,4},{6,7},{7,6},{8,9},{9,8},{10,11... | collective-permute-start | bytes 2359304 | tf_op jit(solution)/shard_map/ppermute | solution.py:300
  60.8 1.0 constant_dynamic-slice_fusion.5
  61.9 0.1 dynamic-slice_dynamic-update-slice_fusion.2
  62.0 1.4 copy-done.10
  63.5 1.0 pad_maximum_fusion.2
  64.6 0.2 collective-permute-start.9
  64.8 9.4 %collective-permute-done.7 = bf16[2560,128]{1,0:T(8,128)(2,1)} collective-permute-done((bf16[2560,128]{1,0:T(8,128)(2,1)S(1)}, bf16[2560,128]{1,0:T(8,128)(2,1)}, u32[]{:S(2)}, u32[]{:S(2)}) %collective-permute-start.7) | collective-permute-done | bytes 655392 | tf_op jit(solution)/shard_map/ppermute | solution.py:391
  74.2 0.5 collective-permute-start.6
  74.7 0.6 pad_add_fusion.2.place
  75.3 7.2 %collective-permute-done.9 = bf16[3072,128]{1,0:T(8,128)(2,1)S(1)} collective-permute-done((bf16[3072,128]{1,0:T(8,128)(2,1)}, bf16[3072,128]{1,0:T(8,128)(2,1)S(1)}, u32[]{:S(2)}, u32[]{:S(2)}) %collective-permute-start.9) | collective-permute-done | bytes 786464 | tf_op jit(solution)/shard_map/ppermute | solution.py:391
  82.7 1.2 pad_maximum_fusion.1
  83.9 0.9 collective-permute-done.11
  84.8 0.9 copy-done.7
  85.7 6.3 %gram.2.refs_0_ = f32[128,1024]{1,0:T(8,128)} custom-call(s32[4]{0:T(128)} %pad_add_fusion.2.place, bf16[5120,128]{1,0:T(8,128)(2,1)} %bitcast.29, bf16[5120,128]{1,0:T(8,128)(2,1)} %copy-done, bf16[2,2560,128]{2,1,0:T(8,128)(2,1)} %bitcast.33, bf16[2,2560,128]{2,1,0:T(8,128)(2,1)} %bitcast.13.refs_3_, bf16[2,1280,128]{2,1,0:T(8,128)(2,1)} %bitcast.17.refs_4_, ...), custom_call_target="tpu_custom_call" | custom-call | flops 671088640 | bytes 7864320 | tf_op jit(solution)/shard_map/gram/pallas_call | solution.py:410
  92.1 1.6 collective-permute-start.13
  93.7 0.7 dynamic-slice_dynamic-update-slice_fusion.5
  94.3 0.7 dynamic-slice_dynamic-update-slice_fusion.4
  95.0 0.2 collective-permute-done.13
  95.2 0.7 copy-done.8
  96.0 5.2 %gram.3 = bf16[128,1024]{1,0:T(8,128)(2,1)} custom-call(s32[4]{0:T(128)} %pad_add_fusion.2.place, f32[128,1024]{1,0:T(8,128)} %gram.2.refs_0_, bf16[3072,128]{1,0:T(8,128)(2,1)} %bitcast.41, bf16[3072,128]{1,0:T(8,128)(2,1)} %copy-done.4, bf16[2,1536,128]{2,1,0:T(8,128)(2,1)} %bitcast.37, bf16[2,1536,128]{2,1,0:T(8,128)(2,1)} %bitcast.47, ...), custom_call_target="tpu_custom_call" | custom-call | flops 402653184 | bytes 4718592 | tf_op jit(solution)/shard_map/gram/pallas_call | solution.py:410
  101.2 4.5 %all-to-all-start = ((bf16[16,8,1024]{2,1,0:T(8,128)(2,1)}), bf16[16,8,1024]{2,1,0:T(8,128)(2,1)S(1)}, u32[]{:S(2)}, u32[]{:S(2)}) async-start(bf16[16,8,1024]{2,1,0:T(8,128)(2,1)} %bitcast.46), calls=%async_computation | async-start | bytes 524288 | tf_op jit(solution)/shard_map/all_to_all | solution.py:465
  105.8 0.8 dynamic-slice_dynamic-update-slice_fusion.1
  106.6 0.8 dynamic-slice_dynamic-update-slice_fusion
  107.3 6.0 %all-to-all-done = bf16[16,8,1024]{2,1,0:T(8,128)(2,1)S(1)} async-done(((bf16[16,8,1024]{2,1,0:T(8,128)(2,1)}), bf16[16,8,1024]{2,1,0:T(8,128)(2,1)S(1)}, u32[]{:S(2)}, u32[]{:S(2)}) %all-to-all-start) | async-done | bytes 262176 | tf_op jit(solution)/shard_map/all_to_all | solution.py:465
  113.4 0.9 collective-permute-start.17
  114.3 2.1 %collective-permute-start.16 = (bf16[1,8,1024]{2,1,0:T(8,128)(2,1)S(1)}, bf16[1,8,1024]{2,1,0:T(8,128)(2,1)S(1)}, u32[]{:S(2)}, u32[]{:S(2)}) collective-permute-start(bf16[1,8,1024]{2,1,0:T(8,128)(2,1)S(1)} %bitcast.52), channel_id=1, source_target_pairs={{0,4},{1,5},{2,6},{3,7},{4,0},{5,1},{6,2},{7,3},{8,12},{9,13},{10,... | collective-permute-start | bytes 49160 | tf_op jit(solution)/shard_map/ppermute | solution.py:472
  116.3 1.0 collective-permute-start.15
  117.3 2.7 %collective-permute-start.21 = (bf16[5120,128]{1,0:T(8,128)(2,1)}, bf16[5120,128]{1,0:T(8,128)(2,1)S(1)}, u32[]{:S(2)}, u32[]{:S(2)}) collective-permute-start(bf16[5120,128]{1,0:T(8,128)(2,1)} %collective-permute-done.14.refs_12_), channel_id=1, source_target_pairs={{0,1},{1,0},{2,3},{3,2},{4,5},{5,4},{6,7},{7,6},{8,9},{9,8},{10,11... | collective-permute-start | bytes 3932168 | tf_op jit(solution)/shard_map/ppermute | solution.py:300
  120.1 0.3 collective-permute-start.26
  120.4 0.7 collective-permute-start.18
  121.1 0.8 collective-permute-start.20
  121.9 1.2 collective-permute-start.19
  123.1 0.5 collective-permute-done.18
  123.6 3.0 %collective-permute-done.19 = bf16[4,8,1024]{2,1,0:T(8,128)(2,1)S(1)} collective-permute-done((bf16[4,8,1024]{2,1,0:T(8,128)(2,1)S(1)}, bf16[4,8,1024]{2,1,0:T(8,128)(2,1)S(1)}, u32[]{:S(2)}, u32[]{:S(2)}) %collective-permute-start.19) | collective-permute-done | bytes 65568 | tf_op jit(solution)/shard_map/ppermute | solution.py:472
  126.6 0.8 collective-permute-start.22
  127.4 1.0 collective-permute-start.23
  128.4 0.2 collective-permute-start.24
  128.6 3.6 %collective-permute-done.22 = bf16[16,8,1024]{2,1,0:T(8,128)(2,1)S(1)} collective-permute-done((bf16[16,8,1024]{2,1,0:T(8,128)(2,1)S(1)}, bf16[16,8,1024]{2,1,0:T(8,128)(2,1)S(1)}, u32[]{:S(2)}, u32[]{:S(2)}) %collective-permute-start.22) | collective-permute-done | bytes 262176 | tf_op jit(solution)/shard_map/ppermute | solution.py:472
  132.2 2.0 %collective-permute-done.23 = bf16[16,8,1024]{2,1,0:T(8,128)(2,1)S(1)} collective-permute-done((bf16[16,8,1024]{2,1,0:T(8,128)(2,1)S(1)}, bf16[16,8,1024]{2,1,0:T(8,128)(2,1)S(1)}, u32[]{:S(2)}, u32[]{:S(2)}) %collective-permute-start.23) | collective-permute-done | bytes 262176 | tf_op jit(solution)/shard_map/ppermute | solution.py:472
  134.2 2.7 %collective-permute-done.24 = bf16[16,8,1024]{2,1,0:T(8,128)(2,1)S(1)} collective-permute-done((bf16[16,8,1024]{2,1,0:T(8,128)(2,1)S(1)}, bf16[16,8,1024]{2,1,0:T(8,128)(2,1)S(1)}, u32[]{:S(2)}, u32[]{:S(2)}) %collective-permute-start.24) | collective-permute-done | bytes 262176 | tf_op jit(solution)/shard_map/ppermute | solution.py:472
  137.0 7.0 %collective-permute-done.26.refs_14_ = bf16[7168,128]{1,0:T(8,128)(2,1)S(1)} collective-permute-done((bf16[7168,128]{1,0:T(8,128)(2,1)}, bf16[7168,128]{1,0:T(8,128)(2,1)S(1)}, u32[]{:S(2)}, u32[]{:S(2)}) %collective-permute-start.26) | collective-permute-done | bytes 1835040 | tf_op jit(solution)/shard_map/ppermute | solution.py:391
  144.0 2.2 %collective-permute-start.27 = (bf16[7168,128]{1,0:T(8,128)(2,1)S(1)}, bf16[7168,128]{1,0:T(8,128)(2,1)S(1)}, u32[]{:S(2)}, u32[]{:S(2)}) collective-permute-start(bf16[7168,128]{1,0:T(8,128)(2,1)S(1)} %collective-permute-done.26.refs_14_), channel_id=1, source_target_pairs={{0,1},{1,0},{2,3},{3,2},{4,5},{5,4},{6,7},{7,6},{8,9},{9,8},{10,11... | collective-permute-start | bytes 5505032 | tf_op jit(solution)/shard_map/ppermute | solution.py:300
  146.8 4.3 %collective-permute-done.25.gathered_twin = bf16[64,8,1024]{2,1,0:T(8,128)(2,1)S(1)} collective-permute-done((bf16[64,8,1024]{2,1,0:T(8,128)(2,1)S(1)}, bf16[64,8,1024]{2,1,0:T(8,128)(2,1)S(1)}, u32[]{:S(2)}, u32[]{:S(2)}) %collective-permute-start.25) | collective-permute-done | bytes 1048608 | tf_op jit(solution)/shard_map/ppermute | solution.py:300
  151.1 1.0 copy-done.17
  152.1 1.2 copy-done.15
  153.3 14.7 %final.1 = bf16[8192,128]{1,0:T(8,128)(2,1)} custom-call(s32[4]{0:T(128)} %pad_add_fusion.2.place, f32[1]{0:T(128)S(6)} %copy.42.scale_in, bf16[64,8,1024]{2,1,0:T(8,128)(2,1)} %copy-done.9, bf16[64,8,1024]{2,1,0:T(8,128)(2,1)} %copy-done.17, bf16[5120,128]{1,0:T(8,128)(2,1)} %bitcast.30, bf16[5120,128]{1,0:T(8,128)(2,1)} %copy-done, ...), custom_call_target="tpu_custom_call" | custom-call | flops 6000000000 | bytes 20971520 | tf_op jit(solution)/shard_map/final/pallas_call | solution.py:500
  (87 shorter events, 1.1 us)
Async XLA Ops:
  0.0 7.9 %copy-start.11 = (s32[64,4]{0,1:T(4,128)S(1)}, s32[64,4]{0,1:T(4,128)}, u32[]{:S(2)}) copy-start(s32[64,4]{0,1:T(4,128)} %param.6) | copy-start | bytes 3076
  1.4 30.5 %collective-permute-start = (bf16[40,128,128]{2,1,0:T(8,128)(2,1)S(1)}, bf16[40,128,128]{2,1,0:T(8,128)(2,1)}, u32[]{:S(2)}, u32[]{:S(2)}) collective-permute-start(bf16[40,128,128]{2,1,0:T(8,128)(2,1)S(1)} %constant_dynamic-slice_fusion.10), channel_id=1, source_target_pairs={{0,8},{1,121},{2,10},{3,123},{4,12},{5,125},{6,14},{7,127},{8,16},... | collective-permute-start | bytes 3932168 | tf_op jit(solution)/shard_map/ppermute | solution.py:326
  9.9 21.9 %collective-permute-start.1 = (bf16[13,128,128]{2,1,0:T(8,128)(2,1)S(1)}, bf16[13,128,128]{2,1,0:T(8,128)(2,1)S(1)}, u32[]{:S(2)}, u32[]{:S(2)}) collective-permute-start(bf16[13,128,128]{2,1,0:T(8,128)(2,1)S(1)} %pad_maximum_fusion.4), channel_id=1, source_target_pairs={{0,8},{8,16},{16,24},{24,32},{32,40},{40,48},{48,56},{56,64},{64,7... | collective-permute-start | bytes 1277960 | tf_op jit(solution)/shard_map/ppermute | solution.py:333
  10.1 21.8 %collective-permute-start.2 = (bf16[13,128,128]{2,1,0:T(8,128)(2,1)S(1)}, bf16[13,128,128]{2,1,0:T(8,128)(2,1)S(1)}, u32[]{:S(2)}, u32[]{:S(2)}) collective-permute-start(bf16[13,128,128]{2,1,0:T(8,128)(2,1)S(1)} %pad_maximum_fusion.5), channel_id=1, source_target_pairs={{0,120},{8,0},{16,8},{24,16},{32,24},{40,32},{48,40},{56,48},{64,5... | collective-permute-start | bytes 1277960 | tf_op jit(solution)/shard_map/ppermute | solution.py:336
  31.9 5.1 %copy-start.12 = (bf16[13,128,128]{2,1,0:T(8,128)(2,1)}, bf16[13,128,128]{2,1,0:T(8,128)(2,1)S(1)}, u32[]{:S(2)}) copy-start(bf16[13,128,128]{2,1,0:T(8,128)(2,1)S(1)} %collective-permute-done.1.vlow) | copy-start | bytes 1277956
  31.9 5.1 %copy-start.13 = (bf16[13,128,128]{2,1,0:T(8,128)(2,1)}, bf16[13,128,128]{2,1,0:T(8,128)(2,1)S(1)}, u32[]{:S(2)}) copy-start(bf16[13,128,128]{2,1,0:T(8,128)(2,1)S(1)} %collective-permute-done.2.vhigh) | copy-start | bytes 1277956
  31.9 4.0 %collective-permute-start.3 = (bf16[5120,128]{1,0:T(8,128)(2,1)}, bf16[5120,128]{1,0:T(8,128)(2,1)S(1)}, u32[]{:S(2)}, u32[]{:S(2)}) collective-permute-start(bf16[5120,128]{1,0:T(8,128)(2,1)} %bitcast.27), channel_id=1, source_target_pairs={{0,1},{1,0},{2,3},{3,2},{4,5},{5,4},{6,7},{7,6},{8,9},{9,8},{10,11... | collective-permute-start | bytes 3932168 | tf_op jit(solution)/shard_map/ppermute | solution.py:300
  34.4 3.7 %collective-permute-start.4 = (bf16[40,128,128]{2,1,0:T(8,128)(2,1)}, bf16[40,128,128]{2,1,0:T(8,128)(2,1)}, u32[]{:S(2)}, u32[]{:S(2)}) collective-permute-start(bf16[40,128,128]{2,1,0:T(8,128)(2,1)} %collective-permute-done.near), channel_id=1, source_target_pairs={{0,1},{1,0},{2,3},{3,2},{4,5},{5,4},{6,7},{7,6},{8,9},{9,8},{10,11... | collective-permute-start | bytes 3932168 | tf_op jit(solution)/shard_map/ppermute | solution.py:300
  35.9 2.2 %copy-start = (bf16[5120,128]{1,0:T(8,128)(2,1)}, bf16[5120,128]{1,0:T(8,128)(2,1)S(1)}, u32[]{:S(2)}) copy-start(bf16[5120,128]{1,0:T(8,128)(2,1)S(1)} %collective-permute-done.3.refs_1_) | copy-start | bytes 3932164
  38.1 23.7 %collective-permute-start.5 = (bf16[5120,128]{1,0:T(8,128)(2,1)}, bf16[5120,128]{1,0:T(8,128)(2,1)S(1)}, u32[]{:S(2)}, u32[]{:S(2)}) collective-permute-start(bf16[5120,128]{1,0:T(8,128)(2,1)} %pad_maximum_fusion), channel_id=1, source_target_pairs={{0,6},{1,3},{2,0},{3,5},{4,2},{5,7},{6,4},{7,1},{8,14},{9,11},{10,... | collective-permute-start | bytes 3932168 | tf_op jit(solution)/shard_map/ppermute | solution.py:391
  57.9 5.5 %collective-permute-start.8 = (bf16[3072,128]{1,0:T(8,128)(2,1)}, bf16[3072,128]{1,0:T(8,128)(2,1)S(1)}, u32[]{:S(2)}, u32[]{:S(2)}) collective-permute-start(bf16[3072,128]{1,0:T(8,128)(2,1)} %bitcast.39), channel_id=1, source_target_pairs={{0,1},{1,0},{2,3},{3,2},{4,5},{5,4},{6,7},{7,6},{8,9},{9,8},{10,11... | collective-permute-start | bytes 2359304 | tf_op jit(solution)/shard_map/ppermute | solution.py:300
  61.8 12.4 %copy-start.1 = (bf16[5120,128]{1,0:T(8,128)(2,1)}, bf16[5120,128]{1,0:T(8,128)(2,1)S(1)}, u32[]{:S(2)}) copy-start(bf16[5120,128]{1,0:T(8,128)(2,1)S(1)} %collective-permute-done.5) | copy-start | bytes 3932164
  62.0 1.4 copy-start.10
  63.4 10.8 %collective-permute-start.7 = (bf16[2560,128]{1,0:T(8,128)(2,1)S(1)}, bf16[2560,128]{1,0:T(8,128)(2,1)}, u32[]{:S(2)}, u32[]{:S(2)}) collective-permute-start(bf16[2560,128]{1,0:T(8,128)(2,1)S(1)} %pad_maximum_fusion.3), channel_id=1, source_target_pairs={{0,6},{1,3},{2,0},{3,5},{4,2},{5,7},{6,4},{7,1},{8,14},{9,11},{10,... | collective-permute-start | bytes 1966088 | tf_op jit(solution)/shard_map/ppermute | solution.py:391
  63.5 19.1 %copy-start.4 = (bf16[3072,128]{1,0:T(8,128)(2,1)}, bf16[3072,128]{1,0:T(8,128)(2,1)S(1)}, u32[]{:S(2)}) copy-start(bf16[3072,128]{1,0:T(8,128)(2,1)S(1)} %collective-permute-done.8.refs_2_.refs_7_) | copy-start | bytes 2359300
  64.6 18.0 %collective-permute-start.9 = (bf16[3072,128]{1,0:T(8,128)(2,1)}, bf16[3072,128]{1,0:T(8,128)(2,1)S(1)}, u32[]{:S(2)}, u32[]{:S(2)}) collective-permute-start(bf16[3072,128]{1,0:T(8,128)(2,1)} %pad_maximum_fusion.2), channel_id=1, source_target_pairs={{0,6},{1,3},{2,0},{3,5},{4,2},{5,7},{6,4},{7,1},{8,14},{9,11},{10,... | collective-permute-start | bytes 2359304 | tf_op jit(solution)/shard_map/ppermute | solution.py:391
  74.2 8.3 %collective-permute-start.10 = (bf16[2560,128]{1,0:T(8,128)(2,1)}, bf16[2560,128]{1,0:T(8,128)(2,1)}, u32[]{:S(2)}, u32[]{:S(2)}) collective-permute-start(bf16[2560,128]{1,0:T(8,128)(2,1)} %collective-permute-done.7), channel_id=1, source_target_pairs={{0,1},{1,0},{2,3},{3,2},{4,5},{5,4},{6,7},{7,6},{8,9},{9,8},{10,11... | collective-permute-start | bytes 1966088 | tf_op jit(solution)/shard_map/ppermute | solution.py:300
  74.2 10.6 %collective-permute-start.6 = (bf16[5120,128]{1,0:T(8,128)(2,1)S(1)}, bf16[5120,128]{1,0:T(8,128)(2,1)}, u32[]{:S(2)}, u32[]{:S(2)}) collective-permute-start(bf16[5120,128]{1,0:T(8,128)(2,1)S(1)} %collective-permute-done.5), channel_id=1, source_target_pairs={{0,1},{1,0},{2,3},{3,2},{4,5},{5,4},{6,7},{7,6},{8,9},{9,8},{10,11... | collective-permute-start | bytes 3932168 | tf_op jit(solution)/shard_map/ppermute | solution.py:300
  74.7 8.0 %copy-start.6 = (bf16[2560,128]{1,0:T(8,128)(2,1)S(1)}, bf16[2560,128]{1,0:T(8,128)(2,1)}, u32[]{:S(2)}) copy-start(bf16[2560,128]{1,0:T(8,128)(2,1)} %get-tuple-element.46) | copy-start | bytes 1966084
  82.5 11.8 %copy-start.2 = (bf16[3072,128]{1,0:T(8,128)(2,1)}, bf16[3072,128]{1,0:T(8,128)(2,1)S(1)}, u32[]{:S(2)}) copy-start(bf16[3072,128]{1,0:T(8,128)(2,1)S(1)} %collective-permute-done.9) | copy-start | bytes 2359300
  82.5 2.3 %collective-permute-start.11 = (bf16[3072,128]{1,0:T(8,128)(2,1)S(1)}, bf16[3072,128]{1,0:T(8,128)(2,1)S(1)}, u32[]{:S(2)}, u32[]{:S(2)}) collective-permute-start(bf16[3072,128]{1,0:T(8,128)(2,1)S(1)} %collective-permute-done.9), channel_id=1, source_target_pairs={{0,1},{1,0},{2,3},{3,2},{4,5},{5,4},{6,7},{7,6},{8,9},{9,8},{10,11... | collective-permute-start | bytes 2359304 | tf_op jit(solution)/shard_map/ppermute | solution.py:300
  82.6 9.4 %collective-permute-start.12 = (bf16[1536,128]{1,0:T(8,128)(2,1)S(1)}, bf16[1536,128]{1,0:T(8,128)(2,1)}, u32[]{:S(2)}, u32[]{:S(2)}) collective-permute-start(bf16[1536,128]{1,0:T(8,128)(2,1)S(1)} %pad_maximum_fusion.6), channel_id=1, source_target_pairs={{0,6},{1,3},{2,0},{3,5},{4,2},{5,7},{6,4},{7,1},{8,14},{9,11},{10,... | collective-permute-start | bytes 1179656 | tf_op jit(solution)/shard_map/ppermute | solution.py:391
  84.8 0.9 copy-start.7
  92.0 21.4 %collective-permute-start.14 = (bf16[5120,128]{1,0:T(8,128)(2,1)}, bf16[5120,128]{1,0:T(8,128)(2,1)}, u32[]{:S(2)}, u32[]{:S(2)}) collective-permute-start(bf16[5120,128]{1,0:T(8,128)(2,1)} %pad_maximum_fusion.1), channel_id=1, source_target_pairs={{0,6},{1,3},{2,0},{3,5},{4,2},{5,7},{6,4},{7,1},{8,14},{9,11},{10,... | collective-permute-start | bytes 3932168 | tf_op jit(solution)/shard_map/ppermute | solution.py:391
  92.1 3.1 %collective-permute-start.13 = (bf16[1536,128]{1,0:T(8,128)(2,1)}, bf16[1536,128]{1,0:T(8,128)(2,1)S(1)}, u32[]{:S(2)}, u32[]{:S(2)}) collective-permute-start(bf16[1536,128]{1,0:T(8,128)(2,1)} %collective-permute-done.12), channel_id=1, source_target_pairs={{0,1},{1,0},{2,3},{3,2},{4,5},{5,4},{6,7},{7,6},{8,9},{9,8},{10,11... | collective-permute-start | bytes 1179656 | tf_op jit(solution)/shard_map/ppermute | solution.py:300
  95.2 0.8 copy-start.8
  96.0 9.8 %copy-start.3 = (bf16[24,128,128]{2,1,0:T(8,128)(2,1)S(1)}, bf16[24,128,128]{2,1,0:T(8,128)(2,1)}, u32[]{:S(2)}) copy-start(bf16[24,128,128]{2,1,0:T(8,128)(2,1)} %edge_filter.1) | copy-start | bytes 2359300
  96.0 10.6 %copy-start.5 = (bf16[3072,128]{1,0:T(8,128)(2,1)S(1)}, bf16[3072,128]{1,0:T(8,128)(2,1)}, u32[]{:S(2)}) copy-start(bf16[3072,128]{1,0:T(8,128)(2,1)} %copy-done.4) | copy-start | bytes 2359300
  101.2 12.1 %all-to-all-start = ((bf16[16,8,1024]{2,1,0:T(8,128)(2,1)}), bf16[16,8,1024]{2,1,0:T(8,128)(2,1)S(1)}, u32[]{:S(2)}, u32[]{:S(2)}) async-start(bf16[16,8,1024]{2,1,0:T(8,128)(2,1)} %bitcast.46), calls=%async_computation | async-start | bytes 524288 | tf_op jit(solution)/shard_map/all_to_all | solution.py:465
  113.4 6.7 %collective-permute-start.17 = (bf16[1,8,1024]{2,1,0:T(8,128)(2,1)S(1)}, bf16[1,8,1024]{2,1,0:T(8,128)(2,1)S(1)}, u32[]{:S(2)}, u32[]{:S(2)}) collective-permute-start(bf16[1,8,1024]{2,1,0:T(8,128)(2,1)S(1)} %bitcast.51), channel_id=1, source_target_pairs={{0,2},{1,3},{2,4},{3,5},{4,6},{5,7},{6,0},{7,1},{8,10},{9,11},{10,... | collective-permute-start | bytes 49160 | tf_op jit(solution)/shard_map/ppermute | solution.py:472
  114.3 5.8 %collective-permute-start.16 = (bf16[1,8,1024]{2,1,0:T(8,128)(2,1)S(1)}, bf16[1,8,1024]{2,1,0:T(8,128)(2,1)S(1)}, u32[]{:S(2)}, u32[]{:S(2)}) collective-permute-start(bf16[1,8,1024]{2,1,0:T(8,128)(2,1)S(1)} %bitcast.52), channel_id=1, source_target_pairs={{0,4},{1,5},{2,6},{3,7},{4,0},{5,1},{6,2},{7,3},{8,12},{9,13},{10,... | collective-permute-start | bytes 49160 | tf_op jit(solution)/shard_map/ppermute | solution.py:472
  116.3 3.8 %collective-permute-start.15 = (bf16[1,8,1024]{2,1,0:T(8,128)(2,1)S(1)}, bf16[1,8,1024]{2,1,0:T(8,128)(2,1)S(1)}, u32[]{:S(2)}, u32[]{:S(2)}) collective-permute-start(bf16[1,8,1024]{2,1,0:T(8,128)(2,1)S(1)} %bitcast.53), channel_id=1, source_target_pairs={{0,6},{1,7},{2,0},{3,1},{4,2},{5,3},{6,4},{7,5},{8,14},{9,15},{10,... | collective-permute-start | bytes 49160 | tf_op jit(solution)/shard_map/ppermute | solution.py:472
  117.3 9.2 %collective-permute-start.21 = (bf16[5120,128]{1,0:T(8,128)(2,1)}, bf16[5120,128]{1,0:T(8,128)(2,1)S(1)}, u32[]{:S(2)}, u32[]{:S(2)}) collective-permute-start(bf16[5120,128]{1,0:T(8,128)(2,1)} %collective-permute-done.14.refs_12_), channel_id=1, source_target_pairs={{0,1},{1,0},{2,3},{3,2},{4,5},{5,4},{6,7},{7,6},{8,9},{9,8},{10,11... | collective-permute-start | bytes 3932168 | tf_op jit(solution)/shard_map/ppermute | solution.py:300
  120.1 23.9 %collective-permute-start.26 = (bf16[7168,128]{1,0:T(8,128)(2,1)}, bf16[7168,128]{1,0:T(8,128)(2,1)S(1)}, u32[]{:S(2)}, u32[]{:S(2)}) collective-permute-start(bf16[7168,128]{1,0:T(8,128)(2,1)} %dynamic-slice_dynamic-update-slice_fusion), channel_id=1, source_target_pairs={{0,6},{1,3},{2,0},{3,5},{4,2},{5,7},{6,4},{7,1},{8,14},{9,11},{10,... | collective-permute-start | bytes 5505032 | tf_op jit(solution)/shard_map/ppermute | solution.py:391
  120.4 3.1 %collective-permute-start.18 = (bf16[4,8,1024]{2,1,0:T(8,128)(2,1)S(1)}, bf16[4,8,1024]{2,1,0:T(8,128)(2,1)S(1)}, u32[]{:S(2)}, u32[]{:S(2)}) collective-permute-start(bf16[4,8,1024]{2,1,0:T(8,128)(2,1)S(1)} %get-tuple-element.52), channel_id=1, source_target_pairs={{0,24},{8,0},{16,8},{24,16},{32,56},{40,32},{48,40},{56,48},{64,88... | collective-permute-start | bytes 196616 | tf_op jit(solution)/shard_map/ppermute | solution.py:472
  121.1 5.4 %collective-permute-start.20 = (bf16[4,8,1024]{2,1,0:T(8,128)(2,1)S(1)}, bf16[4,8,1024]{2,1,0:T(8,128)(2,1)S(1)}, u32[]{:S(2)}, u32[]{:S(2)}) collective-permute-start(bf16[4,8,1024]{2,1,0:T(8,128)(2,1)S(1)} %get-tuple-element.52), channel_id=1, source_target_pairs={{0,8},{8,16},{16,24},{24,0},{32,40},{40,48},{48,56},{56,32},{64,72... | collective-permute-start | bytes 196616 | tf_op jit(solution)/shard_map/ppermute | solution.py:472
  121.9 4.6 %collective-permute-start.19 = (bf16[4,8,1024]{2,1,0:T(8,128)(2,1)S(1)}, bf16[4,8,1024]{2,1,0:T(8,128)(2,1)S(1)}, u32[]{:S(2)}, u32[]{:S(2)}) collective-permute-start(bf16[4,8,1024]{2,1,0:T(8,128)(2,1)S(1)} %get-tuple-element.52), channel_id=1, source_target_pairs={{0,16},{8,24},{16,0},{24,8},{32,48},{40,56},{48,32},{56,40},{64,80... | collective-permute-start | bytes 196616 | tf_op jit(solution)/shard_map/ppermute | solution.py:472
  126.6 25.5 %copy-start.16 = (bf16[5120,128]{1,0:T(8,128)(2,1)}, bf16[5120,128]{1,0:T(8,128)(2,1)S(1)}, u32[]{:S(2)}) copy-start(bf16[5120,128]{1,0:T(8,128)(2,1)S(1)} %collective-permute-done.21.refs_13_) | copy-start | bytes 3932164
  126.6 5.6 %collective-permute-start.22 = (bf16[16,8,1024]{2,1,0:T(8,128)(2,1)S(1)}, bf16[16,8,1024]{2,1,0:T(8,128)(2,1)S(1)}, u32[]{:S(2)}, u32[]{:S(2)}) collective-permute-start(bf16[16,8,1024]{2,1,0:T(8,128)(2,1)S(1)} %constant_dynamic-update-slice_fusion.4), channel_id=1, source_target_pairs={{0,96},{8,104},{16,112},{24,120},{32,0},{40,8},{48,16},{56,24},{64... | collective-permute-start | bytes 786440 | tf_op jit(solution)/shard_map/ppermute | solution.py:472
  127.4 6.8 %collective-permute-start.23 = (bf16[16,8,1024]{2,1,0:T(8,128)(2,1)S(1)}, bf16[16,8,1024]{2,1,0:T(8,128)(2,1)S(1)}, u32[]{:S(2)}, u32[]{:S(2)}) collective-permute-start(bf16[16,8,1024]{2,1,0:T(8,128)(2,1)S(1)} %constant_dynamic-update-slice_fusion.4), channel_id=1, source_target_pairs={{0,64},{8,72},{16,80},{24,88},{32,96},{40,104},{48,112},{56,120},{... | collective-permute-start | bytes 786440 | tf_op jit(solution)/shard_map/ppermute | solution.py:472
  128.4 8.6 %collective-permute-start.24 = (bf16[16,8,1024]{2,1,0:T(8,128)(2,1)S(1)}, bf16[16,8,1024]{2,1,0:T(8,128)(2,1)S(1)}, u32[]{:S(2)}, u32[]{:S(2)}) collective-permute-start(bf16[16,8,1024]{2,1,0:T(8,128)(2,1)S(1)} %constant_dynamic-update-slice_fusion.4), channel_id=1, source_target_pairs={{0,32},{8,40},{16,48},{24,56},{32,64},{40,72},{48,80},{56,88},{64,... | collective-permute-start | bytes 786440 | tf_op jit(solution)/shard_map/ppermute | solution.py:472
  137.0 15.1 %copy-start.9 = (bf16[64,8,1024]{2,1,0:T(8,128)(2,1)}, bf16[64,8,1024]{2,1,0:T(8,128)(2,1)S(1)}, u32[]{:S(2)}) copy-start(bf16[64,8,1024]{2,1,0:T(8,128)(2,1)S(1)} %constant_dynamic-update-slice_fusion.11.gathered) | copy-start | bytes 3145732
  144.0 8.1 %copy-start.14 = (bf16[7168,128]{1,0:T(8,128)(2,1)}, bf16[7168,128]{1,0:T(8,128)(2,1)S(1)}, u32[]{:S(2)}) copy-start(bf16[7168,128]{1,0:T(8,128)(2,1)S(1)} %collective-permute-done.26.refs_14_) | copy-start | bytes 5505028
  144.0 8.1 %collective-permute-start.27 = (bf16[7168,128]{1,0:T(8,128)(2,1)S(1)}, bf16[7168,128]{1,0:T(8,128)(2,1)S(1)}, u32[]{:S(2)}, u32[]{:S(2)}) collective-permute-start(bf16[7168,128]{1,0:T(8,128)(2,1)S(1)} %collective-permute-done.26.refs_14_), channel_id=1, source_target_pairs={{0,1},{1,0},{2,3},{3,2},{4,5},{5,4},{6,7},{7,6},{8,9},{9,8},{10,11... | collective-permute-start | bytes 5505032 | tf_op jit(solution)/shard_map/ppermute | solution.py:300
  146.2 4.9 %collective-permute-start.25 = (bf16[64,8,1024]{2,1,0:T(8,128)(2,1)S(1)}, bf16[64,8,1024]{2,1,0:T(8,128)(2,1)S(1)}, u32[]{:S(2)}, u32[]{:S(2)}) collective-permute-start(bf16[64,8,1024]{2,1,0:T(8,128)(2,1)S(1)} %constant_dynamic-update-slice_fusion.11.gathered), channel_id=1, source_target_pairs={{0,1},{1,0},{2,3},{3,2},{4,5},{5,4},{6,7},{7,6},{8,9},{9,8},{10,11... | collective-permute-start | bytes 3145736 | tf_op jit(solution)/shard_map/ppermute | solution.py:300
  151.1 1.0 copy-start.17
  152.1 1.2 copy-start.15

commit v7 on v6

--- a/solution.py
+++ b/solution.py
@@ -102,14 +102,19 @@
         own_t = 0 if segment == 0 else count - own_rows
         copy(halo.at[pl.ds(0, DEEP)], seg_v.at[segment, pl.ds(near_v, DEEP)])
         copy(vectors.at[pl.ds(own_v, 2 * DEEP)], seg_v.at[segment, pl.ds(far_v, 2 * DEEP)])
-        copy(
-            tiles.at[pl.ds(own_t * 4, own_rows * 4)],
-            seg_t.at[segment, pl.ds(far_t * 4, own_rows * 4)],
-        )
+        soon = (span // 2 - REACH - far_t) * 4
+        for begin, end in ((0, soon), (soon, own_rows * 4)):
+            copy(
+                tiles.at[pl.ds(own_t * 4 + begin, end - begin)],
+                seg_t.at[segment, pl.ds(far_t * 4 + begin, end - begin)],
+            )
     copy(near, seg_t.at[c, pl.ds(c * (own_rows * 4), moved)])
     copy(far, seg_t.at[1 - c, pl.ds((1 - c) * (own_rows * 4), moved)])
-    for c in copies:
-        c.wait()
+    order = (copies[:3] + copies[4:7] + copies[8:], (copies[3], copies[7]))
+
+    def ready(turn):
+        for copied in order[turn]:
+            copied.wait()
 
     class Rows:
         def __init__(self, which):
@@ -127,7 +132,7 @@
         ],
         [(even, odd), (even1, odd1)],
         out,
-        None,
+        ready,
     )
 
 
@@ -438,7 +443,7 @@
             pltpu.VMEM((2, (3 * DEEP - 2 * REACH) * 4, 128, 128), BF),
         ]
         + [pltpu.VMEM((3 * DEEP, 128, panel), BF)] * 4
-        + [pltpu.SemaphoreType.DMA((10,))],
+        + [pltpu.SemaphoreType.DMA((12,))],
         compiler_params=params(58),
         cost_estimate=cost(8 * 10**9, 11 * 2**20),
         name="edge_filter",

time: 169 us -> 169 us (level)
  no operation moved by 1% of the time
where the time goes in v7:
time: 169 us; the launch traced here: 168 us
  Pallas kernels  60.4 us (36%)
  waiting for transfers between devices  47.7 us (28%)
  starting transfers between devices  37.7 us (22%)
  local copies, waits for them, and re-layouts  14.9 us (9%)
  other arithmetic  5.59 us (3%)
  between operations  1.97 us (1%)
    ppermute x6, waiting for transfers between devices, by_side(): return lax.ppermute(value, 'vec', sides)  23.7 us
    pallas_call x1, Pallas kernels, local(): pl.pallas_call(functools.partial(edge_kernel, blocks), out_shape=jax.Shap...  17.3 us
    pallas_call x1, Pallas kernels, local(): pl.pallas_call(functools.partial(inner_kernel, blocks), out_shape=jax.Sha...  16.9 us
    pallas_call x1, Pallas kernels, local(): pl.pallas_call(final_kernel, out_shape=jax.ShapeDtypeStruct((row_count, p...  14.7 us
    ppermute x9, waiting for transfers between devices, around(): parts = [value] + [lax.ppermute(value, axis, perm_of(d)) for d in (1, 2, 3)]  11.7 us
    pallas_call x2, Pallas kernels, gram(): pl.pallas_call(functools.partial(gram_kernel, half, base is not None), ou...  11.5 us
    ppermute x10, starting transfers between devices, swap(): return lax.ppermute(value, 'vec', z_perm(0, 1))  11.4 us
    ppermute x9, starting transfers between devices, around(): parts = [value] + [lax.ppermute(value, axis, perm_of(d)) for d in (1, 2, 3)]  8.58 us
  transfers between devices with their start and end apart: 29, of which 13 were waited for; matrix products, arithmetic and copies ran while one was open for 8% of the time, Pallas kernels for 27%

profile of v7, /device:TPU:1, one launch (start us, length us, event | category | flops | bytes accessed | tf_op | source)
XLA Modules:
  0.0 168.2 jit_solution(6679716537766774032)
XLA Ops:
  0.0 1.4 constant_dynamic-slice_fusion.10
  1.4 5.8 %collective-permute-start = (bf16[40,128,128]{2,1,0:T(8,128)(2,1)S(1)}, bf16[40,128,128]{2,1,0:T(8,128)(2,1)}, u32[]{:S(2)}, u32[]{:S(2)}) collective-permute-start(bf16[40,128,128]{2,1,0:T(8,128)(2,1)S(1)} %constant_dynamic-slice_fusion.10), channel_id=1, source_target_pairs={{0,8},{1,121},{2,10},{3,123},{4,12},{5,125},{6,14},{7,127},{8,16},... | collective-permute-start | bytes 3932168 | tf_op jit(solution)/shard_map/ppermute | solution.py:331
  8.0 0.1 copy.18
  8.1 0.6 fusion.4
  8.7 1.2 fusion.3
  10.1 4.8 %collective-permute-start.2 = (bf16[13,128,128]{2,1,0:T(8,128)(2,1)S(1)}, bf16[13,128,128]{2,1,0:T(8,128)(2,1)S(1)}, u32[]{:S(2)}, u32[]{:S(2)}) collective-permute-start(bf16[13,128,128]{2,1,0:T(8,128)(2,1)S(1)} %pad_maximum_fusion.5), channel_id=1, source_target_pairs={{0,120},{8,0},{16,8},{24,16},{32,24},{40,32},{48,40},{56,48},{64,5... | collective-permute-start | bytes 1277960 | tf_op jit(solution)/shard_map/ppermute | solution.py:341
  14.9 16.9 %inner_filter.1 = bf16[40,128,128]{2,1,0:T(8,128)(2,1)} custom-call(s32[64,8]{1,0:T(8,128)} %get-tuple-element.51.facts, bf16[64,4,128,128]{3,2,1,0:T(8,128)(2,1)} %tiles.1, bf16[64,128,128]{2,1,0:T(8,128)(2,1)} %bitcast.35), custom_call_target="tpu_custom_call" | custom-call | flops 1000000 | bytes 1048576 | tf_op jit(solution)/shard_map/inner_filter/pallas_call | solution.py:350
  31.9 1.2 collective-permute-start.3
  33.1 1.4 constant_dynamic-slice_fusion.1
  34.4 0.3 collective-permute-start.4
  34.8 0.1 copy.21
  35.0 1.0 collective-permute-done.3.refs_1_
  35.9 1.0 constant_dynamic-slice_fusion
  37.0 1.1 pad_maximum_fusion
  38.1 1.7 %collective-permute-start.5 = (bf16[5120,128]{1,0:T(8,128)(2,1)}, bf16[5120,128]{1,0:T(8,128)(2,1)S(1)}, u32[]{:S(2)}, u32[]{:S(2)}) collective-permute-start(bf16[5120,128]{1,0:T(8,128)(2,1)} %pad_maximum_fusion), channel_id=1, source_target_pairs={{0,6},{1,3},{2,0},{3,5},{4,2},{5,7},{6,4},{7,1},{8,14},{9,11},{10,... | collective-permute-start | bytes 3932168 | tf_op jit(solution)/shard_map/ppermute | solution.py:396
  39.9 0.1 copy.23
  40.0 0.7 multiply_add_fusion.facts
  40.7 17.3 %edge_filter.1 = bf16[24,128,128]{2,1,0:T(8,128)(2,1)} custom-call(s32[64,8]{1,0:T(8,128)} %multiply_add_fusion.facts, s32[1]{0:T(128)} %bitcast.3.core, bf16[256,128,128]{2,1,0:T(8,128)(2,1)} %bitcast.32, bf16[64,128,128]{2,1,0:T(8,128)(2,1)} %bitcast.36, bf16[40,128,128]{2,1,0:T(8,128)(2,1)} %collective-permute-done.near, ...), custom_call_target="tpu_custom_call" | custom-call | flops 8000000000 | bytes 11534336 | tf_op jit(solution)/shard_map/edge_filter/pallas_call | solution.py:436
  58.0 2.9 %collective-permute-start.8 = (bf16[3072,128]{1,0:T(8,128)(2,1)}, bf16[3072,128]{1,0:T(8,128)(2,1)S(1)}, u32[]{:S(2)}, u32[]{:S(2)}) collective-permute-start(bf16[3072,128]{1,0:T(8,128)(2,1)} %bitcast.39), channel_id=1, source_target_pairs={{0,1},{1,0},{2,3},{3,2},{4,5},{5,4},{6,7},{7,6},{8,9},{9,8},{10,11... | collective-permute-start | bytes 2359304 | tf_op jit(solution)/shard_map/ppermute | solution.py:305
  60.8 1.0 constant_dynamic-slice_fusion.5
  61.9 0.1 dynamic-slice_dynamic-update-slice_fusion.2
  62.0 1.4 copy-done.10
  63.6 1.0 pad_maximum_fusion.2
  64.6 0.2 collective-permute-start.9
  64.8 9.4 %collective-permute-done.7 = bf16[2560,128]{1,0:T(8,128)(2,1)} collective-permute-done((bf16[2560,128]{1,0:T(8,128)(2,1)S(1)}, bf16[2560,128]{1,0:T(8,128)(2,1)}, u32[]{:S(2)}, u32[]{:S(2)}) %collective-permute-start.7) | collective-permute-done | bytes 655392 | tf_op jit(solution)/shard_map/ppermute | solution.py:396
  74.2 0.5 collective-permute-start.6
  74.8 0.6 pad_add_fusion.2.place
  75.3 7.2 %collective-permute-done.9 = bf16[3072,128]{1,0:T(8,128)(2,1)S(1)} collective-permute-done((bf16[3072,128]{1,0:T(8,128)(2,1)}, bf16[3072,128]{1,0:T(8,128)(2,1)S(1)}, u32[]{:S(2)}, u32[]{:S(2)}) %collective-permute-start.9) | collective-permute-done | bytes 786464 | tf_op jit(solution)/shard_map/ppermute | solution.py:396
  82.8 1.2 pad_maximum_fusion.1
  83.9 0.9 collective-permute-done.11
  84.9 0.9 copy-done.7
  85.7 6.3 %gram.2.refs_0_ = f32[128,1024]{1,0:T(8,128)} custom-call(s32[4]{0:T(128)} %pad_add_fusion.2.place, bf16[5120,128]{1,0:T(8,128)(2,1)} %bitcast.29, bf16[5120,128]{1,0:T(8,128)(2,1)} %copy-done, bf16[2,2560,128]{2,1,0:T(8,128)(2,1)} %bitcast.33, bf16[2,2560,128]{2,1,0:T(8,128)(2,1)} %bitcast.13.refs_3_, bf16[2,1280,128]{2,1,0:T(8,128)(2,1)} %bitcast.17.refs_4_, ...), custom_call_target="tpu_custom_call" | custom-call | flops 671088640 | bytes 7864320 | tf_op jit(solution)/shard_map/gram/pallas_call | solution.py:415
  92.1 1.6 collective-permute-start.13
  93.7 0.7 dynamic-slice_dynamic-update-slice_fusion.5
  94.4 0.7 dynamic-slice_dynamic-update-slice_fusion.4
  95.1 0.2 collective-permute-done.13
  95.2 0.7 copy-done.8
  96.0 5.2 %gram.3 = bf16[128,1024]{1,0:T(8,128)(2,1)} custom-call(s32[4]{0:T(128)} %pad_add_fusion.2.place, f32[128,1024]{1,0:T(8,128)} %gram.2.refs_0_, bf16[3072,128]{1,0:T(8,128)(2,1)} %bitcast.41, bf16[3072,128]{1,0:T(8,128)(2,1)} %copy-done.4, bf16[2,1536,128]{2,1,0:T(8,128)(2,1)} %bitcast.37, bf16[2,1536,128]{2,1,0:T(8,128)(2,1)} %bitcast.47, ...), custom_call_target="tpu_custom_call" | custom-call | flops 402653184 | bytes 4718592 | tf_op jit(solution)/shard_map/gram/pallas_call | solution.py:415
  101.2 4.5 %all-to-all-start = ((bf16[16,8,1024]{2,1,0:T(8,128)(2,1)}), bf16[16,8,1024]{2,1,0:T(8,128)(2,1)S(1)}, u32[]{:S(2)}, u32[]{:S(2)}) async-start(bf16[16,8,1024]{2,1,0:T(8,128)(2,1)} %bitcast.46), calls=%async_computation | async-start | bytes 524288 | tf_op jit(solution)/shard_map/all_to_all | solution.py:470
  105.8 0.8 dynamic-slice_dynamic-update-slice_fusion.1
  106.6 0.8 dynamic-slice_dynamic-update-slice_fusion
  107.4 6.0 %all-to-all-done = bf16[16,8,1024]{2,1,0:T(8,128)(2,1)S(1)} async-done(((bf16[16,8,1024]{2,1,0:T(8,128)(2,1)}), bf16[16,8,1024]{2,1,0:T(8,128)(2,1)S(1)}, u32[]{:S(2)}, u32[]{:S(2)}) %all-to-all-start) | async-done | bytes 262176 | tf_op jit(solution)/shard_map/all_to_all | solution.py:470
  113.4 0.9 collective-permute-start.17
  114.3 2.1 %collective-permute-start.16 = (bf16[1,8,1024]{2,1,0:T(8,128)(2,1)S(1)}, bf16[1,8,1024]{2,1,0:T(8,128)(2,1)S(1)}, u32[]{:S(2)}, u32[]{:S(2)}) collective-permute-start(bf16[1,8,1024]{2,1,0:T(8,128)(2,1)S(1)} %bitcast.52), channel_id=1, source_target_pairs={{0,4},{1,5},{2,6},{3,7},{4,0},{5,1},{6,2},{7,3},{8,12},{9,13},{10,... | collective-permute-start | bytes 49160 | tf_op jit(solution)/shard_map/ppermute | solution.py:477
  116.3 1.0 collective-permute-start.15
  117.3 2.8 %collective-permute-start.21 = (bf16[5120,128]{1,0:T(8,128)(2,1)}, bf16[5120,128]{1,0:T(8,128)(2,1)S(1)}, u32[]{:S(2)}, u32[]{:S(2)}) collective-permute-start(bf16[5120,128]{1,0:T(8,128)(2,1)} %collective-permute-done.14.refs_12_), channel_id=1, source_target_pairs={{0,1},{1,0},{2,3},{3,2},{4,5},{5,4},{6,7},{7,6},{8,9},{9,8},{10,11... | collective-permute-start | bytes 3932168 | tf_op jit(solution)/shard_map/ppermute | solution.py:305
  120.1 0.3 collective-permute-start.26
  120.5 0.7 collective-permute-start.18
  121.1 0.8 collective-permute-start.20
  121.9 1.2 collective-permute-start.19
  123.1 0.5 collective-permute-done.18
  123.6 3.0 %collective-permute-done.19 = bf16[4,8,1024]{2,1,0:T(8,128)(2,1)S(1)} collective-permute-done((bf16[4,8,1024]{2,1,0:T(8,128)(2,1)S(1)}, bf16[4,8,1024]{2,1,0:T(8,128)(2,1)S(1)}, u32[]{:S(2)}, u32[]{:S(2)}) %collective-permute-start.19) | collective-permute-done | bytes 65568 | tf_op jit(solution)/shard_map/ppermute | solution.py:477
  126.6 0.8 collective-permute-start.22
  127.4 1.0 collective-permute-start.23
  128.4 0.2 collective-permute-start.24
  128.6 3.6 %collective-permute-done.22 = bf16[16,8,1024]{2,1,0:T(8,128)(2,1)S(1)} collective-permute-done((bf16[16,8,1024]{2,1,0:T(8,128)(2,1)S(1)}, bf16[16,8,1024]{2,1,0:T(8,128)(2,1)S(1)}, u32[]{:S(2)}, u32[]{:S(2)}) %collective-permute-start.22) | collective-permute-done | bytes 262176 | tf_op jit(solution)/shard_map/ppermute | solution.py:477
  132.2 2.0 %collective-permute-done.23 = bf16[16,8,1024]{2,1,0:T(8,128)(2,1)S(1)} collective-permute-done((bf16[16,8,1024]{2,1,0:T(8,128)(2,1)S(1)}, bf16[16,8,1024]{2,1,0:T(8,128)(2,1)S(1)}, u32[]{:S(2)}, u32[]{:S(2)}) %collective-permute-start.23) | collective-permute-done | bytes 262176 | tf_op jit(solution)/shard_map/ppermute | solution.py:477
  134.3 2.7 %collective-permute-done.24 = bf16[16,8,1024]{2,1,0:T(8,128)(2,1)S(1)} collective-permute-done((bf16[16,8,1024]{2,1,0:T(8,128)(2,1)S(1)}, bf16[16,8,1024]{2,1,0:T(8,128)(2,1)S(1)}, u32[]{:S(2)}, u32[]{:S(2)}) %collective-permute-start.24) | collective-permute-done | bytes 262176 | tf_op jit(solution)/shard_map/ppermute | solution.py:477
  137.0 7.0 %collective-permute-done.26.refs_14_ = bf16[7168,128]{1,0:T(8,128)(2,1)S(1)} collective-permute-done((bf16[7168,128]{1,0:T(8,128)(2,1)}, bf16[7168,128]{1,0:T(8,128)(2,1)S(1)}, u32[]{:S(2)}, u32[]{:S(2)}) %collective-permute-start.26) | collective-permute-done | bytes 1835040 | tf_op jit(solution)/shard_map/ppermute | solution.py:396
  144.0 2.2 %collective-permute-start.27 = (bf16[7168,128]{1,0:T(8,128)(2,1)S(1)}, bf16[7168,128]{1,0:T(8,128)(2,1)S(1)}, u32[]{:S(2)}, u32[]{:S(2)}) collective-permute-start(bf16[7168,128]{1,0:T(8,128)(2,1)S(1)} %collective-permute-done.26.refs_14_), channel_id=1, source_target_pairs={{0,1},{1,0},{2,3},{3,2},{4,5},{5,4},{6,7},{7,6},{8,9},{9,8},{10,11... | collective-permute-start | bytes 5505032 | tf_op jit(solution)/shard_map/ppermute | solution.py:305
  146.9 4.3 %collective-permute-done.25.gathered_twin = bf16[64,8,1024]{2,1,0:T(8,128)(2,1)S(1)} collective-permute-done((bf16[64,8,1024]{2,1,0:T(8,128)(2,1)S(1)}, bf16[64,8,1024]{2,1,0:T(8,128)(2,1)S(1)}, u32[]{:S(2)}, u32[]{:S(2)}) %collective-permute-start.25) | collective-permute-done | bytes 1048608 | tf_op jit(solution)/shard_map/ppermute | solution.py:305
  151.1 1.0 copy-done.17
  152.1 1.2 copy-done.15
  153.3 14.7 %final.1 = bf16[8192,128]{1,0:T(8,128)(2,1)} custom-call(s32[4]{0:T(128)} %pad_add_fusion.2.place, f32[1]{0:T(128)S(6)} %copy.42.scale_in, bf16[64,8,1024]{2,1,0:T(8,128)(2,1)} %copy-done.9, bf16[64,8,1024]{2,1,0:T(8,128)(2,1)} %copy-done.17, bf16[5120,128]{1,0:T(8,128)(2,1)} %bitcast.30, bf16[5120,128]{1,0:T(8,128)(2,1)} %copy-done, ...), custom_call_target="tpu_custom_call" | custom-call | flops 6000000000 | bytes 20971520 | tf_op jit(solution)/shard_map/final/pallas_call | solution.py:505
  (87 shorter events, 1.1 us)
Async XLA Ops:
  0.0 7.9 %copy-start.11 = (s32[64,4]{0,1:T(4,128)S(1)}, s32[64,4]{0,1:T(4,128)}, u32[]{:S(2)}) copy-start(s32[64,4]{0,1:T(4,128)} %param.6) | copy-start | bytes 3076
  1.4 30.5 %collective-permute-start = (bf16[40,128,128]{2,1,0:T(8,128)(2,1)S(1)}, bf16[40,128,128]{2,1,0:T(8,128)(2,1)}, u32[]{:S(2)}, u32[]{:S(2)}) collective-permute-start(bf16[40,128,128]{2,1,0:T(8,128)(2,1)S(1)} %constant_dynamic-slice_fusion.10), channel_id=1, source_target_pairs={{0,8},{1,121},{2,10},{3,123},{4,12},{5,125},{6,14},{7,127},{8,16},... | collective-permute-start | bytes 3932168 | tf_op jit(solution)/shard_map/ppermute | solution.py:331
  9.9 21.9 %collective-permute-start.1 = (bf16[13,128,128]{2,1,0:T(8,128)(2,1)S(1)}, bf16[13,128,128]{2,1,0:T(8,128)(2,1)S(1)}, u32[]{:S(2)}, u32[]{:S(2)}) collective-permute-start(bf16[13,128,128]{2,1,0:T(8,128)(2,1)S(1)} %pad_maximum_fusion.4), channel_id=1, source_target_pairs={{0,8},{8,16},{16,24},{24,32},{32,40},{40,48},{48,56},{56,64},{64,7... | collective-permute-start | bytes 1277960 | tf_op jit(solution)/shard_map/ppermute | solution.py:338
  10.1 21.8 %collective-permute-start.2 = (bf16[13,128,128]{2,1,0:T(8,128)(2,1)S(1)}, bf16[13,128,128]{2,1,0:T(8,128)(2,1)S(1)}, u32[]{:S(2)}, u32[]{:S(2)}) collective-permute-start(bf16[13,128,128]{2,1,0:T(8,128)(2,1)S(1)} %pad_maximum_fusion.5), channel_id=1, source_target_pairs={{0,120},{8,0},{16,8},{24,16},{32,24},{40,32},{48,40},{56,48},{64,5... | collective-permute-start | bytes 1277960 | tf_op jit(solution)/shard_map/ppermute | solution.py:341
  31.9 5.1 %copy-start.12 = (bf16[13,128,128]{2,1,0:T(8,128)(2,1)}, bf16[13,128,128]{2,1,0:T(8,128)(2,1)S(1)}, u32[]{:S(2)}) copy-start(bf16[13,128,128]{2,1,0:T(8,128)(2,1)S(1)} %collective-permute-done.1.vlow) | copy-start | bytes 1277956
  31.9 5.1 %copy-start.13 = (bf16[13,128,128]{2,1,0:T(8,128)(2,1)}, bf16[13,128,128]{2,1,0:T(8,128)(2,1)S(1)}, u32[]{:S(2)}) copy-start(bf16[13,128,128]{2,1,0:T(8,128)(2,1)S(1)} %collective-permute-done.2.vhigh) | copy-start | bytes 1277956
  31.9 4.0 %collective-permute-start.3 = (bf16[5120,128]{1,0:T(8,128)(2,1)}, bf16[5120,128]{1,0:T(8,128)(2,1)S(1)}, u32[]{:S(2)}, u32[]{:S(2)}) collective-permute-start(bf16[5120,128]{1,0:T(8,128)(2,1)} %bitcast.27), channel_id=1, source_target_pairs={{0,1},{1,0},{2,3},{3,2},{4,5},{5,4},{6,7},{7,6},{8,9},{9,8},{10,11... | collective-permute-start | bytes 3932168 | tf_op jit(solution)/shard_map/ppermute | solution.py:305
  34.4 3.7 %collective-permute-start.4 = (bf16[40,128,128]{2,1,0:T(8,128)(2,1)}, bf16[40,128,128]{2,1,0:T(8,128)(2,1)}, u32[]{:S(2)}, u32[]{:S(2)}) collective-permute-start(bf16[40,128,128]{2,1,0:T(8,128)(2,1)} %collective-permute-done.near), channel_id=1, source_target_pairs={{0,1},{1,0},{2,3},{3,2},{4,5},{5,4},{6,7},{7,6},{8,9},{9,8},{10,11... | collective-permute-start | bytes 3932168 | tf_op jit(solution)/shard_map/ppermute | solution.py:305
  35.9 2.2 %copy-start = (bf16[5120,128]{1,0:T(8,128)(2,1)}, bf16[5120,128]{1,0:T(8,128)(2,1)S(1)}, u32[]{:S(2)}) copy-start(bf16[5120,128]{1,0:T(8,128)(2,1)S(1)} %collective-permute-done.3.refs_1_) | copy-start | bytes 3932164
  38.1 23.7 %collective-permute-start.5 = (bf16[5120,128]{1,0:T(8,128)(2,1)}, bf16[5120,128]{1,0:T(8,128)(2,1)S(1)}, u32[]{:S(2)}, u32[]{:S(2)}) collective-permute-start(bf16[5120,128]{1,0:T(8,128)(2,1)} %pad_maximum_fusion), channel_id=1, source_target_pairs={{0,6},{1,3},{2,0},{3,5},{4,2},{5,7},{6,4},{7,1},{8,14},{9,11},{10,... | collective-permute-start | bytes 3932168 | tf_op jit(solution)/shard_map/ppermute | solution.py:396
  58.0 5.5 %collective-permute-start.8 = (bf16[3072,128]{1,0:T(8,128)(2,1)}, bf16[3072,128]{1,0:T(8,128)(2,1)S(1)}, u32[]{:S(2)}, u32[]{:S(2)}) collective-permute-start(bf16[3072,128]{1,0:T(8,128)(2,1)} %bitcast.39), channel_id=1, source_target_pairs={{0,1},{1,0},{2,3},{3,2},{4,5},{5,4},{6,7},{7,6},{8,9},{9,8},{10,11... | collective-permute-start | bytes 2359304 | tf_op jit(solution)/shard_map/ppermute | solution.py:305
  61.8 12.4 %copy-start.1 = (bf16[5120,128]{1,0:T(8,128)(2,1)}, bf16[5120,128]{1,0:T(8,128)(2,1)S(1)}, u32[]{:S(2)}) copy-start(bf16[5120,128]{1,0:T(8,128)(2,1)S(1)} %collective-permute-done.5) | copy-start | bytes 3932164
  62.0 1.4 copy-start.10
  63.4 10.8 %collective-permute-start.7 = (bf16[2560,128]{1,0:T(8,128)(2,1)S(1)}, bf16[2560,128]{1,0:T(8,128)(2,1)}, u32[]{:S(2)}, u32[]{:S(2)}) collective-permute-start(bf16[2560,128]{1,0:T(8,128)(2,1)S(1)} %pad_maximum_fusion.3), channel_id=1, source_target_pairs={{0,6},{1,3},{2,0},{3,5},{4,2},{5,7},{6,4},{7,1},{8,14},{9,11},{10,... | collective-permute-start | bytes 1966088 | tf_op jit(solution)/shard_map/ppermute | solution.py:396
  63.5 19.1 %copy-start.4 = (bf16[3072,128]{1,0:T(8,128)(2,1)}, bf16[3072,128]{1,0:T(8,128)(2,1)S(1)}, u32[]{:S(2)}) copy-start(bf16[3072,128]{1,0:T(8,128)(2,1)S(1)} %collective-permute-done.8.refs_2_.refs_7_) | copy-start | bytes 2359300
  64.6 18.0 %collective-permute-start.9 = (bf16[3072,128]{1,0:T(8,128)(2,1)}, bf16[3072,128]{1,0:T(8,128)(2,1)S(1)}, u32[]{:S(2)}, u32[]{:S(2)}) collective-permute-start(bf16[3072,128]{1,0:T(8,128)(2,1)} %pad_maximum_fusion.2), channel_id=1, source_target_pairs={{0,6},{1,3},{2,0},{3,5},{4,2},{5,7},{6,4},{7,1},{8,14},{9,11},{10,... | collective-permute-start | bytes 2359304 | tf_op jit(solution)/shard_map/ppermute | solution.py:396
  74.2 8.3 %collective-permute-start.10 = (bf16[2560,128]{1,0:T(8,128)(2,1)}, bf16[2560,128]{1,0:T(8,128)(2,1)}, u32[]{:S(2)}, u32[]{:S(2)}) collective-permute-start(bf16[2560,128]{1,0:T(8,128)(2,1)} %collective-permute-done.7), channel_id=1, source_target_pairs={{0,1},{1,0},{2,3},{3,2},{4,5},{5,4},{6,7},{7,6},{8,9},{9,8},{10,11... | collective-permute-start | bytes 1966088 | tf_op jit(solution)/shard_map/ppermute | solution.py:305
  74.2 10.6 %collective-permute-start.6 = (bf16[5120,128]{1,0:T(8,128)(2,1)S(1)}, bf16[5120,128]{1,0:T(8,128)(2,1)}, u32[]{:S(2)}, u32[]{:S(2)}) collective-permute-start(bf16[5120,128]{1,0:T(8,128)(2,1)S(1)} %collective-permute-done.5), channel_id=1, source_target_pairs={{0,1},{1,0},{2,3},{3,2},{4,5},{5,4},{6,7},{7,6},{8,9},{9,8},{10,11... | collective-permute-start | bytes 3932168 | tf_op jit(solution)/shard_map/ppermute | solution.py:305
  74.8 8.0 %copy-start.6 = (bf16[2560,128]{1,0:T(8,128)(2,1)S(1)}, bf16[2560,128]{1,0:T(8,128)(2,1)}, u32[]{:S(2)}) copy-start(bf16[2560,128]{1,0:T(8,128)(2,1)} %get-tuple-element.46) | copy-start | bytes 1966084
  82.6 11.8 %copy-start.2 = (bf16[3072,128]{1,0:T(8,128)(2,1)}, bf16[3072,128]{1,0:T(8,128)(2,1)S(1)}, u32[]{:S(2)}) copy-start(bf16[3072,128]{1,0:T(8,128)(2,1)S(1)} %collective-permute-done.9) | copy-start | bytes 2359300
  82.6 2.3 %collective-permute-start.11 = (bf16[3072,128]{1,0:T(8,128)(2,1)S(1)}, bf16[3072,128]{1,0:T(8,128)(2,1)S(1)}, u32[]{:S(2)}, u32[]{:S(2)}) collective-permute-start(bf16[3072,128]{1,0:T(8,128)(2,1)S(1)} %collective-permute-done.9), channel_id=1, source_target_pairs={{0,1},{1,0},{2,3},{3,2},{4,5},{5,4},{6,7},{7,6},{8,9},{9,8},{10,11... | collective-permute-start | bytes 2359304 | tf_op jit(solution)/shard_map/ppermute | solution.py:305
  82.7 9.4 %collective-permute-start.12 = (bf16[1536,128]{1,0:T(8,128)(2,1)S(1)}, bf16[1536,128]{1,0:T(8,128)(2,1)}, u32[]{:S(2)}, u32[]{:S(2)}) collective-permute-start(bf16[1536,128]{1,0:T(8,128)(2,1)S(1)} %pad_maximum_fusion.6), channel_id=1, source_target_pairs={{0,6},{1,3},{2,0},{3,5},{4,2},{5,7},{6,4},{7,1},{8,14},{9,11},{10,... | collective-permute-start | bytes 1179656 | tf_op jit(solution)/shard_map/ppermute | solution.py:396
  84.8 0.9 copy-start.7
  92.0 21.4 %collective-permute-start.14 = (bf16[5120,128]{1,0:T(8,128)(2,1)}, bf16[5120,128]{1,0:T(8,128)(2,1)}, u32[]{:S(2)}, u32[]{:S(2)}) collective-permute-start(bf16[5120,128]{1,0:T(8,128)(2,1)} %pad_maximum_fusion.1), channel_id=1, source_target_pairs={{0,6},{1,3},{2,0},{3,5},{4,2},{5,7},{6,4},{7,1},{8,14},{9,11},{10,... | collective-permute-start | bytes 3932168 | tf_op jit(solution)/shard_map/ppermute | solution.py:396
  92.1 3.1 %collective-permute-start.13 = (bf16[1536,128]{1,0:T(8,128)(2,1)}, bf16[1536,128]{1,0:T(8,128)(2,1)S(1)}, u32[]{:S(2)}, u32[]{:S(2)}) collective-permute-start(bf16[1536,128]{1,0:T(8,128)(2,1)} %collective-permute-done.12), channel_id=1, source_target_pairs={{0,1},{1,0},{2,3},{3,2},{4,5},{5,4},{6,7},{7,6},{8,9},{9,8},{10,11... | collective-permute-start | bytes 1179656 | tf_op jit(solution)/shard_map/ppermute | solution.py:305
  95.2 0.8 copy-start.8
  96.0 9.8 %copy-start.3 = (bf16[24,128,128]{2,1,0:T(8,128)(2,1)S(1)}, bf16[24,128,128]{2,1,0:T(8,128)(2,1)}, u32[]{:S(2)}) copy-start(bf16[24,128,128]{2,1,0:T(8,128)(2,1)} %edge_filter.1) | copy-start | bytes 2359300
  96.0 10.6 %copy-start.5 = (bf16[3072,128]{1,0:T(8,128)(2,1)S(1)}, bf16[3072,128]{1,0:T(8,128)(2,1)}, u32[]{:S(2)}) copy-start(bf16[3072,128]{1,0:T(8,128)(2,1)} %copy-done.4) | copy-start | bytes 2359300
  101.2 12.1 %all-to-all-start = ((bf16[16,8,1024]{2,1,0:T(8,128)(2,1)}), bf16[16,8,1024]{2,1,0:T(8,128)(2,1)S(1)}, u32[]{:S(2)}, u32[]{:S(2)}) async-start(bf16[16,8,1024]{2,1,0:T(8,128)(2,1)} %bitcast.46), calls=%async_computation | async-start | bytes 524288 | tf_op jit(solution)/shard_map/all_to_all | solution.py:470
  113.4 6.7 %collective-permute-start.17 = (bf16[1,8,1024]{2,1,0:T(8,128)(2,1)S(1)}, bf16[1,8,1024]{2,1,0:T(8,128)(2,1)S(1)}, u32[]{:S(2)}, u32[]{:S(2)}) collective-permute-start(bf16[1,8,1024]{2,1,0:T(8,128)(2,1)S(1)} %bitcast.51), channel_id=1, source_target_pairs={{0,2},{1,3},{2,4},{3,5},{4,6},{5,7},{6,0},{7,1},{8,10},{9,11},{10,... | collective-permute-start | bytes 49160 | tf_op jit(solution)/shard_map/ppermute | solution.py:477
  114.3 5.8 %collective-permute-start.16 = (bf16[1,8,1024]{2,1,0:T(8,128)(2,1)S(1)}, bf16[1,8,1024]{2,1,0:T(8,128)(2,1)S(1)}, u32[]{:S(2)}, u32[]{:S(2)}) collective-permute-start(bf16[1,8,1024]{2,1,0:T(8,128)(2,1)S(1)} %bitcast.52), channel_id=1, source_target_pairs={{0,4},{1,5},{2,6},{3,7},{4,0},{5,1},{6,2},{7,3},{8,12},{9,13},{10,... | collective-permute-start | bytes 49160 | tf_op jit(solution)/shard_map/ppermute | solution.py:477
  116.3 3.7 %collective-permute-start.15 = (bf16[1,8,1024]{2,1,0:T(8,128)(2,1)S(1)}, bf16[1,8,1024]{2,1,0:T(8,128)(2,1)S(1)}, u32[]{:S(2)}, u32[]{:S(2)}) collective-permute-start(bf16[1,8,1024]{2,1,0:T(8,128)(2,1)S(1)} %bitcast.53), channel_id=1, source_target_pairs={{0,6},{1,7},{2,0},{3,1},{4,2},{5,3},{6,4},{7,5},{8,14},{9,15},{10,... | collective-permute-start | bytes 49160 | tf_op jit(solution)/shard_map/ppermute | solution.py:477
  117.3 9.2 %collective-permute-start.21 = (bf16[5120,128]{1,0:T(8,128)(2,1)}, bf16[5120,128]{1,0:T(8,128)(2,1)S(1)}, u32[]{:S(2)}, u32[]{:S(2)}) collective-permute-start(bf16[5120,128]{1,0:T(8,128)(2,1)} %collective-permute-done.14.refs_12_), channel_id=1, source_target_pairs={{0,1},{1,0},{2,3},{3,2},{4,5},{5,4},{6,7},{7,6},{8,9},{9,8},{10,11... | collective-permute-start | bytes 3932168 | tf_op jit(solution)/shard_map/ppermute | solution.py:305
  120.1 23.9 %collective-permute-start.26 = (bf16[7168,128]{1,0:T(8,128)(2,1)}, bf16[7168,128]{1,0:T(8,128)(2,1)S(1)}, u32[]{:S(2)}, u32[]{:S(2)}) collective-permute-start(bf16[7168,128]{1,0:T(8,128)(2,1)} %dynamic-slice_dynamic-update-slice_fusion), channel_id=1, source_target_pairs={{0,6},{1,3},{2,0},{3,5},{4,2},{5,7},{6,4},{7,1},{8,14},{9,11},{10,... | collective-permute-start | bytes 5505032 | tf_op jit(solution)/shard_map/ppermute | solution.py:396
  120.5 3.1 %collective-permute-start.18 = (bf16[4,8,1024]{2,1,0:T(8,128)(2,1)S(1)}, bf16[4,8,1024]{2,1,0:T(8,128)(2,1)S(1)}, u32[]{:S(2)}, u32[]{:S(2)}) collective-permute-start(bf16[4,8,1024]{2,1,0:T(8,128)(2,1)S(1)} %get-tuple-element.52), channel_id=1, source_target_pairs={{0,24},{8,0},{16,8},{24,16},{32,56},{40,32},{48,40},{56,48},{64,88... | collective-permute-start | bytes 196616 | tf_op jit(solution)/shard_map/ppermute | solution.py:477
  121.1 5.4 %collective-permute-start.20 = (bf16[4,8,1024]{2,1,0:T(8,128)(2,1)S(1)}, bf16[4,8,1024]{2,1,0:T(8,128)(2,1)S(1)}, u32[]{:S(2)}, u32[]{:S(2)}) collective-permute-start(bf16[4,8,1024]{2,1,0:T(8,128)(2,1)S(1)} %get-tuple-element.52), channel_id=1, source_target_pairs={{0,8},{8,16},{16,24},{24,0},{32,40},{40,48},{48,56},{56,32},{64,72... | collective-permute-start | bytes 196616 | tf_op jit(solution)/shard_map/ppermute | solution.py:477
  121.9 4.6 %collective-permute-start.19 = (bf16[4,8,1024]{2,1,0:T(8,128)(2,1)S(1)}, bf16[4,8,1024]{2,1,0:T(8,128)(2,1)S(1)}, u32[]{:S(2)}, u32[]{:S(2)}) collective-permute-start(bf16[4,8,1024]{2,1,0:T(8,128)(2,1)S(1)} %get-tuple-element.52), channel_id=1, source_target_pairs={{0,16},{8,24},{16,0},{24,8},{32,48},{40,56},{48,32},{56,40},{64,80... | collective-permute-start | bytes 196616 | tf_op jit(solution)/shard_map/ppermute | solution.py:477
  126.6 25.5 %copy-start.16 = (bf16[5120,128]{1,0:T(8,128)(2,1)}, bf16[5120,128]{1,0:T(8,128)(2,1)S(1)}, u32[]{:S(2)}) copy-start(bf16[5120,128]{1,0:T(8,128)(2,1)S(1)} %collective-permute-done.21.refs_13_) | copy-start | bytes 3932164
  126.6 5.6 %collective-permute-start.22 = (bf16[16,8,1024]{2,1,0:T(8,128)(2,1)S(1)}, bf16[16,8,1024]{2,1,0:T(8,128)(2,1)S(1)}, u32[]{:S(2)}, u32[]{:S(2)}) collective-permute-start(bf16[16,8,1024]{2,1,0:T(8,128)(2,1)S(1)} %constant_dynamic-update-slice_fusion.4), channel_id=1, source_target_pairs={{0,96},{8,104},{16,112},{24,120},{32,0},{40,8},{48,16},{56,24},{64... | collective-permute-start | bytes 786440 | tf_op jit(solution)/shard_map/ppermute | solution.py:477
  127.4 6.8 %collective-permute-start.23 = (bf16[16,8,1024]{2,1,0:T(8,128)(2,1)S(1)}, bf16[16,8,1024]{2,1,0:T(8,128)(2,1)S(1)}, u32[]{:S(2)}, u32[]{:S(2)}) collective-permute-start(bf16[16,8,1024]{2,1,0:T(8,128)(2,1)S(1)} %constant_dynamic-update-slice_fusion.4), channel_id=1, source_target_pairs={{0,64},{8,72},{16,80},{24,88},{32,96},{40,104},{48,112},{56,120},{... | collective-permute-start | bytes 786440 | tf_op jit(solution)/shard_map/ppermute | solution.py:477
  128.4 8.6 %collective-permute-start.24 = (bf16[16,8,1024]{2,1,0:T(8,128)(2,1)S(1)}, bf16[16,8,1024]{2,1,0:T(8,128)(2,1)S(1)}, u32[]{:S(2)}, u32[]{:S(2)}) collective-permute-start(bf16[16,8,1024]{2,1,0:T(8,128)(2,1)S(1)} %constant_dynamic-update-slice_fusion.4), channel_id=1, source_target_pairs={{0,32},{8,40},{16,48},{24,56},{32,64},{40,72},{48,80},{56,88},{64,... | collective-permute-start | bytes 786440 | tf_op jit(solution)/shard_map/ppermute | solution.py:477
  137.0 15.1 %copy-start.9 = (bf16[64,8,1024]{2,1,0:T(8,128)(2,1)}, bf16[64,8,1024]{2,1,0:T(8,128)(2,1)S(1)}, u32[]{:S(2)}) copy-start(bf16[64,8,1024]{2,1,0:T(8,128)(2,1)S(1)} %constant_dynamic-update-slice_fusion.11.gathered) | copy-start | bytes 3145732
  144.0 8.1 %copy-start.14 = (bf16[7168,128]{1,0:T(8,128)(2,1)}, bf16[7168,128]{1,0:T(8,128)(2,1)S(1)}, u32[]{:S(2)}) copy-start(bf16[7168,128]{1,0:T(8,128)(2,1)S(1)} %collective-permute-done.26.refs_14_) | copy-start | bytes 5505028
  144.0 8.1 %collective-permute-start.27 = (bf16[7168,128]{1,0:T(8,128)(2,1)S(1)}, bf16[7168,128]{1,0:T(8,128)(2,1)S(1)}, u32[]{:S(2)}, u32[]{:S(2)}) collective-permute-start(bf16[7168,128]{1,0:T(8,128)(2,1)S(1)} %collective-permute-done.26.refs_14_), channel_id=1, source_target_pairs={{0,1},{1,0},{2,3},{3,2},{4,5},{5,4},{6,7},{7,6},{8,9},{9,8},{10,11... | collective-permute-start | bytes 5505032 | tf_op jit(solution)/shard_map/ppermute | solution.py:305
  146.2 4.9 %collective-permute-start.25 = (bf16[64,8,1024]{2,1,0:T(8,128)(2,1)S(1)}, bf16[64,8,1024]{2,1,0:T(8,128)(2,1)S(1)}, u32[]{:S(2)}, u32[]{:S(2)}) collective-permute-start(bf16[64,8,1024]{2,1,0:T(8,128)(2,1)S(1)} %constant_dynamic-update-slice_fusion.11.gathered), channel_id=1, source_target_pairs={{0,1},{1,0},{2,3},{3,2},{4,5},{5,4},{6,7},{7,6},{8,9},{9,8},{10,11... | collective-permute-start | bytes 3145736 | tf_op jit(solution)/shard_map/ppermute | solution.py:305
  151.1 1.0 copy-start.17
  152.1 1.2 copy-start.15
